TPU v7x, 512 devices: a whole 4x4x16 slice. The times are simulated.
512 devices in a mesh: seq: 32 (over y, z_lo), batch: 16 (over z_hi, x, core).
Axes of the slice: x: 4, y: 4, z: 16 (z_hi: 2, z_lo: 8; z = z_hi * 8 + z_lo), core: 2. Of those that a mesh axis runs over, the one named last changes fastest.
Arguments:
- activations: bfloat16 [16, 16384, 768], P('batch', 'seq'), may hold values from -96 to 96
- norm_gain: float32 [768], replicated, may hold values from 0.25 to 1.75
- dilated_tap_weight: bfloat16 [3, 768, 384], replicated, may hold values from -0.125 to 0.125
- point_weight: bfloat16 [384, 768], replicated, may hold values from -0.15625 to 0.15625
- donor_weight: bfloat16 [768, 256], replicated, may hold values from -0.013671875 to 0.013671875
- acceptor_weight: bfloat16 [768, 256], replicated, may hold values from -0.013671875 to 0.013671875
- pair_sites: int32 [16, 512, 2], P('batch', 'seq'), may hold values from 0 to 16383, as said below
- pair_count: int32 [16, 32], P('batch', 'seq'), may hold values from 8 to 16, as said below
Outputs:
- grad_conv: float32 [3, 768, 384], P(None, 'seq')
- grad_point: bfloat16 [16, 384, 768], P('batch')
- grad_donor: bfloat16 [16, 768, 256], P('batch')
- grad_acceptor: bfloat16 [16, 768, 256], P('batch')
- grad_gain: float32 [16, 768], P('batch')
- loss: float32 [16], P('batch')
Inputs may be any that keep to these rules, and one draw needn't show every extreme that they name: `pair_sites`: slot j's donor position lies among the 512 positions of device j // 16; its acceptor lies on that device or on one of the next 4 devices, within the example; in every draw some live pair reaches exactly 4 devices ahead. The live slots of a device are its first pair_count slots; in every example some device has all 16 live.
All inputs are finite; a program needn't handle non-finite values.
Results may differ from a plain program's by a relative error of at most 0.018.
Values may be sent and summed in bfloat16 or wider, within the bound.
No kernel may reach another device: no remote copies, remote signals or barrier semaphores. Data moves between devices by JAX's collectives and lax.ppermute only.
A program may use at most 64 MiB of HBM per device.

v0:
```python
import jax
import jax.numpy as jnp
from jax import lax
from jax.sharding import PartitionSpec as P

DILATION_STEP = 128
PANEL = 128
SPAN = 4


EPSILON = 1e-06
LOSS_WEIGHT = 1.0 / 128.0


def padded(block, sides, width):
    for axis, dim in sides:
        count = lax.axis_size(axis)
        forward = [(i, i + 1) for i in range(count - 1)]
        backward = [(target, source) for source, target in forward]
        low = lax.ppermute(
            lax.slice_in_dim(block, block.shape[dim] - width, None, axis=dim), axis, forward
        )
        high = lax.ppermute(lax.slice_in_dim(block, 0, width, axis=dim), axis, backward)
        block = jnp.concatenate([low, block, high], axis=dim)
    return block


def shifted(block, axis, distance):
    devices = range(lax.axis_size(axis))
    route = [(i - distance, i) for i in devices if i - distance in devices]
    return lax.ppermute(block, axis, route)


def gelu_slope(values):
    return jax.vjp(jax.nn.gelu, values)[1](jnp.ones_like(values))[0]


def on_device(
    activations,
    norm_gain,
    dilated_tap_weight,
    point_weight,
    donor_weight,
    acceptor_weight,
    pair_sites,
    pair_count,
):
    tokens = activations[0]
    sequence_length, channels = tokens.shape
    tap_count = dilated_tap_weight.shape[0]
    inner = dilated_tap_weight.shape[2]
    heads = donor_weight.shape[1]
    scale = heads ** (-0.5)
    blocks = sequence_length // PANEL
    tokens_f = tokens.astype(jnp.float32)
    inv_rms = lax.rsqrt(jnp.mean(tokens_f * tokens_f, axis=-1, keepdims=True) + EPSILON)
    normed = tokens_f * inv_rms * norm_gain
    hidden_state = jax.nn.gelu(normed).astype(jnp.bfloat16)
    padded_input = padded(hidden_state, (("seq", 0),), DILATION_STEP)
    dilated_output = jnp.zeros((sequence_length, inner), jnp.float32)
    for tap_index in range(tap_count):
        dilated_output = dilated_output + jnp.dot(
            padded_input[tap_index * DILATION_STEP : tap_index * DILATION_STEP + sequence_length],
            dilated_tap_weight[tap_index],
            preferred_element_type=jnp.float32,
        )
    act = jax.nn.gelu(dilated_output).astype(jnp.bfloat16)
    embed = (tokens_f + jnp.dot(act, point_weight, preferred_element_type=jnp.float32)).astype(
        jnp.bfloat16
    )
    donor_feat = jnp.dot(embed, donor_weight, preferred_element_type=jnp.float32).astype(
        jnp.bfloat16
    )
    accept_feat = jnp.dot(embed, acceptor_weight, preferred_element_type=jnp.float32).astype(
        jnp.bfloat16
    )
    nearby = [accept_feat]
    for distance in range(1, SPAN + 1):
        nearby.append(shifted(accept_feat, "seq", -distance))
    accept_blocks = jnp.concatenate(nearby, axis=0).reshape((SPAN + 1) * blocks, PANEL, heads)
    donor_blocks = donor_feat.reshape(blocks, PANEL, heads)
    sites = pair_sites[0]
    slot_count = sites.shape[0]
    first_block = lax.axis_index("seq") * blocks
    donor_block = sites[:, 0] // PANEL - first_block
    accept_block = sites[:, 1] // PANEL - first_block
    donor_cell = sites[:, 0] % PANEL
    accept_cell = sites[:, 1] % PANEL
    live = (jnp.arange(slot_count, dtype=jnp.int32) < pair_count[0, 0]).astype(
        jnp.float32
    ) * LOSS_WEIGHT
    donor_panel = donor_blocks[donor_block]
    accept_panel = accept_blocks[accept_block]
    scores = (
        jnp.einsum("pqh,prh->pqr", donor_panel, accept_panel, preferred_element_type=jnp.float32)
        * scale
    )
    cells = jnp.arange(PANEL, dtype=jnp.int32)
    target = (
        (cells[None, :, None] == donor_cell[:, None, None])
        & (cells[None, None, :] == accept_cell[:, None, None])
    ).astype(jnp.float32)
    loss = jnp.sum((jax.nn.softplus(scores) - target * scores) * live[:, None, None])
    dscore = ((jax.nn.sigmoid(scores) - target) * live[:, None, None]).astype(jnp.bfloat16)
    d_donor_pairs = (
        jnp.einsum("pqr,prh->pqh", dscore, accept_panel, preferred_element_type=jnp.float32) * scale
    )
    d_accept_pairs = (
        jnp.einsum("pqr,pqh->prh", dscore, donor_panel, preferred_element_type=jnp.float32) * scale
    )
    donor_onehot = (donor_block[:, None] == jnp.arange(blocks, dtype=jnp.int32)[None, :]).astype(
        jnp.float32
    )
    accept_onehot = (
        accept_block[:, None] == jnp.arange((SPAN + 1) * blocks, dtype=jnp.int32)[None, :]
    ).astype(jnp.float32)
    d_donor = jnp.einsum("pb,pqh->bqh", donor_onehot, d_donor_pairs).reshape(sequence_length, heads)
    accept_terms = jnp.einsum("pb,pqh->bqh", accept_onehot, d_accept_pairs).reshape(
        SPAN + 1, sequence_length, heads
    )
    d_accept = accept_terms[0]
    for distance in range(1, SPAN + 1):
        d_accept = d_accept + shifted(accept_terms[distance], "seq", distance)
    d_donor = d_donor.astype(jnp.bfloat16)
    d_accept = d_accept.astype(jnp.bfloat16)
    d_embed = (
        jnp.dot(d_donor, donor_weight.T, preferred_element_type=jnp.float32)
        + jnp.dot(d_accept, acceptor_weight.T, preferred_element_type=jnp.float32)
    ).astype(jnp.bfloat16)
    grad_donor = jnp.dot(embed.T, d_donor, preferred_element_type=jnp.float32)
    grad_accept = jnp.dot(embed.T, d_accept, preferred_element_type=jnp.float32)
    grad_point = jnp.dot(act.T, d_embed, preferred_element_type=jnp.float32)
    d_act = jnp.dot(d_embed, point_weight.T, preferred_element_type=jnp.float32)
    dilated_output_gradient = (d_act * gelu_slope(dilated_output)).astype(jnp.bfloat16)
    trailing_padding = padded(dilated_output_gradient, (("seq", 0),), DILATION_STEP)
    tap_gradient_rows = []
    d_hidden = jnp.zeros((sequence_length, channels), jnp.float32)
    for tap_index in range(tap_count):
        tap_gradient_rows.append(
            jnp.dot(
                padded_input[
                    tap_index * DILATION_STEP : tap_index * DILATION_STEP + sequence_length
                ].T,
                dilated_output_gradient,
                preferred_element_type=jnp.float32,
            )
        )
        window_start = (tap_count - 1 - tap_index) * DILATION_STEP
        d_hidden = d_hidden + jnp.dot(
            trailing_padding[window_start : window_start + sequence_length],
            dilated_tap_weight[tap_index].T,
            preferred_element_type=jnp.float32,
        )
    grad_conv = jnp.stack(tap_gradient_rows)
    d_normed = d_hidden * gelu_slope(normed)
    grad_gain = jnp.sum(d_normed * tokens_f * inv_rms, axis=0)
    conv_piece = lax.psum_scatter(
        grad_conv.astype(jnp.bfloat16), "seq", scatter_dimension=1, tiled=True
    ).astype(jnp.float32)
    conv_piece = lax.psum(conv_piece.astype(jnp.bfloat16), "batch").astype(jnp.float32)
    grad_point, grad_donor, grad_accept, grad_gain, loss = lax.psum(
        (grad_point, grad_donor, grad_accept, grad_gain, loss), "seq"
    )
    return (
        conv_piece,
        grad_point.astype(jnp.bfloat16)[None],
        grad_donor.astype(jnp.bfloat16)[None],
        grad_accept.astype(jnp.bfloat16)[None],
        grad_gain[None],
        jnp.reshape(loss, (1,)),
    )


def solution(mesh):
    return jax.shard_map(
        on_device,
        mesh=mesh,
        in_specs=(
            P("batch", "seq", None),
            P(),
            P(),
            P(),
            P(),
            P(),
            P("batch", "seq", None),
            P("batch", "seq"),
        ),
        out_specs=(
            P(None, "seq", None),
            P("batch", None, None),
            P("batch", None, None),
            P("batch", None, None),
            P("batch", None),
            P("batch"),
        ),
        check_vma=False,
    )
```

profile of v0, /device:TPU:1, one launch (start us, length us, event | category | flops | bytes accessed | tf_op | source)
XLA Modules:
  0.0 842.7 jit_solution(13700945813391820106)
XLA Ops:
  8.7 1.8 fusion.15
  11.9 5.0 collective-permute-start
  17.0 1.9 fusion.54
  21.9 1.7 fusion.58
  23.7 1.7 fusion.33
  36.2 1.7 constant_dynamic-update-slice_fusion.3
  37.8 9.7 %collective-permute-done.3 = bf16[512,256]{1,0:T(8,128)(2,1)} collective-permute-done((bf16[512,256]{1,0:T(8,128)(2,1)}, bf16[512,256]{1,0:T(8,128)(2,1)}, u32[]{:S(2)}, u32[]{:S(2)}) %collective-permute-start.3) | collective-permute-done | bytes 262176 | tf_op jit(solution)/shard_map/ppermute | solution.py:31
  49.2 20.0 %collective-permute-done.4 = bf16[512,256]{1,0:T(8,128)(2,1)} collective-permute-done((bf16[512,256]{1,0:T(8,128)(2,1)}, bf16[512,256]{1,0:T(8,128)(2,1)}, u32[]{:S(2)}, u32[]{:S(2)}) %collective-permute-start.4) | collective-permute-done | bytes 262176 | tf_op jit(solution)/shard_map/ppermute | solution.py:31
  69.2 1.7 constant_dynamic-update-slice_fusion.1
  70.9 25.8 %collective-permute-done.5 = bf16[512,256]{1,0:T(8,128)(2,1)} collective-permute-done((bf16[512,256]{1,0:T(8,128)(2,1)}, bf16[512,256]{1,0:T(8,128)(2,1)}, u32[]{:S(2)}, u32[]{:S(2)}) %collective-permute-start.5) | collective-permute-done | bytes 262176 | tf_op jit(solution)/shard_map/ppermute | solution.py:31
  96.6 1.7 constant_dynamic-update-slice_fusion
  98.3 2.9 gather_fusion.1
  101.2 1.7 fusion.68
  109.2 15.2 %collective-permute-start.8 = (f32[512,256]{1,0:T(8,128)S(1)}, f32[512,256]{1,0:T(8,128)S(1)}, u32[]{:S(2)}, u32[]{:S(2)}) collective-permute-start(f32[512,256]{1,0:T(8,128)S(1)} %bitcast.162), channel_id=1, source_target_pairs={{0,48},{16,64},{32,80},{48,96},{64,112},{80,128},{96,144},{112,160... | collective-permute-start | bytes 1572872 | tf_op jit(solution)/shard_map/ppermute | solution.py:31
  124.5 8.6 %collective-permute-start.9 = (f32[512,256]{1,0:T(8,128)S(1)}, f32[512,256]{1,0:T(8,128)S(1)}, u32[]{:S(2)}, u32[]{:S(2)}) collective-permute-start(f32[512,256]{1,0:T(8,128)S(1)} %bitcast.163), channel_id=1, source_target_pairs={{0,64},{16,80},{32,96},{48,112},{64,128},{80,144},{96,160},{112,17... | collective-permute-start | bytes 1572872 | tf_op jit(solution)/shard_map/ppermute | solution.py:31
  136.3 4.8 collective-permute-done.8
  141.0 11.3 %collective-permute-done.9 = f32[512,256]{1,0:T(8,128)S(1)} collective-permute-done((f32[512,256]{1,0:T(8,128)S(1)}, f32[512,256]{1,0:T(8,128)S(1)}, u32[]{:S(2)}, u32[]{:S(2)}) %collective-permute-start.9) | collective-permute-done | bytes 524320 | tf_op jit(solution)/shard_map/ppermute | solution.py:31
  154.5 2.8 fusion.62
  162.2 30.5 %collective-permute-start.11 = (bf16[128,384]{1,0:T(8,128)(2,1)S(1)}, bf16[128,384]{1,0:T(8,128)(2,1)}, u32[]{:S(2)}, u32[]{:S(2)}) collective-permute-start(bf16[128,384]{1,0:T(8,128)(2,1)S(1)} %get-tuple-element.22), channel_id=1, source_target_pairs={{0,16},{16,32},{32,48},{48,64},{64,80},{80,96},{96,112},{112,128},... | collective-permute-start | bytes 294920 | tf_op jit(solution)/shard_map/ppermute | solution.py:20
  196.4 1.9 fusion.65
  198.3 2.8 fusion.19
  201.1 313.8 %all-reduce.6 = (bf16[384,768]{1,0:T(8,128)(2,1)}, bf16[768,256]{1,0:T(8,128)(2,1)}, bf16[768,256]{1,0:T(8,128)(2,1)}, f32[1,768]{1,0:T(1,128)}, f32[1]{0:T(128)}) all-reduce(f32[384,768]{1,0:T(8,128)} %fusion.103, f32[768,256]{1,0:T(8,128)S(1)} %fusion.112, ...), channel_id=1, replica_groups=mesh['seq'=32,'batch'=16] {'seq'}, use_global_device_ids=true, to_apply=%region_3.4 | all-reduce | flops 688897 | bytes 4134920 | tf_op jit(solution)/shard_map/psum | solution.py:161
  514.9 187.1 %all-reduce.5.cloned.1.call-done = bf16[3,768,384]{2,1,0:T(8,128)(2,1)} async-done(((bf16[3,768,384]{2,1,0:T(8,128)(2,1)}), bf16[3,768,384]{2,1,0:T(8,128)(2,1)}) %all-reduce.5.cloned.1.call-update) | async-done | bytes 1769488
  702.8 132.3 %psum.42 = bf16[3,24,384]{2,1,0:T(8,128)(2,1)S(1)} all-reduce(bf16[3,24,384]{2,1,0:T(8,128)(2,1)S(1)} %constant_dynamic-slice_fusion), channel_id=1, replica_groups=mesh['seq'=32,'batch'=16] {'batch'}, use_global_device_ids=true, to_apply=%region_2.3 | all-reduce | flops 27648 | bytes 110592 | tf_op jit(solution)/shard_map/psum | solution.py:160
  (97 shorter events, 38.4 us)
Async XLA Ops:
  7.2 18.3 %copy-start = (bf16[384,768]{1,0:T(8,128)(2,1)S(1)}, bf16[384,768]{1,0:T(8,128)(2,1)}, u32[]{:S(2)}) copy-start(bf16[384,768]{1,0:T(8,128)(2,1)} %param.11) | copy-start | bytes 1769476
  7.2 9.7 %copy-start.2 = (bf16[1,512,768]{2,1,0:T(8,128)(2,1)S(1)}, bf16[1,512,768]{2,1,0:T(8,128)(2,1)}, u32[]{:S(2)}) copy-start(bf16[1,512,768]{2,1,0:T(8,128)(2,1)} %param.8) | copy-start | bytes 2359300
  7.2 9.7 %copy-start.14 = (f32[768]{0:T(1024)S(1)}, f32[768]{0:T(1024)}, u32[]{:S(2)}) copy-start(f32[768]{0:T(1024)} %param.9) | copy-start | bytes 9220
  7.2 694.8 %all-reduce.5.cloned.1.call-start = ((), (), s32[]{:S(2)}) async-start(), calls=%async_computation | async-start | bytes 3538944
  10.6 11.3 %collective-permute-start.1 = (bf16[128,768]{1,0:T(8,128)(2,1)S(1)}, bf16[128,768]{1,0:T(8,128)(2,1)}, u32[]{:S(2)}, u32[]{:S(2)}) collective-permute-start(bf16[128,768]{1,0:T(8,128)(2,1)S(1)} %get-tuple-element.21), channel_id=1, source_target_pairs={{16,0},{32,16},{48,32},{64,48},{80,64},{96,80},{112,96},{128,112},... | collective-permute-start | bytes 589832 | tf_op jit(solution)/shard_map/ppermute | solution.py:23
  11.9 11.8 %collective-permute-start = (bf16[128,768]{1,0:T(8,128)(2,1)S(1)}, bf16[128,768]{1,0:T(8,128)(2,1)S(1)}, u32[]{:S(2)}, u32[]{:S(2)}) collective-permute-start(bf16[128,768]{1,0:T(8,128)(2,1)S(1)} %get-tuple-element.20), channel_id=1, source_target_pairs={{0,16},{16,32},{32,48},{48,64},{64,80},{80,96},{96,112},{112,128},... | collective-permute-start | bytes 589832 | tf_op jit(solution)/shard_map/ppermute | solution.py:20
  16.9 1.9 copy-start.16
  26.7 8.3 copy-start.6
  27.9 8.3 collective-permute-start.2
  31.1 16.4 %collective-permute-start.3 = (bf16[512,256]{1,0:T(8,128)(2,1)}, bf16[512,256]{1,0:T(8,128)(2,1)}, u32[]{:S(2)}, u32[]{:S(2)}) collective-permute-start(bf16[512,256]{1,0:T(8,128)(2,1)} %get-tuple-element.29), channel_id=1, source_target_pairs={{32,0},{48,16},{64,32},{80,48},{96,64},{112,80},{128,96},{144,112}... | collective-permute-start | bytes 786440 | tf_op jit(solution)/shard_map/ppermute | solution.py:31
  32.4 36.8 %collective-permute-start.4 = (bf16[512,256]{1,0:T(8,128)(2,1)}, bf16[512,256]{1,0:T(8,128)(2,1)}, u32[]{:S(2)}, u32[]{:S(2)}) collective-permute-start(bf16[512,256]{1,0:T(8,128)(2,1)} %get-tuple-element.29), channel_id=1, source_target_pairs={{48,0},{64,16},{80,32},{96,48},{112,64},{128,80},{144,96},{160,112... | collective-permute-start | bytes 786440 | tf_op jit(solution)/shard_map/ppermute | solution.py:31
  33.7 62.9 %collective-permute-start.5 = (bf16[512,256]{1,0:T(8,128)(2,1)}, bf16[512,256]{1,0:T(8,128)(2,1)}, u32[]{:S(2)}, u32[]{:S(2)}) collective-permute-start(bf16[512,256]{1,0:T(8,128)(2,1)} %get-tuple-element.29), channel_id=1, source_target_pairs={{64,0},{80,16},{96,32},{112,48},{128,64},{144,80},{160,96},{176,11... | collective-permute-start | bytes 786440 | tf_op jit(solution)/shard_map/ppermute | solution.py:31
  106.3 30.0 %collective-permute-start.6 = (f32[512,256]{1,0:T(8,128)S(1)}, f32[512,256]{1,0:T(8,128)S(1)}, u32[]{:S(2)}, u32[]{:S(2)}) collective-permute-start(f32[512,256]{1,0:T(8,128)S(1)} %bitcast.160), channel_id=1, source_target_pairs={{0,16},{16,32},{32,48},{48,64},{64,80},{80,96},{96,112},{112,128},... | collective-permute-start | bytes 1572872 | tf_op jit(solution)/shard_map/ppermute | solution.py:31
  107.7 28.5 %collective-permute-start.7 = (f32[512,256]{1,0:T(8,128)S(1)}, f32[512,256]{1,0:T(8,128)S(1)}, u32[]{:S(2)}, u32[]{:S(2)}) collective-permute-start(f32[512,256]{1,0:T(8,128)S(1)} %bitcast.161), channel_id=1, source_target_pairs={{0,32},{16,48},{32,64},{48,80},{64,96},{80,112},{96,128},{112,144}... | collective-permute-start | bytes 1572872 | tf_op jit(solution)/shard_map/ppermute | solution.py:31
  109.0 24.2 %copy-start.17 = (s32[16,1]{0,1:T(1,128)S(1)}, s32[16,1]{0,1:T(1,128)}, u32[]{:S(2)}) copy-start(s32[16,1]{0,1:T(1,128)} %get-tuple-element.12) | copy-start | bytes 196
  109.2 31.9 %collective-permute-start.8 = (f32[512,256]{1,0:T(8,128)S(1)}, f32[512,256]{1,0:T(8,128)S(1)}, u32[]{:S(2)}, u32[]{:S(2)}) collective-permute-start(f32[512,256]{1,0:T(8,128)S(1)} %bitcast.162), channel_id=1, source_target_pairs={{0,48},{16,64},{32,80},{48,96},{64,112},{80,128},{96,144},{112,160... | collective-permute-start | bytes 1572872 | tf_op jit(solution)/shard_map/ppermute | solution.py:31
  124.5 27.8 %collective-permute-start.9 = (f32[512,256]{1,0:T(8,128)S(1)}, f32[512,256]{1,0:T(8,128)S(1)}, u32[]{:S(2)}, u32[]{:S(2)}) collective-permute-start(f32[512,256]{1,0:T(8,128)S(1)} %bitcast.163), channel_id=1, source_target_pairs={{0,64},{16,80},{32,96},{48,112},{64,128},{80,144},{96,160},{112,17... | collective-permute-start | bytes 1572872 | tf_op jit(solution)/shard_map/ppermute | solution.py:31
  136.2 16.2 %copy-start.11 = (bf16[768,256]{1,0:T(8,128)(2,1)S(1)}, bf16[768,256]{1,0:T(8,128)(2,1)}, u32[]{:S(2)}) copy-start(bf16[768,256]{1,0:T(8,128)(2,1)} %param.13) | copy-start | bytes 1179652
  159.0 33.7 %copy-start.13 = (bf16[128,768]{1,0:T(8,128)(2,1)S(1)}, bf16[128,768]{1,0:T(8,128)(2,1)}, u32[]{:S(2)}) copy-start(bf16[128,768]{1,0:T(8,128)(2,1)} %copy-done.12) | copy-start | bytes 589828
  160.9 35.5 %collective-permute-start.10 = (bf16[128,384]{1,0:T(8,128)(2,1)S(1)}, bf16[128,384]{1,0:T(8,128)(2,1)}, u32[]{:S(2)}, u32[]{:S(2)}) collective-permute-start(bf16[128,384]{1,0:T(8,128)(2,1)S(1)} %get-tuple-element.23), channel_id=1, source_target_pairs={{16,0},{32,16},{48,32},{64,48},{80,64},{96,80},{112,96},{128,112},... | collective-permute-start | bytes 294920 | tf_op jit(solution)/shard_map/ppermute | solution.py:23
  162.2 36.0 %collective-permute-start.11 = (bf16[128,384]{1,0:T(8,128)(2,1)S(1)}, bf16[128,384]{1,0:T(8,128)(2,1)}, u32[]{:S(2)}, u32[]{:S(2)}) collective-permute-start(bf16[128,384]{1,0:T(8,128)(2,1)S(1)} %get-tuple-element.22), channel_id=1, source_target_pairs={{0,16},{16,32},{32,48},{48,64},{64,80},{80,96},{96,112},{112,128},... | collective-permute-start | bytes 294920 | tf_op jit(solution)/shard_map/ppermute | solution.py:20
  196.3 1.9 copy-start.3
  196.3 1.9 copy-start.5
  198.2 2.9 copy-start.4
  (8 other events, 10.9 us)
Sparse Core Ops, SparseCore 0:
  196.4 505.5 all-reduce.4
where the time goes:
time: 851 us; the launch traced here: 843 us
  blocking collectives  446 us (52%)
  waiting for transfers between devices  259 us (30%)
  starting transfers between devices  69.7 us (8%)
  matrix products  27.9 us (3%)
  between operations  15.9 us (2%)
  local copies, waits for them, and re-layouts  14.9 us (2%)
  other arithmetic  9.46 us (1%)
    psum x1, blocking collectives, on_device(): lax.psum((grad_point, grad_donor, grad_accept, grad_gain, loss), 'seq')  314 us
    unnamed x2, waiting for transfers between devices  187 us
    psum x1, blocking collectives, on_device(): lax.psum(conv_piece.astype(jnp.bfloat16), 'batch').astype(jnp.float32)  132 us
    ppermute x8, waiting for transfers between devices, shifted(): return lax.ppermute(block, axis, route)  71.5 us
    ppermute x2, starting transfers between devices, padded(): lax.ppermute(lax.slice_in_dim(block, block.shape[dim] - width, None, axis...  35.5 us
    ppermute x8, starting transfers between devices, shifted(): return lax.ppermute(block, axis, route)  31.6 us
  transfers between devices with their start and end apart: 13, of which 6 were waited for; matrix products, arithmetic and copies ran while one was open for 3% of the time, Pallas kernels for 0%

commit v1 on v0

v1 whole, which is shorter than its diff:
```python
import jax
import jax.numpy as jnp
import numpy as np
from jax import lax
from jax.experimental import pallas as pl
from jax.experimental.pallas import tpu as pltpu
from jax.sharding import Mesh
from jax.sharding import PartitionSpec as P

STEP = 128
PANEL = 128
SPAN = 4
SLOTS = 16
EPSILON = 1e-06
LOSS_WEIGHT = 1.0 / 128.0
SEQ = ("y", "zb", "zq")
BATCH = ("zhi", "x", "core")
F32 = jnp.float32
BF16 = jnp.bfloat16
ROOT = 0.7978845608028654
CUBIC = 0.044715
VMEM_BYTES = 56 * 1024 * 1024
PIECE = 96
CHUNK_ROWS = 288
EXTRA_ROWS = 16


def dot(a, b):
    return lax.dot_general(a, b, (((1,), (0,)), ((), ())), preferred_element_type=F32)


def dot_t(a, b):
    return lax.dot_general(a, b, (((1,), (1,)), ((), ())), preferred_element_type=F32)


def gelu(v):
    return 0.5 * v * (1.0 + jnp.tanh(ROOT * (v + CUBIC * (v * v * v))))


def gelu_slope(v):
    square = v * v
    t = jnp.tanh(ROOT * (v + CUBIC * (square * v)))
    return 0.5 * (1.0 + t) + 0.5 * v * (1.0 - t * t) * (ROOT * (1.0 + 3.0 * CUBIC * square))


def rms(v):
    return lax.rsqrt(jnp.mean(v * v, axis=-1, keepdims=True) + EPSILON)


def call(kernel, outs, flops, n_bytes, specs=None, scratch=()):
    vmem = pl.BlockSpec(memory_space=pltpu.VMEM)
    return pl.pallas_call(
        kernel,
        out_shape=outs,
        in_specs=specs,
        out_specs=[vmem] * len(outs),
        scratch_shapes=list(scratch),
        compiler_params=pltpu.CompilerParams(vmem_limit_bytes=VMEM_BYTES),
        cost_estimate=pl.CostEstimate(flops=flops, bytes_accessed=n_bytes, transcendentals=0),
    )


VM = pl.BlockSpec(memory_space=pltpu.VMEM)
SM = pl.BlockSpec(memory_space=pltpu.SMEM)


def forward_kernel(
    tok, low, high, gain, taps, point, donor_w, accept_w, meta,
    hidden, conv_out, act_out, embed_out, donor_out, accept_out,
):
    rows = tok.shape[0]

    def activate(src, start, at):
        v = src[pl.ds(start, STEP), :].astype(F32)
        hidden[pl.ds(at, STEP), :] = gelu(v * rms(v) * gain[...]).astype(BF16)

    activate(low, 0, 0)
    activate(high, 0, STEP + rows)

    @pl.loop(0, rows // STEP)
    def _(i):
        start = pl.multiple_of(i * STEP, STEP)
        activate(tok, start, pl.multiple_of(start + STEP, STEP))

    @pl.loop(0, rows // 256)
    def _(i):
        start = pl.multiple_of(i * 256, 256)
        here = pl.ds(start, 256)
        conv = dot(hidden[here, :], taps[0])
        for tap in range(1, taps.shape[0]):
            at = pl.multiple_of(start + tap * STEP, STEP)
            conv = conv + dot(hidden[pl.ds(at, 256), :], taps[tap])
        conv_out[here, :] = conv
        act = gelu(conv).astype(BF16)
        act_out[here, :] = act
        embed = (tok[here, :].astype(F32) + dot(act, point[...])).astype(BF16)
        embed_out[here, :] = embed
        donor_out[here, :] = dot(embed, donor_w[...]).astype(BF16)
        accept_out[here, :] = dot(embed, accept_w[...]).astype(BF16)

    donor_out[pl.ds(rows, SLOTS), :] = meta[...]


def side_kernel(
    tok, low, high, gain, hidden, conv, act, embed, order, eye,
    factor, slope, hidden_t, act_t, embed_t,
):
    rows = tok.shape[0]

    def weigh(src, start, at):
        v = src[pl.ds(start, STEP), :].astype(F32)
        unit = v * rms(v)
        factor[pl.ds(at, STEP), :] = (gelu_slope(unit * gain[...]) * unit).astype(BF16)

    weigh(low, 0, 0)
    weigh(high, 0, STEP + rows)

    @pl.loop(0, rows // STEP)
    def _(i):
        start = pl.multiple_of(i * STEP, STEP)
        weigh(tok, start, pl.multiple_of(start + STEP, STEP))
        slope[pl.ds(start, STEP), :] = gelu_slope(conv[pl.ds(start, STEP), :])

    @pl.loop(0, hidden_t.shape[0] // 256)
    def _(i):
        here = pl.ds(pl.multiple_of(i * 256, 256), 256)
        hidden_t[here, :] = dot_t(order[here, :], hidden[...]).astype(BF16)
        embed_t[here, :] = dot_t(eye[here, :], embed[...]).astype(BF16)

    inner = act.shape[1]

    @pl.loop(0, inner // 128)
    def _(i):
        here = pl.ds(pl.multiple_of(i * 128, 128), 128)
        act_t[here, :] = dot_t(eye[here, :inner], act[...]).astype(BF16)


def pair_kernel(distance, *refs):
    if distance == 0:
        own, dfeat, afeat, d_donor, d_accept, loss = refs
        d_donor[...] = jnp.zeros_like(d_donor)
        d_accept[...] = jnp.zeros_like(d_accept)
        loss[...] = jnp.zeros_like(loss)
        far, afar, dfar = None, afeat, None
    else:
        own, far, dfeat, afeat, dfar, afar, dd_in, da_in, loss_in, d_donor, d_accept, loss = refs
        d_donor[...] = dd_in[...]
        d_accept[...] = da_in[...]
        loss[...] = loss_in[...]
    scale = dfeat.shape[1] ** (-0.5)
    per_device = afeat.shape[0] // PANEL
    row = lax.broadcasted_iota(jnp.int32, (PANEL, PANEL), 0)
    col = lax.broadcasted_iota(jnp.int32, (PANEL, PANEL), 1)

    def panel(ref, block):
        return ref.at[pl.ds(pl.multiple_of(block * PANEL, PANEL), PANEL), :]

    def visit(meta, j, donors, acceptors, is_owner):
        accept_block = meta[j, 2] - distance * per_device
        here = (meta[j, 4] > 0) & (accept_block >= 0) & (accept_block < per_device)

        @pl.when(here)
        def _():
            donor_block = meta[j, 0]
            dpan = panel(donors, donor_block)[...]
            apan = panel(acceptors, accept_block)[...]
            scores = dot_t(dpan, apan) * scale
            target = ((row == meta[j, 1]) & (col == meta[j, 3])).astype(F32)
            small = jnp.exp(-jnp.abs(scores))
            inverse = 1.0 / (1.0 + small)
            sigmoid = jnp.where(scores >= 0, inverse, small * inverse)
            dscore = ((sigmoid - target) * LOSS_WEIGHT).astype(BF16)
            if is_owner:
                loss[...] += (jnp.maximum(scores, 0.0) + jnp.log1p(small)) - target * scores
                into = panel(d_donor, donor_block)
                into[...] += dot(dscore, apan) * scale
            if distance == 0 or not is_owner:
                into = panel(d_accept, accept_block)
                into[...] += (
                    lax.dot_general(
                        dscore, dpan, (((0,), (0,)), ((), ())), preferred_element_type=F32
                    )
                    * scale
                )

    @pl.loop(0, SLOTS)
    def _(j):
        visit(own, j, dfeat, afar, True)
        if distance > 0:
            visit(far, j, dfar, afeat, False)


def backward_kernel(
    d_donor, d_accept, loss, taps, point, donor_w, accept_w, factor, slope, hidden_t, act_t, embed_t,
    conv_sum, head_sum, d_conv, d_feat,
):
    rows = d_donor.shape[0]
    heads = d_donor.shape[1]
    channels = hidden_t.shape[0]
    inner = act_t.shape[0]

    @pl.loop(0, rows // 256)
    def _(i):
        here = pl.ds(pl.multiple_of(i * 256, 256), 256)
        dd = d_donor[here, :].astype(BF16)
        da = d_accept[here, :].astype(BF16)
        d_feat[here, :heads] = dd
        d_feat[here, heads:] = da
        d_embed = (dot_t(dd, donor_w[...]) + dot_t(da, accept_w[...])).astype(BF16)
        d_conv[here, :] = (dot_t(d_embed, point[...]) * slope[here, :]).astype(BF16)

    lanes = inner // 128
    for tap in range(taps.shape[0]):

        @pl.loop(0, channels // (2 * PIECE))
        def _(i):
            here = pl.ds(pl.multiple_of(i * 2 * PIECE, 2 * PIECE), 2 * PIECE)
            part = dot(hidden_t[here, tap * STEP : tap * STEP + rows], d_conv[...]).astype(BF16)
            for half in range(2):
                for lane in range(lanes):
                    conv_sum[i * 2 + half, tap * lanes + lane] = part[
                        half * PIECE : (half + 1) * PIECE, lane * 128 : (lane + 1) * 128
                    ]

    def put(part, base, group_rows, first):
        for lane in range(4):
            for k in range(part.shape[0] // PIECE):
                at = lane * (group_rows // PIECE) + k + base
                piece = first + at
                chunk, place = piece // 3, piece % 3
                head_sum[chunk, place * PIECE : (place + 1) * PIECE, :] = part[
                    k * PIECE : (k + 1) * PIECE, lane * 128 : (lane + 1) * 128
                ]

    for i in range(channels // (2 * PIECE)):
        part = dot(embed_t[i * 2 * PIECE : (i + 1) * 2 * PIECE, :], d_feat[...]).astype(BF16)
        put(part, 2 * i, channels, 0)
    for i in range(inner // (2 * PIECE)):
        part = dot(act_t[i * 2 * PIECE : (i + 1) * 2 * PIECE, :], d_feat[...]).astype(BF16)
        put(part, 2 * i, inner, 4 * channels // PIECE)

    def gain_part(i, total):
        start = pl.multiple_of(i * STEP, STEP)
        for tap in range(taps.shape[0]):
            at = pl.multiple_of(start + tap * STEP, STEP)
            product = dot_t(d_conv[pl.ds(start, STEP), :], taps[tap]) * factor[
                pl.ds(at, STEP), :
            ].astype(F32)
            total = total + jnp.sum(product.reshape(STEP // 8, 8, channels), axis=0)
        return total

    total = lax.fori_loop(0, rows // STEP, gain_part, jnp.zeros((8, channels), F32))
    gain = jnp.sum(total, axis=0, keepdims=True)
    loss_row = jnp.sum(loss[...], axis=0, keepdims=True) * LOSS_WEIGHT
    loss_all = jnp.broadcast_to(jnp.sum(loss_row, axis=1, keepdims=True), (1, 128))
    for chunk in range(head_sum.shape[0]):
        at_row = lax.broadcasted_iota(jnp.int32, (EXTRA_ROWS, 128), 0)
        if chunk < channels // 128:
            value = gain[:, chunk * 128 : (chunk + 1) * 128]
        elif chunk == channels // 128:
            value = loss_all
        else:
            value = jnp.zeros((1, 128), F32)
        coarse = value.astype(BF16).astype(F32)
        block = jnp.where(at_row == 0, coarse, 0.0) + jnp.where(at_row == 8, value - coarse, 0.0)
        head_sum[chunk, CHUNK_ROWS:, :] = block.astype(BF16)


def shifted(block, distance):
    count = lax.axis_size(SEQ)
    route = [(i, i + distance) for i in range(count) if 0 <= i + distance < count]
    return lax.ppermute(block, SEQ, route)


def swap_parts(parts, axis):
    return lax.all_to_all(parts, axis, 0, 0, tiled=True)


def gather_parts(part, axis):
    count = lax.axis_size(axis)
    return swap_parts(jnp.broadcast_to(part[None], (count,) + part.shape), axis)


def summed(parts):
    return jnp.sum(parts.astype(F32), axis=0)


def resplit(total):
    body = total[..., :CHUNK_ROWS, :].astype(BF16)
    value = (
        total[..., CHUNK_ROWS : CHUNK_ROWS + 8, :] + total[..., CHUNK_ROWS + 8 : CHUNK_ROWS + 16, :]
    )
    coarse = lax.reduce_precision(value, 8, 7)
    return jnp.concatenate([body, coarse.astype(BF16), (value - coarse).astype(BF16)], axis=-2)


def on_device(
    activations, norm_gain, dilated_tap_weight, point_weight, donor_weight, acceptor_weight,
    pair_sites, pair_count, order, eye,
):
    tokens = activations[0]
    rows, channels = tokens.shape
    tap_count, _, inner = dilated_tap_weight.shape
    heads = donor_weight.shape[1]
    blocks = rows // PANEL
    shape = jax.ShapeDtypeStruct
    low = shifted(tokens[rows - STEP :], 1)
    high = shifted(tokens[:STEP], -1)
    gain = norm_gain[None]
    sites = pair_sites[0]
    first = lax.axis_index(SEQ) * blocks
    live = (jnp.arange(SLOTS, dtype=jnp.int32) < pair_count[0, 0]).astype(jnp.int32)
    meta = jnp.stack(
        [
            sites[:, 0] // PANEL - first,
            sites[:, 0] % PANEL,
            sites[:, 1] // PANEL - first,
            sites[:, 1] % PANEL,
            live,
        ]
        + [jnp.zeros_like(live)] * 3,
        axis=1,
    )
    meta_rows = jnp.pad(meta.astype(BF16), ((0, 0), (0, heads - meta.shape[1])))

    hidden, conv, act, embed, donor_feat, accept_feat = call(
        forward_kernel,
        [
            shape((rows + 2 * STEP, channels), BF16),
            shape((rows, inner), F32),
            shape((rows, inner), BF16),
            shape((rows, channels), BF16),
            shape((rows + SLOTS, heads), BF16),
            shape((rows, heads), BF16),
        ],
        1_700_000_000,
        8_000_000,
        [VM] * 9,
    )(
        tokens, low, high, gain, dilated_tap_weight, point_weight, donor_weight, acceptor_weight,
        meta_rows,
    )

    acc = call(
        lambda *refs: pair_kernel(0, *refs),
        [shape((rows, heads), F32), shape((rows, heads), F32), shape((PANEL, PANEL), F32)],
        1_000_000_000,
        4_000_000,
        [SM] + [VM] * 2,
    )(meta, donor_feat, accept_feat)
    factor, slope, hidden_t, act_t, embed_t = call(
        side_kernel,
        [
            shape((rows + 2 * STEP, channels), BF16),
            shape((rows, inner), F32),
            shape((channels, rows + 2 * STEP), BF16),
            shape((inner, rows), BF16),
            shape((channels, rows), BF16),
        ],
        4_000_000_000,
        10_000_000,
        [VM] * 10,
    )(tokens, low, high, gain, hidden, conv, act, embed, order, eye)
    far_accept, far_donor = accept_feat, donor_feat
    for distance in range(1, SPAN + 1):
        far_accept = shifted(far_accept, -1)
        far_donor = shifted(far_donor, 1)
        far_meta = far_donor[rows:, :8].astype(jnp.int32)
        acc = call(
            lambda *refs, distance=distance: pair_kernel(distance, *refs),
            [shape((rows, heads), F32), shape((rows, heads), F32), shape((PANEL, PANEL), F32)],
            1_000_000_000,
            4_000_000,
            [SM] * 2 + [VM] * 7,
        )(meta, far_meta, donor_feat, accept_feat, far_donor, far_accept, *acc)

    chunk = CHUNK_ROWS + EXTRA_ROWS
    lanes = inner // 128
    slabs = tap_count * lanes
    conv_sum, head_sum = call(
        backward_kernel,
        [shape((8, slabs, PIECE, 128), BF16), shape((16, chunk, 128), BF16)],
        5_000_000_000,
        12_000_000,
        [VM] * 12,
        [pltpu.VMEM((rows, inner), BF16), pltpu.VMEM((rows, 2 * heads), BF16)],
    )(
        *acc, dilated_tap_weight, point_weight, donor_weight, acceptor_weight,
        factor, slope, hidden_t, act_t, embed_t,
    )

    conv_sum = summed(swap_parts(conv_sum.reshape(2, 4, slabs, PIECE, 128), "core")).astype(BF16)
    conv_sum = summed(swap_parts(conv_sum, "x")).astype(BF16)
    conv_sum = conv_sum.reshape(slabs, 4, 24, 128).transpose(1, 0, 2, 3).reshape(4, slabs * 24, 128)
    head_rows = 4 * chunk
    both = jnp.concatenate([head_sum.reshape(4, head_rows, 128), conv_sum], axis=1)
    both = summed(swap_parts(both, "y"))
    head_sum = resplit(both[:head_rows].reshape(4, chunk, 128))
    conv_sum = both[head_rows:].astype(BF16)
    conv_sum = conv_sum.reshape(slabs, 4, 6, 128).transpose(1, 0, 2, 3).reshape(4, slabs * 6, 128)
    both = jnp.concatenate([head_sum, conv_sum], axis=1)
    both = summed(swap_parts(both, "zq"))
    both = jnp.concatenate([resplit(both[:chunk]), both[chunk:].astype(BF16)], axis=0)
    other = lax.ppermute(both, "zb", [(0, 1), (1, 0)])
    both = both.astype(F32) + other.astype(F32)
    head_sum = resplit(both[:chunk])
    conv_sum = both[chunk:].astype(BF16).reshape(slabs, 2, 3, 128)
    conv_sum = lax.dynamic_index_in_dim(conv_sum, lax.axis_index("zb"), 1, keepdims=False)
    pieces = gather_parts(conv_sum, BATCH).astype(F32)
    pieces = jnp.sum(pieces.reshape(2, 4, 2, tap_count, lanes, 3, 128), axis=0)
    grad_conv = pieces.transpose(2, 1, 0, 4, 3, 5).reshape(tap_count, 24, inner)

    head_sum = gather_parts(head_sum, "zq").reshape(4 * chunk, 128)
    head_sum = gather_parts(head_sum, "y").reshape(16, chunk, 128)
    body = head_sum[:, :CHUNK_ROWS].reshape(16 * CHUNK_ROWS, 128)
    extra = head_sum[:, CHUNK_ROWS].astype(F32) + head_sum[:, CHUNK_ROWS + 8].astype(F32)
    gain_chunks = channels // 128

    def heads_of(start, count):
        return jnp.concatenate([body[start : start + count], body[start + count : start + 2 * count]], axis=1)

    grad_donor = heads_of(0, channels)
    grad_accept = heads_of(2 * channels, channels)
    act_donor = heads_of(4 * channels, inner)
    act_accept = heads_of(4 * channels + 2 * inner, inner)
    grad_point = (dot_t(act_donor, donor_weight) + dot_t(act_accept, acceptor_weight)).astype(BF16)
    grad_gain = extra[:gain_chunks].reshape(1, channels)
    loss = extra[gain_chunks, :1]
    return grad_conv, grad_point[None], grad_donor[None], grad_accept[None], grad_gain, loss


def channel_order():
    core, x, y, zq, zb, k = np.meshgrid(*[np.arange(n) for n in (2, 4, 4, 4, 2, 3)], indexing="ij")
    channel = (24 * (8 * y + 4 * zb + zq) + 12 * core + 3 * x + k).reshape(-1)
    return np.eye(channel.size, dtype=np.float32)[channel]


def solution(mesh):
    fine = Mesh(mesh.devices.reshape(4, 2, 4, 2, 4, 2), SEQ + BATCH)
    placed = jax.shard_map(
        on_device,
        mesh=fine,
        in_specs=(
            P(BATCH, SEQ, None),
            P(),
            P(),
            P(),
            P(),
            P(),
            P(BATCH, SEQ, None),
            P(BATCH, SEQ),
            P(),
            P(),
        ),
        out_specs=(
            P(None, SEQ, None),
            P(BATCH, None, None),
            P(BATCH, None, None),
            P(BATCH, None, None),
            P(BATCH, None),
            P(BATCH),
        ),
        check_vma=False,
    )

    def run(*arrays):
        order = jnp.asarray(channel_order(), BF16)
        eye = jnp.eye(order.shape[0], dtype=BF16)
        return placed(*arrays, order, eye)

    return run
```

time: 851 us -> 282 us (0.33)
  blocking collectives: 446 us -> 114 us
  waiting for transfers between devices: 259 us -> 40.8 us
  Pallas kernels: 0 us -> 48.8 us
  matrix products: 27.9 us -> 1.52 us
  between operations: 15.9 us -> 1.75 us
  starting transfers between devices: 69.7 us -> 56.7 us
    psum x2 -> x0, blocking collectives: 446 us -> none  [the longest x1 314 us: on_device(): lax.psum((grad_point, grad_donor, grad_accept, grad_gain, loss), 'seq')]
    unnamed x2 -> x0, waiting for transfers between devices: 187 us -> none
    all_to_all x0 -> x5, blocking collectives: none -> 114 us  [swap_parts(): return lax.all_to_all(parts, axis, 0, 0, tiled=True)]
    ppermute x12 -> x11, waiting for transfers between devices: 71.5 us -> 11.5 us  [the longest x1 8.26 us: on_device(): other = lax.ppermute(both, 'zb', [(0, 1), (1, 0)])]
    pallas_call x0 -> x8, Pallas kernels: none -> 48.8 us  [the longest x4 15 us: on_device(): call(lambda *refs, distance=distance: pair_kernel(distance, *refs), [shap...]
    ppermute x12 -> x11, starting transfers between devices: 69.7 us -> 35.5 us  [the longest x10 33.6 us: shifted(): return lax.ppermute(block, SEQ, route)]
    all_to_all x0 -> x2, waiting for transfers between devices: none -> 29.3 us  [swap_parts(): return lax.all_to_all(parts, axis, 0, 0, tiled=True)]
    dot_general x23 -> x2, matrix products: 27.9 us -> 1.52 us  [dot_t(): lax.dot_general(a, b, (((1,), (1,)), ((), ())), preferred_element_type=F32)]
  transfers between devices with their start and end apart: 13 -> 13, of which waited for: 6 -> 4; matrix products, arithmetic and copies ran while one was open for 3% -> 3% of each run, Pallas kernels for 0% -> 9%
where the time goes in v1:
time: 282 us; the launch traced here: 281 us
  blocking collectives  114 us (40%)
  starting transfers between devices  56.7 us (20%)
  Pallas kernels  48.8 us (17%)
  waiting for transfers between devices  40.8 us (14%)
  local copies, waits for them, and re-layouts  10.8 us (4%)
  other arithmetic  6.26 us (2%)
    all_to_all x5, blocking collectives, swap_parts(): return lax.all_to_all(parts, axis, 0, 0, tiled=True)  114 us
    ppermute x10, starting transfers between devices, shifted(): return lax.ppermute(block, SEQ, route)  33.6 us
    all_to_all x2, waiting for transfers between devices, swap_parts(): return lax.all_to_all(parts, axis, 0, 0, tiled=True)  29.3 us
    all_to_all x2, starting transfers between devices, swap_parts(): return lax.all_to_all(parts, axis, 0, 0, tiled=True)  21.2 us
    pallas_call x4, Pallas kernels, on_device(): call(lambda *refs, distance=distance: pair_kernel(distance, *refs), [shap...  15 us
    pallas_call x1, Pallas kernels, on_device(): call(backward_kernel, [shape((8, slabs, PIECE, 128), BF16), shape((16, ch...  12.3 us
    pallas_call x1, Pallas kernels, on_device(): call(side_kernel, [shape((rows + 2 * STEP, channels), BF16), shape((rows,...  11.5 us
    ppermute x1, waiting for transfers between devices, on_device(): other = lax.ppermute(both, 'zb', [(0, 1), (1, 0)])  8.26 us
  transfers between devices with their start and end apart: 13, of which 4 were waited for; matrix products, arithmetic and copies ran while one was open for 3% of the time, Pallas kernels for 9%

profile of v1, /device:TPU:1, one launch (start us, length us, event | category | flops | bytes accessed | tf_op | source)
XLA Modules:
  0.0 280.5 jit_solution(17953239553439401091)
XLA Ops:
  3.0 5.0 %collective-permute-start = (bf16[128,768]{1,0:T(8,128)(2,1)S(1)}, bf16[128,768]{1,0:T(8,128)(2,1)S(1)}, u32[]{:S(2)}, u32[]{:S(2)}) collective-permute-start(bf16[128,768]{1,0:T(8,128)(2,1)S(1)} %get-tuple-element.71), channel_id=1, source_target_pairs={{0,16},{16,32},{32,48},{48,64},{64,80},{80,96},{96,112},{112,128},... | collective-permute-start | bytes 589832 | tf_op jit(solution)/shard_map/ppermute | solution.py:272
  13.5 7.3 %shard_map.145 = (bf16[768,768]{1,0:T(8,128)(2,1)}, f32[512,384]{1,0:T(8,128)}, bf16[512,384]{1,0:T(8,128)(2,1)}, bf16[512,768]{1,0:T(8,128)(2,1)}, bf16[528,256]{1,0:T(8,128)(2,1)}, /*index=5*/bf16[512,256]{1,0:T(8,128)(2,1)}) custom-call(bf16[512,768]{1,0:T(8,128)(2,1)} %bitcast.55, bf16[128,768]{1,0:T(8,128)(2,1)} %copy-done.13, ...), custom_call_target="tpu_custom_call" | custom-call | flops 1700000000 | bytes 8000000 | tf_op jit(solution)/shard_map/pallas_call | solution.py:326
  22.0 4.2 %collective-permute-start.2 = (bf16[528,256]{1,0:T(8,128)(2,1)}, bf16[528,256]{1,0:T(8,128)(2,1)S(1)}, u32[]{:S(2)}, u32[]{:S(2)}) collective-permute-start(bf16[528,256]{1,0:T(8,128)(2,1)} %get-tuple-element.34.refs_1_.refs_2_), channel_id=1, source_target_pairs={{0,16},{16,32},{32,48},{48,64},{64,80},{80,96},{96,112},{112,128},... | collective-permute-start | bytes 811016 | tf_op jit(solution)/shard_map/ppermute | solution.py:272
  26.2 2.8 shard_map.146
  29.0 11.5 %shard_map.151 = (bf16[768,768]{1,0:T(8,128)(2,1)}, f32[512,384]{1,0:T(8,128)}, bf16[768,768]{1,0:T(8,128)(2,1)}, bf16[384,512]{1,0:T(8,128)(2,1)}, bf16[768,512]{1,0:T(8,128)(2,1)}) custom-call(bf16[512,768]{1,0:T(8,128)(2,1)} %bitcast.56, bf16[128,768]{1,0:T(8,128)(2,1)} %copy-done.13, bf16[128,768]{1,0:T(8,128)(2,1)} %copy-done.12, ...), custom_call_target="tpu_custom_call" | custom-call | flops 4000000000 | bytes 10000000 | tf_op jit(solution)/shard_map/pallas_call | solution.py:351
  41.8 4.2 %collective-permute-start.3 = (bf16[528,256]{1,0:T(8,128)(2,1)S(1)}, bf16[528,256]{1,0:T(8,128)(2,1)S(1)}, u32[]{:S(2)}, u32[]{:S(2)}) collective-permute-start(bf16[528,256]{1,0:T(8,128)(2,1)S(1)} %collective-permute-done.2.refs_4_), channel_id=1, source_target_pairs={{0,16},{16,32},{32,48},{48,64},{64,80},{80,96},{96,112},{112,128},... | collective-permute-start | bytes 811016 | tf_op jit(solution)/shard_map/ppermute | solution.py:272
  46.6 3.5 %shard_map.147 = (f32[512,256]{1,0:T(8,128)}, f32[512,256]{1,0:T(8,128)}, f32[128,128]{1,0:T(8,128)}) custom-call(s32[16,8]{1,0:T(8,128)} %copy-done.3, s32[16,8]{1,0:T(8,128)} %slice_convert_fusion.4.refs_1_, bf16[528,256]{1,0:T(8,128)(2,1)} %get-tuple-element.34.refs_1_.refs_2_, bf16[512,256]{1,0:T(8,128)(2,1)} %get-tuple-element.35.refs_2_.refs_3_, ...), custom_call_target="tpu_custom_call" | custom-call | flops 1000000000 | bytes 4000000 | tf_op jit(solution)/shard_map/pallas_call | solution.py:369
  51.4 6.0 %collective-permute-start.4 = (bf16[528,256]{1,0:T(8,128)(2,1)S(1)}, bf16[528,256]{1,0:T(8,128)(2,1)S(1)}, u32[]{:S(2)}, u32[]{:S(2)}) collective-permute-start(bf16[528,256]{1,0:T(8,128)(2,1)S(1)} %collective-permute-done.3.refs_4_), channel_id=1, source_target_pairs={{0,16},{16,32},{32,48},{48,64},{64,80},{80,96},{96,112},{112,128},... | collective-permute-start | bytes 811016 | tf_op jit(solution)/shard_map/ppermute | solution.py:272
  58.0 3.4 %shard_map.148 = (f32[512,256]{1,0:T(8,128)}, f32[512,256]{1,0:T(8,128)}, f32[128,128]{1,0:T(8,128)}) custom-call(s32[16,8]{1,0:T(8,128)} %copy-done.3, s32[16,8]{1,0:T(8,128)} %slice_convert_fusion.5.refs_1_, bf16[528,256]{1,0:T(8,128)(2,1)} %get-tuple-element.34.refs_1_.refs_2_, bf16[512,256]{1,0:T(8,128)(2,1)} %get-tuple-element.35.refs_2_.refs_3_, ...), custom_call_target="tpu_custom_call" | custom-call | flops 1000000000 | bytes 4000000 | tf_op jit(solution)/shard_map/pallas_call | solution.py:369
  61.4 3.3 %collective-permute-done.8.refs_5_ = bf16[512,256]{1,0:T(8,128)(2,1)S(1)} collective-permute-done((bf16[512,256]{1,0:T(8,128)(2,1)S(1)}, bf16[512,256]{1,0:T(8,128)(2,1)S(1)}, u32[]{:S(2)}, u32[]{:S(2)}) %collective-permute-start.8) | collective-permute-done | bytes 262176 | tf_op jit(solution)/shard_map/ppermute | solution.py:272
  65.9 7.7 %collective-permute-start.5 = (bf16[528,256]{1,0:T(8,128)(2,1)S(1)}, bf16[528,256]{1,0:T(8,128)(2,1)S(1)}, u32[]{:S(2)}, u32[]{:S(2)}) collective-permute-start(bf16[528,256]{1,0:T(8,128)(2,1)S(1)} %collective-permute-done.4.refs_4_), channel_id=1, source_target_pairs={{0,16},{16,32},{32,48},{48,64},{64,80},{80,96},{96,112},{112,128},... | collective-permute-start | bytes 811016 | tf_op jit(solution)/shard_map/ppermute | solution.py:272
  74.3 3.8 %shard_map.149 = (f32[512,256]{1,0:T(8,128)}, f32[512,256]{1,0:T(8,128)}, f32[128,128]{1,0:T(8,128)}) custom-call(s32[16,8]{1,0:T(8,128)} %copy-done.3, s32[16,8]{1,0:T(8,128)} %slice_convert_fusion.6.refs_1_, bf16[528,256]{1,0:T(8,128)(2,1)} %get-tuple-element.34.refs_1_.refs_2_, bf16[512,256]{1,0:T(8,128)(2,1)} %get-tuple-element.35.refs_2_.refs_3_, ...), custom_call_target="tpu_custom_call" | custom-call | flops 1000000000 | bytes 4000000 | tf_op jit(solution)/shard_map/pallas_call | solution.py:369
  79.4 4.4 %shard_map.150 = (f32[512,256]{1,0:T(8,128)}, f32[512,256]{1,0:T(8,128)}, f32[128,128]{1,0:T(8,128)}) custom-call(s32[16,8]{1,0:T(8,128)} %copy-done.3, s32[16,8]{1,0:T(8,128)} %slice_convert_fusion.7.refs_1_, bf16[528,256]{1,0:T(8,128)(2,1)} %get-tuple-element.34.refs_1_.refs_2_, bf16[512,256]{1,0:T(8,128)(2,1)} %get-tuple-element.35.refs_2_.refs_3_, ...), custom_call_target="tpu_custom_call" | custom-call | flops 1000000000 | bytes 4000000 | tf_op jit(solution)/shard_map/pallas_call | solution.py:369
  83.8 12.3 %shard_map.152 = (bf16[8,9,96,128]{3,2,1,0:T(8,128)(2,1)}, bf16[16,304,128]{2,1,0:T(8,128)(2,1)}) custom-call(f32[512,256]{1,0:T(8,128)} %get-tuple-element.48.d_donor, f32[512,256]{1,0:T(8,128)} %get-tuple-element.49.d_accept, f32[128,128]{1,0:T(8,128)} %get-tuple-element.50.loss, bf16[3,768,384]{2,1,0:T(8,128)(2,1)} %taps.3, bf16[384,768]{1,0:T(8,128)(2,1)} %point.3, ...), custom_call_target="tpu_custom_call" | custom-call | flops 5000000000 | bytes 12000000 | tf_op jit(solution)/shard_map/pallas_call | solution.py:380
  96.1 16.5 %all_to_all.35 = bf16[2,4,9,96,128]{4,3,2,1,0:T(8,128)(2,1)S(1)} all-to-all(bf16[2,4,9,96,128]{4,3,2,1,0:T(8,128)(2,1)} %bitcast.44), channel_id=1, replica_groups=mesh['y'=4,'zb'=2,'zq'=4,'zhi'=2,'x'=4,'core'=2] {'core'}, dimensions={0} | all-to-all | bytes 3538944 | tf_op jit(solution)/shard_map/all_to_all | solution.py:276
  113.0 15.5 %all_to_all.36 = bf16[4,9,96,128]{3,2,1,0:T(8,128)(2,1)S(1)} all-to-all(bf16[4,9,96,128]{3,2,1,0:T(8,128)(2,1)S(1)} %reduce_sum.51), channel_id=1, replica_groups=mesh['y'=4,'zb'=2,'zq'=4,'zhi'=2,'x'=4,'core'=2] {'x'}, dimensions={0} | all-to-all | bytes 1769472 | tf_op jit(solution)/shard_map/all_to_all | solution.py:276
  129.9 58.8 %all_to_all.37 = bf16[4,1432,128]{2,1,0:T(8,128)(2,1)S(1)} all-to-all(bf16[4,1432,128]{2,1,0:T(8,128)(2,1)S(1)} %pad_maximum_fusion), channel_id=1, replica_groups=mesh['y'=4,'zb'=2,'zq'=4,'zhi'=2,'x'=4,'core'=2] {'y'}, dimensions={0} | all-to-all | bytes 2932736 | tf_op jit(solution)/shard_map/all_to_all | solution.py:276
  189.2 10.1 %all_to_all.38 = bf16[4,358,128]{2,1,0:T(8,128)(2,1)S(1)} all-to-all(bf16[4,358,128]{2,1,0:T(8,128)(2,1)S(1)} %pad_maximum_fusion.1), channel_id=1, replica_groups=mesh['y'=4,'zb'=2,'zq'=4,'zhi'=2,'x'=4,'core'=2] {'zq'}, dimensions={0} | all-to-all | bytes 733184 | tf_op jit(solution)/shard_map/all_to_all | solution.py:276
  201.3 8.3 %collective-permute-done.10 = bf16[358,128]{1,0:T(8,128)(2,1)S(1)} collective-permute-done((bf16[358,128]{1,0:T(8,128)(2,1)S(1)}, bf16[358,128]{1,0:T(8,128)(2,1)S(1)}, u32[]{:S(2)}, u32[]{:S(2)}) %collective-permute-start.10) | collective-permute-done | bytes 91680 | tf_op jit(solution)/shard_map/ppermute | solution.py:404
  210.3 17.7 %all-to-all-start.4 = ((bf16[16,9,3,128]{3,2,1,0:T(4,128)(2,1)}), bf16[16,9,3,128]{3,2,1,0:T(4,128)(2,1)S(1)}, u32[]{:S(2)}, u32[]{:S(2)}) async-start(bf16[16,9,3,128]{3,2,1,0:T(4,128)(2,1)} %broadcast_in_dim.35), calls=%async_computation.4 | async-start | bytes 294912 | tf_op jit(solution)/shard_map/all_to_all | solution.py:276
  228.0 15.0 %all-to-all-done.4 = bf16[16,9,3,128]{3,2,1,0:T(4,128)(2,1)S(1)} async-done(((bf16[16,9,3,128]{3,2,1,0:T(4,128)(2,1)}), bf16[16,9,3,128]{3,2,1,0:T(4,128)(2,1)S(1)}, u32[]{:S(2)}, u32[]{:S(2)}) %all-to-all-start.4) | async-done | bytes 110624 | tf_op jit(solution)/shard_map/all_to_all | solution.py:276
  243.1 13.1 %all_to_all.39 = bf16[4,304,128]{2,1,0:T(8,128)(2,1)S(1)} all-to-all(bf16[4,304,128]{2,1,0:T(8,128)(2,1)S(1)} %broadcast_in_dim.36), channel_id=1, replica_groups=mesh['y'=4,'zb'=2,'zq'=4,'zhi'=2,'x'=4,'core'=2] {'zq'}, dimensions={0} | all-to-all | bytes 622592 | tf_op jit(solution)/shard_map/all_to_all | solution.py:276
  257.4 3.5 %all-to-all-start.6 = ((bf16[4,1216,128]{2,1,0:T(8,128)(2,1)}), bf16[4,1216,128]{2,1,0:T(8,128)(2,1)S(1)}, u32[]{:S(2)}, u32[]{:S(2)}) async-start(bf16[4,1216,128]{2,1,0:T(8,128)(2,1)} %broadcast_in_dim.38), calls=%async_computation.6 | async-start | bytes 2490368 | tf_op jit(solution)/shard_map/all_to_all | solution.py:276
  261.8 14.3 %all-to-all-done.6 = bf16[4,1216,128]{2,1,0:T(8,128)(2,1)S(1)} async-done(((bf16[4,1216,128]{2,1,0:T(8,128)(2,1)}), bf16[4,1216,128]{2,1,0:T(8,128)(2,1)S(1)}, u32[]{:S(2)}, u32[]{:S(2)}) %all-to-all-start.6) | async-done | bytes 1245216 | tf_op jit(solution)/shard_map/all_to_all | solution.py:276
  (103 shorter events, 26.9 us)
Async XLA Ops:
  1.7 11.0 %collective-permute-start.1 = (bf16[128,768]{1,0:T(8,128)(2,1)S(1)}, bf16[128,768]{1,0:T(8,128)(2,1)S(1)}, u32[]{:S(2)}, u32[]{:S(2)}) collective-permute-start(bf16[128,768]{1,0:T(8,128)(2,1)S(1)} %get-tuple-element.70), channel_id=1, source_target_pairs={{16,0},{32,16},{48,32},{64,48},{80,64},{96,80},{112,96},{128,112},... | collective-permute-start | bytes 589832 | tf_op jit(solution)/shard_map/ppermute | solution.py:272
  3.0 9.7 %collective-permute-start = (bf16[128,768]{1,0:T(8,128)(2,1)S(1)}, bf16[128,768]{1,0:T(8,128)(2,1)S(1)}, u32[]{:S(2)}, u32[]{:S(2)}) collective-permute-start(bf16[128,768]{1,0:T(8,128)(2,1)S(1)} %get-tuple-element.71), channel_id=1, source_target_pairs={{0,16},{16,32},{32,48},{48,64},{64,80},{80,96},{96,112},{112,128},... | collective-permute-start | bytes 589832 | tf_op jit(solution)/shard_map/ppermute | solution.py:272
  11.0 9.8 %copy-start.3 = (s32[16,8]{1,0:T(8,128)}, s32[16,8]{1,0:T(8,128)S(1)}, u32[]{:S(2)}) copy-start(s32[16,8]{1,0:T(8,128)S(1)} %stack.5.refs_0_) | copy-start | bytes 1540
  12.7 0.8 copy-start.13
  20.8 19.7 %collective-permute-start.6 = (bf16[512,256]{1,0:T(8,128)(2,1)}, bf16[512,256]{1,0:T(8,128)(2,1)S(1)}, u32[]{:S(2)}, u32[]{:S(2)}) collective-permute-start(bf16[512,256]{1,0:T(8,128)(2,1)} %get-tuple-element.35.refs_2_.refs_3_), channel_id=1, source_target_pairs={{16,0},{32,16},{48,32},{64,48},{80,64},{96,80},{112,96},{128,112},... | collective-permute-start | bytes 786440 | tf_op jit(solution)/shard_map/ppermute | solution.py:272
  22.0 19.7 %collective-permute-start.2 = (bf16[528,256]{1,0:T(8,128)(2,1)}, bf16[528,256]{1,0:T(8,128)(2,1)S(1)}, u32[]{:S(2)}, u32[]{:S(2)}) collective-permute-start(bf16[528,256]{1,0:T(8,128)(2,1)} %get-tuple-element.34.refs_1_.refs_2_), channel_id=1, source_target_pairs={{0,16},{16,32},{32,48},{48,64},{64,80},{80,96},{96,112},{112,128},... | collective-permute-start | bytes 811016 | tf_op jit(solution)/shard_map/ppermute | solution.py:272
  40.5 6.1 %copy-start.9 = (bf16[512,256]{1,0:T(8,128)(2,1)}, bf16[512,256]{1,0:T(8,128)(2,1)S(1)}, u32[]{:S(2)}) copy-start(bf16[512,256]{1,0:T(8,128)(2,1)S(1)} %collective-permute-done.6.refs_5_) | copy-start | bytes 786436
  40.5 9.6 %collective-permute-start.7 = (bf16[512,256]{1,0:T(8,128)(2,1)S(1)}, bf16[512,256]{1,0:T(8,128)(2,1)S(1)}, u32[]{:S(2)}, u32[]{:S(2)}) collective-permute-start(bf16[512,256]{1,0:T(8,128)(2,1)S(1)} %collective-permute-done.6.refs_5_), channel_id=1, source_target_pairs={{16,0},{32,16},{48,32},{64,48},{80,64},{96,80},{112,96},{128,112},... | collective-permute-start | bytes 786440 | tf_op jit(solution)/shard_map/ppermute | solution.py:272
  41.8 4.8 %copy-start.4 = (bf16[528,256]{1,0:T(8,128)(2,1)}, bf16[528,256]{1,0:T(8,128)(2,1)S(1)}, u32[]{:S(2)}) copy-start(bf16[528,256]{1,0:T(8,128)(2,1)S(1)} %collective-permute-done.2.refs_4_) | copy-start | bytes 811012
  41.8 9.5 %collective-permute-start.3 = (bf16[528,256]{1,0:T(8,128)(2,1)S(1)}, bf16[528,256]{1,0:T(8,128)(2,1)S(1)}, u32[]{:S(2)}, u32[]{:S(2)}) collective-permute-start(bf16[528,256]{1,0:T(8,128)(2,1)S(1)} %collective-permute-done.2.refs_4_), channel_id=1, source_target_pairs={{0,16},{16,32},{32,48},{48,64},{64,80},{80,96},{96,112},{112,128},... | collective-permute-start | bytes 811016 | tf_op jit(solution)/shard_map/ppermute | solution.py:272
  50.0 8.0 %copy-start.10 = (bf16[512,256]{1,0:T(8,128)(2,1)}, bf16[512,256]{1,0:T(8,128)(2,1)S(1)}, u32[]{:S(2)}) copy-start(bf16[512,256]{1,0:T(8,128)(2,1)S(1)} %collective-permute-done.7.refs_5_) | copy-start | bytes 786436
  50.0 14.6 %collective-permute-start.8 = (bf16[512,256]{1,0:T(8,128)(2,1)S(1)}, bf16[512,256]{1,0:T(8,128)(2,1)S(1)}, u32[]{:S(2)}, u32[]{:S(2)}) collective-permute-start(bf16[512,256]{1,0:T(8,128)(2,1)S(1)} %collective-permute-done.7.refs_5_), channel_id=1, source_target_pairs={{16,0},{32,16},{48,32},{64,48},{80,64},{96,80},{112,96},{128,112},... | collective-permute-start | bytes 786440 | tf_op jit(solution)/shard_map/ppermute | solution.py:272
  51.3 6.7 %copy-start.5 = (bf16[528,256]{1,0:T(8,128)(2,1)}, bf16[528,256]{1,0:T(8,128)(2,1)S(1)}, u32[]{:S(2)}) copy-start(bf16[528,256]{1,0:T(8,128)(2,1)S(1)} %collective-permute-done.3.refs_4_) | copy-start | bytes 811012
  51.4 14.6 %collective-permute-start.4 = (bf16[528,256]{1,0:T(8,128)(2,1)S(1)}, bf16[528,256]{1,0:T(8,128)(2,1)S(1)}, u32[]{:S(2)}, u32[]{:S(2)}) collective-permute-start(bf16[528,256]{1,0:T(8,128)(2,1)S(1)} %collective-permute-done.3.refs_4_), channel_id=1, source_target_pairs={{0,16},{16,32},{32,48},{48,64},{64,80},{80,96},{96,112},{112,128},... | collective-permute-start | bytes 811016 | tf_op jit(solution)/shard_map/ppermute | solution.py:272
  64.6 9.7 %copy-start.8 = (bf16[512,256]{1,0:T(8,128)(2,1)}, bf16[512,256]{1,0:T(8,128)(2,1)S(1)}, u32[]{:S(2)}) copy-start(bf16[512,256]{1,0:T(8,128)(2,1)S(1)} %collective-permute-done.8.refs_5_) | copy-start | bytes 786436
  64.6 14.1 %collective-permute-start.9 = (bf16[512,256]{1,0:T(8,128)(2,1)S(1)}, bf16[512,256]{1,0:T(8,128)(2,1)S(1)}, u32[]{:S(2)}, u32[]{:S(2)}) collective-permute-start(bf16[512,256]{1,0:T(8,128)(2,1)S(1)} %collective-permute-done.8.refs_5_), channel_id=1, source_target_pairs={{16,0},{32,16},{48,32},{64,48},{80,64},{96,80},{112,96},{128,112},... | collective-permute-start | bytes 786440 | tf_op jit(solution)/shard_map/ppermute | solution.py:272
  65.9 8.4 %copy-start.6 = (bf16[528,256]{1,0:T(8,128)(2,1)}, bf16[528,256]{1,0:T(8,128)(2,1)S(1)}, u32[]{:S(2)}) copy-start(bf16[528,256]{1,0:T(8,128)(2,1)S(1)} %collective-permute-done.4.refs_4_) | copy-start | bytes 811012
  65.9 12.2 %collective-permute-start.5 = (bf16[528,256]{1,0:T(8,128)(2,1)S(1)}, bf16[528,256]{1,0:T(8,128)(2,1)S(1)}, u32[]{:S(2)}, u32[]{:S(2)}) collective-permute-start(bf16[528,256]{1,0:T(8,128)(2,1)S(1)} %collective-permute-done.4.refs_4_), channel_id=1, source_target_pairs={{0,16},{16,32},{32,48},{48,64},{64,80},{80,96},{96,112},{112,128},... | collective-permute-start | bytes 811016 | tf_op jit(solution)/shard_map/ppermute | solution.py:272
  128.5 1.3 copy-start
  199.3 10.2 %collective-permute-start.10 = (bf16[358,128]{1,0:T(8,128)(2,1)S(1)}, bf16[358,128]{1,0:T(8,128)(2,1)S(1)}, u32[]{:S(2)}, u32[]{:S(2)}) collective-permute-start(bf16[358,128]{1,0:T(8,128)(2,1)S(1)} %pad_maximum_fusion.2), channel_id=1, source_target_pairs={{0,64},{64,0},{1,65},{65,1},{2,66},{66,2},{3,67},{67,3},{4,68},{68... | collective-permute-start | bytes 274952 | tf_op jit(solution)/shard_map/ppermute | solution.py:404
  210.3 32.7 %all-to-all-start.4 = ((bf16[16,9,3,128]{3,2,1,0:T(4,128)(2,1)}), bf16[16,9,3,128]{3,2,1,0:T(4,128)(2,1)S(1)}, u32[]{:S(2)}, u32[]{:S(2)}) async-start(bf16[16,9,3,128]{3,2,1,0:T(4,128)(2,1)} %broadcast_in_dim.35), calls=%async_computation.4 | async-start | bytes 294912 | tf_op jit(solution)/shard_map/all_to_all | solution.py:276
  257.4 18.7 %all-to-all-start.6 = ((bf16[4,1216,128]{2,1,0:T(8,128)(2,1)}), bf16[4,1216,128]{2,1,0:T(8,128)(2,1)S(1)}, u32[]{:S(2)}, u32[]{:S(2)}) async-start(bf16[4,1216,128]{2,1,0:T(8,128)(2,1)} %broadcast_in_dim.38), calls=%async_computation.6 | async-start | bytes 2490368 | tf_op jit(solution)/shard_map/all_to_all | solution.py:276
  276.2 2.8 copy-start.1
  278.2 1.1 copy-start.2
  (3 other events, 2.1 us)

commit v2 on v1

v2 whole, which is shorter than its diff:
```python
import jax
import jax.numpy as jnp
import numpy as np
from jax import lax
from jax.experimental import pallas as pl
from jax.experimental.pallas import tpu as pltpu
from jax.sharding import Mesh
from jax.sharding import PartitionSpec as P

STEP = 128
PANEL = 128
SPAN = 4
SLOTS = 16
EPSILON = 1e-06
LOSS_WEIGHT = 1.0 / 128.0
SEQ = ("y", "zb", "zq")
BATCH = ("zhi", "x", "core")
F32 = jnp.float32
BF16 = jnp.bfloat16
ROOT = 0.7978845608028654
CUBIC = 0.044715
PIECE = 96
CHUNK_ROWS = 288
EXTRA_ROWS = 16


def dot(a, b):
    return lax.dot_general(a, b, (((1,), (0,)), ((), ())), preferred_element_type=F32)


def dot_t(a, b):
    return lax.dot_general(a, b, (((1,), (1,)), ((), ())), preferred_element_type=F32)


def gelu(v):
    return 0.5 * v * (1.0 + jnp.tanh(ROOT * (v + CUBIC * (v * v * v))))


def gelu_both(v):
    square = v * v
    t = jnp.tanh(ROOT * (v + CUBIC * (square * v)))
    half = 0.5 * (1.0 + t)
    return v * half, half + 0.5 * v * (1.0 - t * t) * (ROOT * (1.0 + 3.0 * CUBIC * square))


def rms(v):
    return lax.rsqrt(jnp.mean(v * v, axis=-1, keepdims=True) + EPSILON)


def call(kernel, outs, specs, megabytes, flops, scratch=()):
    return pl.pallas_call(
        kernel,
        out_shape=outs,
        in_specs=specs,
        out_specs=[VM] * len(outs),
        scratch_shapes=list(scratch),
        compiler_params=pltpu.CompilerParams(vmem_limit_bytes=megabytes * 1024 * 1024),
        cost_estimate=pl.CostEstimate(flops=flops, bytes_accessed=1_000_000, transcendentals=0),
    )


VM = pl.BlockSpec(memory_space=pltpu.VMEM)
SM = pl.BlockSpec(memory_space=pltpu.SMEM)


def own_kernel(tok, gain, hidden, factor):
    @pl.loop(0, tok.shape[0] // STEP)
    def _(i):
        here = pl.ds(pl.multiple_of(i * STEP, STEP), STEP)
        v = tok[here, :].astype(F32)
        unit = v * rms(v)
        value, slope = gelu_both(unit * gain[...])
        hidden[here, :] = value.astype(BF16)
        factor[here, :] = (slope * unit).astype(BF16)


def forward_kernel(
    odd, tok, mine, even_edge, odd_edge, gain, taps, point, donor_w, accept_w, meta,
    hidden, conv_out, act_out, embed_out, even_feat, odd_feat,
):
    rows = tok.shape[0]
    is_odd = odd[0] > 0
    low = jnp.where(is_odd, even_edge[...], odd_edge[...])
    high = jnp.where(is_odd, odd_edge[...], even_edge[...])
    for edge, at in ((low, 0), (high, STEP + rows)):
        v = edge.astype(F32)
        hidden[pl.ds(at, STEP), :] = gelu(v * rms(v) * gain[...]).astype(BF16)
    hidden[pl.ds(STEP, rows), :] = mine[...]

    @pl.loop(0, rows // 256)
    def _(i):
        start = pl.multiple_of(i * 256, 256)
        here = pl.ds(start, 256)
        conv = dot(hidden[here, :], taps[0])
        for tap in range(1, taps.shape[0]):
            at = pl.multiple_of(start + tap * STEP, STEP)
            conv = conv + dot(hidden[pl.ds(at, 256), :], taps[tap])
        conv_out[here, :] = conv
        act = gelu(conv).astype(BF16)
        act_out[here, :] = act
        embed = (tok[here, :].astype(F32) + dot(act, point[...])).astype(BF16)
        embed_out[here, :] = embed
        donor = dot(embed, donor_w[...]).astype(BF16)
        accept = dot(embed, accept_w[...]).astype(BF16)
        even_feat[here, :] = jnp.where(is_odd, accept, donor)
        odd_feat[here, :] = jnp.where(is_odd, donor, accept)

    even_feat[pl.ds(rows, SLOTS), :] = meta[...]
    odd_feat[pl.ds(rows, SLOTS), :] = meta[...]


def side_kernel(
    odd, even_edge, odd_edge, gain, hidden, conv, act, embed, order, eye,
    factor, slope, hidden_t, act_t, embed_t,
):
    is_odd = odd[0] > 0
    low = jnp.where(is_odd, even_edge[...], odd_edge[...])
    high = jnp.where(is_odd, odd_edge[...], even_edge[...])
    for edge, at in ((low, 0), (high, STEP)):
        v = edge.astype(F32)
        unit = v * rms(v)
        factor[pl.ds(at, STEP), :] = (gelu_both(unit * gain[...])[1] * unit).astype(BF16)

    @pl.loop(0, conv.shape[0] // STEP)
    def _(i):
        here = pl.ds(pl.multiple_of(i * STEP, STEP), STEP)
        slope[here, :] = gelu_both(conv[here, :])[1]

    @pl.loop(0, hidden_t.shape[0] // 256)
    def _(i):
        here = pl.ds(pl.multiple_of(i * 256, 256), 256)
        hidden_t[here, :] = dot_t(order[here, :], hidden[...]).astype(BF16)
        embed_t[here, :] = dot_t(eye[here, :], embed[...]).astype(BF16)

    inner = act.shape[1]

    @pl.loop(0, inner // 128)
    def _(i):
        here = pl.ds(pl.multiple_of(i * 128, 128), 128)
        act_t[here, :] = dot_t(eye[here, :inner], act[...]).astype(BF16)


def pair_kernel(distance, *refs):
    if distance == 0:
        odd, own, even0, odd0, d_donor, d_accept, loss = refs
        d_donor[...] = jnp.zeros_like(d_donor)
        d_accept[...] = jnp.zeros_like(d_accept)
        loss[...] = jnp.zeros_like(loss)
    else:
        odd, own, far, even0, odd0, even1, odd1, dd_in, da_in, loss_in, d_donor, d_accept, loss = refs
        d_donor[...] = dd_in[...]
        d_accept[...] = da_in[...]
        loss[...] = loss_in[...]
    is_odd = odd[0] > 0
    scale = even0.shape[1] ** (-0.5)
    per_device = d_donor.shape[0] // PANEL
    row = lax.broadcasted_iota(jnp.int32, (PANEL, PANEL), 0)
    col = lax.broadcasted_iota(jnp.int32, (PANEL, PANEL), 1)

    def place(block):
        return pl.ds(pl.multiple_of(block * PANEL, PANEL), PANEL)

    def own_donor(block):
        return jnp.where(is_odd, odd0[place(block), :], even0[place(block), :])

    def own_accept(block):
        return jnp.where(is_odd, even0[place(block), :], odd0[place(block), :])

    if distance == 0:
        far_accept, far_donor = own_accept, None
    else:

        def far_accept(block):
            return jnp.where(is_odd, odd1[place(block), :], even1[place(block), :])

        def far_donor(block):
            return jnp.where(is_odd, even1[place(block), :], odd1[place(block), :])

    def visit(meta, j, donors, acceptors, is_owner):
        accept_block = meta[j, 2] - distance * per_device
        here = (meta[j, 4] > 0) & (accept_block >= 0) & (accept_block < per_device)

        @pl.when(here)
        def _():
            donor_block = meta[j, 0]
            dpan = donors(donor_block)
            apan = acceptors(accept_block)
            scores = dot_t(dpan, apan) * scale
            target = ((row == meta[j, 1]) & (col == meta[j, 3])).astype(F32)
            small = jnp.exp(-jnp.abs(scores))
            inverse = 1.0 / (1.0 + small)
            sigmoid = jnp.where(scores >= 0, inverse, small * inverse)
            dscore = ((sigmoid - target) * LOSS_WEIGHT).astype(BF16)
            if is_owner:
                loss[...] += (jnp.maximum(scores, 0.0) + jnp.log1p(small)) - target * scores
                d_donor[place(donor_block), :] += dot(dscore, apan) * scale
            if distance == 0 or not is_owner:
                d_accept[place(accept_block), :] += scale * lax.dot_general(
                    dscore, dpan, (((0,), (0,)), ((), ())), preferred_element_type=F32
                )

    @pl.loop(0, SLOTS)
    def _(j):
        visit(own, j, own_donor, far_accept, True)
        if distance > 0:
            visit(far, j, far_donor, own_accept, False)


def tap_grad_kernel(
    core, d_donor, d_accept, point, donor_w, accept_w, slope, hidden_t,
    keep, send, d_conv, d_feat,
):
    rows, heads = d_donor.shape
    channels = hidden_t.shape[0]

    @pl.loop(0, rows // 256)
    def _(i):
        here = pl.ds(pl.multiple_of(i * 256, 256), 256)
        dd = d_donor[here, :].astype(BF16)
        da = d_accept[here, :].astype(BF16)
        d_feat[here, :heads] = dd
        d_feat[here, heads:] = da
        d_embed = (dot_t(dd, donor_w[...]) + dot_t(da, accept_w[...])).astype(BF16)
        d_conv[here, :] = (dot_t(d_embed, point[...]) * slope[here, :]).astype(BF16)

    lanes = d_conv.shape[1] // 128
    half_rows = channels // 2
    for tap in range(3):
        for half in range(2):
            into_keep = core[0] == half

            @pl.loop(0, half_rows // (2 * PIECE))
            def _(i):
                at = pl.multiple_of(half * half_rows + i * 2 * PIECE, 2 * PIECE)
                part = dot(
                    hidden_t[pl.ds(at, 2 * PIECE), tap * STEP : tap * STEP + rows], d_conv[...]
                ).astype(BF16)

                def store(into):
                    for k in range(2):
                        for lane in range(lanes):
                            into[i * 2 + k, tap * lanes + lane] = part[
                                k * PIECE : (k + 1) * PIECE, lane * 128 : (lane + 1) * 128
                            ]

                pl.when(into_keep)(lambda: store(keep))
                pl.when(jnp.logical_not(into_keep))(lambda: store(send))


def head_grad_kernel(
    d_conv, d_feat, loss, taps, factor, edge_factor, act_t, embed_t, head_sum,
):
    rows = d_conv.shape[0]
    channels = embed_t.shape[0]
    inner = act_t.shape[0]

    def put(part, base, group_rows, first):
        for lane in range(4):
            for k in range(part.shape[0] // PIECE):
                piece = first + lane * (group_rows // PIECE) + k + base
                chunk, place = piece // 3, piece % 3
                head_sum[chunk, place * PIECE : (place + 1) * PIECE, :] = part[
                    k * PIECE : (k + 1) * PIECE, lane * 128 : (lane + 1) * 128
                ]

    for i in range(channels // (2 * PIECE)):
        part = dot(embed_t[i * 2 * PIECE : (i + 1) * 2 * PIECE, :], d_feat[...]).astype(BF16)
        put(part, 2 * i, channels, 0)
    for i in range(inner // (2 * PIECE)):
        part = dot(act_t[i * 2 * PIECE : (i + 1) * 2 * PIECE, :], d_feat[...]).astype(BF16)
        put(part, 2 * i, inner, 4 * channels // PIECE)

    total = jnp.zeros((8, channels), F32)
    last = taps.shape[0] - 1
    blocks = rows // STEP

    def weighed(block, tap, weights):
        product = dot_t(d_conv[block * STEP : (block + 1) * STEP, :], taps[tap]) * weights.astype(F32)
        return jnp.sum(product.reshape(STEP // 8, 8, channels), axis=0)

    for block in range(blocks):
        for tap in range(taps.shape[0]):
            at = block + tap - 1
            if at < 0:
                weights = edge_factor[:STEP, :]
            elif at >= blocks:
                weights = edge_factor[STEP:, :]
            else:
                weights = factor[at * STEP : (at + 1) * STEP, :]
            total = total + weighed(block, tap, weights)
    gain = jnp.sum(total, axis=0, keepdims=True)
    loss_row = jnp.sum(loss[...], axis=0, keepdims=True) * LOSS_WEIGHT
    loss_all = jnp.broadcast_to(jnp.sum(loss_row, axis=1, keepdims=True), (1, 128))
    at_row = lax.broadcasted_iota(jnp.int32, (EXTRA_ROWS, 128), 0)
    for chunk in range(head_sum.shape[0]):
        if chunk < channels // 128:
            value = gain[:, chunk * 128 : (chunk + 1) * 128]
        elif chunk == channels // 128:
            value = loss_all
        else:
            value = jnp.zeros((1, 128), F32)
        coarse = value.astype(BF16).astype(F32)
        block = jnp.where(at_row == 0, coarse, 0.0) + jnp.where(at_row == 8, value - coarse, 0.0)
        head_sum[chunk, CHUNK_ROWS:, :] = block.astype(BF16)


def finish_kernel(
    place_y, own, one, two, three, donor_w, accept_w,
    grad_donor, grad_accept, grad_point, gain, loss, held, act_donor, act_accept,
):
    count = held.shape[0]
    for back, part in enumerate((own, one, two, three)):
        held[lax.rem(place_y[0] + count - back, count)] = part[...]
    channels = grad_donor.shape[0]
    inner = act_donor.shape[0]
    chunk_rows = CHUNK_ROWS + EXTRA_ROWS
    piece = 0
    for into in (grad_donor, grad_accept, act_donor, act_accept):
        for lane in range(2):
            for k in range(into.shape[0] // PIECE):
                chunk, place = piece // 3, piece % 3
                at = (chunk % 4) * chunk_rows + place * PIECE
                into[k * PIECE : (k + 1) * PIECE, lane * 128 : (lane + 1) * 128] = held[
                    chunk // 4, at : at + PIECE, :
                ]
                piece += 1

    @pl.loop(0, inner // 128)
    def _(i):
        here = pl.ds(pl.multiple_of(i * 128, 128), 128)
        grad_point[here, :] = (
            dot_t(act_donor[here, :], donor_w[...]) + dot_t(act_accept[here, :], accept_w[...])
        ).astype(BF16)

    for chunk in range(channels // 128 + 1):
        at = (chunk % 4) * chunk_rows + CHUNK_ROWS
        block = held[chunk // 4, at : at + EXTRA_ROWS, :].astype(F32)
        value = block[0:1, :] + block[8:9, :]
        if chunk < channels // 128:
            gain[:, chunk * 128 : (chunk + 1) * 128] = value
        else:
            loss[...] = value


def swapped(block, first):
    count = lax.axis_size(SEQ)
    pairs = [(i, i + 1) for i in range(first, count - 1, 2)]
    return lax.ppermute(block, SEQ, pairs + [(j, i) for i, j in pairs])


def swap_parts(parts, axis):
    return lax.all_to_all(parts, axis, 0, 0, tiled=True)


def gather_parts(part, axis):
    count = lax.axis_size(axis)
    return swap_parts(jnp.broadcast_to(part[None], (count,) + part.shape), axis)


def summed(parts):
    return jnp.sum(parts.astype(F32), axis=0)


def resplit(total):
    body = total[..., :CHUNK_ROWS, :].astype(BF16)
    value = (
        total[..., CHUNK_ROWS : CHUNK_ROWS + 8, :] + total[..., CHUNK_ROWS + 8 : CHUNK_ROWS + 16, :]
    )
    coarse = lax.reduce_precision(value, 8, 7)
    return jnp.concatenate([body, coarse.astype(BF16), (value - coarse).astype(BF16)], axis=-2)


def on_device(
    activations, norm_gain, dilated_tap_weight, point_weight, donor_weight, acceptor_weight,
    pair_sites, pair_count, order, eye,
):
    tokens = activations[0]
    rows, channels = tokens.shape
    tap_count, _, inner = dilated_tap_weight.shape
    heads = donor_weight.shape[1]
    blocks = rows // PANEL
    shape = jax.ShapeDtypeStruct
    here = lax.axis_index(SEQ)
    odd = (here % 2).astype(jnp.int32)[None]
    is_odd = odd[0] > 0
    start, end = tokens[:STEP], tokens[rows - STEP :]
    even_edge = swapped(jnp.where(is_odd, start, end), 0)
    odd_edge = swapped(jnp.where(is_odd, end, start), 1)
    gain = norm_gain[None]
    sites = pair_sites[0]
    first = here * blocks
    live = (jnp.arange(SLOTS, dtype=jnp.int32) < pair_count[0, 0]).astype(jnp.int32)
    meta = jnp.stack(
        [
            sites[:, 0] // PANEL - first,
            sites[:, 0] % PANEL,
            sites[:, 1] // PANEL - first,
            sites[:, 1] % PANEL,
            live,
        ]
        + [jnp.zeros_like(live)] * 3,
        axis=1,
    )
    meta_rows = jnp.pad(meta.astype(BF16), ((0, 0), (0, heads - meta.shape[1])))

    mine, factor = call(
        own_kernel, [shape((rows, channels), BF16)] * 2, [VM] * 2, 12, 2_000_000_000
    )(tokens, gain)
    feat = shape((rows + SLOTS, heads), BF16)
    hidden, conv, act, embed, even_feat, odd_feat = call(
        forward_kernel,
        [
            shape((rows + 2 * STEP, channels), BF16),
            shape((rows, inner), F32),
            shape((rows, inner), BF16),
            shape((rows, channels), BF16),
            feat,
            feat,
        ],
        [SM] + [VM] * 10,
        20,
        4_000_000_000,
    )(
        odd, tokens, mine, even_edge, odd_edge, gain, dilated_tap_weight, point_weight,
        donor_weight, acceptor_weight, meta_rows,
    )

    acc_shapes = [shape((rows, heads), F32), shape((rows, heads), F32), shape((PANEL, PANEL), F32)]
    acc = call(
        lambda *refs: pair_kernel(0, *refs), acc_shapes, [SM] * 2 + [VM] * 2, 12, 2_000_000_000
    )(odd, meta, even_feat, odd_feat)
    edge_factor, slope, hidden_t, act_t, embed_t = call(
        side_kernel,
        [
            shape((2 * STEP, channels), BF16),
            shape((rows, inner), F32),
            shape((channels, rows + 2 * STEP), BF16),
            shape((inner, rows), BF16),
            shape((channels, rows), BF16),
        ],
        [SM] + [VM] * 9,
        20,
        6_000_000_000,
    )(odd, even_edge, odd_edge, gain, hidden, conv, act, embed, order, eye)
    even_far, odd_far = even_feat, odd_feat
    for distance in range(1, SPAN + 1):
        if distance == 1:
            even_far, odd_far = swapped(even_feat, 0), swapped(odd_feat, 1)
        else:
            even_far, odd_far = swapped(odd_far, 0), swapped(even_far, 1)
        far_meta = jnp.where(is_odd, even_far[rows:, :8], odd_far[rows:, :8]).astype(jnp.int32)
        acc = call(
            lambda *refs, distance=distance: pair_kernel(distance, *refs),
            acc_shapes,
            [SM] * 3 + [VM] * 7,
            12,
            2_500_000_000,
        )(odd, meta, far_meta, even_feat, odd_feat, even_far, odd_far, *acc)

    chunk = CHUNK_ROWS + EXTRA_ROWS
    lanes = inner // 128
    slabs = tap_count * lanes
    half = shape((4, slabs, PIECE, 128), BF16)
    keep, send, d_conv, d_feat = call(
        tap_grad_kernel,
        [half, half, shape((rows, inner), BF16), shape((rows, 2 * heads), BF16)],
        [SM] + [VM] * 7,
        20,
        4_000_000_000,
    )(
        lax.axis_index("core").astype(jnp.int32)[None], acc[0], acc[1], point_weight, donor_weight,
        acceptor_weight, slope, hidden_t,
    )
    received = lax.ppermute(send, "core", [(0, 1), (1, 0)])
    (head_sum,) = call(
        head_grad_kernel, [shape((16, chunk, 128), BF16)], [VM] * 8, 20, 4_000_000_000
    )(d_conv, d_feat, acc[2], dilated_tap_weight, factor, edge_factor, act_t, embed_t)

    conv_sum = (keep.astype(F32) + received.astype(F32)).astype(BF16)
    head_rows = 4 * chunk
    both = jnp.concatenate(
        [head_sum.reshape(4, head_rows, 128), conv_sum.reshape(4, slabs * PIECE, 128)], axis=1
    )
    both = summed(swap_parts(both, "y"))
    head_sum = resplit(both[:head_rows].reshape(4, chunk, 128))
    conv_sum = both[head_rows:].astype(BF16)
    conv_sum = conv_sum.reshape(slabs, 4, 24, 128).transpose(1, 0, 2, 3).reshape(4, slabs * 24, 128)
    both = jnp.concatenate([head_sum, conv_sum], axis=1)
    both = summed(swap_parts(both, "zq"))
    both = jnp.concatenate([resplit(both[:chunk]), both[chunk:].astype(BF16)], axis=0)
    other = lax.ppermute(both, "zb", [(0, 1), (1, 0)])
    both = both.astype(F32) + other.astype(F32)
    head_sum = resplit(both[:chunk])
    conv_sum = both[chunk:].astype(BF16).reshape(slabs, 2, 12, 128)
    conv_sum = lax.dynamic_index_in_dim(conv_sum, lax.axis_index("zb"), 1, keepdims=False)
    other = lax.ppermute(conv_sum, "zhi", [(0, 1), (1, 0)])

    head_sum = gather_parts(head_sum, "zq").reshape(head_rows, 128)
    ring = [
        lax.ppermute(head_sum, "y", [(i, (i + ahead) % 4) for i in range(4)]) for ahead in (1, 2, 3)
    ]
    conv_sum = (conv_sum.astype(F32) + other.astype(F32)).astype(BF16)
    pieces = gather_parts(conv_sum, ("x", "core")).astype(F32)
    pieces = jnp.sum(pieces.reshape(4, 2, tap_count, lanes, 12, 128), axis=0)
    grad_conv = pieces.transpose(1, 0, 3, 2, 4).reshape(tap_count, 24, inner)
    head_weight = shape((channels, heads), BF16)
    grad_donor, grad_accept, grad_point, grad_gain, loss = call(
        finish_kernel,
        [head_weight, head_weight, shape((inner, channels), BF16), shape((1, channels), F32), shape((1, 128), F32)],
        [SM] + [VM] * 6,
        16,
        1_000_000_000,
        [
            pltpu.VMEM((4, head_rows, 128), BF16),
            pltpu.VMEM((inner, heads), BF16),
            pltpu.VMEM((inner, heads), BF16),
        ],
    )(lax.axis_index("y").astype(jnp.int32)[None], head_sum, *ring, donor_weight, acceptor_weight)
    return grad_conv, grad_point[None], grad_donor[None], grad_accept[None], grad_gain, loss[0, :1]


def channel_order():
    core, y, zq, zb, k = np.meshgrid(*[np.arange(n) for n in (2, 4, 4, 2, 12)], indexing="ij")
    channel = (24 * (8 * y + 4 * zb + zq) + 12 * core + k).reshape(-1)
    return np.eye(channel.size, dtype=np.float32)[channel]


def solution(mesh):
    fine = Mesh(mesh.devices.reshape(4, 2, 4, 2, 4, 2), SEQ + BATCH)
    placed = jax.shard_map(
        on_device,
        mesh=fine,
        in_specs=(
            P(BATCH, SEQ, None),
            P(),
            P(),
            P(),
            P(),
            P(),
            P(BATCH, SEQ, None),
            P(BATCH, SEQ),
            P(),
            P(),
        ),
        out_specs=(
            P(None, SEQ, None),
            P(BATCH, None, None),
            P(BATCH, None, None),
            P(BATCH, None, None),
            P(BATCH, None),
            P(BATCH),
        ),
        check_vma=False,
    )

    def run(*arrays):
        order = jnp.asarray(channel_order(), BF16)
        eye = jnp.eye(order.shape[0], dtype=BF16)
        return placed(*arrays, order, eye)

    return run
```

time: 282 us -> 230 us (0.82)
  blocking collectives: 114 us -> 63.1 us
  Pallas kernels: 48.8 us -> 31.1 us
  starting transfers between devices: 56.7 us -> 72.6 us
  waiting for transfers between devices: 40.8 us -> 55.1 us
  local copies, waits for them, and re-layouts: 10.8 us -> 2.85 us
  other arithmetic: 6.26 us -> 2.46 us
    all_to_all x5 -> x2, blocking collectives: 114 us -> 63.1 us  [swap_parts(): return lax.all_to_all(parts, axis, 0, 0, tiled=True)]
    ppermute x10 -> x15, waiting for transfers between devices: 3.28 us -> 40.7 us  [the longest x10 23.4 us: swapped(): return lax.ppermute(block, SEQ, pairs + [(j, i) for i, j in pairs])]
    all_to_all x2, waiting for transfers between devices: 29.3 us -> 0.01 us  [swap_parts(): return lax.all_to_all(parts, axis, 0, 0, tiled=True)]
    ppermute x10 -> x15, starting transfers between devices: 33.6 us -> 59.1 us  [the longest x10 35.2 us: swapped(): return lax.ppermute(block, SEQ, pairs + [(j, i) for i, j in pairs])]
    pallas_call x7 -> x10, Pallas kernels: 41.5 us -> 27.9 us  [the longest x4 10 us: on_device(): call(lambda *refs, distance=distance: pair_kernel(distance, *refs), acc_s...]
    all_to_all x2, starting transfers between devices: 21.2 us -> 8.34 us  [swap_parts(): return lax.all_to_all(parts, axis, 0, 0, tiled=True)]
    ppermute x1, waiting for transfers between devices: 8.26 us -> 14.4 us  [on_device(): other = lax.ppermute(both, 'zb', [(0, 1), (1, 0)])]
    pallas_call x1, Pallas kernels: 7.27 us -> 3.19 us  [on_device(): call(forward_kernel, [shape((rows + 2 * STEP, channels), BF16), shape((ro...]
  transfers between devices with their start and end apart: 13 -> 18, of which waited for: 4 -> 8; matrix products, arithmetic and copies ran while one was open for 3% -> 1% of each run, Pallas kernels for 9% -> 8%
where the time goes in v2:
time: 230 us; the launch traced here: 229 us
  starting transfers between devices  72.6 us (32%)
  blocking collectives  63.1 us (27%)
  waiting for transfers between devices  55.1 us (24%)
  Pallas kernels  31.1 us (14%)
  local copies, waits for them, and re-layouts  2.85 us (1%)
  other arithmetic  2.46 us (1%)
    all_to_all x2, blocking collectives, swap_parts(): return lax.all_to_all(parts, axis, 0, 0, tiled=True)  63.1 us
    ppermute x10, starting transfers between devices, swapped(): return lax.ppermute(block, SEQ, pairs + [(j, i) for i, j in pairs])  35.2 us
    ppermute x10, waiting for transfers between devices, swapped(): return lax.ppermute(block, SEQ, pairs + [(j, i) for i, j in pairs])  23.4 us
    ppermute x1, waiting for transfers between devices, on_device(): other = lax.ppermute(both, 'zb', [(0, 1), (1, 0)])  14.4 us
    ppermute x1, starting transfers between devices, on_device(): other = lax.ppermute(conv_sum, 'zhi', [(0, 1), (1, 0)])  13.6 us
    ppermute x3, waiting for transfers between devices, on_device(): lax.ppermute(head_sum, 'y', [(i, (i + ahead) % 4) for i in range(4)])  13.2 us
    pallas_call x4, Pallas kernels, on_device(): call(lambda *refs, distance=distance: pair_kernel(distance, *refs), acc_s...  10 us
    all_to_all x2, starting transfers between devices, swap_parts(): return lax.all_to_all(parts, axis, 0, 0, tiled=True)  8.34 us
  transfers between devices with their start and end apart: 18, of which 8 were waited for; matrix products, arithmetic and copies ran while one was open for 1% of the time, Pallas kernels for 8%

profile of v2, /device:TPU:1, one launch (start us, length us, event | category | flops | bytes accessed | tf_op | source)
XLA Modules:
  0.0 229.1 jit_solution(6582729683518783898)
XLA Ops:
  2.5 7.2 %collective-permute-start = (bf16[128,768]{1,0:T(8,128)(2,1)S(1)}, bf16[128,768]{1,0:T(8,128)(2,1)S(1)}, u32[]{:S(2)}, u32[]{:S(2)}) collective-permute-start(bf16[128,768]{1,0:T(8,128)(2,1)S(1)} %get-tuple-element.81), channel_id=1, source_target_pairs={{0,16},{32,48},{64,80},{96,112},{128,144},{160,176},{192,208},{224... | collective-permute-start | bytes 589832 | tf_op jit(solution)/shard_map/ppermute | solution.py:348
  13.2 3.2 %shard_map.146 = (bf16[768,768]{1,0:T(8,128)(2,1)S(1)}, f32[512,384]{1,0:T(8,128)S(1)}, bf16[512,384]{1,0:T(8,128)(2,1)S(1)}, bf16[512,768]{1,0:T(8,128)(2,1)S(1...) custom-call(s32[1]{0:T(128)} %bitcast.1.odd.refs_0_, bf16[512,768]{1,0:T(8,128)(2,1)S(1)} %bitcast.39, ...), custom_call_target="tpu_custom_call" | custom-call | flops 4000000000 | bytes 1000000 | tf_op jit(solution)/shard_map/pallas_call | solution.py:410
  17.1 12.7 %collective-permute-start.6 = (bf16[528,256]{1,0:T(8,128)(2,1)S(1)}, bf16[528,256]{1,0:T(8,128)(2,1)S(1)}, u32[]{:S(2)}, u32[]{:S(2)}) collective-permute-start(bf16[528,256]{1,0:T(8,128)(2,1)S(1)} %get-tuple-element.45.refs_2_.refs_3_), channel_id=1, source_target_pairs={{0,16},{32,48},{64,80},{96,112},{128,144},{160,176},{192,208},{224... | collective-permute-start | bytes 811016 | tf_op jit(solution)/shard_map/ppermute | solution.py:348
  29.8 4.4 %shard_map.152 = (bf16[256,768]{1,0:T(8,128)(2,1)S(1)}, f32[512,384]{1,0:T(8,128)S(1)}, bf16[768,768]{1,0:T(8,128)(2,1)S(1)}, bf16[384,512]{1,0:T(8,128)(2,1)S(1)}, bf16[768,512]{1,0:T(8,128)(2,1)S(1)}) custom-call(s32[1]{0:T(128)} %bitcast.1.odd.refs_0_, bf16[128,768]{1,0:T(8,128)(2,1)S(1)} %collective-permute-done.even_edge, ...), custom_call_target="tpu_custom_call" | custom-call | flops 6000000000 | bytes 1000000 | tf_op jit(solution)/shard_map/pallas_call | solution.py:432
  35.6 3.5 %collective-permute-start.3 = (bf16[528,256]{1,0:T(8,128)(2,1)S(1)}, bf16[528,256]{1,0:T(8,128)(2,1)S(1)}, u32[]{:S(2)}, u32[]{:S(2)}) collective-permute-start(bf16[528,256]{1,0:T(8,128)(2,1)S(1)} %collective-permute-done.2.refs_6_), channel_id=1, source_target_pairs={{0,16},{32,48},{64,80},{96,112},{128,144},{160,176},{192,208},{224... | collective-permute-start | bytes 811016 | tf_op jit(solution)/shard_map/ppermute | solution.py:348
  42.2 9.6 %collective-permute-done.3.refs_5_ = bf16[528,256]{1,0:T(8,128)(2,1)S(1)} collective-permute-done((bf16[528,256]{1,0:T(8,128)(2,1)S(1)}, bf16[528,256]{1,0:T(8,128)(2,1)S(1)}, u32[]{:S(2)}, u32[]{:S(2)}) %collective-permute-start.3) | collective-permute-done | bytes 270368 | tf_op jit(solution)/shard_map/ppermute | solution.py:348
  52.5 3.7 %collective-permute-start.8 = (bf16[528,256]{1,0:T(8,128)(2,1)S(1)}, bf16[528,256]{1,0:T(8,128)(2,1)S(1)}, u32[]{:S(2)}, u32[]{:S(2)}) collective-permute-start(bf16[528,256]{1,0:T(8,128)(2,1)S(1)} %collective-permute-done.7.refs_6_), channel_id=1, source_target_pairs={{0,16},{32,48},{64,80},{96,112},{128,144},{160,176},{192,208},{224... | collective-permute-start | bytes 811016 | tf_op jit(solution)/shard_map/ppermute | solution.py:348
  57.9 4.7 %collective-permute-start.5 = (bf16[528,256]{1,0:T(8,128)(2,1)S(1)}, bf16[528,256]{1,0:T(8,128)(2,1)S(1)}, u32[]{:S(2)}, u32[]{:S(2)}) collective-permute-start(bf16[528,256]{1,0:T(8,128)(2,1)S(1)} %collective-permute-done.4.refs_6_), channel_id=1, source_target_pairs={{0,16},{32,48},{64,80},{96,112},{128,144},{160,176},{192,208},{224... | collective-permute-start | bytes 811016 | tf_op jit(solution)/shard_map/ppermute | solution.py:348
  62.6 5.3 %collective-permute-done.8.refs_5_ = bf16[528,256]{1,0:T(8,128)(2,1)S(1)} collective-permute-done((bf16[528,256]{1,0:T(8,128)(2,1)S(1)}, bf16[528,256]{1,0:T(8,128)(2,1)S(1)}, u32[]{:S(2)}, u32[]{:S(2)}) %collective-permute-start.8) | collective-permute-done | bytes 270368 | tf_op jit(solution)/shard_map/ppermute | solution.py:348
  70.9 8.6 %collective-permute-done.5.refs_5_ = bf16[528,256]{1,0:T(8,128)(2,1)S(1)} collective-permute-done((bf16[528,256]{1,0:T(8,128)(2,1)S(1)}, bf16[528,256]{1,0:T(8,128)(2,1)S(1)}, u32[]{:S(2)}, u32[]{:S(2)}) %collective-permute-start.5) | collective-permute-done | bytes 270368 | tf_op jit(solution)/shard_map/ppermute | solution.py:348
  79.5 3.7 %shard_map.151 = (f32[512,256]{1,0:T(8,128)S(1)}, f32[512,256]{1,0:T(8,128)S(1)}, f32[128,128]{1,0:T(8,128)S(1)}) custom-call(s32[1]{0:T(128)} %bitcast.1.odd.refs_0_, s32[16,8]{1,0:T(8,128)S(1)} %stack.5.refs_1_, s32[16,8]{1,0:T(8,128)S(1)} %fusion.14.refs_2_, bf16[528,256]{1,0:T(8,128)(2,1)S(1)} %get-tuple-element.45.refs_2_.refs_3_, ...), custom_call_target="tpu_custom_call" | custom-call | flops 2500000000 | bytes 1000000 | tf_op jit(solution)/shard_map/pallas_call | solution.py:452
  83.1 4.6 %shard_map.153 = (bf16[4,9,96,128]{3,2,1,0:T(8,128)(2,1)S(1)}, bf16[4,9,96,128]{3,2,1,0:T(8,128)(2,1)S(1)}, bf16[512,384]{1,0:T(8,128)(2,1)S(1)}, bf16[512,512]{1,0:T(8,128)(2,1)S(1)}) custom-call(s32[1]{0:T(128)} %bitcast.core, f32[512,256]{1,0:T(8,128)S(1)} %get-tuple-element.58.d_donor, f32[512,256]{1,0:T(8,128)S(1)} %get-tuple-element.59.d_accept, ...), custom_call_target="tpu_custom_call" | custom-call | flops 4000000000 | bytes 1000000 | tf_op jit(solution)/shard_map/pallas_call | solution.py:464
  90.2 3.0 %shard_map.154 = bf16[16,304,128]{2,1,0:T(8,128)(2,1)S(1)} custom-call(bf16[512,384]{1,0:T(8,128)(2,1)S(1)} %get-tuple-element.66.d_conv, bf16[512,512]{1,0:T(8,128)(2,1)S(1)} %get-tuple-element.67.d_feat, f32[128,128]{1,0:T(8,128)S(1)} %get-tuple-element.68.loss, bf16[3,768,384]{2,1,0:T(8,128)(2,1)S(1)} %copy-done.1, ...), custom_call_target="tpu_custom_call" | custom-call | flops 4000000000 | bytes 1000000 | tf_op jit(solution)/shard_map/pallas_call | solution.py:475
  93.6 47.0 %all_to_all.20 = bf16[4,2080,128]{2,1,0:T(8,128)(2,1)S(1)} all-to-all(bf16[4,2080,128]{2,1,0:T(8,128)(2,1)S(1)} %pad_maximum_fusion), channel_id=1, replica_groups=mesh['y'=4,'zb'=2,'zq'=4,'zhi'=2,'x'=4,'core'=2] {'y'}, dimensions={0} | all-to-all | bytes 4259840 | tf_op jit(solution)/shard_map/all_to_all | solution.py:352
  141.2 16.0 %all_to_all.21 = bf16[4,520,128]{2,1,0:T(8,128)(2,1)S(1)} all-to-all(bf16[4,520,128]{2,1,0:T(8,128)(2,1)S(1)} %pad_maximum_fusion.1), channel_id=1, replica_groups=mesh['y'=4,'zb'=2,'zq'=4,'zhi'=2,'x'=4,'core'=2] {'zq'}, dimensions={0} | all-to-all | bytes 1064960 | tf_op jit(solution)/shard_map/all_to_all | solution.py:352
  157.4 5.2 %collective-permute-start.11 = (bf16[520,128]{1,0:T(8,128)(2,1)S(1)}, bf16[520,128]{1,0:T(8,128)(2,1)S(1)}, u32[]{:S(2)}, u32[]{:S(2)}) collective-permute-start(bf16[520,128]{1,0:T(8,128)(2,1)S(1)} %pad_maximum_fusion.2), channel_id=1, source_target_pairs={{0,64},{64,0},{1,65},{65,1},{2,66},{66,2},{3,67},{67,3},{4,68},{68... | collective-permute-start | bytes 399368 | tf_op jit(solution)/shard_map/ppermute | solution.py:491
  162.6 14.4 %collective-permute-done.11 = bf16[520,128]{1,0:T(8,128)(2,1)S(1)} collective-permute-done((bf16[520,128]{1,0:T(8,128)(2,1)S(1)}, bf16[520,128]{1,0:T(8,128)(2,1)S(1)}, u32[]{:S(2)}, u32[]{:S(2)}) %collective-permute-start.11) | collective-permute-done | bytes 133152 | tf_op jit(solution)/shard_map/ppermute | solution.py:491
  177.9 3.5 %all-to-all-start.3 = ((bf16[4,304,128]{2,1,0:T(8,128)(2,1)}), bf16[4,304,128]{2,1,0:T(8,128)(2,1)S(1)}, u32[]{:S(2)}, u32[]{:S(2)}) async-start(bf16[4,304,128]{2,1,0:T(8,128)(2,1)} %broadcast_in_dim.38), calls=%async_computation.3 | async-start | bytes 622592 | tf_op jit(solution)/shard_map/all_to_all | solution.py:352
  181.4 13.6 %collective-permute-start.12 = (bf16[9,12,128]{2,1,0:T(8,128)(2,1)S(1)}, bf16[9,12,128]{2,1,0:T(8,128)(2,1)S(1)}, u32[]{:S(2)}, u32[]{:S(2)}) collective-permute-start(bf16[9,12,128]{2,1,0:T(8,128)(2,1)S(1)} %dynamic-slice_bitcast_fusion), channel_id=1, source_target_pairs={{0,8},{8,0},{1,9},{9,1},{2,10},{10,2},{3,11},{11,3},{4,12},{12,4},... | collective-permute-start | bytes 82952 | tf_op jit(solution)/shard_map/ppermute | solution.py:496
  195.0 4.1 %collective-permute-done.12 = bf16[9,12,128]{2,1,0:T(8,128)(2,1)S(1)} collective-permute-done((bf16[9,12,128]{2,1,0:T(8,128)(2,1)S(1)}, bf16[9,12,128]{2,1,0:T(8,128)(2,1)S(1)}, u32[]{:S(2)}, u32[]{:S(2)}) %collective-permute-start.12) | collective-permute-done | bytes 27680 | tf_op jit(solution)/shard_map/ppermute | solution.py:496
  199.8 4.9 %all-to-all-start.2 = ((bf16[8,9,12,128]{3,2,1,0:T(8,128)(2,1)}), bf16[8,9,12,128]{3,2,1,0:T(8,128)(2,1)S(1)}, u32[]{:S(2)}, u32[]{:S(2)}) async-start(bf16[8,9,12,128]{3,2,1,0:T(8,128)(2,1)} %broadcast_in_dim.36), calls=%async_computation.2 | async-start | bytes 589824 | tf_op jit(solution)/shard_map/all_to_all | solution.py:352
  207.5 3.1 %collective-permute-start.14 = (bf16[1216,128]{1,0:T(8,128)(2,1)S(1)}, bf16[1216,128]{1,0:T(8,128)(2,1)S(1)}, u32[]{:S(2)}, u32[]{:S(2)}) collective-permute-start(bf16[1216,128]{1,0:T(8,128)(2,1)S(1)} %bitcast.35), channel_id=1, source_target_pairs={{0,256},{128,384},{256,0},{384,128},{1,257},{129,385},{257,1},{385... | collective-permute-start | bytes 933896 | tf_op jit(solution)/shard_map/ppermute | solution.py:500
  215.4 4.0 %collective-permute-done.14.two = bf16[1216,128]{1,0:T(8,128)(2,1)S(1)} collective-permute-done((bf16[1216,128]{1,0:T(8,128)(2,1)S(1)}, bf16[1216,128]{1,0:T(8,128)(2,1)S(1)}, u32[]{:S(2)}, u32[]{:S(2)}) %collective-permute-start.14) | collective-permute-done | bytes 311328 | tf_op jit(solution)/shard_map/ppermute | solution.py:500
  219.5 7.4 %collective-permute-done.13.one = bf16[1216,128]{1,0:T(8,128)(2,1)S(1)} collective-permute-done((bf16[1216,128]{1,0:T(8,128)(2,1)S(1)}, bf16[1216,128]{1,0:T(8,128)(2,1)S(1)}, u32[]{:S(2)}, u32[]{:S(2)}) %collective-permute-start.13) | collective-permute-done | bytes 311328 | tf_op jit(solution)/shard_map/ppermute | solution.py:500
  (88 shorter events, 29.8 us)
Async XLA Ops:
  0.6 10.2 %copy-start = (bf16[1,512,768]{2,1,0:T(8,128)(2,1)S(1)}, bf16[1,512,768]{2,1,0:T(8,128)(2,1)}, u32[]{:S(2)}) copy-start(bf16[1,512,768]{2,1,0:T(8,128)(2,1)} %param.10) | copy-start | bytes 2359300
  0.6 9.8 %copy-start.7 = (s32[1,16,2]{1,2,0:T(2,128)S(1)}, s32[1,16,2]{1,2,0:T(2,128)}, u32[]{:S(2)}) copy-start(s32[1,16,2]{1,2,0:T(2,128)} %param.16) | copy-start | bytes 388
  0.7 10.1 %copy-start.6 = (f32[768]{0:T(1024)S(1)}, f32[768]{0:T(1024)}, u32[]{:S(2)}) copy-start(f32[768]{0:T(1024)} %param.11) | copy-start | bytes 9220
  1.8 11.4 %collective-permute-start.1 = (bf16[128,768]{1,0:T(8,128)(2,1)S(1)}, bf16[128,768]{1,0:T(8,128)(2,1)S(1)}, u32[]{:S(2)}, u32[]{:S(2)}) collective-permute-start(bf16[128,768]{1,0:T(8,128)(2,1)S(1)} %get-tuple-element.80), channel_id=1, source_target_pairs={{16,32},{48,64},{80,96},{112,128},{144,160},{176,192},{208,224},{2... | collective-permute-start | bytes 589832 | tf_op jit(solution)/shard_map/ppermute | solution.py:348
  2.5 10.7 %collective-permute-start = (bf16[128,768]{1,0:T(8,128)(2,1)S(1)}, bf16[128,768]{1,0:T(8,128)(2,1)S(1)}, u32[]{:S(2)}, u32[]{:S(2)}) collective-permute-start(bf16[128,768]{1,0:T(8,128)(2,1)S(1)} %get-tuple-element.81), channel_id=1, source_target_pairs={{0,16},{32,48},{64,80},{96,112},{128,144},{160,176},{192,208},{224... | collective-permute-start | bytes 589832 | tf_op jit(solution)/shard_map/ppermute | solution.py:348
  10.9 2.3 %copy-start.1 = (bf16[3,768,384]{2,1,0:T(8,128)(2,1)S(1)}, bf16[3,768,384]{2,1,0:T(8,128)(2,1)}, u32[]{:S(2)}) copy-start(bf16[3,768,384]{2,1,0:T(8,128)(2,1)} %taps.3) | copy-start | bytes 5308420
  10.9 2.3 %copy-start.2 = (bf16[384,768]{1,0:T(8,128)(2,1)S(1)}, bf16[384,768]{1,0:T(8,128)(2,1)}, u32[]{:S(2)}) copy-start(bf16[384,768]{1,0:T(8,128)(2,1)} %point.3) | copy-start | bytes 1769476
  13.2 16.6 %copy-start.5 = (bf16[768,768]{1,0:T(8,128)(2,1)S(1)}, bf16[768,768]{1,0:T(8,128)(2,1)}, u32[]{:S(2)}) copy-start(bf16[768,768]{1,0:T(8,128)(2,1)} %constant.86.clone.order) | copy-start | bytes 3538948
  16.4 19.2 %collective-permute-start.2 = (bf16[528,256]{1,0:T(8,128)(2,1)S(1)}, bf16[528,256]{1,0:T(8,128)(2,1)S(1)}, u32[]{:S(2)}, u32[]{:S(2)}) collective-permute-start(bf16[528,256]{1,0:T(8,128)(2,1)S(1)} %get-tuple-element.44.refs_3_.refs_4_), channel_id=1, source_target_pairs={{16,32},{48,64},{80,96},{112,128},{144,160},{176,192},{208,224},{2... | collective-permute-start | bytes 811016 | tf_op jit(solution)/shard_map/ppermute | solution.py:348
  17.1 22.1 %collective-permute-start.6 = (bf16[528,256]{1,0:T(8,128)(2,1)S(1)}, bf16[528,256]{1,0:T(8,128)(2,1)S(1)}, u32[]{:S(2)}, u32[]{:S(2)}) collective-permute-start(bf16[528,256]{1,0:T(8,128)(2,1)S(1)} %get-tuple-element.45.refs_2_.refs_3_), channel_id=1, source_target_pairs={{0,16},{32,48},{64,80},{96,112},{128,144},{160,176},{192,208},{224... | collective-permute-start | bytes 811016 | tf_op jit(solution)/shard_map/ppermute | solution.py:348
  35.6 16.2 %collective-permute-start.3 = (bf16[528,256]{1,0:T(8,128)(2,1)S(1)}, bf16[528,256]{1,0:T(8,128)(2,1)S(1)}, u32[]{:S(2)}, u32[]{:S(2)}) collective-permute-start(bf16[528,256]{1,0:T(8,128)(2,1)S(1)} %collective-permute-done.2.refs_6_), channel_id=1, source_target_pairs={{0,16},{32,48},{64,80},{96,112},{128,144},{160,176},{192,208},{224... | collective-permute-start | bytes 811016 | tf_op jit(solution)/shard_map/ppermute | solution.py:348
  39.2 13.3 %collective-permute-start.7 = (bf16[528,256]{1,0:T(8,128)(2,1)S(1)}, bf16[528,256]{1,0:T(8,128)(2,1)S(1)}, u32[]{:S(2)}, u32[]{:S(2)}) collective-permute-start(bf16[528,256]{1,0:T(8,128)(2,1)S(1)} %collective-permute-done.6.refs_5_), channel_id=1, source_target_pairs={{16,32},{48,64},{80,96},{112,128},{144,160},{176,192},{208,224},{2... | collective-permute-start | bytes 811016 | tf_op jit(solution)/shard_map/ppermute | solution.py:348
  51.8 6.1 %collective-permute-start.4 = (bf16[528,256]{1,0:T(8,128)(2,1)S(1)}, bf16[528,256]{1,0:T(8,128)(2,1)S(1)}, u32[]{:S(2)}, u32[]{:S(2)}) collective-permute-start(bf16[528,256]{1,0:T(8,128)(2,1)S(1)} %collective-permute-done.3.refs_5_), channel_id=1, source_target_pairs={{16,32},{48,64},{80,96},{112,128},{144,160},{176,192},{208,224},{2... | collective-permute-start | bytes 811016 | tf_op jit(solution)/shard_map/ppermute | solution.py:348
  52.5 15.4 %collective-permute-start.8 = (bf16[528,256]{1,0:T(8,128)(2,1)S(1)}, bf16[528,256]{1,0:T(8,128)(2,1)S(1)}, u32[]{:S(2)}, u32[]{:S(2)}) collective-permute-start(bf16[528,256]{1,0:T(8,128)(2,1)S(1)} %collective-permute-done.7.refs_6_), channel_id=1, source_target_pairs={{0,16},{32,48},{64,80},{96,112},{128,144},{160,176},{192,208},{224... | collective-permute-start | bytes 811016 | tf_op jit(solution)/shard_map/ppermute | solution.py:348
  57.9 21.6 %collective-permute-start.5 = (bf16[528,256]{1,0:T(8,128)(2,1)S(1)}, bf16[528,256]{1,0:T(8,128)(2,1)S(1)}, u32[]{:S(2)}, u32[]{:S(2)}) collective-permute-start(bf16[528,256]{1,0:T(8,128)(2,1)S(1)} %collective-permute-done.4.refs_6_), channel_id=1, source_target_pairs={{0,16},{32,48},{64,80},{96,112},{128,144},{160,176},{192,208},{224... | collective-permute-start | bytes 811016 | tf_op jit(solution)/shard_map/ppermute | solution.py:348
  67.9 11.6 %collective-permute-start.9 = (bf16[528,256]{1,0:T(8,128)(2,1)S(1)}, bf16[528,256]{1,0:T(8,128)(2,1)S(1)}, u32[]{:S(2)}, u32[]{:S(2)}) collective-permute-start(bf16[528,256]{1,0:T(8,128)(2,1)S(1)} %collective-permute-done.8.refs_5_), channel_id=1, source_target_pairs={{16,32},{48,64},{80,96},{112,128},{144,160},{176,192},{208,224},{2... | collective-permute-start | bytes 811016 | tf_op jit(solution)/shard_map/ppermute | solution.py:348
  87.7 5.5 %collective-permute-start.10 = (bf16[4,9,96,128]{3,2,1,0:T(8,128)(2,1)S(1)}, bf16[4,9,96,128]{3,2,1,0:T(8,128)(2,1)S(1)}, u32[]{:S(2)}, u32[]{:S(2)}) collective-permute-start(bf16[4,9,96,128]{3,2,1,0:T(8,128)(2,1)S(1)} %get-tuple-element.74), channel_id=1, source_target_pairs={{0,1},{1,0},{2,3},{3,2},{4,5},{5,4},{6,7},{7,6},{8,9},{9,8},{10,11... | collective-permute-start | bytes 2654216 | tf_op jit(solution)/shard_map/ppermute | solution.py:474
  157.4 19.6 %collective-permute-start.11 = (bf16[520,128]{1,0:T(8,128)(2,1)S(1)}, bf16[520,128]{1,0:T(8,128)(2,1)S(1)}, u32[]{:S(2)}, u32[]{:S(2)}) collective-permute-start(bf16[520,128]{1,0:T(8,128)(2,1)S(1)} %pad_maximum_fusion.2), channel_id=1, source_target_pairs={{0,64},{64,0},{1,65},{65,1},{2,66},{66,2},{3,67},{67,3},{4,68},{68... | collective-permute-start | bytes 399368 | tf_op jit(solution)/shard_map/ppermute | solution.py:491
  177.9 21.2 %all-to-all-start.3 = ((bf16[4,304,128]{2,1,0:T(8,128)(2,1)}), bf16[4,304,128]{2,1,0:T(8,128)(2,1)S(1)}, u32[]{:S(2)}, u32[]{:S(2)}) async-start(bf16[4,304,128]{2,1,0:T(8,128)(2,1)} %broadcast_in_dim.38), calls=%async_computation.3 | async-start | bytes 622592 | tf_op jit(solution)/shard_map/all_to_all | solution.py:352
  181.4 17.7 %collective-permute-start.12 = (bf16[9,12,128]{2,1,0:T(8,128)(2,1)S(1)}, bf16[9,12,128]{2,1,0:T(8,128)(2,1)S(1)}, u32[]{:S(2)}, u32[]{:S(2)}) collective-permute-start(bf16[9,12,128]{2,1,0:T(8,128)(2,1)S(1)} %dynamic-slice_bitcast_fusion), channel_id=1, source_target_pairs={{0,8},{8,0},{1,9},{9,1},{2,10},{10,2},{3,11},{11,3},{4,12},{12,4},... | collective-permute-start | bytes 82952 | tf_op jit(solution)/shard_map/ppermute | solution.py:496
  199.8 12.7 %all-to-all-start.2 = ((bf16[8,9,12,128]{3,2,1,0:T(8,128)(2,1)}), bf16[8,9,12,128]{3,2,1,0:T(8,128)(2,1)S(1)}, u32[]{:S(2)}, u32[]{:S(2)}) async-start(bf16[8,9,12,128]{3,2,1,0:T(8,128)(2,1)} %broadcast_in_dim.36), calls=%async_computation.2 | async-start | bytes 589824 | tf_op jit(solution)/shard_map/all_to_all | solution.py:352
  204.7 10.7 %collective-permute-start.15 = (bf16[1216,128]{1,0:T(8,128)(2,1)S(1)}, bf16[1216,128]{1,0:T(8,128)(2,1)S(1)}, u32[]{:S(2)}, u32[]{:S(2)}) collective-permute-start(bf16[1216,128]{1,0:T(8,128)(2,1)S(1)} %bitcast.34), channel_id=1, source_target_pairs={{0,384},{128,0},{256,128},{384,256},{1,385},{129,1},{257,129},{385... | collective-permute-start | bytes 933896 | tf_op jit(solution)/shard_map/ppermute | solution.py:500
  207.5 11.9 %collective-permute-start.14 = (bf16[1216,128]{1,0:T(8,128)(2,1)S(1)}, bf16[1216,128]{1,0:T(8,128)(2,1)S(1)}, u32[]{:S(2)}, u32[]{:S(2)}) collective-permute-start(bf16[1216,128]{1,0:T(8,128)(2,1)S(1)} %bitcast.35), channel_id=1, source_target_pairs={{0,256},{128,384},{256,0},{384,128},{1,257},{129,385},{257,1},{385... | collective-permute-start | bytes 933896 | tf_op jit(solution)/shard_map/ppermute | solution.py:500
  210.6 16.2 %collective-permute-start.13 = (bf16[1216,128]{1,0:T(8,128)(2,1)S(1)}, bf16[1216,128]{1,0:T(8,128)(2,1)S(1)}, u32[]{:S(2)}, u32[]{:S(2)}) collective-permute-start(bf16[1216,128]{1,0:T(8,128)(2,1)S(1)} %bitcast.36), channel_id=1, source_target_pairs={{0,128},{128,256},{256,384},{384,0},{1,129},{129,257},{257,385},{3... | collective-permute-start | bytes 933896 | tf_op jit(solution)/shard_map/ppermute | solution.py:500
  (2 other events, 4.6 us)

commit v3 on v2

--- a/solution.py
+++ b/solution.py
@@ -102,8 +102,8 @@
         embed_out[here, :] = embed
         donor = dot(embed, donor_w[...]).astype(BF16)
         accept = dot(embed, accept_w[...]).astype(BF16)
-        even_feat[here, :] = jnp.where(is_odd, accept, donor)
-        odd_feat[here, :] = jnp.where(is_odd, donor, accept)
+        even_feat[here, :] = jnp.where(is_odd, donor, accept)
+        odd_feat[here, :] = jnp.where(is_odd, accept, donor)
 
     even_feat[pl.ds(rows, SLOTS), :] = meta[...]
     odd_feat[pl.ds(rows, SLOTS), :] = meta[...]
@@ -141,8 +141,8 @@
 
 
 def pair_kernel(distance, *refs):
-    if distance == 0:
-        odd, own, even0, odd0, d_donor, d_accept, loss = refs
+    if distance == 1:
+        odd, own, far, even0, odd0, even1, odd1, d_donor, d_accept, loss = refs
         d_donor[...] = jnp.zeros_like(d_donor)
         d_accept[...] = jnp.zeros_like(d_accept)
         loss[...] = jnp.zeros_like(loss)
@@ -166,17 +166,13 @@
     def own_accept(block):
         return jnp.where(is_odd, even0[place(block), :], odd0[place(block), :])
 
-    if distance == 0:
-        far_accept, far_donor = own_accept, None
-    else:
-
-        def far_accept(block):
-            return jnp.where(is_odd, odd1[place(block), :], even1[place(block), :])
-
-        def far_donor(block):
-            return jnp.where(is_odd, even1[place(block), :], odd1[place(block), :])
-
-    def visit(meta, j, donors, acceptors, is_owner):
+    def far_accept(block):
+        return jnp.where(is_odd, odd1[place(block), :], even1[place(block), :])
+
+    def far_donor(block):
+        return jnp.where(is_odd, even1[place(block), :], odd1[place(block), :])
+
+    def visit(meta, j, donors, acceptors, distance, is_owner):
         accept_block = meta[j, 2] - distance * per_device
         here = (meta[j, 4] > 0) & (accept_block >= 0) & (accept_block < per_device)
 
@@ -201,13 +197,20 @@
 
     @pl.loop(0, SLOTS)
     def _(j):
-        visit(own, j, own_donor, far_accept, True)
-        if distance > 0:
-            visit(far, j, far_donor, own_accept, False)
+        if distance == 1:
+            visit(own, j, own_donor, own_accept, 0, True)
+        visit(own, j, own_donor, far_accept, distance, True)
+        visit(far, j, far_donor, own_accept, distance, False)
+
+
+def relative(target, y, first):
+    code = (target ^ (target >> 1)) ^ (y ^ (y >> 1))
+    low, high = code & 1, code >> 1
+    return low * 2 + high if first == 0 else high * 2 + low
 
 
 def tap_grad_kernel(
-    core, d_donor, d_accept, point, donor_w, accept_w, slope, hidden_t,
+    place, d_donor, d_accept, point, donor_w, accept_w, slope, hidden_t,
     keep, send, d_conv, d_feat,
 ):
     rows, heads = d_donor.shape
@@ -227,7 +230,7 @@
     half_rows = channels // 2
     for tap in range(3):
         for half in range(2):
-            into_keep = core[0] == half
+            into_keep = place[0] == half
 
             @pl.loop(0, half_rows // (2 * PIECE))
             def _(i):
@@ -239,7 +242,7 @@
                 def store(into):
                     for k in range(2):
                         for lane in range(lanes):
-                            into[i * 2 + k, tap * lanes + lane] = part[
+                            into[relative(i * 2 + k, place[1], 1), tap * lanes + lane] = part[
                                 k * PIECE : (k + 1) * PIECE, lane * 128 : (lane + 1) * 128
                             ]
 
@@ -248,18 +251,19 @@
 
 
 def head_grad_kernel(
-    d_conv, d_feat, loss, taps, factor, edge_factor, act_t, embed_t, head_sum,
+    place, d_conv, d_feat, loss, taps, factor, edge_factor, act_t, embed_t, head_sum,
 ):
     rows = d_conv.shape[0]
     channels = embed_t.shape[0]
     inner = act_t.shape[0]
+    slab = [relative(target, place[1], 0) for target in range(4)]
 
     def put(part, base, group_rows, first):
         for lane in range(4):
             for k in range(part.shape[0] // PIECE):
                 piece = first + lane * (group_rows // PIECE) + k + base
-                chunk, place = piece // 3, piece % 3
-                head_sum[chunk, place * PIECE : (place + 1) * PIECE, :] = part[
+                chunk, third = piece // 3, piece % 3
+                head_sum[slab[chunk // 4], chunk % 4, third * PIECE : (third + 1) * PIECE, :] = part[
                     k * PIECE : (k + 1) * PIECE, lane * 128 : (lane + 1) * 128
                 ]
 
@@ -292,7 +296,7 @@
     loss_row = jnp.sum(loss[...], axis=0, keepdims=True) * LOSS_WEIGHT
     loss_all = jnp.broadcast_to(jnp.sum(loss_row, axis=1, keepdims=True), (1, 128))
     at_row = lax.broadcasted_iota(jnp.int32, (EXTRA_ROWS, 128), 0)
-    for chunk in range(head_sum.shape[0]):
+    for chunk in range(16):
         if chunk < channels // 128:
             value = gain[:, chunk * 128 : (chunk + 1) * 128]
         elif chunk == channels // 128:
@@ -301,16 +305,76 @@
             value = jnp.zeros((1, 128), F32)
         coarse = value.astype(BF16).astype(F32)
         block = jnp.where(at_row == 0, coarse, 0.0) + jnp.where(at_row == 8, value - coarse, 0.0)
-        head_sum[chunk, CHUNK_ROWS:, :] = block.astype(BF16)
+        head_sum[slab[chunk // 4], chunk % 4, CHUNK_ROWS:, :] = block.astype(BF16)
+
+
+def split_rows(total):
+    value = total[CHUNK_ROWS : CHUNK_ROWS + 8] + total[CHUNK_ROWS + 8 : CHUNK_ROWS + 16]
+    coarse = value.astype(BF16).astype(F32)
+    return jnp.concatenate([total[:CHUNK_ROWS], coarse, value - coarse], axis=0).astype(BF16)
+
+
+def core_sum_kernel(keep, received, kept, send):
+    for k in range(2):
+        for slab in range(keep.shape[1]):
+            kept[k, slab] = keep[k, slab].astype(F32) + received[k, slab].astype(F32)
+            send[k, slab] = (keep[k + 2, slab].astype(F32) + received[k + 2, slab].astype(F32)).astype(BF16)
+
+
+def head_sum_kernel(head, received, kept, send):
+    for zq in range(4):
+        kept[zq] = head[0, zq].astype(F32) + received[0, zq].astype(F32)
+        send[zq] = split_rows(head[1, zq].astype(F32) + received[1, zq].astype(F32))
+
+
+def tap_sum_kernel(before, received, kept, send):
+    for slab in range(before.shape[1]):
+        kept[slab] = before[0, slab] + received[0, slab].astype(F32)
+        send[slab] = (before[1, slab] + received[1, slab].astype(F32)).astype(BF16)
+
+
+def join_kernel(head, head_in, taps, taps_in, both):
+    chunk_rows = head.shape[1]
+    for zq in range(4):
+        both[zq, :chunk_rows, :] = split_rows(head[zq] + head_in[zq].astype(F32))
+        here = slice(zq * 24, (zq + 1) * 24)
+        parts = [taps[k, here] + taps_in[k, here].astype(F32) for k in range(taps.shape[0])]
+        parts.append(jnp.zeros((8, 128), F32))
+        both[zq, chunk_rows:, :] = jnp.concatenate(parts, axis=0).astype(BF16)
+
+
+def line_sum_kernel(place, parts, pick, send, mine):
+    total = parts[0].astype(F32)
+    for zq in range(1, 4):
+        total = total + parts[zq].astype(F32)
+    chunk_rows = CHUNK_ROWS + EXTRA_ROWS
+    send[:chunk_rows, :] = split_rows(total[:chunk_rows])
+    taps = total[chunk_rows:].astype(BF16)
+    half = mine.shape[0]
+    zb = place[2]
+
+    def picked(which):
+        return dot(pick[pl.ds(pl.multiple_of(which * half, half), half), :], taps).astype(BF16)
+
+    send[chunk_rows:, :] = picked(1 - zb)
+    mine[...] = picked(zb)
+
+
+def far_sum_kernel(sent, received, mine, head, taps):
+    chunk_rows = CHUNK_ROWS + EXTRA_ROWS
+    total = split_rows(sent[:chunk_rows, :].astype(F32) + received[:chunk_rows, :].astype(F32))
+    for zq in range(head.shape[0]):
+        head[zq] = total
+    taps[...] = (mine[...].astype(F32) + received[chunk_rows:, :].astype(F32)).astype(BF16)
 
 
 def finish_kernel(
-    place_y, own, one, two, three, donor_w, accept_w,
+    place, own, one, two, three, donor_w, accept_w,
     grad_donor, grad_accept, grad_point, gain, loss, held, act_donor, act_accept,
 ):
     count = held.shape[0]
     for back, part in enumerate((own, one, two, three)):
-        held[lax.rem(place_y[0] + count - back, count)] = part[...]
+        held[lax.rem(place[1] + count - back, count)] = part[...]
     channels = grad_donor.shape[0]
     inner = act_donor.shape[0]
     chunk_rows = CHUNK_ROWS + EXTRA_ROWS
@@ -318,8 +382,8 @@
     for into in (grad_donor, grad_accept, act_donor, act_accept):
         for lane in range(2):
             for k in range(into.shape[0] // PIECE):
-                chunk, place = piece // 3, piece % 3
-                at = (chunk % 4) * chunk_rows + place * PIECE
+                chunk, third = piece // 3, piece % 3
+                at = (chunk % 4) * chunk_rows + third * PIECE
                 into[k * PIECE : (k + 1) * PIECE, lane * 128 : (lane + 1) * 128] = held[
                     chunk // 4, at : at + PIECE, :
                 ]
@@ -357,22 +421,9 @@
     return swap_parts(jnp.broadcast_to(part[None], (count,) + part.shape), axis)
 
 
-def summed(parts):
-    return jnp.sum(parts.astype(F32), axis=0)
-
-
-def resplit(total):
-    body = total[..., :CHUNK_ROWS, :].astype(BF16)
-    value = (
-        total[..., CHUNK_ROWS : CHUNK_ROWS + 8, :] + total[..., CHUNK_ROWS + 8 : CHUNK_ROWS + 16, :]
-    )
-    coarse = lax.reduce_precision(value, 8, 7)
-    return jnp.concatenate([body, coarse.astype(BF16), (value - coarse).astype(BF16)], axis=-2)
-
-
 def on_device(
     activations, norm_gain, dilated_tap_weight, point_weight, donor_weight, acceptor_weight,
-    pair_sites, pair_count, order, eye,
+    pair_sites, pair_count, order, eye, pick,
 ):
     tokens = activations[0]
     rows, channels = tokens.shape
@@ -426,9 +477,7 @@
     )
 
     acc_shapes = [shape((rows, heads), F32), shape((rows, heads), F32), shape((PANEL, PANEL), F32)]
-    acc = call(
-        lambda *refs: pair_kernel(0, *refs), acc_shapes, [SM] * 2 + [VM] * 2, 12, 2_000_000_000
-    )(odd, meta, even_feat, odd_feat)
+    acc = ()
     edge_factor, slope, hidden_t, act_t, embed_t = call(
         side_kernel,
         [
@@ -445,63 +494,80 @@
     even_far, odd_far = even_feat, odd_feat
     for distance in range(1, SPAN + 1):
         if distance == 1:
-            even_far, odd_far = swapped(even_feat, 0), swapped(odd_feat, 1)
+            odd_far, even_far = swapped(odd_feat, 0), swapped(even_feat, 1)
         else:
-            even_far, odd_far = swapped(odd_far, 0), swapped(even_far, 1)
-        far_meta = jnp.where(is_odd, even_far[rows:, :8], odd_far[rows:, :8]).astype(jnp.int32)
+            odd_far, even_far = swapped(even_far, 0), swapped(odd_far, 1)
+        far_meta = jnp.where(is_odd, odd_far[rows:, :8], even_far[rows:, :8]).astype(jnp.int32)
         acc = call(
             lambda *refs, distance=distance: pair_kernel(distance, *refs),
             acc_shapes,
-            [SM] * 3 + [VM] * 7,
+            [SM] * 3 + [VM] * (4 + len(acc)),
             12,
             2_500_000_000,
-        )(odd, meta, far_meta, even_feat, odd_feat, even_far, odd_far, *acc)
+        )(1 - odd, meta, far_meta, even_feat, odd_feat, even_far, odd_far, *acc)
 
     chunk = CHUNK_ROWS + EXTRA_ROWS
     lanes = inner // 128
     slabs = tap_count * lanes
     half = shape((4, slabs, PIECE, 128), BF16)
+    y = lax.axis_index("y")
+    place = jnp.stack([lax.axis_index("core"), y, lax.axis_index("zb")]).astype(jnp.int32)
     keep, send, d_conv, d_feat = call(
         tap_grad_kernel,
         [half, half, shape((rows, inner), BF16), shape((rows, 2 * heads), BF16)],
         [SM] + [VM] * 7,
         20,
         4_000_000_000,
-    )(
-        lax.axis_index("core").astype(jnp.int32)[None], acc[0], acc[1], point_weight, donor_weight,
-        acceptor_weight, slope, hidden_t,
-    )
+    )(place, acc[0], acc[1], point_weight, donor_weight, acceptor_weight, slope, hidden_t)
     received = lax.ppermute(send, "core", [(0, 1), (1, 0)])
     (head_sum,) = call(
-        head_grad_kernel, [shape((16, chunk, 128), BF16)], [VM] * 8, 20, 4_000_000_000
-    )(d_conv, d_feat, acc[2], dilated_tap_weight, factor, edge_factor, act_t, embed_t)
-
-    conv_sum = (keep.astype(F32) + received.astype(F32)).astype(BF16)
+        head_grad_kernel, [shape((4, 4, chunk, 128), BF16)], [SM] + [VM] * 8, 20, 4_000_000_000
+    )(place, d_conv, d_feat, acc[2], dilated_tap_weight, factor, edge_factor, act_t, embed_t)
+
+    first_pairs = [(0, 1), (1, 0), (2, 3), (3, 2)]
+    second_pairs = [(1, 2), (2, 1), (3, 0), (0, 3)]
+    quick = 1_000_000
+    conv_kept, conv_send = call(
+        core_sum_kernel, [shape((2, slabs, PIECE, 128), F32), shape((2, slabs, PIECE, 128), BF16)],
+        [VM] * 2, 12, quick,
+    )(keep, received)
+    other = lax.ppermute(head_sum[2:], "y", first_pairs)
+    heads_kept, heads_send = call(
+        head_sum_kernel, [shape((4, chunk, 128), F32), shape((4, chunk, 128), BF16)], [VM] * 2, 12, quick
+    )(head_sum, other)
+    other = lax.ppermute(conv_send, "y", second_pairs)
+    conv_kept, conv_send = call(
+        tap_sum_kernel, [shape((slabs, PIECE, 128), F32), shape((slabs, PIECE, 128), BF16)],
+        [VM] * 2, 12, quick,
+    )(conv_kept, other)
+    heads_in = lax.ppermute(heads_send, "y", second_pairs)
+    conv_in = lax.ppermute(conv_send, "y", first_pairs)
+
+    joint = chunk + 224
+    (both,) = call(join_kernel, [shape((4, joint, 128), BF16)], [VM] * 4, 12, quick)(
+        heads_kept, heads_in, conv_kept, conv_in
+    )
+    parts = swap_parts(both, "zq")
+    sent, mine = call(
+        line_sum_kernel, [shape((chunk + 112, 128), BF16), shape((112, 128), BF16)],
+        [SM] + [VM] * 2, 8, quick,
+    )(place, parts, pick)
+    received = lax.ppermute(sent, "zb", [(0, 1), (1, 0)])
+    head_parts, conv_sum = call(
+        far_sum_kernel, [shape((4, chunk, 128), BF16), shape((112, 128), BF16)], [VM] * 3, 8, quick
+    )(sent, received, mine)
+    other = lax.ppermute(conv_sum, "zhi", [(0, 1), (1, 0)])
+
     head_rows = 4 * chunk
-    both = jnp.concatenate(
-        [head_sum.reshape(4, head_rows, 128), conv_sum.reshape(4, slabs * PIECE, 128)], axis=1
-    )
-    both = summed(swap_parts(both, "y"))
-    head_sum = resplit(both[:head_rows].reshape(4, chunk, 128))
-    conv_sum = both[head_rows:].astype(BF16)
-    conv_sum = conv_sum.reshape(slabs, 4, 24, 128).transpose(1, 0, 2, 3).reshape(4, slabs * 24, 128)
-    both = jnp.concatenate([head_sum, conv_sum], axis=1)
-    both = summed(swap_parts(both, "zq"))
-    both = jnp.concatenate([resplit(both[:chunk]), both[chunk:].astype(BF16)], axis=0)
-    other = lax.ppermute(both, "zb", [(0, 1), (1, 0)])
-    both = both.astype(F32) + other.astype(F32)
-    head_sum = resplit(both[:chunk])
-    conv_sum = both[chunk:].astype(BF16).reshape(slabs, 2, 12, 128)
-    conv_sum = lax.dynamic_index_in_dim(conv_sum, lax.axis_index("zb"), 1, keepdims=False)
-    other = lax.ppermute(conv_sum, "zhi", [(0, 1), (1, 0)])
-
-    head_sum = gather_parts(head_sum, "zq").reshape(head_rows, 128)
+    head_sum = swap_parts(head_parts, "zq").reshape(head_rows, 128)
     ring = [
         lax.ppermute(head_sum, "y", [(i, (i + ahead) % 4) for i in range(4)]) for ahead in (1, 2, 3)
     ]
+    other, head_sum = lax.optimization_barrier((other, head_sum))
     conv_sum = (conv_sum.astype(F32) + other.astype(F32)).astype(BF16)
     pieces = gather_parts(conv_sum, ("x", "core")).astype(F32)
-    pieces = jnp.sum(pieces.reshape(4, 2, tap_count, lanes, 12, 128), axis=0)
+    pieces = jnp.sum(pieces.reshape(4, 2, 112, 128), axis=0)[:, : slabs * 12]
+    pieces = pieces.reshape(2, tap_count, lanes, 12, 128)
     grad_conv = pieces.transpose(1, 0, 3, 2, 4).reshape(tap_count, 24, inner)
     head_weight = shape((channels, heads), BF16)
     grad_donor, grad_accept, grad_point, grad_gain, loss = call(
@@ -515,7 +581,7 @@
             pltpu.VMEM((inner, heads), BF16),
             pltpu.VMEM((inner, heads), BF16),
         ],
-    )(lax.axis_index("y").astype(jnp.int32)[None], head_sum, *ring, donor_weight, acceptor_weight)
+    )(place, head_sum, *ring, donor_weight, acceptor_weight)
     return grad_conv, grad_point[None], grad_donor[None], grad_accept[None], grad_gain, loss[0, :1]
 
 
@@ -523,6 +589,15 @@
     core, y, zq, zb, k = np.meshgrid(*[np.arange(n) for n in (2, 4, 4, 2, 12)], indexing="ij")
     channel = (24 * (8 * y + 4 * zb + zq) + 12 * core + k).reshape(-1)
     return np.eye(channel.size, dtype=np.float32)[channel]
+
+
+def zb_halves():
+    pick = np.zeros((224, 224), np.float32)
+    for zb in range(2):
+        for slab in range(9):
+            for k in range(12):
+                pick[112 * zb + 12 * slab + k, 24 * slab + 12 * zb + k] = 1.0
+    return pick
 
 
 def solution(mesh):
@@ -539,6 +614,7 @@
             P(),
             P(BATCH, SEQ, None),
             P(BATCH, SEQ),
+            P(),
             P(),
             P(),
         ),
@@ -556,6 +632,6 @@
     def run(*arrays):
         order = jnp.asarray(channel_order(), BF16)
         eye = jnp.eye(order.shape[0], dtype=BF16)
-        return placed(*arrays, order, eye)
+        return placed(*arrays, order, eye, jnp.asarray(zb_halves(), BF16))
 
     return run

time: 230 us -> 232 us (level)
  blocking collectives: 63.1 us -> 16.2 us
  starting transfers between devices: 72.6 us -> 105 us
  waiting for transfers between devices: 55.1 us -> 71.5 us
    all_to_all x2 -> x1, blocking collectives: 63.1 us -> 16.2 us  [swap_parts(): return lax.all_to_all(parts, axis, 0, 0, tiled=True)]
    ppermute x1 -> x5, starting transfers between devices: 5.22 us -> 35.5 us  [the longest x1 24.9 us: on_device(): other = lax.ppermute(head_sum[2:], 'y', first_pairs)]
    ppermute x1 -> x5, waiting for transfers between devices: 14.4 us -> 32.3 us  [the longest x1 14.4 us: on_device(): received = lax.ppermute(sent, 'zb', [(0, 1), (1, 0)])]
    ppermute x1, starting transfers between devices: 13.6 us -> 8.31 us  [on_device(): other = lax.ppermute(conv_sum, 'zhi', [(0, 1), (1, 0)])]
    ppermute x10, starting transfers between devices: 35.2 us -> 39.8 us  [swapped(): return lax.ppermute(block, SEQ, pairs + [(j, i) for i, j in pairs])]
    ppermute x10, waiting for transfers between devices: 23.4 us -> 20.3 us  [swapped(): return lax.ppermute(block, SEQ, pairs + [(j, i) for i, j in pairs])]
    all_to_all x2, starting transfers between devices: 8.34 us -> 11.1 us  [swap_parts(): return lax.all_to_all(parts, axis, 0, 0, tiled=True)]
    pallas_call x2 -> x7, Pallas kernels: 4.41 us -> 5.58 us  [the longest x1 3.58 us: on_device(): call(head_grad_kernel, [shape((4, 4, chunk, 128), BF16)], [SM] + [VM] * 8...]
  transfers between devices with their start and end apart: 18 -> 22, of which waited for: 8 -> 10; matrix products, arithmetic and copies ran while one was open for 1% -> 1% of each run, Pallas kernels for 8% -> 7%
where the time goes in v3:
time: 232 us; the launch traced here: 231 us
  starting transfers between devices  105 us (45%)
  waiting for transfers between devices  71.5 us (31%)
  Pallas kernels  33.3 us (14%)
  blocking collectives  16.2 us (7%)
    ppermute x10, starting transfers between devices, swapped(): return lax.ppermute(block, SEQ, pairs + [(j, i) for i, j in pairs])  39.8 us
    ppermute x1, starting transfers between devices, on_device(): other = lax.ppermute(head_sum[2:], 'y', first_pairs)  24.9 us
    ppermute x10, waiting for transfers between devices, swapped(): return lax.ppermute(block, SEQ, pairs + [(j, i) for i, j in pairs])  20.3 us
    all_to_all x1, blocking collectives, swap_parts(): return lax.all_to_all(parts, axis, 0, 0, tiled=True)  16.2 us
    ppermute x1, waiting for transfers between devices, on_device(): received = lax.ppermute(sent, 'zb', [(0, 1), (1, 0)])  14.4 us
    ppermute x3, waiting for transfers between devices, on_device(): lax.ppermute(head_sum, 'y', [(i, (i + ahead) % 4) for i in range(4)])  13.8 us
    ppermute x1, waiting for transfers between devices, on_device(): other = lax.ppermute(head_sum[2:], 'y', first_pairs)  11.6 us
    all_to_all x2, starting transfers between devices, swap_parts(): return lax.all_to_all(parts, axis, 0, 0, tiled=True)  11.1 us
  transfers between devices with their start and end apart: 22, of which 10 were waited for; matrix products, arithmetic and copies ran while one was open for 1% of the time, Pallas kernels for 7%

profile of v3, /device:TPU:1, one launch (start us, length us, event | category | flops | bytes accessed | tf_op | source)
XLA Modules:
  0.0 230.7 jit_solution(4167854798602966881)
XLA Ops:
  2.5 7.2 %collective-permute-start = (bf16[128,768]{1,0:T(8,128)(2,1)S(1)}, bf16[128,768]{1,0:T(8,128)(2,1)S(1)}, u32[]{:S(2)}, u32[]{:S(2)}) collective-permute-start(bf16[128,768]{1,0:T(8,128)(2,1)S(1)} %get-tuple-element.99), channel_id=1, source_target_pairs={{0,16},{32,48},{64,80},{96,112},{128,144},{160,176},{192,208},{224... | collective-permute-start | bytes 589832 | tf_op jit(solution)/shard_map/ppermute | solution.py:412
  13.3 3.2 %shard_map.155 = (bf16[768,768]{1,0:T(8,128)(2,1)S(1)}, f32[512,384]{1,0:T(8,128)S(1)}, bf16[512,384]{1,0:T(8,128)(2,1)S(1)}, bf16[512,768]{1,0:T(8,128)(2,1)S(1...) custom-call(s32[1]{0:T(128)} %bitcast.3.odd, bf16[512,768]{1,0:T(8,128)(2,1)S(1)} %bitcast.29, ...), custom_call_target="tpu_custom_call" | custom-call | flops 4000000000 | bytes 1000000 | tf_op jit(solution)/shard_map/pallas_call | solution.py:461
  17.2 12.6 %collective-permute-start.6 = (bf16[528,256]{1,0:T(8,128)(2,1)S(1)}, bf16[528,256]{1,0:T(8,128)(2,1)S(1)}, u32[]{:S(2)}, u32[]{:S(2)}) collective-permute-start(bf16[528,256]{1,0:T(8,128)(2,1)S(1)} %get-tuple-element.54.refs_4_), channel_id=1, source_target_pairs={{0,16},{32,48},{64,80},{96,112},{128,144},{160,176},{192,208},{224... | collective-permute-start | bytes 811016 | tf_op jit(solution)/shard_map/ppermute | solution.py:412
  29.8 4.4 %shard_map.160 = (bf16[256,768]{1,0:T(8,128)(2,1)S(1)}, f32[512,384]{1,0:T(8,128)S(1)}, bf16[768,768]{1,0:T(8,128)(2,1)S(1)}, bf16[384,512]{1,0:T(8,128)(2,1)S(1)}, bf16[768,512]{1,0:T(8,128)(2,1)S(1)}) custom-call(s32[1]{0:T(128)} %bitcast.3.odd, bf16[128,768]{1,0:T(8,128)(2,1)S(1)} %collective-permute-done.even_edge, ...), custom_call_target="tpu_custom_call" | custom-call | flops 6000000000 | bytes 1000000 | tf_op jit(solution)/shard_map/pallas_call | solution.py:481
  39.8 8.8 %collective-permute-done.3.refs_6_ = bf16[528,256]{1,0:T(8,128)(2,1)S(1)} collective-permute-done((bf16[528,256]{1,0:T(8,128)(2,1)S(1)}, bf16[528,256]{1,0:T(8,128)(2,1)S(1)}, u32[]{:S(2)}, u32[]{:S(2)}) %collective-permute-start.3) | collective-permute-done | bytes 270368 | tf_op jit(solution)/shard_map/ppermute | solution.py:412
  49.3 7.1 %collective-permute-start.8 = (bf16[528,256]{1,0:T(8,128)(2,1)S(1)}, bf16[528,256]{1,0:T(8,128)(2,1)S(1)}, u32[]{:S(2)}, u32[]{:S(2)}) collective-permute-start(bf16[528,256]{1,0:T(8,128)(2,1)S(1)} %collective-permute-done.7.refs_5_), channel_id=1, source_target_pairs={{0,16},{32,48},{64,80},{96,112},{128,144},{160,176},{192,208},{224... | collective-permute-start | bytes 811016 | tf_op jit(solution)/shard_map/ppermute | solution.py:412
  58.1 7.6 %collective-permute-start.5 = (bf16[528,256]{1,0:T(8,128)(2,1)S(1)}, bf16[528,256]{1,0:T(8,128)(2,1)S(1)}, u32[]{:S(2)}, u32[]{:S(2)}) collective-permute-start(bf16[528,256]{1,0:T(8,128)(2,1)S(1)} %collective-permute-done.4.refs_5_), channel_id=1, source_target_pairs={{0,16},{32,48},{64,80},{96,112},{128,144},{160,176},{192,208},{224... | collective-permute-start | bytes 811016 | tf_op jit(solution)/shard_map/ppermute | solution.py:412
  65.7 5.5 %collective-permute-done.8.refs_6_ = bf16[528,256]{1,0:T(8,128)(2,1)S(1)} collective-permute-done((bf16[528,256]{1,0:T(8,128)(2,1)S(1)}, bf16[528,256]{1,0:T(8,128)(2,1)S(1)}, u32[]{:S(2)}, u32[]{:S(2)}) %collective-permute-start.8) | collective-permute-done | bytes 270368 | tf_op jit(solution)/shard_map/ppermute | solution.py:412
  73.8 6.0 %collective-permute-done.5.refs_6_ = bf16[528,256]{1,0:T(8,128)(2,1)S(1)} collective-permute-done((bf16[528,256]{1,0:T(8,128)(2,1)S(1)}, bf16[528,256]{1,0:T(8,128)(2,1)S(1)}, u32[]{:S(2)}, u32[]{:S(2)}) %collective-permute-start.5) | collective-permute-done | bytes 270368 | tf_op jit(solution)/shard_map/ppermute | solution.py:412
  79.9 3.3 %shard_map.159 = (f32[512,256]{1,0:T(8,128)S(1)}, f32[512,256]{1,0:T(8,128)S(1)}, f32[128,128]{1,0:T(8,128)S(1)}) custom-call(s32[1]{0:T(128)S(6)} %sub.25.refs_0_, s32[16,8]{1,0:T(8,128)S(1)} %stack.28.refs_1_, s32[16,8]{1,0:T(8,128)S(1)} %fusion.11.refs_2_, bf16[528,256]{1,0:T(8,128)(2,1)S(1)} %get-tuple-element.53.refs_3_, ...), custom_call_target="tpu_custom_call" | custom-call | flops 2500000000 | bytes 1000000 | tf_op jit(solution)/shard_map/pallas_call | solution.py:501
  83.2 5.1 %shard_map.161 = (bf16[4,9,96,128]{3,2,1,0:T(8,128)(2,1)S(1)}, bf16[4,9,96,128]{3,2,1,0:T(8,128)(2,1)S(1)}, bf16[512,384]{1,0:T(8,128)(2,1)S(1)}, bf16[512,512]{1,0:T(8,128)(2,1)S(1)}) custom-call(s32[3]{0:T(128)S(1)} %pad_add_fusion.place, f32[512,256]{1,0:T(8,128)S(1)} %get-tuple-element.64.d_donor, f32[512,256]{1,0:T(8,128)S(1)} %get-tuple-element.65.d_accept, ...), custom_call_target="tpu_custom_call" | custom-call | flops 4000000000 | bytes 1000000 | tf_op jit(solution)/shard_map/pallas_call | solution.py:515
  90.5 3.6 %shard_map.162.head = bf16[4,4,304,128]{3,2,1,0:T(8,128)(2,1)S(1)} custom-call(s32[3]{0:T(128)S(1)} %pad_add_fusion.place, bf16[512,384]{1,0:T(8,128)(2,1)S(1)} %get-tuple-element.72.d_conv, bf16[512,512]{1,0:T(8,128)(2,1)S(1)} %get-tuple-element.73.d_feat, f32[128,128]{1,0:T(8,128)S(1)} %get-tuple-element.74.loss, bf16[3,768,384]{2,1,0:T(8,128)(2,1)S(1)} %copy-done.2, ...), custom_call_target="tpu_custom_call" | custom-call | flops 4000000000 | bytes 1000000 | tf_op jit(solution)/shard_map/pallas_call | solution.py:523
  94.2 24.9 %collective-permute-start.10 = (bf16[2,4,304,128]{3,2,1,0:T(8,128)(2,1)S(1)}, bf16[2,4,304,128]{3,2,1,0:T(8,128)(2,1)S(1)}, u32[]{:S(2)}, u32[]{:S(2)}) collective-permute-start(bf16[2,4,304,128]{3,2,1,0:T(8,128)(2,1)S(1)} %slice.72), channel_id=1, source_target_pairs={{0,128},{128,0},{256,384},{384,256},{1,129},{129,1},{257,385},{385... | collective-permute-start | bytes 1867784 | tf_op jit(solution)/shard_map/ppermute | solution.py:534
  121.8 11.6 %collective-permute-done.10.received = bf16[2,4,304,128]{3,2,1,0:T(8,128)(2,1)S(1)} collective-permute-done((bf16[2,4,304,128]{3,2,1,0:T(8,128)(2,1)S(1)}, bf16[2,4,304,128]{3,2,1,0:T(8,128)(2,1)S(1)}, u32[]{:S(2)}, u32[]{:S(2)}) %collective-permute-start.10) | collective-permute-done | bytes 622624 | tf_op jit(solution)/shard_map/ppermute | solution.py:534
  138.8 6.2 %collective-permute-done.11.head_in = bf16[4,304,128]{2,1,0:T(8,128)(2,1)S(1)} collective-permute-done((bf16[4,304,128]{2,1,0:T(8,128)(2,1)S(1)}, bf16[4,304,128]{2,1,0:T(8,128)(2,1)S(1)}, u32[]{:S(2)}, u32[]{:S(2)}) %collective-permute-start.11) | collective-permute-done | bytes 311328 | tf_op jit(solution)/shard_map/ppermute | solution.py:543
  145.2 16.2 %all_to_all.15.parts = bf16[4,528,128]{2,1,0:T(8,128)(2,1)S(1)} all-to-all(bf16[4,528,128]{2,1,0:T(8,128)(2,1)S(1)} %shard_map.166), channel_id=1, replica_groups=mesh['y'=4,'zb'=2,'zq'=4,'zhi'=2,'x'=4,'core'=2] {'zq'}, dimensions={0} | all-to-all | bytes 1081344 | tf_op jit(solution)/shard_map/all_to_all | solution.py:416
  165.0 14.4 %collective-permute-done.15.received = bf16[416,128]{1,0:T(8,128)(2,1)S(1)} collective-permute-done((bf16[416,128]{1,0:T(8,128)(2,1)S(1)}, bf16[416,128]{1,0:T(8,128)(2,1)S(1)}, u32[]{:S(2)}, u32[]{:S(2)}) %collective-permute-start.15) | collective-permute-done | bytes 106528 | tf_op jit(solution)/shard_map/ppermute | solution.py:555
  180.2 3.5 %all-to-all-start.1 = ((bf16[4,304,128]{2,1,0:T(8,128)(2,1)}), bf16[4,304,128]{2,1,0:T(8,128)(2,1)S(1)}, u32[]{:S(2)}, u32[]{:S(2)}) async-start(bf16[4,304,128]{2,1,0:T(8,128)(2,1)} %get-tuple-element.90), calls=%async_computation.1 | async-start | bytes 622592 | tf_op jit(solution)/shard_map/all_to_all | solution.py:416
  183.6 8.3 %collective-permute-start.16 = (bf16[112,128]{1,0:T(8,128)(2,1)S(1)}, bf16[112,128]{1,0:T(8,128)(2,1)S(1)}, u32[]{:S(2)}, u32[]{:S(2)}) collective-permute-start(bf16[112,128]{1,0:T(8,128)(2,1)S(1)} %get-tuple-element.89), channel_id=1, source_target_pairs={{0,8},{8,0},{1,9},{9,1},{2,10},{10,2},{3,11},{11,3},{4,12},{12,4},... | collective-permute-start | bytes 86024 | tf_op jit(solution)/shard_map/ppermute | solution.py:559
  191.9 5.1 %collective-permute-done.16 = bf16[112,128]{1,0:T(8,128)(2,1)S(1)} collective-permute-done((bf16[112,128]{1,0:T(8,128)(2,1)S(1)}, bf16[112,128]{1,0:T(8,128)(2,1)S(1)}, u32[]{:S(2)}, u32[]{:S(2)}) %collective-permute-start.16) | collective-permute-done | bytes 28704 | tf_op jit(solution)/shard_map/ppermute | solution.py:559
  197.8 7.6 %all-to-all-start.2 = ((bf16[8,112,128]{2,1,0:T(8,128)(2,1)}), bf16[8,112,128]{2,1,0:T(8,128)(2,1)S(1)}, u32[]{:S(2)}, u32[]{:S(2)}) async-start(bf16[8,112,128]{2,1,0:T(8,128)(2,1)} %broadcast_in_dim.23), calls=%async_computation.2 | async-start | bytes 458752 | tf_op jit(solution)/shard_map/all_to_all | solution.py:416
  205.4 3.1 %collective-permute-start.19 = (bf16[1216,128]{1,0:T(8,128)(2,1)S(1)}, bf16[1216,128]{1,0:T(8,128)(2,1)S(1)}, u32[]{:S(2)}, u32[]{:S(2)}) collective-permute-start(bf16[1216,128]{1,0:T(8,128)(2,1)S(1)} %bitcast.24), channel_id=1, source_target_pairs={{0,384},{128,0},{256,128},{384,256},{1,385},{129,1},{257,129},{385... | collective-permute-start | bytes 933896 | tf_op jit(solution)/shard_map/ppermute | solution.py:564
  216.3 4.3 %collective-permute-done.18.two = bf16[1216,128]{1,0:T(8,128)(2,1)S(1)} collective-permute-done((bf16[1216,128]{1,0:T(8,128)(2,1)S(1)}, bf16[1216,128]{1,0:T(8,128)(2,1)S(1)}, u32[]{:S(2)}, u32[]{:S(2)}) %collective-permute-start.18) | collective-permute-done | bytes 311328 | tf_op jit(solution)/shard_map/ppermute | solution.py:564
  220.6 7.2 %collective-permute-done.17.one = bf16[1216,128]{1,0:T(8,128)(2,1)S(1)} collective-permute-done((bf16[1216,128]{1,0:T(8,128)(2,1)S(1)}, bf16[1216,128]{1,0:T(8,128)(2,1)S(1)}, u32[]{:S(2)}, u32[]{:S(2)}) %collective-permute-start.17) | collective-permute-done | bytes 311328 | tf_op jit(solution)/shard_map/ppermute | solution.py:564
  (80 shorter events, 41.9 us)
Async XLA Ops:
  1.8 11.4 %collective-permute-start.1 = (bf16[128,768]{1,0:T(8,128)(2,1)S(1)}, bf16[128,768]{1,0:T(8,128)(2,1)S(1)}, u32[]{:S(2)}, u32[]{:S(2)}) collective-permute-start(bf16[128,768]{1,0:T(8,128)(2,1)S(1)} %get-tuple-element.98), channel_id=1, source_target_pairs={{16,32},{48,64},{80,96},{112,128},{144,160},{176,192},{208,224},{2... | collective-permute-start | bytes 589832 | tf_op jit(solution)/shard_map/ppermute | solution.py:412
  2.5 10.7 %collective-permute-start = (bf16[128,768]{1,0:T(8,128)(2,1)S(1)}, bf16[128,768]{1,0:T(8,128)(2,1)S(1)}, u32[]{:S(2)}, u32[]{:S(2)}) collective-permute-start(bf16[128,768]{1,0:T(8,128)(2,1)S(1)} %get-tuple-element.99), channel_id=1, source_target_pairs={{0,16},{32,48},{64,80},{96,112},{128,144},{160,176},{192,208},{224... | collective-permute-start | bytes 589832 | tf_op jit(solution)/shard_map/ppermute | solution.py:412
  13.3 16.5 %copy-start.6 = (bf16[768,768]{1,0:T(8,128)(2,1)S(1)}, bf16[768,768]{1,0:T(8,128)(2,1)}, u32[]{:S(2)}) copy-start(bf16[768,768]{1,0:T(8,128)(2,1)} %constant.86.clone.order) | copy-start | bytes 3538948
  16.5 17.7 %collective-permute-start.2 = (bf16[528,256]{1,0:T(8,128)(2,1)S(1)}, bf16[528,256]{1,0:T(8,128)(2,1)S(1)}, u32[]{:S(2)}, u32[]{:S(2)}) collective-permute-start(bf16[528,256]{1,0:T(8,128)(2,1)S(1)} %get-tuple-element.53.refs_3_), channel_id=1, source_target_pairs={{16,32},{48,64},{80,96},{112,128},{144,160},{176,192},{208,224},{2... | collective-permute-start | bytes 811016 | tf_op jit(solution)/shard_map/ppermute | solution.py:412
  17.2 19.0 %collective-permute-start.6 = (bf16[528,256]{1,0:T(8,128)(2,1)S(1)}, bf16[528,256]{1,0:T(8,128)(2,1)S(1)}, u32[]{:S(2)}, u32[]{:S(2)}) collective-permute-start(bf16[528,256]{1,0:T(8,128)(2,1)S(1)} %get-tuple-element.54.refs_4_), channel_id=1, source_target_pairs={{0,16},{32,48},{64,80},{96,112},{128,144},{160,176},{192,208},{224... | collective-permute-start | bytes 811016 | tf_op jit(solution)/shard_map/ppermute | solution.py:412
  34.2 14.4 %collective-permute-start.3 = (bf16[528,256]{1,0:T(8,128)(2,1)S(1)}, bf16[528,256]{1,0:T(8,128)(2,1)S(1)}, u32[]{:S(2)}, u32[]{:S(2)}) collective-permute-start(bf16[528,256]{1,0:T(8,128)(2,1)S(1)} %collective-permute-done.2.refs_5_), channel_id=1, source_target_pairs={{0,16},{32,48},{64,80},{96,112},{128,144},{160,176},{192,208},{224... | collective-permute-start | bytes 811016 | tf_op jit(solution)/shard_map/ppermute | solution.py:412
  36.2 13.1 %collective-permute-start.7 = (bf16[528,256]{1,0:T(8,128)(2,1)S(1)}, bf16[528,256]{1,0:T(8,128)(2,1)S(1)}, u32[]{:S(2)}, u32[]{:S(2)}) collective-permute-start(bf16[528,256]{1,0:T(8,128)(2,1)S(1)} %collective-permute-done.6.refs_6_), channel_id=1, source_target_pairs={{16,32},{48,64},{80,96},{112,128},{144,160},{176,192},{208,224},{2... | collective-permute-start | bytes 811016 | tf_op jit(solution)/shard_map/ppermute | solution.py:412
  48.6 9.5 %collective-permute-start.4 = (bf16[528,256]{1,0:T(8,128)(2,1)S(1)}, bf16[528,256]{1,0:T(8,128)(2,1)S(1)}, u32[]{:S(2)}, u32[]{:S(2)}) collective-permute-start(bf16[528,256]{1,0:T(8,128)(2,1)S(1)} %collective-permute-done.3.refs_6_), channel_id=1, source_target_pairs={{16,32},{48,64},{80,96},{112,128},{144,160},{176,192},{208,224},{2... | collective-permute-start | bytes 811016 | tf_op jit(solution)/shard_map/ppermute | solution.py:412
  49.3 21.9 %collective-permute-start.8 = (bf16[528,256]{1,0:T(8,128)(2,1)S(1)}, bf16[528,256]{1,0:T(8,128)(2,1)S(1)}, u32[]{:S(2)}, u32[]{:S(2)}) collective-permute-start(bf16[528,256]{1,0:T(8,128)(2,1)S(1)} %collective-permute-done.7.refs_5_), channel_id=1, source_target_pairs={{0,16},{32,48},{64,80},{96,112},{128,144},{160,176},{192,208},{224... | collective-permute-start | bytes 811016 | tf_op jit(solution)/shard_map/ppermute | solution.py:412
  58.1 21.8 %collective-permute-start.5 = (bf16[528,256]{1,0:T(8,128)(2,1)S(1)}, bf16[528,256]{1,0:T(8,128)(2,1)S(1)}, u32[]{:S(2)}, u32[]{:S(2)}) collective-permute-start(bf16[528,256]{1,0:T(8,128)(2,1)S(1)} %collective-permute-done.4.refs_5_), channel_id=1, source_target_pairs={{0,16},{32,48},{64,80},{96,112},{128,144},{160,176},{192,208},{224... | collective-permute-start | bytes 811016 | tf_op jit(solution)/shard_map/ppermute | solution.py:412
  71.2 8.7 %collective-permute-start.9 = (bf16[528,256]{1,0:T(8,128)(2,1)S(1)}, bf16[528,256]{1,0:T(8,128)(2,1)S(1)}, u32[]{:S(2)}, u32[]{:S(2)}) collective-permute-start(bf16[528,256]{1,0:T(8,128)(2,1)S(1)} %collective-permute-done.8.refs_6_), channel_id=1, source_target_pairs={{16,32},{48,64},{80,96},{112,128},{144,160},{176,192},{208,224},{2... | collective-permute-start | bytes 811016 | tf_op jit(solution)/shard_map/ppermute | solution.py:412
  88.3 30.8 %collective-permute-start.12 = (bf16[4,9,96,128]{3,2,1,0:T(8,128)(2,1)S(1)}, bf16[4,9,96,128]{3,2,1,0:T(8,128)(2,1)S(1)}, u32[]{:S(2)}, u32[]{:S(2)}) collective-permute-start(bf16[4,9,96,128]{3,2,1,0:T(8,128)(2,1)S(1)} %get-tuple-element.82), channel_id=1, source_target_pairs={{0,1},{1,0},{2,3},{3,2},{4,5},{5,4},{6,7},{7,6},{8,9},{9,8},{10,11... | collective-permute-start | bytes 2654216 | tf_op jit(solution)/shard_map/ppermute | solution.py:522
  94.2 39.3 %collective-permute-start.10 = (bf16[2,4,304,128]{3,2,1,0:T(8,128)(2,1)S(1)}, bf16[2,4,304,128]{3,2,1,0:T(8,128)(2,1)S(1)}, u32[]{:S(2)}, u32[]{:S(2)}) collective-permute-start(bf16[2,4,304,128]{3,2,1,0:T(8,128)(2,1)S(1)} %slice.72), channel_id=1, source_target_pairs={{0,128},{128,0},{256,384},{384,256},{1,129},{129,1},{257,385},{385... | collective-permute-start | bytes 1867784 | tf_op jit(solution)/shard_map/ppermute | solution.py:534
  119.3 16.8 %collective-permute-start.13 = (bf16[2,9,96,128]{3,2,1,0:T(8,128)(2,1)S(1)}, bf16[2,9,96,128]{3,2,1,0:T(8,128)(2,1)S(1)}, u32[]{:S(2)}, u32[]{:S(2)}) collective-permute-start(bf16[2,9,96,128]{3,2,1,0:T(8,128)(2,1)S(1)} %get-tuple-element.84), channel_id=1, source_target_pairs={{128,256},{256,128},{384,0},{0,384},{129,257},{257,129},{385,1},{1... | collective-permute-start | bytes 1327112 | tf_op jit(solution)/shard_map/ppermute | solution.py:538
  133.6 11.4 %collective-permute-start.11 = (bf16[4,304,128]{2,1,0:T(8,128)(2,1)S(1)}, bf16[4,304,128]{2,1,0:T(8,128)(2,1)S(1)}, u32[]{:S(2)}, u32[]{:S(2)}) collective-permute-start(bf16[4,304,128]{2,1,0:T(8,128)(2,1)S(1)} %get-tuple-element.80), channel_id=1, source_target_pairs={{128,256},{256,128},{384,0},{0,384},{129,257},{257,129},{385,1},{1... | collective-permute-start | bytes 933896 | tf_op jit(solution)/shard_map/ppermute | solution.py:543
  136.2 8.8 %collective-permute-start.14 = (bf16[9,96,128]{2,1,0:T(8,128)(2,1)S(1)}, bf16[9,96,128]{2,1,0:T(8,128)(2,1)S(1)}, u32[]{:S(2)}, u32[]{:S(2)}) collective-permute-start(bf16[9,96,128]{2,1,0:T(8,128)(2,1)S(1)} %get-tuple-element.86), channel_id=1, source_target_pairs={{0,128},{128,0},{256,384},{384,256},{1,129},{129,1},{257,385},{385... | collective-permute-start | bytes 663560 | tf_op jit(solution)/shard_map/ppermute | solution.py:544
  145.0 16.3 %copy-start.1 = (bf16[224,224]{1,0:T(8,128)(2,1)S(1)}, bf16[224,224]{1,0:T(8,128)(2,1)}, u32[]{:S(2)}) copy-start(bf16[224,224]{1,0:T(8,128)(2,1)} %constant.87.clone.pick) | copy-start | bytes 301060
  162.1 17.3 %collective-permute-start.15 = (bf16[416,128]{1,0:T(8,128)(2,1)S(1)}, bf16[416,128]{1,0:T(8,128)(2,1)S(1)}, u32[]{:S(2)}, u32[]{:S(2)}) collective-permute-start(bf16[416,128]{1,0:T(8,128)(2,1)S(1)} %get-tuple-element.87.sent), channel_id=1, source_target_pairs={{0,64},{64,0},{1,65},{65,1},{2,66},{66,2},{3,67},{67,3},{4,68},{68... | collective-permute-start | bytes 319496 | tf_op jit(solution)/shard_map/ppermute | solution.py:555
  180.2 16.9 %all-to-all-start.1 = ((bf16[4,304,128]{2,1,0:T(8,128)(2,1)}), bf16[4,304,128]{2,1,0:T(8,128)(2,1)S(1)}, u32[]{:S(2)}, u32[]{:S(2)}) async-start(bf16[4,304,128]{2,1,0:T(8,128)(2,1)} %get-tuple-element.90), calls=%async_computation.1 | async-start | bytes 622592 | tf_op jit(solution)/shard_map/all_to_all | solution.py:416
  183.6 13.4 %collective-permute-start.16 = (bf16[112,128]{1,0:T(8,128)(2,1)S(1)}, bf16[112,128]{1,0:T(8,128)(2,1)S(1)}, u32[]{:S(2)}, u32[]{:S(2)}) collective-permute-start(bf16[112,128]{1,0:T(8,128)(2,1)S(1)} %get-tuple-element.89), channel_id=1, source_target_pairs={{0,8},{8,0},{1,9},{9,1},{2,10},{10,2},{3,11},{11,3},{4,12},{12,4},... | collective-permute-start | bytes 86024 | tf_op jit(solution)/shard_map/ppermute | solution.py:559
  197.8 15.4 %all-to-all-start.2 = ((bf16[8,112,128]{2,1,0:T(8,128)(2,1)}), bf16[8,112,128]{2,1,0:T(8,128)(2,1)S(1)}, u32[]{:S(2)}, u32[]{:S(2)}) async-start(bf16[8,112,128]{2,1,0:T(8,128)(2,1)} %broadcast_in_dim.23), calls=%async_computation.2 | async-start | bytes 458752 | tf_op jit(solution)/shard_map/all_to_all | solution.py:416
  205.4 10.9 %collective-permute-start.19 = (bf16[1216,128]{1,0:T(8,128)(2,1)S(1)}, bf16[1216,128]{1,0:T(8,128)(2,1)S(1)}, u32[]{:S(2)}, u32[]{:S(2)}) collective-permute-start(bf16[1216,128]{1,0:T(8,128)(2,1)S(1)} %bitcast.24), channel_id=1, source_target_pairs={{0,384},{128,0},{256,128},{384,256},{1,385},{129,1},{257,129},{385... | collective-permute-start | bytes 933896 | tf_op jit(solution)/shard_map/ppermute | solution.py:564
  208.5 12.1 %collective-permute-start.18 = (bf16[1216,128]{1,0:T(8,128)(2,1)S(1)}, bf16[1216,128]{1,0:T(8,128)(2,1)S(1)}, u32[]{:S(2)}, u32[]{:S(2)}) collective-permute-start(bf16[1216,128]{1,0:T(8,128)(2,1)S(1)} %bitcast.25), channel_id=1, source_target_pairs={{0,256},{128,384},{256,0},{384,128},{1,257},{129,385},{257,1},{385... | collective-permute-start | bytes 933896 | tf_op jit(solution)/shard_map/ppermute | solution.py:564
  210.9 17.0 %collective-permute-start.17 = (bf16[1216,128]{1,0:T(8,128)(2,1)S(1)}, bf16[1216,128]{1,0:T(8,128)(2,1)S(1)}, u32[]{:S(2)}, u32[]{:S(2)}) collective-permute-start(bf16[1216,128]{1,0:T(8,128)(2,1)S(1)} %bitcast.26), channel_id=1, source_target_pairs={{0,128},{128,256},{256,384},{384,0},{1,129},{129,257},{257,385},{3... | collective-permute-start | bytes 933896 | tf_op jit(solution)/shard_map/ppermute | solution.py:564
  (7 other events, 39.5 us)

commit v4 on v3

--- a/solution.py
+++ b/solution.py
@@ -87,24 +87,18 @@
         hidden[pl.ds(at, STEP), :] = gelu(v * rms(v) * gain[...]).astype(BF16)
     hidden[pl.ds(STEP, rows), :] = mine[...]
 
-    @pl.loop(0, rows // 256)
-    def _(i):
-        start = pl.multiple_of(i * 256, 256)
-        here = pl.ds(start, 256)
-        conv = dot(hidden[here, :], taps[0])
-        for tap in range(1, taps.shape[0]):
-            at = pl.multiple_of(start + tap * STEP, STEP)
-            conv = conv + dot(hidden[pl.ds(at, 256), :], taps[tap])
-        conv_out[here, :] = conv
-        act = gelu(conv).astype(BF16)
-        act_out[here, :] = act
-        embed = (tok[here, :].astype(F32) + dot(act, point[...])).astype(BF16)
-        embed_out[here, :] = embed
-        donor = dot(embed, donor_w[...]).astype(BF16)
-        accept = dot(embed, accept_w[...]).astype(BF16)
-        even_feat[here, :] = jnp.where(is_odd, donor, accept)
-        odd_feat[here, :] = jnp.where(is_odd, accept, donor)
-
+    conv = dot(hidden[:rows, :], taps[0])
+    for tap in range(1, taps.shape[0]):
+        conv = conv + dot(hidden[tap * STEP : tap * STEP + rows, :], taps[tap])
+    conv_out[...] = conv
+    act = gelu(conv).astype(BF16)
+    act_out[...] = act
+    embed = (tok[...].astype(F32) + dot(act, point[...])).astype(BF16)
+    embed_out[...] = embed
+    donor = dot(embed, donor_w[...]).astype(BF16)
+    accept = dot(embed, accept_w[...]).astype(BF16)
+    even_feat[:rows, :] = jnp.where(is_odd, donor, accept)
+    odd_feat[:rows, :] = jnp.where(is_odd, accept, donor)
     even_feat[pl.ds(rows, SLOTS), :] = meta[...]
     odd_feat[pl.ds(rows, SLOTS), :] = meta[...]
 
@@ -126,23 +120,15 @@
         here = pl.ds(pl.multiple_of(i * STEP, STEP), STEP)
         slope[here, :] = gelu_both(conv[here, :])[1]
 
-    @pl.loop(0, hidden_t.shape[0] // 256)
-    def _(i):
-        here = pl.ds(pl.multiple_of(i * 256, 256), 256)
-        hidden_t[here, :] = dot_t(order[here, :], hidden[...]).astype(BF16)
-        embed_t[here, :] = dot_t(eye[here, :], embed[...]).astype(BF16)
-
+    hidden_t[...] = dot_t(order[...], hidden[...]).astype(BF16)
+    embed_t[...] = dot_t(eye[...], embed[...]).astype(BF16)
     inner = act.shape[1]
-
-    @pl.loop(0, inner // 128)
-    def _(i):
-        here = pl.ds(pl.multiple_of(i * 128, 128), 128)
-        act_t[here, :] = dot_t(eye[here, :inner], act[...]).astype(BF16)
+    act_t[...] = dot_t(eye[:inner, :inner], act[...]).astype(BF16)
 
 
 def pair_kernel(distance, *refs):
-    if distance == 1:
-        odd, own, far, even0, odd0, even1, odd1, d_donor, d_accept, loss = refs
+    if distance == 0:
+        odd, own, even0, odd0, d_donor, d_accept, loss = refs
         d_donor[...] = jnp.zeros_like(d_donor)
         d_accept[...] = jnp.zeros_like(d_accept)
         loss[...] = jnp.zeros_like(loss)
@@ -166,13 +152,17 @@
     def own_accept(block):
         return jnp.where(is_odd, even0[place(block), :], odd0[place(block), :])
 
-    def far_accept(block):
-        return jnp.where(is_odd, odd1[place(block), :], even1[place(block), :])
-
-    def far_donor(block):
-        return jnp.where(is_odd, even1[place(block), :], odd1[place(block), :])
-
-    def visit(meta, j, donors, acceptors, distance, is_owner):
+    if distance == 0:
+        far_accept, far_donor = own_accept, None
+    else:
+
+        def far_accept(block):
+            return jnp.where(is_odd, odd1[place(block), :], even1[place(block), :])
+
+        def far_donor(block):
+            return jnp.where(is_odd, even1[place(block), :], odd1[place(block), :])
+
+    def visit(meta, j, donors, acceptors, is_owner):
         accept_block = meta[j, 2] - distance * per_device
         here = (meta[j, 4] > 0) & (accept_block >= 0) & (accept_block < per_device)
 
@@ -197,10 +187,9 @@
 
     @pl.loop(0, SLOTS)
     def _(j):
-        if distance == 1:
-            visit(own, j, own_donor, own_accept, 0, True)
-        visit(own, j, own_donor, far_accept, distance, True)
-        visit(far, j, far_donor, own_accept, distance, False)
+        visit(own, j, own_donor, far_accept, True)
+        if distance > 0:
+            visit(far, j, far_donor, own_accept, False)
 
 
 def relative(target, y, first):
@@ -216,38 +205,32 @@
     rows, heads = d_donor.shape
     channels = hidden_t.shape[0]
 
-    @pl.loop(0, rows // 256)
-    def _(i):
-        here = pl.ds(pl.multiple_of(i * 256, 256), 256)
-        dd = d_donor[here, :].astype(BF16)
-        da = d_accept[here, :].astype(BF16)
-        d_feat[here, :heads] = dd
-        d_feat[here, heads:] = da
-        d_embed = (dot_t(dd, donor_w[...]) + dot_t(da, accept_w[...])).astype(BF16)
-        d_conv[here, :] = (dot_t(d_embed, point[...]) * slope[here, :]).astype(BF16)
+    dd = d_donor[...].astype(BF16)
+    da = d_accept[...].astype(BF16)
+    d_feat[:, :heads] = dd
+    d_feat[:, heads:] = da
+    d_embed = (dot_t(dd, donor_w[...]) + dot_t(da, accept_w[...])).astype(BF16)
+    d_conv[...] = (dot_t(d_embed, point[...]) * slope[...]).astype(BF16)
 
     lanes = d_conv.shape[1] // 128
     half_rows = channels // 2
+    slab = [relative(target, place[1], 1) for target in range(4)]
     for tap in range(3):
         for half in range(2):
-            into_keep = place[0] == half
-
-            @pl.loop(0, half_rows // (2 * PIECE))
-            def _(i):
-                at = pl.multiple_of(half * half_rows + i * 2 * PIECE, 2 * PIECE)
-                part = dot(
-                    hidden_t[pl.ds(at, 2 * PIECE), tap * STEP : tap * STEP + rows], d_conv[...]
-                ).astype(BF16)
-
-                def store(into):
-                    for k in range(2):
-                        for lane in range(lanes):
-                            into[relative(i * 2 + k, place[1], 1), tap * lanes + lane] = part[
-                                k * PIECE : (k + 1) * PIECE, lane * 128 : (lane + 1) * 128
-                            ]
-
-                pl.when(into_keep)(lambda: store(keep))
-                pl.when(jnp.logical_not(into_keep))(lambda: store(send))
+            part = dot(
+                hidden_t[half * half_rows : (half + 1) * half_rows, tap * STEP : tap * STEP + rows],
+                d_conv[...],
+            ).astype(BF16)
+
+            def store(into, part=part, tap=tap):
+                for k in range(4):
+                    for lane in range(lanes):
+                        into[slab[k], tap * lanes + lane] = part[
+                            k * PIECE : (k + 1) * PIECE, lane * 128 : (lane + 1) * 128
+                        ]
+
+            pl.when(place[0] == half)(lambda: store(keep))
+            pl.when(place[0] != half)(lambda: store(send))
 
 
 def head_grad_kernel(
@@ -267,31 +250,23 @@
                     k * PIECE : (k + 1) * PIECE, lane * 128 : (lane + 1) * 128
                 ]
 
-    for i in range(channels // (2 * PIECE)):
-        part = dot(embed_t[i * 2 * PIECE : (i + 1) * 2 * PIECE, :], d_feat[...]).astype(BF16)
-        put(part, 2 * i, channels, 0)
-    for i in range(inner // (2 * PIECE)):
-        part = dot(act_t[i * 2 * PIECE : (i + 1) * 2 * PIECE, :], d_feat[...]).astype(BF16)
-        put(part, 2 * i, inner, 4 * channels // PIECE)
+    for i in range(2):
+        part = dot(embed_t[i * 4 * PIECE : (i + 1) * 4 * PIECE, :], d_feat[...]).astype(BF16)
+        put(part, 4 * i, channels, 0)
+    put(dot(act_t[...], d_feat[...]).astype(BF16), 0, inner, 4 * channels // PIECE)
 
     total = jnp.zeros((8, channels), F32)
-    last = taps.shape[0] - 1
-    blocks = rows // STEP
-
-    def weighed(block, tap, weights):
-        product = dot_t(d_conv[block * STEP : (block + 1) * STEP, :], taps[tap]) * weights.astype(F32)
-        return jnp.sum(product.reshape(STEP // 8, 8, channels), axis=0)
-
-    for block in range(blocks):
-        for tap in range(taps.shape[0]):
-            at = block + tap - 1
-            if at < 0:
-                weights = edge_factor[:STEP, :]
-            elif at >= blocks:
-                weights = edge_factor[STEP:, :]
-            else:
-                weights = factor[at * STEP : (at + 1) * STEP, :]
-            total = total + weighed(block, tap, weights)
+    edge = edge_factor.shape[0] // 2
+    for tap in range(taps.shape[0]):
+        product = dot_t(d_conv[...], taps[tap])
+        if tap == 0:
+            weights = jnp.concatenate([edge_factor[:edge, :], factor[: rows - edge, :]], axis=0)
+        elif tap == 1:
+            weights = factor[...]
+        else:
+            weights = jnp.concatenate([factor[edge:, :], edge_factor[edge:, :]], axis=0)
+        product = product * weights.astype(F32)
+        total = total + jnp.sum(product.reshape(rows // 8, 8, channels), axis=0)
     gain = jnp.sum(total, axis=0, keepdims=True)
     loss_row = jnp.sum(loss[...], axis=0, keepdims=True) * LOSS_WEIGHT
     loss_all = jnp.broadcast_to(jnp.sum(loss_row, axis=1, keepdims=True), (1, 128))
@@ -314,11 +289,13 @@
     return jnp.concatenate([total[:CHUNK_ROWS], coarse, value - coarse], axis=0).astype(BF16)
 
 
-def core_sum_kernel(keep, received, kept, send):
+def core_sum_kernel(taps, received, kept, send):
     for k in range(2):
-        for slab in range(keep.shape[1]):
-            kept[k, slab] = keep[k, slab].astype(F32) + received[k, slab].astype(F32)
-            send[k, slab] = (keep[k + 2, slab].astype(F32) + received[k + 2, slab].astype(F32)).astype(BF16)
+        for slab in range(taps.shape[1]):
+            kept[k, slab] = taps[k, slab].astype(F32) + received[k, slab].astype(F32)
+            send[k, slab] = (
+                taps[k + 2, slab].astype(F32) + received[k + 2, slab].astype(F32)
+            ).astype(BF16)
 
 
 def head_sum_kernel(head, received, kept, send):
@@ -360,21 +337,31 @@
     mine[...] = picked(zb)
 
 
-def far_sum_kernel(sent, received, mine, head, taps):
-    chunk_rows = CHUNK_ROWS + EXTRA_ROWS
+def far_sum_kernel(sent, received, mine, one, two, head, taps):
+    chunk_rows = head.shape[1]
     total = split_rows(sent[:chunk_rows, :].astype(F32) + received[:chunk_rows, :].astype(F32))
     for zq in range(head.shape[0]):
         head[zq] = total
-    taps[...] = (mine[...].astype(F32) + received[chunk_rows:, :].astype(F32)).astype(BF16)
+    near = mine[...].astype(F32) + received[chunk_rows:, :].astype(F32)
+    taps[...] = (near + (one[...].astype(F32) + two[...].astype(F32))).astype(BF16)
+
+
+def line_total_kernel(own, one, two, three, total):
+    even = own[...].astype(F32) + two[...].astype(F32)
+    total[...] = even + (one[...].astype(F32) + three[...].astype(F32))
 
 
 def finish_kernel(
-    place, own, one, two, three, donor_w, accept_w,
+    place, own, behind, ahead, low, high, donor_w, accept_w,
     grad_donor, grad_accept, grad_point, gain, loss, held, act_donor, act_accept,
 ):
     count = held.shape[0]
-    for back, part in enumerate((own, one, two, three)):
-        held[lax.rem(place[1] + count - back, count)] = part[...]
+    for step, part in ((0, own), (3, behind), (1, ahead)):
+        held[lax.rem(place[1] + step, count)] = part[...]
+    opposite = lax.rem(place[1] + 2, count)
+    middle = low.shape[0]
+    held[opposite, :middle, :] = low[...]
+    held[opposite, middle:, :] = high[...]
     channels = grad_donor.shape[0]
     inner = act_donor.shape[0]
     chunk_rows = CHUNK_ROWS + EXTRA_ROWS
@@ -389,12 +376,9 @@
                 ]
                 piece += 1
 
-    @pl.loop(0, inner // 128)
-    def _(i):
-        here = pl.ds(pl.multiple_of(i * 128, 128), 128)
-        grad_point[here, :] = (
-            dot_t(act_donor[here, :], donor_w[...]) + dot_t(act_accept[here, :], accept_w[...])
-        ).astype(BF16)
+    grad_point[...] = (
+        dot_t(act_donor[...], donor_w[...]) + dot_t(act_accept[...], accept_w[...])
+    ).astype(BF16)
 
     for chunk in range(channels // 128 + 1):
         at = (chunk % 4) * chunk_rows + CHUNK_ROWS
@@ -414,11 +398,6 @@
 
 def swap_parts(parts, axis):
     return lax.all_to_all(parts, axis, 0, 0, tiled=True)
-
-
-def gather_parts(part, axis):
-    count = lax.axis_size(axis)
-    return swap_parts(jnp.broadcast_to(part[None], (count,) + part.shape), axis)
 
 
 def on_device(
@@ -477,7 +456,9 @@
     )
 
     acc_shapes = [shape((rows, heads), F32), shape((rows, heads), F32), shape((PANEL, PANEL), F32)]
-    acc = ()
+    acc = call(
+        lambda *refs: pair_kernel(0, *refs), acc_shapes, [SM] * 2 + [VM] * 2, 12, 2_000_000_000
+    )(1 - odd, meta, even_feat, odd_feat)
     edge_factor, slope, hidden_t, act_t, embed_t = call(
         side_kernel,
         [
@@ -501,7 +482,7 @@
         acc = call(
             lambda *refs, distance=distance: pair_kernel(distance, *refs),
             acc_shapes,
-            [SM] * 3 + [VM] * (4 + len(acc)),
+            [SM] * 3 + [VM] * 7,
             12,
             2_500_000_000,
         )(1 - odd, meta, far_meta, even_feat, odd_feat, even_far, odd_far, *acc)
@@ -509,14 +490,14 @@
     chunk = CHUNK_ROWS + EXTRA_ROWS
     lanes = inner // 128
     slabs = tap_count * lanes
-    half = shape((4, slabs, PIECE, 128), BF16)
     y = lax.axis_index("y")
     place = jnp.stack([lax.axis_index("core"), y, lax.axis_index("zb")]).astype(jnp.int32)
+    half = shape((4, slabs, PIECE, 128), BF16)
     keep, send, d_conv, d_feat = call(
         tap_grad_kernel,
         [half, half, shape((rows, inner), BF16), shape((rows, 2 * heads), BF16)],
         [SM] + [VM] * 7,
-        20,
+        24,
         4_000_000_000,
     )(place, acc[0], acc[1], point_weight, donor_weight, acceptor_weight, slope, hidden_t)
     received = lax.ppermute(send, "core", [(0, 1), (1, 0)])
@@ -553,35 +534,45 @@
         [SM] + [VM] * 2, 8, quick,
     )(place, parts, pick)
     received = lax.ppermute(sent, "zb", [(0, 1), (1, 0)])
+    across = lax.ppermute(mine, "zhi", [(0, 1), (1, 0)])
+    corner = lax.ppermute(
+        sent[chunk:], ("zb", "zhi"), [(0, 3), (3, 0), (1, 2), (2, 1)]
+    )
     head_parts, conv_sum = call(
-        far_sum_kernel, [shape((4, chunk, 128), BF16), shape((112, 128), BF16)], [VM] * 3, 8, quick
-    )(sent, received, mine)
-    other = lax.ppermute(conv_sum, "zhi", [(0, 1), (1, 0)])
+        far_sum_kernel, [shape((4, chunk, 128), BF16), shape((112, 128), BF16)], [VM] * 5, 8, quick
+    )(sent, received, mine, across, corner)
 
     head_rows = 4 * chunk
     head_sum = swap_parts(head_parts, "zq").reshape(head_rows, 128)
-    ring = [
-        lax.ppermute(head_sum, "y", [(i, (i + ahead) % 4) for i in range(4)]) for ahead in (1, 2, 3)
+    line = [
+        lax.ppermute(conv_sum, "x", [(i, (i + step) % 4) for i in range(4)]) for step in (1, 2, 3)
     ]
-    other, head_sum = lax.optimization_barrier((other, head_sum))
-    conv_sum = (conv_sum.astype(F32) + other.astype(F32)).astype(BF16)
-    pieces = gather_parts(conv_sum, ("x", "core")).astype(F32)
-    pieces = jnp.sum(pieces.reshape(4, 2, 112, 128), axis=0)[:, : slabs * 12]
-    pieces = pieces.reshape(2, tap_count, lanes, 12, 128)
+    (conv_sum,) = call(line_total_kernel, [shape((112, 128), F32)], [VM] * 4, 8, quick)(conv_sum, *line)
+    head_sum, conv_sum = lax.optimization_barrier((head_sum, conv_sum))
+    other = lax.ppermute(conv_sum, "core", [(0, 1), (1, 0)])
+    around = [(i, (i + 1) % 4) for i in range(4)]
+    back = [(j, i) for i, j in around]
+    behind = lax.ppermute(head_sum, "y", around)
+    ahead = lax.ppermute(head_sum, "y", back)
+    low = lax.ppermute(behind[: head_rows // 2], "y", around)
+    high = lax.ppermute(ahead[head_rows // 2 :], "y", back)
+    is_first = lax.axis_index("core") == 0
+    pieces = jnp.stack([jnp.where(is_first, conv_sum, other), jnp.where(is_first, other, conv_sum)])
+    pieces = pieces[:, : slabs * 12].reshape(2, tap_count, lanes, 12, 128)
     grad_conv = pieces.transpose(1, 0, 3, 2, 4).reshape(tap_count, 24, inner)
     head_weight = shape((channels, heads), BF16)
     grad_donor, grad_accept, grad_point, grad_gain, loss = call(
         finish_kernel,
         [head_weight, head_weight, shape((inner, channels), BF16), shape((1, channels), F32), shape((1, 128), F32)],
-        [SM] + [VM] * 6,
-        16,
+        [SM] + [VM] * 7,
+        20,
         1_000_000_000,
         [
             pltpu.VMEM((4, head_rows, 128), BF16),
             pltpu.VMEM((inner, heads), BF16),
             pltpu.VMEM((inner, heads), BF16),
         ],
-    )(place, head_sum, *ring, donor_weight, acceptor_weight)
+    )(place, head_sum, behind, ahead, low, high, donor_weight, acceptor_weight)
     return grad_conv, grad_point[None], grad_donor[None], grad_accept[None], grad_gain, loss[0, :1]
 
 

time: 232 us -> 230 us (level)
  starting transfers between devices: 105 us -> 122 us
  waiting for transfers between devices: 71.5 us -> 55.4 us
  Pallas kernels: 33.3 us -> 29.7 us
    ppermute x4 -> x10, starting transfers between devices: 16 us -> 40.8 us  [the longest x3 9.37 us: on_device(): lax.ppermute(conv_sum, 'x', [(i, (i + step) % 4) for i in range(4)])]
    ppermute x1, waiting for transfers between devices: 14.4 us -> 0.01 us  [on_device(): received = lax.ppermute(sent, 'zb', [(0, 1), (1, 0)])]
    all_to_all x2 -> x1, starting transfers between devices: 11.1 us -> 3.45 us  [swap_parts(): return lax.all_to_all(parts, axis, 0, 0, tiled=True)]
    ppermute x1, starting transfers between devices: 24.9 us -> 20.6 us  [on_device(): other = lax.ppermute(head_sum[2:], 'y', first_pairs)]
    ppermute x4 -> x10, waiting for transfers between devices: 18.9 us -> 17.9 us  [the longest x1 10.1 us: on_device(): across = lax.ppermute(mine, 'zhi', [(0, 1), (1, 0)])]
  transfers between devices with their start and end apart: 22 -> 27, of which waited for: 10 -> 10; matrix products, arithmetic and copies ran while one was open for 1% -> 1% of each run, Pallas kernels for 7% -> 7%
where the time goes in v4:
time: 230 us; the launch traced here: 228 us
  starting transfers between devices  122 us (53%)
  waiting for transfers between devices  55.4 us (24%)
  Pallas kernels  29.7 us (13%)
  blocking collectives  16.2 us (7%)
    ppermute x10, starting transfers between devices, swapped(): return lax.ppermute(block, SEQ, pairs + [(j, i) for i, j in pairs])  37.7 us
    ppermute x10, waiting for transfers between devices, swapped(): return lax.ppermute(block, SEQ, pairs + [(j, i) for i, j in pairs])  21.8 us
    ppermute x1, starting transfers between devices, on_device(): other = lax.ppermute(head_sum[2:], 'y', first_pairs)  20.6 us
    all_to_all x1, blocking collectives, swap_parts(): return lax.all_to_all(parts, axis, 0, 0, tiled=True)  16.2 us
    ppermute x1, waiting for transfers between devices, on_device(): other = lax.ppermute(head_sum[2:], 'y', first_pairs)  10.2 us
    ppermute x1, waiting for transfers between devices, on_device(): across = lax.ppermute(mine, 'zhi', [(0, 1), (1, 0)])  10.1 us
    ppermute x3, starting transfers between devices, on_device(): lax.ppermute(conv_sum, 'x', [(i, (i + step) % 4) for i in range(4)])  9.37 us
    pallas_call x4, Pallas kernels, on_device(): call(lambda *refs, distance=distance: pair_kernel(distance, *refs), acc_s...  8.32 us
  transfers between devices with their start and end apart: 27, of which 10 were waited for; matrix products, arithmetic and copies ran while one was open for 1% of the time, Pallas kernels for 7%

profile of v4, /device:TPU:1, one launch (start us, length us, event | category | flops | bytes accessed | tf_op | source)
XLA Modules:
  0.0 227.8 jit_solution(13926697707899192625)
XLA Ops:
  2.5 7.2 %collective-permute-start = (bf16[128,768]{1,0:T(8,128)(2,1)S(1)}, bf16[128,768]{1,0:T(8,128)(2,1)S(1)}, u32[]{:S(2)}, u32[]{:S(2)}) collective-permute-start(bf16[128,768]{1,0:T(8,128)(2,1)S(1)} %get-tuple-element.105), channel_id=1, source_target_pairs={{0,16},{32,48},{64,80},{96,112},{128,144},{160,176},{192,208},{224... | collective-permute-start | bytes 589832 | tf_op jit(solution)/shard_map/ppermute | solution.py:396
  16.4 12.6 %collective-permute-start.6 = (bf16[528,256]{1,0:T(8,128)(2,1)S(1)}, bf16[528,256]{1,0:T(8,128)(2,1)S(1)}, u32[]{:S(2)}, u32[]{:S(2)}) collective-permute-start(bf16[528,256]{1,0:T(8,128)(2,1)S(1)} %get-tuple-element.57.refs_3_.refs_4_), channel_id=1, source_target_pairs={{0,16},{32,48},{64,80},{96,112},{128,144},{160,176},{192,208},{224... | collective-permute-start | bytes 811016 | tf_op jit(solution)/shard_map/ppermute | solution.py:396
  39.6 10.7 %collective-permute-done.3.refs_6_ = bf16[528,256]{1,0:T(8,128)(2,1)S(1)} collective-permute-done((bf16[528,256]{1,0:T(8,128)(2,1)S(1)}, bf16[528,256]{1,0:T(8,128)(2,1)S(1)}, u32[]{:S(2)}, u32[]{:S(2)}) %collective-permute-start.3) | collective-permute-done | bytes 270368 | tf_op jit(solution)/shard_map/ppermute | solution.py:396
  51.0 4.6 %collective-permute-start.8 = (bf16[528,256]{1,0:T(8,128)(2,1)S(1)}, bf16[528,256]{1,0:T(8,128)(2,1)S(1)}, u32[]{:S(2)}, u32[]{:S(2)}) collective-permute-start(bf16[528,256]{1,0:T(8,128)(2,1)S(1)} %collective-permute-done.7.refs_5_), channel_id=1, source_target_pairs={{0,16},{32,48},{64,80},{96,112},{128,144},{160,176},{192,208},{224... | collective-permute-start | bytes 811016 | tf_op jit(solution)/shard_map/ppermute | solution.py:396
  56.9 7.9 %collective-permute-start.5 = (bf16[528,256]{1,0:T(8,128)(2,1)S(1)}, bf16[528,256]{1,0:T(8,128)(2,1)S(1)}, u32[]{:S(2)}, u32[]{:S(2)}) collective-permute-start(bf16[528,256]{1,0:T(8,128)(2,1)S(1)} %collective-permute-done.4.refs_5_), channel_id=1, source_target_pairs={{0,16},{32,48},{64,80},{96,112},{128,144},{160,176},{192,208},{224... | collective-permute-start | bytes 811016 | tf_op jit(solution)/shard_map/ppermute | solution.py:396
  64.9 5.5 %collective-permute-done.8.refs_6_ = bf16[528,256]{1,0:T(8,128)(2,1)S(1)} collective-permute-done((bf16[528,256]{1,0:T(8,128)(2,1)S(1)}, bf16[528,256]{1,0:T(8,128)(2,1)S(1)}, u32[]{:S(2)}, u32[]{:S(2)}) %collective-permute-start.8) | collective-permute-done | bytes 270368 | tf_op jit(solution)/shard_map/ppermute | solution.py:396
  73.4 5.7 %collective-permute-done.5.refs_6_ = bf16[528,256]{1,0:T(8,128)(2,1)S(1)} collective-permute-done((bf16[528,256]{1,0:T(8,128)(2,1)S(1)}, bf16[528,256]{1,0:T(8,128)(2,1)S(1)}, u32[]{:S(2)}, u32[]{:S(2)}) %collective-permute-start.5) | collective-permute-done | bytes 270368 | tf_op jit(solution)/shard_map/ppermute | solution.py:396
  81.4 4.1 %shard_map.162 = (bf16[4,9,96,128]{3,2,1,0:T(8,128)(2,1)S(1)}, bf16[4,9,96,128]{3,2,1,0:T(8,128)(2,1)S(1)}, bf16[512,384]{1,0:T(8,128)(2,1)S(1)}, bf16[512,512]{1,0:T(8,128)(2,1)S(1)}) custom-call(s32[3]{0:T(128)S(1)} %pad_add_fusion.place, f32[512,256]{1,0:T(8,128)S(1)} %get-tuple-element.70.d_donor, f32[512,256]{1,0:T(8,128)S(1)} %get-tuple-element.71.d_accept, ...), custom_call_target="tpu_custom_call" | custom-call | flops 4000000000 | bytes 1000000 | tf_op jit(solution)/shard_map/pallas_call | solution.py:496
  85.5 4.1 %collective-permute-start.12 = (bf16[4,9,96,128]{3,2,1,0:T(8,128)(2,1)S(1)}, bf16[4,9,96,128]{3,2,1,0:T(8,128)(2,1)S(1)}, u32[]{:S(2)}, u32[]{:S(2)}) collective-permute-start(bf16[4,9,96,128]{3,2,1,0:T(8,128)(2,1)S(1)} %get-tuple-element.88), channel_id=1, source_target_pairs={{0,1},{1,0},{2,3},{3,2},{4,5},{5,4},{6,7},{7,6},{8,9},{9,8},{10,11... | collective-permute-start | bytes 2654216 | tf_op jit(solution)/shard_map/ppermute | solution.py:503
  92.4 20.6 %collective-permute-start.10 = (bf16[2,4,304,128]{3,2,1,0:T(8,128)(2,1)S(1)}, bf16[2,4,304,128]{3,2,1,0:T(8,128)(2,1)S(1)}, u32[]{:S(2)}, u32[]{:S(2)}) collective-permute-start(bf16[2,4,304,128]{3,2,1,0:T(8,128)(2,1)S(1)} %slice.84), channel_id=1, source_target_pairs={{0,128},{128,0},{256,384},{384,256},{1,129},{129,1},{257,385},{385... | collective-permute-start | bytes 1867784 | tf_op jit(solution)/shard_map/ppermute | solution.py:515
  113.2 3.9 %collective-permute-start.13 = (bf16[2,9,96,128]{3,2,1,0:T(8,128)(2,1)S(1)}, bf16[2,9,96,128]{3,2,1,0:T(8,128)(2,1)S(1)}, u32[]{:S(2)}, u32[]{:S(2)}) collective-permute-start(bf16[2,9,96,128]{3,2,1,0:T(8,128)(2,1)S(1)} %get-tuple-element.90), channel_id=1, source_target_pairs={{128,256},{256,128},{384,0},{0,384},{129,257},{257,129},{385,1},{1... | collective-permute-start | bytes 1327112 | tf_op jit(solution)/shard_map/ppermute | solution.py:519
  117.1 10.2 %collective-permute-done.10.received = bf16[2,4,304,128]{3,2,1,0:T(8,128)(2,1)S(1)} collective-permute-done((bf16[2,4,304,128]{3,2,1,0:T(8,128)(2,1)S(1)}, bf16[2,4,304,128]{3,2,1,0:T(8,128)(2,1)S(1)}, u32[]{:S(2)}, u32[]{:S(2)}) %collective-permute-start.10) | collective-permute-done | bytes 622624 | tf_op jit(solution)/shard_map/ppermute | solution.py:515
  127.5 3.9 %collective-permute-start.11 = (bf16[4,304,128]{2,1,0:T(8,128)(2,1)S(1)}, bf16[4,304,128]{2,1,0:T(8,128)(2,1)S(1)}, u32[]{:S(2)}, u32[]{:S(2)}) collective-permute-start(bf16[4,304,128]{2,1,0:T(8,128)(2,1)S(1)} %get-tuple-element.86), channel_id=1, source_target_pairs={{128,256},{256,128},{384,0},{0,384},{129,257},{257,129},{385,1},{1... | collective-permute-start | bytes 933896 | tf_op jit(solution)/shard_map/ppermute | solution.py:524
  134.1 4.8 %collective-permute-done.11.head_in = bf16[4,304,128]{2,1,0:T(8,128)(2,1)S(1)} collective-permute-done((bf16[4,304,128]{2,1,0:T(8,128)(2,1)S(1)}, bf16[4,304,128]{2,1,0:T(8,128)(2,1)S(1)}, u32[]{:S(2)}, u32[]{:S(2)}) %collective-permute-start.11) | collective-permute-done | bytes 311328 | tf_op jit(solution)/shard_map/ppermute | solution.py:524
  139.6 16.2 %all_to_all.10.parts = bf16[4,528,128]{2,1,0:T(8,128)(2,1)S(1)} all-to-all(bf16[4,528,128]{2,1,0:T(8,128)(2,1)S(1)} %shard_map.167), channel_id=1, replica_groups=mesh['y'=4,'zb'=2,'zq'=4,'zhi'=2,'x'=4,'core'=2] {'zq'}, dimensions={0} | all-to-all | bytes 1081344 | tf_op jit(solution)/shard_map/all_to_all | solution.py:400
  156.5 5.0 %collective-permute-start.15 = (bf16[416,128]{1,0:T(8,128)(2,1)S(1)}, bf16[416,128]{1,0:T(8,128)(2,1)S(1)}, u32[]{:S(2)}, u32[]{:S(2)}) collective-permute-start(bf16[416,128]{1,0:T(8,128)(2,1)S(1)} %get-tuple-element.93.sent), channel_id=1, source_target_pairs={{0,64},{64,0},{1,65},{65,1},{2,66},{66,2},{3,67},{67,3},{4,68},{68... | collective-permute-start | bytes 319496 | tf_op jit(solution)/shard_map/ppermute | solution.py:536
  161.5 8.1 %collective-permute-start.17 = (bf16[112,128]{1,0:T(8,128)(2,1)S(1)}, bf16[112,128]{1,0:T(8,128)(2,1)S(1)}, u32[]{:S(2)}, u32[]{:S(2)}) collective-permute-start(bf16[112,128]{1,0:T(8,128)(2,1)S(1)} %slice.71), channel_id=1, source_target_pairs={{0,72},{72,0},{8,64},{64,8},{1,73},{73,1},{9,65},{65,9},{2,74},{74... | collective-permute-start | bytes 86024 | tf_op jit(solution)/shard_map/ppermute | solution.py:538
  169.7 3.9 %collective-permute-start.16 = (bf16[112,128]{1,0:T(8,128)(2,1)S(1)}, bf16[112,128]{1,0:T(8,128)(2,1)S(1)}, u32[]{:S(2)}, u32[]{:S(2)}) collective-permute-start(bf16[112,128]{1,0:T(8,128)(2,1)S(1)} %get-tuple-element.94.mine), channel_id=1, source_target_pairs={{0,8},{8,0},{1,9},{9,1},{2,10},{10,2},{3,11},{11,3},{4,12},{12,4},... | collective-permute-start | bytes 86024 | tf_op jit(solution)/shard_map/ppermute | solution.py:537
  173.6 10.1 %collective-permute-done.16.one = bf16[112,128]{1,0:T(8,128)(2,1)S(1)} collective-permute-done((bf16[112,128]{1,0:T(8,128)(2,1)S(1)}, bf16[112,128]{1,0:T(8,128)(2,1)S(1)}, u32[]{:S(2)}, u32[]{:S(2)}) %collective-permute-start.16) | collective-permute-done | bytes 28704 | tf_op jit(solution)/shard_map/ppermute | solution.py:537
  187.9 5.0 %collective-permute-start.20 = (bf16[112,128]{1,0:T(8,128)(2,1)S(1)}, bf16[112,128]{1,0:T(8,128)(2,1)S(1)}, u32[]{:S(2)}, u32[]{:S(2)}) collective-permute-start(bf16[112,128]{1,0:T(8,128)(2,1)S(1)} %get-tuple-element.96.own), channel_id=1, source_target_pairs={{0,6},{2,0},{4,2},{6,4},{1,7},{3,1},{5,3},{7,5},{8,14},{10,8},{12,... | collective-permute-start | bytes 86024 | tf_op jit(solution)/shard_map/ppermute | solution.py:548
  200.7 3.5 %collective-permute-start.23 = (bf16[1216,128]{1,0:T(8,128)(2,1)S(1)}, bf16[1216,128]{1,0:T(8,128)(2,1)S(1)}, u32[]{:S(2)}, u32[]{:S(2)}) collective-permute-start(bf16[1216,128]{1,0:T(8,128)(2,1)S(1)} %bitcast.25), channel_id=1, source_target_pairs={{128,0},{256,128},{384,256},{0,384},{129,1},{257,129},{385,257},{1... | collective-permute-start | bytes 933896 | tf_op jit(solution)/shard_map/ppermute | solution.py:556
  206.2 7.4 %collective-permute-start.21 = (f32[112,128]{1,0:T(8,128)S(1)}, f32[112,128]{1,0:T(8,128)S(1)}, u32[]{:S(2)}, u32[]{:S(2)}) collective-permute-start(f32[112,128]{1,0:T(8,128)S(1)} %shard_map.170), channel_id=1, source_target_pairs={{0,1},{1,0},{2,3},{3,2},{4,5},{5,4},{6,7},{7,6},{8,9},{9,8},{10,11... | collective-permute-start | bytes 172040 | tf_op jit(solution)/shard_map/ppermute | solution.py:552
  213.6 4.6 %collective-permute-start.25 = (bf16[608,128]{1,0:T(8,128)(2,1)S(1)}, bf16[608,128]{1,0:T(8,128)(2,1)S(1)}, u32[]{:S(2)}, u32[]{:S(2)}) collective-permute-start(bf16[608,128]{1,0:T(8,128)(2,1)S(1)} %slice.86), channel_id=1, source_target_pairs={{128,0},{256,128},{384,256},{0,384},{129,1},{257,129},{385,257},{1... | collective-permute-start | bytes 466952 | tf_op jit(solution)/shard_map/ppermute | solution.py:558
  221.1 4.4 %collective-permute-done.24.low = bf16[608,128]{1,0:T(8,128)(2,1)S(1)} collective-permute-done((bf16[608,128]{1,0:T(8,128)(2,1)S(1)}, bf16[608,128]{1,0:T(8,128)(2,1)S(1)}, u32[]{:S(2)}, u32[]{:S(2)}) %collective-permute-start.24) | collective-permute-done | bytes 155680 | tf_op jit(solution)/shard_map/ppermute | solution.py:557
  (94 shorter events, 51.8 us)
Async XLA Ops:
  1.8 11.4 %collective-permute-start.1 = (bf16[128,768]{1,0:T(8,128)(2,1)S(1)}, bf16[128,768]{1,0:T(8,128)(2,1)S(1)}, u32[]{:S(2)}, u32[]{:S(2)}) collective-permute-start(bf16[128,768]{1,0:T(8,128)(2,1)S(1)} %get-tuple-element.104), channel_id=1, source_target_pairs={{16,32},{48,64},{80,96},{112,128},{144,160},{176,192},{208,224},{2... | collective-permute-start | bytes 589832 | tf_op jit(solution)/shard_map/ppermute | solution.py:396
  2.5 10.7 %collective-permute-start = (bf16[128,768]{1,0:T(8,128)(2,1)S(1)}, bf16[128,768]{1,0:T(8,128)(2,1)S(1)}, u32[]{:S(2)}, u32[]{:S(2)}) collective-permute-start(bf16[128,768]{1,0:T(8,128)(2,1)S(1)} %get-tuple-element.105), channel_id=1, source_target_pairs={{0,16},{32,48},{64,80},{96,112},{128,144},{160,176},{192,208},{224... | collective-permute-start | bytes 589832 | tf_op jit(solution)/shard_map/ppermute | solution.py:396
  15.7 19.0 %collective-permute-start.2 = (bf16[528,256]{1,0:T(8,128)(2,1)S(1)}, bf16[528,256]{1,0:T(8,128)(2,1)S(1)}, u32[]{:S(2)}, u32[]{:S(2)}) collective-permute-start(bf16[528,256]{1,0:T(8,128)(2,1)S(1)} %get-tuple-element.56.refs_2_.refs_3_), channel_id=1, source_target_pairs={{16,32},{48,64},{80,96},{112,128},{144,160},{176,192},{208,224},{2... | collective-permute-start | bytes 811016 | tf_op jit(solution)/shard_map/ppermute | solution.py:396
  16.4 20.2 %collective-permute-start.6 = (bf16[528,256]{1,0:T(8,128)(2,1)S(1)}, bf16[528,256]{1,0:T(8,128)(2,1)S(1)}, u32[]{:S(2)}, u32[]{:S(2)}) collective-permute-start(bf16[528,256]{1,0:T(8,128)(2,1)S(1)} %get-tuple-element.57.refs_3_.refs_4_), channel_id=1, source_target_pairs={{0,16},{32,48},{64,80},{96,112},{128,144},{160,176},{192,208},{224... | collective-permute-start | bytes 811016 | tf_op jit(solution)/shard_map/ppermute | solution.py:396
  34.7 15.6 %collective-permute-start.3 = (bf16[528,256]{1,0:T(8,128)(2,1)S(1)}, bf16[528,256]{1,0:T(8,128)(2,1)S(1)}, u32[]{:S(2)}, u32[]{:S(2)}) collective-permute-start(bf16[528,256]{1,0:T(8,128)(2,1)S(1)} %collective-permute-done.2.refs_5_), channel_id=1, source_target_pairs={{0,16},{32,48},{64,80},{96,112},{128,144},{160,176},{192,208},{224... | collective-permute-start | bytes 811016 | tf_op jit(solution)/shard_map/ppermute | solution.py:396
  36.6 14.4 %collective-permute-start.7 = (bf16[528,256]{1,0:T(8,128)(2,1)S(1)}, bf16[528,256]{1,0:T(8,128)(2,1)S(1)}, u32[]{:S(2)}, u32[]{:S(2)}) collective-permute-start(bf16[528,256]{1,0:T(8,128)(2,1)S(1)} %collective-permute-done.6.refs_6_), channel_id=1, source_target_pairs={{16,32},{48,64},{80,96},{112,128},{144,160},{176,192},{208,224},{2... | collective-permute-start | bytes 811016 | tf_op jit(solution)/shard_map/ppermute | solution.py:396
  51.0 19.4 %collective-permute-start.8 = (bf16[528,256]{1,0:T(8,128)(2,1)S(1)}, bf16[528,256]{1,0:T(8,128)(2,1)S(1)}, u32[]{:S(2)}, u32[]{:S(2)}) collective-permute-start(bf16[528,256]{1,0:T(8,128)(2,1)S(1)} %collective-permute-done.7.refs_5_), channel_id=1, source_target_pairs={{0,16},{32,48},{64,80},{96,112},{128,144},{160,176},{192,208},{224... | collective-permute-start | bytes 811016 | tf_op jit(solution)/shard_map/ppermute | solution.py:396
  56.9 22.1 %collective-permute-start.5 = (bf16[528,256]{1,0:T(8,128)(2,1)S(1)}, bf16[528,256]{1,0:T(8,128)(2,1)S(1)}, u32[]{:S(2)}, u32[]{:S(2)}) collective-permute-start(bf16[528,256]{1,0:T(8,128)(2,1)S(1)} %collective-permute-done.4.refs_5_), channel_id=1, source_target_pairs={{0,16},{32,48},{64,80},{96,112},{128,144},{160,176},{192,208},{224... | collective-permute-start | bytes 811016 | tf_op jit(solution)/shard_map/ppermute | solution.py:396
  70.4 8.7 %collective-permute-start.9 = (bf16[528,256]{1,0:T(8,128)(2,1)S(1)}, bf16[528,256]{1,0:T(8,128)(2,1)S(1)}, u32[]{:S(2)}, u32[]{:S(2)}) collective-permute-start(bf16[528,256]{1,0:T(8,128)(2,1)S(1)} %collective-permute-done.8.refs_6_), channel_id=1, source_target_pairs={{16,32},{48,64},{80,96},{112,128},{144,160},{176,192},{208,224},{2... | collective-permute-start | bytes 811016 | tf_op jit(solution)/shard_map/ppermute | solution.py:396
  85.5 27.4 %collective-permute-start.12 = (bf16[4,9,96,128]{3,2,1,0:T(8,128)(2,1)S(1)}, bf16[4,9,96,128]{3,2,1,0:T(8,128)(2,1)S(1)}, u32[]{:S(2)}, u32[]{:S(2)}) collective-permute-start(bf16[4,9,96,128]{3,2,1,0:T(8,128)(2,1)S(1)} %get-tuple-element.88), channel_id=1, source_target_pairs={{0,1},{1,0},{2,3},{3,2},{4,5},{5,4},{6,7},{7,6},{8,9},{9,8},{10,11... | collective-permute-start | bytes 2654216 | tf_op jit(solution)/shard_map/ppermute | solution.py:503
  92.4 35.0 %collective-permute-start.10 = (bf16[2,4,304,128]{3,2,1,0:T(8,128)(2,1)S(1)}, bf16[2,4,304,128]{3,2,1,0:T(8,128)(2,1)S(1)}, u32[]{:S(2)}, u32[]{:S(2)}) collective-permute-start(bf16[2,4,304,128]{3,2,1,0:T(8,128)(2,1)S(1)} %slice.84), channel_id=1, source_target_pairs={{0,128},{128,0},{256,384},{384,256},{1,129},{129,1},{257,385},{385... | collective-permute-start | bytes 1867784 | tf_op jit(solution)/shard_map/ppermute | solution.py:515
  113.2 18.3 %collective-permute-start.13 = (bf16[2,9,96,128]{3,2,1,0:T(8,128)(2,1)S(1)}, bf16[2,9,96,128]{3,2,1,0:T(8,128)(2,1)S(1)}, u32[]{:S(2)}, u32[]{:S(2)}) collective-permute-start(bf16[2,9,96,128]{3,2,1,0:T(8,128)(2,1)S(1)} %get-tuple-element.90), channel_id=1, source_target_pairs={{128,256},{256,128},{384,0},{0,384},{129,257},{257,129},{385,1},{1... | collective-permute-start | bytes 1327112 | tf_op jit(solution)/shard_map/ppermute | solution.py:519
  127.5 11.4 %collective-permute-start.11 = (bf16[4,304,128]{2,1,0:T(8,128)(2,1)S(1)}, bf16[4,304,128]{2,1,0:T(8,128)(2,1)S(1)}, u32[]{:S(2)}, u32[]{:S(2)}) collective-permute-start(bf16[4,304,128]{2,1,0:T(8,128)(2,1)S(1)} %get-tuple-element.86), channel_id=1, source_target_pairs={{128,256},{256,128},{384,0},{0,384},{129,257},{257,129},{385,1},{1... | collective-permute-start | bytes 933896 | tf_op jit(solution)/shard_map/ppermute | solution.py:524
  131.5 8.0 %collective-permute-start.14 = (bf16[9,96,128]{2,1,0:T(8,128)(2,1)S(1)}, bf16[9,96,128]{2,1,0:T(8,128)(2,1)S(1)}, u32[]{:S(2)}, u32[]{:S(2)}) collective-permute-start(bf16[9,96,128]{2,1,0:T(8,128)(2,1)S(1)} %get-tuple-element.92), channel_id=1, source_target_pairs={{0,128},{128,0},{256,384},{384,256},{1,129},{129,1},{257,385},{385... | collective-permute-start | bytes 663560 | tf_op jit(solution)/shard_map/ppermute | solution.py:525
  156.5 27.1 %collective-permute-start.15 = (bf16[416,128]{1,0:T(8,128)(2,1)S(1)}, bf16[416,128]{1,0:T(8,128)(2,1)S(1)}, u32[]{:S(2)}, u32[]{:S(2)}) collective-permute-start(bf16[416,128]{1,0:T(8,128)(2,1)S(1)} %get-tuple-element.93.sent), channel_id=1, source_target_pairs={{0,64},{64,0},{1,65},{65,1},{2,66},{66,2},{3,67},{67,3},{4,68},{68... | collective-permute-start | bytes 319496 | tf_op jit(solution)/shard_map/ppermute | solution.py:536
  161.5 12.1 %collective-permute-start.17 = (bf16[112,128]{1,0:T(8,128)(2,1)S(1)}, bf16[112,128]{1,0:T(8,128)(2,1)S(1)}, u32[]{:S(2)}, u32[]{:S(2)}) collective-permute-start(bf16[112,128]{1,0:T(8,128)(2,1)S(1)} %slice.71), channel_id=1, source_target_pairs={{0,72},{72,0},{8,64},{64,8},{1,73},{73,1},{9,65},{65,9},{2,74},{74... | collective-permute-start | bytes 86024 | tf_op jit(solution)/shard_map/ppermute | solution.py:538
  169.7 14.0 %collective-permute-start.16 = (bf16[112,128]{1,0:T(8,128)(2,1)S(1)}, bf16[112,128]{1,0:T(8,128)(2,1)S(1)}, u32[]{:S(2)}, u32[]{:S(2)}) collective-permute-start(bf16[112,128]{1,0:T(8,128)(2,1)S(1)} %get-tuple-element.94.mine), channel_id=1, source_target_pairs={{0,8},{8,0},{1,9},{9,1},{2,10},{10,2},{3,11},{11,3},{4,12},{12,4},... | collective-permute-start | bytes 86024 | tf_op jit(solution)/shard_map/ppermute | solution.py:537
  184.4 16.3 %all-to-all-start.1 = ((bf16[4,304,128]{2,1,0:T(8,128)(2,1)}), bf16[4,304,128]{2,1,0:T(8,128)(2,1)S(1)}, u32[]{:S(2)}, u32[]{:S(2)}) async-start(bf16[4,304,128]{2,1,0:T(8,128)(2,1)} %get-tuple-element.95), calls=%async_computation.1 | async-start | bytes 622592 | tf_op jit(solution)/shard_map/all_to_all | solution.py:400
  187.9 9.4 %collective-permute-start.20 = (bf16[112,128]{1,0:T(8,128)(2,1)S(1)}, bf16[112,128]{1,0:T(8,128)(2,1)S(1)}, u32[]{:S(2)}, u32[]{:S(2)}) collective-permute-start(bf16[112,128]{1,0:T(8,128)(2,1)S(1)} %get-tuple-element.96.own), channel_id=1, source_target_pairs={{0,6},{2,0},{4,2},{6,4},{1,7},{3,1},{5,3},{7,5},{8,14},{10,8},{12,... | collective-permute-start | bytes 86024 | tf_op jit(solution)/shard_map/ppermute | solution.py:548
  200.7 12.9 %collective-permute-start.23 = (bf16[1216,128]{1,0:T(8,128)(2,1)S(1)}, bf16[1216,128]{1,0:T(8,128)(2,1)S(1)}, u32[]{:S(2)}, u32[]{:S(2)}) collective-permute-start(bf16[1216,128]{1,0:T(8,128)(2,1)S(1)} %bitcast.25), channel_id=1, source_target_pairs={{128,0},{256,128},{384,256},{0,384},{129,1},{257,129},{385,257},{1... | collective-permute-start | bytes 933896 | tf_op jit(solution)/shard_map/ppermute | solution.py:556
  204.3 14.0 %collective-permute-start.22 = (bf16[1216,128]{1,0:T(8,128)(2,1)S(1)}, bf16[1216,128]{1,0:T(8,128)(2,1)S(1)}, u32[]{:S(2)}, u32[]{:S(2)}) collective-permute-start(bf16[1216,128]{1,0:T(8,128)(2,1)S(1)} %bitcast.26), channel_id=1, source_target_pairs={{0,128},{128,256},{256,384},{384,0},{1,129},{129,257},{257,385},{3... | collective-permute-start | bytes 933896 | tf_op jit(solution)/shard_map/ppermute | solution.py:555
  206.2 14.0 %collective-permute-start.21 = (f32[112,128]{1,0:T(8,128)S(1)}, f32[112,128]{1,0:T(8,128)S(1)}, u32[]{:S(2)}, u32[]{:S(2)}) collective-permute-start(f32[112,128]{1,0:T(8,128)S(1)} %shard_map.170), channel_id=1, source_target_pairs={{0,1},{1,0},{2,3},{3,2},{4,5},{5,4},{6,7},{7,6},{8,9},{9,8},{10,11... | collective-permute-start | bytes 172040 | tf_op jit(solution)/shard_map/ppermute | solution.py:552
  213.6 7.4 %collective-permute-start.25 = (bf16[608,128]{1,0:T(8,128)(2,1)S(1)}, bf16[608,128]{1,0:T(8,128)(2,1)S(1)}, u32[]{:S(2)}, u32[]{:S(2)}) collective-permute-start(bf16[608,128]{1,0:T(8,128)(2,1)S(1)} %slice.86), channel_id=1, source_target_pairs={{128,0},{256,128},{384,256},{0,384},{129,1},{257,129},{385,257},{1... | collective-permute-start | bytes 466952 | tf_op jit(solution)/shard_map/ppermute | solution.py:558
  218.3 7.2 %collective-permute-start.24 = (bf16[608,128]{1,0:T(8,128)(2,1)S(1)}, bf16[608,128]{1,0:T(8,128)(2,1)S(1)}, u32[]{:S(2)}, u32[]{:S(2)}) collective-permute-start(bf16[608,128]{1,0:T(8,128)(2,1)S(1)} %slice.85), channel_id=1, source_target_pairs={{0,128},{128,256},{256,384},{384,0},{1,129},{129,257},{257,385},{3... | collective-permute-start | bytes 466952 | tf_op jit(solution)/shard_map/ppermute | solution.py:557
  (12 other events, 90.0 us)

commit v5 on v4

--- a/solution.py
+++ b/solution.py
@@ -128,68 +128,90 @@
 
 def pair_kernel(distance, *refs):
     if distance == 0:
-        odd, own, even0, odd0, d_donor, d_accept, loss = refs
+        flag, own, first0, second0, d_donor, d_accept, loss, own_list, _ = refs
         d_donor[...] = jnp.zeros_like(d_donor)
         d_accept[...] = jnp.zeros_like(d_accept)
         loss[...] = jnp.zeros_like(loss)
+        first1, second1, far, far_list = second0, first0, None, None
     else:
-        odd, own, far, even0, odd0, even1, odd1, dd_in, da_in, loss_in, d_donor, d_accept, loss = refs
+        (
+            flag, own, far, first0, second0, first1, second1, dd_in, da_in, loss_in,
+            d_donor, d_accept, loss, own_list, far_list,
+        ) = refs
         d_donor[...] = dd_in[...]
         d_accept[...] = da_in[...]
         loss[...] = loss_in[...]
-    is_odd = odd[0] > 0
-    scale = even0.shape[1] ** (-0.5)
+    scale = first0.shape[1] ** (-0.5)
     per_device = d_donor.shape[0] // PANEL
     row = lax.broadcasted_iota(jnp.int32, (PANEL, PANEL), 0)
     col = lax.broadcasted_iota(jnp.int32, (PANEL, PANEL), 1)
 
+    def collect(meta, into):
+        def step(j, count):
+            block = meta[j, 2] - distance * per_device
+            here = (meta[j, 4] > 0) & (block >= 0) & (block < per_device)
+            into[count, 0] = meta[j, 0]
+            into[count, 1] = meta[j, 1]
+            into[count, 2] = jnp.clip(block, 0, per_device - 1)
+            into[count, 3] = meta[j, 3]
+            return count + here.astype(jnp.int32)
+
+        return lax.fori_loop(0, SLOTS, step, jnp.int32(0), unroll=True)
+
     def place(block):
         return pl.ds(pl.multiple_of(block * PANEL, PANEL), PANEL)
 
-    def own_donor(block):
-        return jnp.where(is_odd, odd0[place(block), :], even0[place(block), :])
-
-    def own_accept(block):
-        return jnp.where(is_odd, even0[place(block), :], odd0[place(block), :])
-
-    if distance == 0:
-        far_accept, far_donor = own_accept, None
-    else:
-
-        def far_accept(block):
-            return jnp.where(is_odd, odd1[place(block), :], even1[place(block), :])
-
-        def far_donor(block):
-            return jnp.where(is_odd, even1[place(block), :], odd1[place(block), :])
-
-    def visit(meta, j, donors, acceptors, is_owner):
-        accept_block = meta[j, 2] - distance * per_device
-        here = (meta[j, 4] > 0) & (accept_block >= 0) & (accept_block < per_device)
-
-        @pl.when(here)
-        def _():
-            donor_block = meta[j, 0]
-            dpan = donors(donor_block)
-            apan = acceptors(accept_block)
-            scores = dot_t(dpan, apan) * scale
-            target = ((row == meta[j, 1]) & (col == meta[j, 3])).astype(F32)
-            small = jnp.exp(-jnp.abs(scores))
-            inverse = 1.0 / (1.0 + small)
-            sigmoid = jnp.where(scores >= 0, inverse, small * inverse)
-            dscore = ((sigmoid - target) * LOSS_WEIGHT).astype(BF16)
-            if is_owner:
-                loss[...] += (jnp.maximum(scores, 0.0) + jnp.log1p(small)) - target * scores
-                d_donor[place(donor_block), :] += dot(dscore, apan) * scale
-            if distance == 0 or not is_owner:
-                d_accept[place(accept_block), :] += scale * lax.dot_general(
-                    dscore, dpan, (((0,), (0,)), ((), ())), preferred_element_type=F32
-                )
-
-    @pl.loop(0, SLOTS)
-    def _(j):
-        visit(own, j, own_donor, far_accept, True)
-        if distance > 0:
-            visit(far, j, far_donor, own_accept, False)
+    def visit(slots, i, count, donors, acceptors, is_owner):
+        j = jnp.minimum(i, jnp.maximum(count - 1, 0))
+        used = jnp.where(i < count, 1.0, 0.0).astype(F32)
+        donor_block, accept_block = slots[j, 0], slots[j, 2]
+        dpan = donors[place(donor_block), :]
+        apan = acceptors[place(accept_block), :]
+        scores = dot_t(dpan, apan) * scale
+        target = ((row == slots[j, 1]) & (col == slots[j, 3])).astype(F32)
+        small = jnp.exp(-jnp.abs(scores))
+        inverse = 1.0 / (1.0 + small)
+        sigmoid = jnp.where(scores >= 0, inverse, small * inverse)
+        dscore = ((sigmoid - target) * (used * LOSS_WEIGHT)).astype(BF16)
+        results = []
+        if is_owner:
+            term = (jnp.maximum(scores, 0.0) + jnp.log1p(small)) - target * scores
+            results.append((d_donor, donor_block, dot(dscore, apan) * scale))
+            results.append((loss, None, term * used))
+        if distance == 0 or not is_owner:
+            back = lax.dot_general(
+                dscore, dpan, (((0,), (0,)), ((), ())), preferred_element_type=F32
+            )
+            results.append((d_accept, accept_block, back * scale))
+        return results
+
+    def add(results):
+        for ref, block, value in results:
+            if block is None:
+                ref[...] += value
+            else:
+                ref[place(block), :] += value
+
+    def run(donors, own_accept, far_donor, far_accept):
+        count = collect(own, own_list)
+        if distance == 0:
+
+            @pl.loop(0, count)
+            def _(i):
+                add(visit(own_list, i, count, donors, own_accept, True))
+
+        else:
+            far_count = collect(far, far_list)
+
+            @pl.loop(0, jnp.maximum(count, far_count))
+            def _(i):
+                mine = visit(own_list, i, count, donors, far_accept, True)
+                theirs = visit(far_list, i, far_count, far_donor, own_accept, False)
+                add(mine)
+                add(theirs)
+
+    pl.when(flag[0] > 0)(lambda: run(second0, first0, first1, second1))
+    pl.when(flag[0] <= 0)(lambda: run(first0, second0, second1, first1))
 
 
 def relative(target, y, first):
@@ -337,18 +359,19 @@
     mine[...] = picked(zb)
 
 
-def far_sum_kernel(sent, received, mine, one, two, head, taps):
+def far_sum_kernel(sent, received, mine, head, taps):
     chunk_rows = head.shape[1]
     total = split_rows(sent[:chunk_rows, :].astype(F32) + received[:chunk_rows, :].astype(F32))
     for zq in range(head.shape[0]):
         head[zq] = total
-    near = mine[...].astype(F32) + received[chunk_rows:, :].astype(F32)
-    taps[...] = (near + (one[...].astype(F32) + two[...].astype(F32))).astype(BF16)
-
-
-def line_total_kernel(own, one, two, three, total):
+    taps[...] = (mine[...].astype(F32) + received[chunk_rows:, :].astype(F32)).astype(BF16)
+
+
+def line_total_kernel(own, one, two, three, parts):
     even = own[...].astype(F32) + two[...].astype(F32)
-    total[...] = even + (one[...].astype(F32) + three[...].astype(F32))
+    total = (even + (one[...].astype(F32) + three[...].astype(F32))).astype(BF16)
+    for k in range(parts.shape[0]):
+        parts[k] = total
 
 
 def finish_kernel(
@@ -455,10 +478,24 @@
         donor_weight, acceptor_weight, meta_rows,
     )
 
+    lists = [pltpu.SMEM((SLOTS, 4), jnp.int32)] * 2
     acc_shapes = [shape((rows, heads), F32), shape((rows, heads), F32), shape((PANEL, PANEL), F32)]
     acc = call(
-        lambda *refs: pair_kernel(0, *refs), acc_shapes, [SM] * 2 + [VM] * 2, 12, 2_000_000_000
+        lambda *refs: pair_kernel(0, *refs), acc_shapes, [SM] * 2 + [VM] * 2, 12, 2_000_000_000, lists
     )(1 - odd, meta, even_feat, odd_feat)
+    def pairs_at(distance, short_far, long_far, acc):
+        far_meta = jnp.where(is_odd, short_far[rows:, :8], long_far[rows:, :8]).astype(jnp.int32)
+        return call(
+            lambda *refs: pair_kernel(distance, *refs), acc_shapes, [SM] * 3 + [VM] * 7, 12, 2_500_000_000,
+            lists,
+        )(1 - odd, meta, far_meta, even_feat, odd_feat, long_far, short_far, *acc)
+
+    barrier = lax.optimization_barrier
+    short1 = swapped(odd_feat, 0)
+    late_feat, acc = barrier((even_feat, acc))
+    long1 = swapped(late_feat, 1)
+    long2 = swapped(short1, 1)
+    conv, _ = barrier((conv, short1))
     edge_factor, slope, hidden_t, act_t, embed_t = call(
         side_kernel,
         [
@@ -472,20 +509,14 @@
         20,
         6_000_000_000,
     )(odd, even_edge, odd_edge, gain, hidden, conv, act, embed, order, eye)
-    even_far, odd_far = even_feat, odd_feat
-    for distance in range(1, SPAN + 1):
-        if distance == 1:
-            odd_far, even_far = swapped(odd_feat, 0), swapped(even_feat, 1)
-        else:
-            odd_far, even_far = swapped(even_far, 0), swapped(odd_far, 1)
-        far_meta = jnp.where(is_odd, odd_far[rows:, :8], even_far[rows:, :8]).astype(jnp.int32)
-        acc = call(
-            lambda *refs, distance=distance: pair_kernel(distance, *refs),
-            acc_shapes,
-            [SM] * 3 + [VM] * 7,
-            12,
-            2_500_000_000,
-        )(1 - odd, meta, far_meta, even_feat, odd_feat, even_far, odd_far, *acc)
+    short2 = swapped(long1, 0)
+    acc = pairs_at(1, short1, long1, acc)
+    short3, long3 = swapped(long2, 0), swapped(short2, 1)
+    _, acc = barrier((short3, tuple(acc)))
+    acc = pairs_at(2, short2, long2, acc)
+    short4, long4 = swapped(long3, 0), swapped(short3, 1)
+    acc = pairs_at(3, short3, long3, acc)
+    acc = pairs_at(4, short4, long4, acc)
 
     chunk = CHUNK_ROWS + EXTRA_ROWS
     lanes = inner // 128
@@ -534,30 +565,25 @@
         [SM] + [VM] * 2, 8, quick,
     )(place, parts, pick)
     received = lax.ppermute(sent, "zb", [(0, 1), (1, 0)])
-    across = lax.ppermute(mine, "zhi", [(0, 1), (1, 0)])
-    corner = lax.ppermute(
-        sent[chunk:], ("zb", "zhi"), [(0, 3), (3, 0), (1, 2), (2, 1)]
-    )
     head_parts, conv_sum = call(
-        far_sum_kernel, [shape((4, chunk, 128), BF16), shape((112, 128), BF16)], [VM] * 5, 8, quick
-    )(sent, received, mine, across, corner)
+        far_sum_kernel, [shape((4, chunk, 128), BF16), shape((112, 128), BF16)], [VM] * 3, 8, quick
+    )(sent, received, mine)
 
     head_rows = 4 * chunk
     head_sum = swap_parts(head_parts, "zq").reshape(head_rows, 128)
     line = [
         lax.ppermute(conv_sum, "x", [(i, (i + step) % 4) for i in range(4)]) for step in (1, 2, 3)
     ]
-    (conv_sum,) = call(line_total_kernel, [shape((112, 128), F32)], [VM] * 4, 8, quick)(conv_sum, *line)
+    (conv_sum,) = call(line_total_kernel, [shape((4, 112, 128), BF16)], [VM] * 4, 8, quick)(conv_sum, *line)
     head_sum, conv_sum = lax.optimization_barrier((head_sum, conv_sum))
-    other = lax.ppermute(conv_sum, "core", [(0, 1), (1, 0)])
     around = [(i, (i + 1) % 4) for i in range(4)]
     back = [(j, i) for i, j in around]
     behind = lax.ppermute(head_sum, "y", around)
     ahead = lax.ppermute(head_sum, "y", back)
     low = lax.ppermute(behind[: head_rows // 2], "y", around)
     high = lax.ppermute(ahead[head_rows // 2 :], "y", back)
-    is_first = lax.axis_index("core") == 0
-    pieces = jnp.stack([jnp.where(is_first, conv_sum, other), jnp.where(is_first, other, conv_sum)])
+    pieces = swap_parts(conv_sum, ("zhi", "core")).astype(F32).reshape(2, 2, 112, 128)
+    pieces = pieces[0] + pieces[1]
     pieces = pieces[:, : slabs * 12].reshape(2, tap_count, lanes, 12, 128)
     grad_conv = pieces.transpose(1, 0, 3, 2, 4).reshape(tap_count, 24, inner)
     head_weight = shape((channels, heads), BF16)

time: 230 us -> 242 us (1.052)
  local copies, waits for them, and re-layouts: 1.19 us -> 10.8 us
  Pallas kernels: 29.7 us -> 37.8 us
  waiting for transfers between devices: 55.4 us -> 51.4 us
  starting transfers between devices: 122 us -> 119 us
    ppermute x3 -> x0, starting transfers between devices: 19.4 us -> none  [the longest x1 8.14 us: on_device(): lax.ppermute(sent[chunk:], ('zb', 'zhi'), [(0, 3), (3, 0), (1, 2), (2, 1)])]
    all_to_all x1 -> x2, starting transfers between devices: 3.45 us -> 18.1 us  [swap_parts(): return lax.all_to_all(parts, axis, 0, 0, tiled=True)]
    ppermute x1, waiting for transfers between devices: 0.01 us -> 11.6 us  [on_device(): received = lax.ppermute(sent, 'zb', [(0, 1), (1, 0)])]
    ppermute x10, waiting for transfers between devices: 21.8 us -> 11.3 us  [swapped(): return lax.ppermute(block, SEQ, pairs + [(j, i) for i, j in pairs])]
    ppermute x3 -> x0, waiting for transfers between devices: 10.1 us -> none  [the longest x1 10.1 us: on_device(): across = lax.ppermute(mine, 'zhi', [(0, 1), (1, 0)])]
    unnamed x20 -> x54, local copies, waits for them, and re-layouts: 0.21 us -> 8.39 us
    ppermute x1, waiting for transfers between devices: 0.01 us -> 5.58 us  [on_device(): ahead = lax.ppermute(head_sum, 'y', back)]
    pallas_call x5, Pallas kernels: 8.33 us -> 13.4 us  [the longest x4 12.7 us: pairs_at(): call(lambda *refs: pair_kernel(distance, *refs), acc_shapes, [SM] * 3 + [...]
  transfers between devices with their start and end apart: 27 -> 25, of which waited for: 10 -> 10; matrix products, arithmetic and copies ran while one was open for 1% -> 1% of each run, Pallas kernels for 7% -> 9%
where the time goes in v5:
time: 242 us; the launch traced here: 240 us
  starting transfers between devices  119 us (49%)
  waiting for transfers between devices  51.4 us (21%)
  Pallas kernels  37.8 us (16%)
  blocking collectives  16.3 us (7%)
  local copies, waits for them, and re-layouts  10.8 us (4%)
    ppermute x10, starting transfers between devices, swapped(): return lax.ppermute(block, SEQ, pairs + [(j, i) for i, j in pairs])  33.3 us
    ppermute x1, starting transfers between devices, on_device(): other = lax.ppermute(head_sum[2:], 'y', first_pairs)  23.3 us
    all_to_all x2, starting transfers between devices, swap_parts(): return lax.all_to_all(parts, axis, 0, 0, tiled=True)  18.1 us
    all_to_all x1, blocking collectives, swap_parts(): return lax.all_to_all(parts, axis, 0, 0, tiled=True)  16.3 us
    pallas_call x4, Pallas kernels, pairs_at(): call(lambda *refs: pair_kernel(distance, *refs), acc_shapes, [SM] * 3 + [...  12.7 us
    ppermute x1, waiting for transfers between devices, on_device(): received = lax.ppermute(sent, 'zb', [(0, 1), (1, 0)])  11.6 us
    ppermute x10, waiting for transfers between devices, swapped(): return lax.ppermute(block, SEQ, pairs + [(j, i) for i, j in pairs])  11.3 us
    ppermute x3, starting transfers between devices, on_device(): lax.ppermute(conv_sum, 'x', [(i, (i + step) % 4) for i in range(4)])  10.1 us
  transfers between devices with their start and end apart: 25, of which 10 were waited for; matrix products, arithmetic and copies ran while one was open for 1% of the time, Pallas kernels for 9%

profile of v5, /device:TPU:1, one launch (start us, length us, event | category | flops | bytes accessed | tf_op | source)
XLA Modules:
  0.0 239.8 jit_solution(7885601244869632891)
XLA Ops:
  3.1 7.2 %collective-permute-start = (bf16[128,768]{1,0:T(8,128)(2,1)}, bf16[128,768]{1,0:T(8,128)(2,1)}, u32[]{:S(2)}, u32[]{:S(2)}) collective-permute-start(bf16[128,768]{1,0:T(8,128)(2,1)} %get-tuple-element.121), channel_id=1, source_target_pairs={{0,16},{32,48},{64,80},{96,112},{128,144},{160,176},{192,208},{224... | collective-permute-start | bytes 589832 | tf_op jit(solution)/shard_map/ppermute | solution.py:419
  17.1 4.2 %shard_map.155 = (bf16[768,768]{1,0:T(8,128)(2,1)S(1)}, f32[512,384]{1,0:T(8,128)S(1)}, bf16[512,384]{1,0:T(8,128)(2,1)S(1)}, bf16[512,768]{1,0:T(8,128)(2,1)S(1...) custom-call(s32[1]{0:T(128)} %bitcast.3.odd, bf16[512,768]{1,0:T(8,128)(2,1)S(1)} %bitcast.25, ...), custom_call_target="tpu_custom_call" | custom-call | flops 4000000000 | bytes 1000000 | tf_op jit(solution)/shard_map/pallas_call | solution.py:463
  30.5 11.9 %collective-permute-start.3 = (bf16[528,256]{1,0:T(8,128)(2,1)S(1)}, bf16[528,256]{1,0:T(8,128)(2,1)S(1)}, u32[]{:S(2)}, u32[]{:S(2)}) collective-permute-start(bf16[528,256]{1,0:T(8,128)(2,1)S(1)} %collective-permute-done.2.refs_5_), channel_id=1, source_target_pairs={{0,16},{32,48},{64,80},{96,112},{128,144},{160,176},{192,208},{224... | collective-permute-start | bytes 811016 | tf_op jit(solution)/shard_map/ppermute | solution.py:419
  46.9 4.4 %shard_map.161 = (bf16[256,768]{1,0:T(8,128)(2,1)S(1)}, f32[512,384]{1,0:T(8,128)S(1)}, bf16[768,768]{1,0:T(8,128)(2,1)S(1)}, bf16[384,512]{1,0:T(8,128)(2,1)S(1)}, bf16[768,512]{1,0:T(8,128)(2,1)S(1)}) custom-call(s32[1]{0:T(128)} %bitcast.3.odd, bf16[128,768]{1,0:T(8,128)(2,1)} %collective-permute-done.even_edge, ...), custom_call_target="tpu_custom_call" | custom-call | flops 6000000000 | bytes 1000000 | tf_op jit(solution)/shard_map/pallas_call | solution.py:499
  56.6 9.7 %collective-permute-done.8.refs_6_ = bf16[528,256]{1,0:T(8,128)(2,1)S(1)} collective-permute-done((bf16[528,256]{1,0:T(8,128)(2,1)S(1)}, bf16[528,256]{1,0:T(8,128)(2,1)S(1)}, u32[]{:S(2)}, u32[]{:S(2)}) %collective-permute-start.8) | collective-permute-done | bytes 270368 | tf_op jit(solution)/shard_map/ppermute | solution.py:419
  67.0 7.1 %collective-permute-start.5 = (bf16[528,256]{1,0:T(8,128)(2,1)S(1)}, bf16[528,256]{1,0:T(8,128)(2,1)S(1)}, u32[]{:S(2)}, u32[]{:S(2)}) collective-permute-start(bf16[528,256]{1,0:T(8,128)(2,1)S(1)} %collective-permute-done.4.refs_5_), channel_id=1, source_target_pairs={{0,16},{32,48},{64,80},{96,112},{128,144},{160,176},{192,208},{224... | collective-permute-start | bytes 811016 | tf_op jit(solution)/shard_map/ppermute | solution.py:419
  79.8 4.5 %shard_map.160 = (f32[512,256]{1,0:T(8,128)S(1)}, f32[512,256]{1,0:T(8,128)S(1)}, f32[128,128]{1,0:T(8,128)S(1)}) custom-call(s32[1]{0:T(128)S(6)} %sub.26.refs_0_, s32[16,8]{1,0:T(8,128)S(1)} %stack.28.refs_1_, s32[16,8]{1,0:T(8,128)S(1)} %fusion.11.refs_2_, bf16[528,256]{1,0:T(8,128)(2,1)} %get-tuple-element.69.refs_2_.refs_3_, ...), custom_call_target="tpu_custom_call" | custom-call | flops 2500000000 | bytes 1000000 | tf_op jit(solution)/shard_map/pallas_call | solution.py:488
  84.4 4.1 %shard_map.162 = (bf16[4,9,96,128]{3,2,1,0:T(8,128)(2,1)S(1)}, bf16[4,9,96,128]{3,2,1,0:T(8,128)(2,1)S(1)}, bf16[512,384]{1,0:T(8,128)(2,1)S(1)}, bf16[512,512]{1,0:T(8,128)(2,1)S(1)}) custom-call(s32[3]{0:T(128)S(1)} %pad_add_fusion.place, f32[512,256]{1,0:T(8,128)S(1)} %get-tuple-element.85.d_donor, f32[512,256]{1,0:T(8,128)S(1)} %get-tuple-element.86.d_accept, ...), custom_call_target="tpu_custom_call" | custom-call | flops 4000000000 | bytes 1000000 | tf_op jit(solution)/shard_map/pallas_call | solution.py:527
  88.5 4.9 %collective-permute-start.12 = (bf16[4,9,96,128]{3,2,1,0:T(8,128)(2,1)S(1)}, bf16[4,9,96,128]{3,2,1,0:T(8,128)(2,1)S(1)}, u32[]{:S(2)}, u32[]{:S(2)}) collective-permute-start(bf16[4,9,96,128]{3,2,1,0:T(8,128)(2,1)S(1)} %get-tuple-element.104), channel_id=1, source_target_pairs={{0,1},{1,0},{2,3},{3,2},{4,5},{5,4},{6,7},{7,6},{8,9},{9,8},{10,11... | collective-permute-start | bytes 2654216 | tf_op jit(solution)/shard_map/ppermute | solution.py:534
  96.2 23.3 %collective-permute-start.10 = (bf16[2,4,304,128]{3,2,1,0:T(8,128)(2,1)S(1)}, bf16[2,4,304,128]{3,2,1,0:T(8,128)(2,1)S(1)}, u32[]{:S(2)}, u32[]{:S(2)}) collective-permute-start(bf16[2,4,304,128]{3,2,1,0:T(8,128)(2,1)S(1)} %slice.90), channel_id=1, source_target_pairs={{0,128},{128,0},{256,384},{384,256},{1,129},{129,1},{257,385},{385... | collective-permute-start | bytes 1867784 | tf_op jit(solution)/shard_map/ppermute | solution.py:546
  119.6 4.9 %collective-permute-start.13 = (bf16[2,9,96,128]{3,2,1,0:T(8,128)(2,1)S(1)}, bf16[2,9,96,128]{3,2,1,0:T(8,128)(2,1)S(1)}, u32[]{:S(2)}, u32[]{:S(2)}) collective-permute-start(bf16[2,9,96,128]{3,2,1,0:T(8,128)(2,1)S(1)} %get-tuple-element.106), channel_id=1, source_target_pairs={{128,256},{256,128},{384,0},{0,384},{129,257},{257,129},{385,1},{1... | collective-permute-start | bytes 1327112 | tf_op jit(solution)/shard_map/ppermute | solution.py:550
  124.6 9.2 %collective-permute-done.10.received = bf16[2,4,304,128]{3,2,1,0:T(8,128)(2,1)S(1)} collective-permute-done((bf16[2,4,304,128]{3,2,1,0:T(8,128)(2,1)S(1)}, bf16[2,4,304,128]{3,2,1,0:T(8,128)(2,1)S(1)}, u32[]{:S(2)}, u32[]{:S(2)}) %collective-permute-start.10) | collective-permute-done | bytes 622624 | tf_op jit(solution)/shard_map/ppermute | solution.py:546
  134.0 4.9 %collective-permute-start.11 = (bf16[4,304,128]{2,1,0:T(8,128)(2,1)S(1)}, bf16[4,304,128]{2,1,0:T(8,128)(2,1)S(1)}, u32[]{:S(2)}, u32[]{:S(2)}) collective-permute-start(bf16[4,304,128]{2,1,0:T(8,128)(2,1)S(1)} %get-tuple-element.102), channel_id=1, source_target_pairs={{128,256},{256,128},{384,0},{0,384},{129,257},{257,129},{385,1},{1... | collective-permute-start | bytes 933896 | tf_op jit(solution)/shard_map/ppermute | solution.py:555
  141.6 4.5 %collective-permute-done.11.head_in = bf16[4,304,128]{2,1,0:T(8,128)(2,1)S(1)} collective-permute-done((bf16[4,304,128]{2,1,0:T(8,128)(2,1)S(1)}, bf16[4,304,128]{2,1,0:T(8,128)(2,1)S(1)}, u32[]{:S(2)}, u32[]{:S(2)}) %collective-permute-start.11) | collective-permute-done | bytes 311328 | tf_op jit(solution)/shard_map/ppermute | solution.py:555
  147.1 16.3 %all_to_all.15.parts = bf16[4,528,128]{2,1,0:T(8,128)(2,1)S(1)} all-to-all(bf16[4,528,128]{2,1,0:T(8,128)(2,1)S(1)} %shard_map.167), channel_id=1, replica_groups=mesh['y'=4,'zb'=2,'zq'=4,'zhi'=2,'x'=4,'core'=2] {'zq'}, dimensions={0} | all-to-all | bytes 1081344 | tf_op jit(solution)/shard_map/all_to_all | solution.py:423
  164.1 5.5 %collective-permute-start.15 = (bf16[416,128]{1,0:T(8,128)(2,1)S(1)}, bf16[416,128]{1,0:T(8,128)(2,1)S(1)}, u32[]{:S(2)}, u32[]{:S(2)}) collective-permute-start(bf16[416,128]{1,0:T(8,128)(2,1)S(1)} %get-tuple-element.109.sent), channel_id=1, source_target_pairs={{0,64},{64,0},{1,65},{65,1},{2,66},{66,2},{3,67},{67,3},{4,68},{68... | collective-permute-start | bytes 319496 | tf_op jit(solution)/shard_map/ppermute | solution.py:567
  169.7 11.6 %collective-permute-done.15.received = bf16[416,128]{1,0:T(8,128)(2,1)S(1)} collective-permute-done((bf16[416,128]{1,0:T(8,128)(2,1)S(1)}, bf16[416,128]{1,0:T(8,128)(2,1)S(1)}, u32[]{:S(2)}, u32[]{:S(2)}) %collective-permute-start.15) | collective-permute-done | bytes 106528 | tf_op jit(solution)/shard_map/ppermute | solution.py:567
  182.0 3.5 %all-to-all-start.1 = ((bf16[4,304,128]{2,1,0:T(8,128)(2,1)}), bf16[4,304,128]{2,1,0:T(8,128)(2,1)S(1)}, u32[]{:S(2)}, u32[]{:S(2)}) async-start(bf16[4,304,128]{2,1,0:T(8,128)(2,1)} %get-tuple-element.111), calls=%async_computation.1 | async-start | bytes 622592 | tf_op jit(solution)/shard_map/all_to_all | solution.py:423
  185.5 5.7 %collective-permute-start.18 = (bf16[112,128]{1,0:T(8,128)(2,1)S(1)}, bf16[112,128]{1,0:T(8,128)(2,1)S(1)}, u32[]{:S(2)}, u32[]{:S(2)}) collective-permute-start(bf16[112,128]{1,0:T(8,128)(2,1)S(1)} %get-tuple-element.112.own), channel_id=1, source_target_pairs={{0,6},{2,0},{4,2},{6,4},{1,7},{3,1},{5,3},{7,5},{8,14},{10,8},{12,... | collective-permute-start | bytes 86024 | tf_op jit(solution)/shard_map/ppermute | solution.py:575
  199.7 14.7 %all-to-all-start.2 = ((bf16[4,112,128]{2,1,0:T(8,128)(2,1)}), bf16[4,112,128]{2,1,0:T(8,128)(2,1)S(1)}, u32[]{:S(2)}, u32[]{:S(2)}) async-start(bf16[4,112,128]{2,1,0:T(8,128)(2,1)} %shard_map.170), calls=%async_computation.2 | async-start | bytes 229376 | tf_op jit(solution)/shard_map/all_to_all | solution.py:423
  214.4 3.4 %collective-permute-start.20 = (bf16[1216,128]{1,0:T(8,128)(2,1)S(1)}, bf16[1216,128]{1,0:T(8,128)(2,1)S(1)}, u32[]{:S(2)}, u32[]{:S(2)}) collective-permute-start(bf16[1216,128]{1,0:T(8,128)(2,1)S(1)} %bitcast.21), channel_id=1, source_target_pairs={{128,0},{256,128},{384,256},{0,384},{129,1},{257,129},{385,257},{1... | collective-permute-start | bytes 933896 | tf_op jit(solution)/shard_map/ppermute | solution.py:582
  219.7 5.6 %collective-permute-done.20.ahead = bf16[1216,128]{1,0:T(8,128)(2,1)S(1)} collective-permute-done((bf16[1216,128]{1,0:T(8,128)(2,1)S(1)}, bf16[1216,128]{1,0:T(8,128)(2,1)S(1)}, u32[]{:S(2)}, u32[]{:S(2)}) %collective-permute-start.20) | collective-permute-done | bytes 311328 | tf_op jit(solution)/shard_map/ppermute | solution.py:582
  225.3 4.6 %collective-permute-start.22 = (bf16[608,128]{1,0:T(8,128)(2,1)S(1)}, bf16[608,128]{1,0:T(8,128)(2,1)S(1)}, u32[]{:S(2)}, u32[]{:S(2)}) collective-permute-start(bf16[608,128]{1,0:T(8,128)(2,1)S(1)} %slice.96), channel_id=1, source_target_pairs={{128,0},{256,128},{384,256},{0,384},{129,1},{257,129},{385,257},{1... | collective-permute-start | bytes 466952 | tf_op jit(solution)/shard_map/ppermute | solution.py:584
  232.7 4.7 %collective-permute-done.21.low = bf16[608,128]{1,0:T(8,128)(2,1)S(1)} collective-permute-done((bf16[608,128]{1,0:T(8,128)(2,1)S(1)}, bf16[608,128]{1,0:T(8,128)(2,1)S(1)}, u32[]{:S(2)}, u32[]{:S(2)}) %collective-permute-start.21) | collective-permute-done | bytes 155680 | tf_op jit(solution)/shard_map/ppermute | solution.py:583
  (123 shorter events, 57.4 us)
Async XLA Ops:
  2.4 14.6 %collective-permute-start.1 = (bf16[128,768]{1,0:T(8,128)(2,1)}, bf16[128,768]{1,0:T(8,128)(2,1)S(1)}, u32[]{:S(2)}, u32[]{:S(2)}) collective-permute-start(bf16[128,768]{1,0:T(8,128)(2,1)} %get-tuple-element.120), channel_id=1, source_target_pairs={{16,32},{48,64},{80,96},{112,128},{144,160},{176,192},{208,224},{2... | collective-permute-start | bytes 589832 | tf_op jit(solution)/shard_map/ppermute | solution.py:419
  3.1 14.0 %collective-permute-start = (bf16[128,768]{1,0:T(8,128)(2,1)}, bf16[128,768]{1,0:T(8,128)(2,1)}, u32[]{:S(2)}, u32[]{:S(2)}) collective-permute-start(bf16[128,768]{1,0:T(8,128)(2,1)} %get-tuple-element.121), channel_id=1, source_target_pairs={{0,16},{32,48},{64,80},{96,112},{128,144},{160,176},{192,208},{224... | collective-permute-start | bytes 589832 | tf_op jit(solution)/shard_map/ppermute | solution.py:419
  21.3 8.5 %collective-permute-start.6 = (bf16[528,256]{1,0:T(8,128)(2,1)}, bf16[528,256]{1,0:T(8,128)(2,1)S(1)}, u32[]{:S(2)}, u32[]{:S(2)}) collective-permute-start(bf16[528,256]{1,0:T(8,128)(2,1)} %get-tuple-element.65.refs_3_.refs_4_), channel_id=1, source_target_pairs={{0,16},{32,48},{64,80},{96,112},{128,144},{160,176},{192,208},{224... | collective-permute-start | bytes 811016 | tf_op jit(solution)/shard_map/ppermute | solution.py:419
  29.8 21.5 %collective-permute-start.7 = (bf16[528,256]{1,0:T(8,128)(2,1)S(1)}, bf16[528,256]{1,0:T(8,128)(2,1)S(1)}, u32[]{:S(2)}, u32[]{:S(2)}) collective-permute-start(bf16[528,256]{1,0:T(8,128)(2,1)S(1)} %collective-permute-done.6.refs_6_), channel_id=1, source_target_pairs={{16,32},{48,64},{80,96},{112,128},{144,160},{176,192},{208,224},{2... | collective-permute-start | bytes 811016 | tf_op jit(solution)/shard_map/ppermute | solution.py:419
  30.5 22.8 %collective-permute-start.3 = (bf16[528,256]{1,0:T(8,128)(2,1)S(1)}, bf16[528,256]{1,0:T(8,128)(2,1)S(1)}, u32[]{:S(2)}, u32[]{:S(2)}) collective-permute-start(bf16[528,256]{1,0:T(8,128)(2,1)S(1)} %collective-permute-done.2.refs_5_), channel_id=1, source_target_pairs={{0,16},{32,48},{64,80},{96,112},{128,144},{160,176},{192,208},{224... | collective-permute-start | bytes 811016 | tf_op jit(solution)/shard_map/ppermute | solution.py:419
  51.4 14.9 %collective-permute-start.8 = (bf16[528,256]{1,0:T(8,128)(2,1)S(1)}, bf16[528,256]{1,0:T(8,128)(2,1)S(1)}, u32[]{:S(2)}, u32[]{:S(2)}) collective-permute-start(bf16[528,256]{1,0:T(8,128)(2,1)S(1)} %collective-permute-done.7.refs_5_), channel_id=1, source_target_pairs={{0,16},{32,48},{64,80},{96,112},{128,144},{160,176},{192,208},{224... | collective-permute-start | bytes 811016 | tf_op jit(solution)/shard_map/ppermute | solution.py:419
  53.3 13.7 %collective-permute-start.4 = (bf16[528,256]{1,0:T(8,128)(2,1)S(1)}, bf16[528,256]{1,0:T(8,128)(2,1)S(1)}, u32[]{:S(2)}, u32[]{:S(2)}) collective-permute-start(bf16[528,256]{1,0:T(8,128)(2,1)S(1)} %collective-permute-done.3.refs_6_), channel_id=1, source_target_pairs={{16,32},{48,64},{80,96},{112,128},{144,160},{176,192},{208,224},{2... | collective-permute-start | bytes 811016 | tf_op jit(solution)/shard_map/ppermute | solution.py:419
  66.3 13.4 %collective-permute-start.9 = (bf16[528,256]{1,0:T(8,128)(2,1)S(1)}, bf16[528,256]{1,0:T(8,128)(2,1)S(1)}, u32[]{:S(2)}, u32[]{:S(2)}) collective-permute-start(bf16[528,256]{1,0:T(8,128)(2,1)S(1)} %collective-permute-done.8.refs_6_), channel_id=1, source_target_pairs={{16,32},{48,64},{80,96},{112,128},{144,160},{176,192},{208,224},{2... | collective-permute-start | bytes 811016 | tf_op jit(solution)/shard_map/ppermute | solution.py:419
  67.0 12.8 %collective-permute-start.5 = (bf16[528,256]{1,0:T(8,128)(2,1)S(1)}, bf16[528,256]{1,0:T(8,128)(2,1)S(1)}, u32[]{:S(2)}, u32[]{:S(2)}) collective-permute-start(bf16[528,256]{1,0:T(8,128)(2,1)S(1)} %collective-permute-done.4.refs_5_), channel_id=1, source_target_pairs={{0,16},{32,48},{64,80},{96,112},{128,144},{160,176},{192,208},{224... | collective-permute-start | bytes 811016 | tf_op jit(solution)/shard_map/ppermute | solution.py:419
  88.5 30.9 %collective-permute-start.12 = (bf16[4,9,96,128]{3,2,1,0:T(8,128)(2,1)S(1)}, bf16[4,9,96,128]{3,2,1,0:T(8,128)(2,1)S(1)}, u32[]{:S(2)}, u32[]{:S(2)}) collective-permute-start(bf16[4,9,96,128]{3,2,1,0:T(8,128)(2,1)S(1)} %get-tuple-element.104), channel_id=1, source_target_pairs={{0,1},{1,0},{2,3},{3,2},{4,5},{5,4},{6,7},{7,6},{8,9},{9,8},{10,11... | collective-permute-start | bytes 2654216 | tf_op jit(solution)/shard_map/ppermute | solution.py:534
  96.2 37.7 %collective-permute-start.10 = (bf16[2,4,304,128]{3,2,1,0:T(8,128)(2,1)S(1)}, bf16[2,4,304,128]{3,2,1,0:T(8,128)(2,1)S(1)}, u32[]{:S(2)}, u32[]{:S(2)}) collective-permute-start(bf16[2,4,304,128]{3,2,1,0:T(8,128)(2,1)S(1)} %slice.90), channel_id=1, source_target_pairs={{0,128},{128,0},{256,384},{384,256},{1,129},{129,1},{257,385},{385... | collective-permute-start | bytes 1867784 | tf_op jit(solution)/shard_map/ppermute | solution.py:546
  119.6 19.3 %collective-permute-start.13 = (bf16[2,9,96,128]{3,2,1,0:T(8,128)(2,1)S(1)}, bf16[2,9,96,128]{3,2,1,0:T(8,128)(2,1)S(1)}, u32[]{:S(2)}, u32[]{:S(2)}) collective-permute-start(bf16[2,9,96,128]{3,2,1,0:T(8,128)(2,1)S(1)} %get-tuple-element.106), channel_id=1, source_target_pairs={{128,256},{256,128},{384,0},{0,384},{129,257},{257,129},{385,1},{1... | collective-permute-start | bytes 1327112 | tf_op jit(solution)/shard_map/ppermute | solution.py:550
  134.0 12.1 %collective-permute-start.11 = (bf16[4,304,128]{2,1,0:T(8,128)(2,1)S(1)}, bf16[4,304,128]{2,1,0:T(8,128)(2,1)S(1)}, u32[]{:S(2)}, u32[]{:S(2)}) collective-permute-start(bf16[4,304,128]{2,1,0:T(8,128)(2,1)S(1)} %get-tuple-element.102), channel_id=1, source_target_pairs={{128,256},{256,128},{384,0},{0,384},{129,257},{257,129},{385,1},{1... | collective-permute-start | bytes 933896 | tf_op jit(solution)/shard_map/ppermute | solution.py:555
  139.0 8.0 %collective-permute-start.14 = (bf16[9,96,128]{2,1,0:T(8,128)(2,1)S(1)}, bf16[9,96,128]{2,1,0:T(8,128)(2,1)S(1)}, u32[]{:S(2)}, u32[]{:S(2)}) collective-permute-start(bf16[9,96,128]{2,1,0:T(8,128)(2,1)S(1)} %get-tuple-element.108), channel_id=1, source_target_pairs={{0,128},{128,0},{256,384},{384,256},{1,129},{129,1},{257,385},{385... | collective-permute-start | bytes 663560 | tf_op jit(solution)/shard_map/ppermute | solution.py:556
  164.1 17.2 %collective-permute-start.15 = (bf16[416,128]{1,0:T(8,128)(2,1)S(1)}, bf16[416,128]{1,0:T(8,128)(2,1)S(1)}, u32[]{:S(2)}, u32[]{:S(2)}) collective-permute-start(bf16[416,128]{1,0:T(8,128)(2,1)S(1)} %get-tuple-element.109.sent), channel_id=1, source_target_pairs={{0,64},{64,0},{1,65},{65,1},{2,66},{66,2},{3,67},{67,3},{4,68},{68... | collective-permute-start | bytes 319496 | tf_op jit(solution)/shard_map/ppermute | solution.py:567
  182.0 17.7 %all-to-all-start.1 = ((bf16[4,304,128]{2,1,0:T(8,128)(2,1)}), bf16[4,304,128]{2,1,0:T(8,128)(2,1)S(1)}, u32[]{:S(2)}, u32[]{:S(2)}) async-start(bf16[4,304,128]{2,1,0:T(8,128)(2,1)} %get-tuple-element.111), calls=%async_computation.1 | async-start | bytes 622592 | tf_op jit(solution)/shard_map/all_to_all | solution.py:423
  185.5 10.1 %collective-permute-start.18 = (bf16[112,128]{1,0:T(8,128)(2,1)S(1)}, bf16[112,128]{1,0:T(8,128)(2,1)S(1)}, u32[]{:S(2)}, u32[]{:S(2)}) collective-permute-start(bf16[112,128]{1,0:T(8,128)(2,1)S(1)} %get-tuple-element.112.own), channel_id=1, source_target_pairs={{0,6},{2,0},{4,2},{6,4},{1,7},{3,1},{5,3},{7,5},{8,14},{10,8},{12,... | collective-permute-start | bytes 86024 | tf_op jit(solution)/shard_map/ppermute | solution.py:575
  191.2 6.1 %collective-permute-start.17 = (bf16[112,128]{1,0:T(8,128)(2,1)S(1)}, bf16[112,128]{1,0:T(8,128)(2,1)S(1)}, u32[]{:S(2)}, u32[]{:S(2)}) collective-permute-start(bf16[112,128]{1,0:T(8,128)(2,1)S(1)} %get-tuple-element.112.own), channel_id=1, source_target_pairs={{0,4},{2,6},{4,0},{6,2},{1,5},{3,7},{5,1},{7,3},{8,12},{10,14},{12... | collective-permute-start | bytes 86024 | tf_op jit(solution)/shard_map/ppermute | solution.py:575
  193.1 5.9 %collective-permute-start.16 = (bf16[112,128]{1,0:T(8,128)(2,1)S(1)}, bf16[112,128]{1,0:T(8,128)(2,1)S(1)}, u32[]{:S(2)}, u32[]{:S(2)}) collective-permute-start(bf16[112,128]{1,0:T(8,128)(2,1)S(1)} %get-tuple-element.112.own), channel_id=1, source_target_pairs={{0,2},{2,4},{4,6},{6,0},{1,3},{3,5},{5,7},{7,1},{8,10},{10,12},{12... | collective-permute-start | bytes 86024 | tf_op jit(solution)/shard_map/ppermute | solution.py:575
  199.7 32.1 %all-to-all-start.2 = ((bf16[4,112,128]{2,1,0:T(8,128)(2,1)}), bf16[4,112,128]{2,1,0:T(8,128)(2,1)S(1)}, u32[]{:S(2)}, u32[]{:S(2)}) async-start(bf16[4,112,128]{2,1,0:T(8,128)(2,1)} %shard_map.170), calls=%async_computation.2 | async-start | bytes 229376 | tf_op jit(solution)/shard_map/all_to_all | solution.py:423
  214.4 10.9 %collective-permute-start.20 = (bf16[1216,128]{1,0:T(8,128)(2,1)S(1)}, bf16[1216,128]{1,0:T(8,128)(2,1)S(1)}, u32[]{:S(2)}, u32[]{:S(2)}) collective-permute-start(bf16[1216,128]{1,0:T(8,128)(2,1)S(1)} %bitcast.21), channel_id=1, source_target_pairs={{128,0},{256,128},{384,256},{0,384},{129,1},{257,129},{385,257},{1... | collective-permute-start | bytes 933896 | tf_op jit(solution)/shard_map/ppermute | solution.py:582
  217.8 12.1 %collective-permute-start.19 = (bf16[1216,128]{1,0:T(8,128)(2,1)S(1)}, bf16[1216,128]{1,0:T(8,128)(2,1)S(1)}, u32[]{:S(2)}, u32[]{:S(2)}) collective-permute-start(bf16[1216,128]{1,0:T(8,128)(2,1)S(1)} %bitcast.22), channel_id=1, source_target_pairs={{0,128},{128,256},{256,384},{384,0},{1,129},{129,257},{257,385},{3... | collective-permute-start | bytes 933896 | tf_op jit(solution)/shard_map/ppermute | solution.py:581
  225.3 7.4 %collective-permute-start.22 = (bf16[608,128]{1,0:T(8,128)(2,1)S(1)}, bf16[608,128]{1,0:T(8,128)(2,1)S(1)}, u32[]{:S(2)}, u32[]{:S(2)}) collective-permute-start(bf16[608,128]{1,0:T(8,128)(2,1)S(1)} %slice.96), channel_id=1, source_target_pairs={{128,0},{256,128},{384,256},{0,384},{129,1},{257,129},{385,257},{1... | collective-permute-start | bytes 466952 | tf_op jit(solution)/shard_map/ppermute | solution.py:584
  229.9 7.6 %collective-permute-start.21 = (bf16[608,128]{1,0:T(8,128)(2,1)S(1)}, bf16[608,128]{1,0:T(8,128)(2,1)S(1)}, u32[]{:S(2)}, u32[]{:S(2)}) collective-permute-start(bf16[608,128]{1,0:T(8,128)(2,1)S(1)} %slice.95), channel_id=1, source_target_pairs={{0,128},{128,256},{256,384},{384,0},{1,129},{129,257},{257,385},{3... | collective-permute-start | bytes 466952 | tf_op jit(solution)/shard_map/ppermute | solution.py:583
  (27 other events, 183.5 us)

commit v6 on v4

--- a/solution.py
+++ b/solution.py
@@ -76,7 +76,7 @@
 
 def forward_kernel(
     odd, tok, mine, even_edge, odd_edge, gain, taps, point, donor_w, accept_w, meta,
-    hidden, conv_out, act_out, embed_out, even_feat, odd_feat,
+    hidden, conv_out, act_out, embed_out, even_feat, odd_feat, wide_feat,
 ):
     rows = tok.shape[0]
     is_odd = odd[0] > 0
@@ -99,8 +99,10 @@
     accept = dot(embed, accept_w[...]).astype(BF16)
     even_feat[:rows, :] = jnp.where(is_odd, donor, accept)
     odd_feat[:rows, :] = jnp.where(is_odd, accept, donor)
+    wide_feat[:rows, :] = jnp.where(odd[1] < 4, accept, donor)
     even_feat[pl.ds(rows, SLOTS), :] = meta[...]
     odd_feat[pl.ds(rows, SLOTS), :] = meta[...]
+    wide_feat[pl.ds(rows, SLOTS), :] = meta[...]
 
 
 def side_kernel(
@@ -390,9 +392,9 @@
             loss[...] = value
 
 
-def swapped(block, first):
+def swapped(block, first, between_lines=True):
     count = lax.axis_size(SEQ)
-    pairs = [(i, i + 1) for i in range(first, count - 1, 2)]
+    pairs = [(i, i + 1) for i in range(first, count - 1, 2) if between_lines or i % 8 < 7]
     return lax.ppermute(block, SEQ, pairs + [(j, i) for i, j in pairs])
 
 
@@ -411,7 +413,8 @@
     blocks = rows // PANEL
     shape = jax.ShapeDtypeStruct
     here = lax.axis_index(SEQ)
-    odd = (here % 2).astype(jnp.int32)[None]
+    line = here % 8
+    odd = jnp.stack([here % 2, line]).astype(jnp.int32)
     is_odd = odd[0] > 0
     start, end = tokens[:STEP], tokens[rows - STEP :]
     even_edge = swapped(jnp.where(is_odd, start, end), 0)
@@ -437,13 +440,14 @@
         own_kernel, [shape((rows, channels), BF16)] * 2, [VM] * 2, 12, 2_000_000_000
     )(tokens, gain)
     feat = shape((rows + SLOTS, heads), BF16)
-    hidden, conv, act, embed, even_feat, odd_feat = call(
+    hidden, conv, act, embed, even_feat, odd_feat, wide_feat = call(
         forward_kernel,
         [
             shape((rows + 2 * STEP, channels), BF16),
             shape((rows, inner), F32),
             shape((rows, inner), BF16),
             shape((rows, channels), BF16),
+            feat,
             feat,
             feat,
         ],
@@ -458,7 +462,7 @@
     acc_shapes = [shape((rows, heads), F32), shape((rows, heads), F32), shape((PANEL, PANEL), F32)]
     acc = call(
         lambda *refs: pair_kernel(0, *refs), acc_shapes, [SM] * 2 + [VM] * 2, 12, 2_000_000_000
-    )(1 - odd, meta, even_feat, odd_feat)
+    )(1 - odd[:1], meta, even_feat, odd_feat)
     edge_factor, slope, hidden_t, act_t, embed_t = call(
         side_kernel,
         [
@@ -472,20 +476,35 @@
         20,
         6_000_000_000,
     )(odd, even_edge, odd_edge, gain, hidden, conv, act, embed, order, eye)
-    even_far, odd_far = even_feat, odd_feat
+    count = lax.axis_size(SEQ)
+    starts = range(0, count, 8)
+    wide_pairs = [(i + k, i - 4 + k) for i in starts if i > 0 for k in (2, 3)]
+    wide_pairs += [(i + k, i + 4 + k) for i in starts if i + 8 < count for k in (4, 5)]
+    relay_pairs = [(i + 6, i + 7) for i in starts] + [(i + 1, i) for i in starts]
+    wide = lax.ppermute(wide_feat, SEQ, wide_pairs)
+    relay = lax.ppermute(wide, SEQ, relay_pairs)
+    at_end = (line == 0) | (line == 7)
+    near_end = (line == 1) | (line == 6)
+    short_far, long_far = odd_feat, even_feat
     for distance in range(1, SPAN + 1):
         if distance == 1:
-            odd_far, even_far = swapped(odd_feat, 0), swapped(even_feat, 1)
+            short_far, long_far = swapped(odd_feat, 0), swapped(even_feat, 1)
         else:
-            odd_far, even_far = swapped(even_far, 0), swapped(odd_far, 1)
-        far_meta = jnp.where(is_odd, odd_far[rows:, :8], even_far[rows:, :8]).astype(jnp.int32)
+            short_far, long_far = swapped(long_far, 0), swapped(short_far, 1, distance <= 2)
+        short_use, long_use = short_far, long_far
+        if distance == 3:
+            long_use = jnp.where(at_end, relay, long_far)
+        if distance == 4:
+            short_use = jnp.where(near_end, wide, short_far)
+            long_use = jnp.where(at_end, wide, long_far)
+        far_meta = jnp.where(odd[0] > 0, short_use[rows:, :8], long_use[rows:, :8]).astype(jnp.int32)
         acc = call(
             lambda *refs, distance=distance: pair_kernel(distance, *refs),
             acc_shapes,
             [SM] * 3 + [VM] * 7,
             12,
             2_500_000_000,
-        )(1 - odd, meta, far_meta, even_feat, odd_feat, even_far, odd_far, *acc)
+        )(1 - odd[:1], meta, far_meta, even_feat, odd_feat, long_use, short_use, *acc)
 
     chunk = CHUNK_ROWS + EXTRA_ROWS
     lanes = inner // 128

time: 230 us -> 225 us (0.978)
  waiting for transfers between devices: 55.4 us -> 37.7 us
  starting transfers between devices: 122 us -> 133 us
    ppermute x10, starting transfers between devices: 37.7 us -> 49.9 us  [swapped(): return lax.ppermute(block, SEQ, pairs + [(j, i) for i, j in pairs])]
    ppermute x1, starting transfers between devices: 20.6 us -> 8.68 us  [on_device(): other = lax.ppermute(head_sum[2:], 'y', first_pairs)]
    ppermute x10, waiting for transfers between devices: 21.8 us -> 11.3 us  [swapped(): return lax.ppermute(block, SEQ, pairs + [(j, i) for i, j in pairs])]
    ppermute x1, waiting for transfers between devices: 4.38 us -> 0.22 us  [on_device(): low = lax.ppermute(behind[:head_rows // 2], 'y', around)]
    ppermute x1, starting transfers between devices: 4.1 us -> 6.83 us  [on_device(): received = lax.ppermute(send, 'core', [(0, 1), (1, 0)])]
    ppermute x1, waiting for transfers between devices: 10.2 us -> 7.92 us  [on_device(): other = lax.ppermute(head_sum[2:], 'y', first_pairs)]
  transfers between devices with their start and end apart: 27 -> 29, of which waited for: 10 -> 10; matrix products, arithmetic and copies ran while one was open for 1% -> 1% of each run, Pallas kernels for 7% -> 8%
where the time goes in v6:
time: 225 us; the launch traced here: 222 us
  starting transfers between devices  133 us (59%)
  waiting for transfers between devices  37.7 us (17%)
  Pallas kernels  30.2 us (13%)
  blocking collectives  16.2 us (7%)
    ppermute x10, starting transfers between devices, swapped(): return lax.ppermute(block, SEQ, pairs + [(j, i) for i, j in pairs])  49.9 us
    all_to_all x1, blocking collectives, swap_parts(): return lax.all_to_all(parts, axis, 0, 0, tiled=True)  16.2 us
    ppermute x10, waiting for transfers between devices, swapped(): return lax.ppermute(block, SEQ, pairs + [(j, i) for i, j in pairs])  11.3 us
    ppermute x3, starting transfers between devices, on_device(): lax.ppermute(conv_sum, 'x', [(i, (i + step) % 4) for i in range(4)])  10.6 us
    ppermute x1, waiting for transfers between devices, on_device(): across = lax.ppermute(mine, 'zhi', [(0, 1), (1, 0)])  8.89 us
    ppermute x1, starting transfers between devices, on_device(): other = lax.ppermute(head_sum[2:], 'y', first_pairs)  8.68 us
    ppermute x1, waiting for transfers between devices, on_device(): other = lax.ppermute(head_sum[2:], 'y', first_pairs)  7.92 us
    ppermute x1, starting transfers between devices, on_device(): lax.ppermute(sent[chunk:], ('zb', 'zhi'), [(0, 3), (3, 0), (1, 2), (2, 1)])  7.35 us
  transfers between devices with their start and end apart: 29, of which 10 were waited for; matrix products, arithmetic and copies ran while one was open for 1% of the time, Pallas kernels for 8%

profile of v6, /device:TPU:1, one launch (start us, length us, event | category | flops | bytes accessed | tf_op | source)
XLA Modules:
  0.0 222.2 jit_solution(2426323167735334303)
XLA Ops:
  2.5 4.4 %collective-permute-start = (bf16[128,768]{1,0:T(8,128)(2,1)}, bf16[128,768]{1,0:T(8,128)(2,1)S(1)}, u32[]{:S(2)}, u32[]{:S(2)}) collective-permute-start(bf16[128,768]{1,0:T(8,128)(2,1)} %get-tuple-element.107), channel_id=1, source_target_pairs={{0,16},{32,48},{64,80},{96,112},{128,144},{160,176},{192,208},{224... | collective-permute-start | bytes 589832 | tf_op jit(solution)/shard_map/ppermute | solution.py:398
  11.2 3.0 %shard_map.155 = (bf16[768,768]{1,0:T(8,128)(2,1)S(1)}, f32[512,384]{1,0:T(8,128)S(1)}, bf16[512,384]{1,0:T(8,128)(2,1)S(1)}, bf16[512,768]{1,0:T(8,128)(2,1)S(1...) custom-call(s32[2]{0:T(128)S(1)} %pad_add_fusion.1.odd, ...), custom_call_target="tpu_custom_call" | custom-call | flops 4000000000 | bytes 1000000 | tf_op jit(solution)/shard_map/pallas_call | solution.py:443
  14.8 8.5 %collective-permute-start.7 = (bf16[528,256]{1,0:T(8,128)(2,1)S(1)}, bf16[528,256]{1,0:T(8,128)(2,1)S(1)}, u32[]{:S(2)}, u32[]{:S(2)}) collective-permute-start(bf16[528,256]{1,0:T(8,128)(2,1)S(1)} %get-tuple-element.59.refs_3_.refs_4_), channel_id=1, source_target_pairs={{0,16},{32,48},{64,80},{96,112},{128,144},{160,176},{192,208},{224... | collective-permute-start | bytes 811016 | tf_op jit(solution)/shard_map/ppermute | solution.py:398
  24.1 3.9 %shard_map.161 = (bf16[256,768]{1,0:T(8,128)(2,1)S(1)}, f32[512,384]{1,0:T(8,128)S(1)}, bf16[768,768]{1,0:T(8,128)(2,1)S(1)}, bf16[384,512]{1,0:T(8,128)(2,1)S(1)}, bf16[768,512]{1,0:T(8,128)(2,1)S(1)}) custom-call(s32[2]{0:T(128)S(1)} %pad_add_fusion.1.odd, bf16[128,768]{1,0:T(8,128)(2,1)S(1)} %collective-permute-done.even_edge, ...), custom_call_target="tpu_custom_call" | custom-call | flops 6000000000 | bytes 1000000 | tf_op jit(solution)/shard_map/pallas_call | solution.py:466
  38.5 29.3 %collective-permute-start.9 = (bf16[528,256]{1,0:T(8,128)(2,1)S(1)}, bf16[528,256]{1,0:T(8,128)(2,1)S(1)}, u32[]{:S(2)}, u32[]{:S(2)}) collective-permute-start(bf16[528,256]{1,0:T(8,128)(2,1)S(1)} %collective-permute-done.8.refs_5_), channel_id=1, source_target_pairs={{0,16},{32,48},{64,80},{96,112},{128,144},{160,176},{192,208},{224... | collective-permute-start | bytes 811016 | tf_op jit(solution)/shard_map/ppermute | solution.py:398
  69.5 7.3 %collective-permute-done.9.refs_6_ = bf16[528,256]{1,0:T(8,128)(2,1)S(1)} collective-permute-done((bf16[528,256]{1,0:T(8,128)(2,1)S(1)}, bf16[528,256]{1,0:T(8,128)(2,1)S(1)}, u32[]{:S(2)}, u32[]{:S(2)}) %collective-permute-start.9) | collective-permute-done | bytes 270368 | tf_op jit(solution)/shard_map/ppermute | solution.py:398
  86.4 4.1 %shard_map.162 = (bf16[4,9,96,128]{3,2,1,0:T(8,128)(2,1)S(1)}, bf16[4,9,96,128]{3,2,1,0:T(8,128)(2,1)S(1)}, bf16[512,384]{1,0:T(8,128)(2,1)S(1)}, bf16[512,512]{1,0:T(8,128)(2,1)S(1)}) custom-call(s32[3]{0:T(128)S(1)} %pad_add_fusion.place, f32[512,256]{1,0:T(8,128)S(1)} %get-tuple-element.72.d_donor, f32[512,256]{1,0:T(8,128)S(1)} %get-tuple-element.73.d_accept, ...), custom_call_target="tpu_custom_call" | custom-call | flops 4000000000 | bytes 1000000 | tf_op jit(solution)/shard_map/pallas_call | solution.py:515
  90.5 6.8 %collective-permute-start.14 = (bf16[4,9,96,128]{3,2,1,0:T(8,128)(2,1)S(1)}, bf16[4,9,96,128]{3,2,1,0:T(8,128)(2,1)S(1)}, u32[]{:S(2)}, u32[]{:S(2)}) collective-permute-start(bf16[4,9,96,128]{3,2,1,0:T(8,128)(2,1)S(1)} %get-tuple-element.90), channel_id=1, source_target_pairs={{0,1},{1,0},{2,3},{3,2},{4,5},{5,4},{6,7},{7,6},{8,9},{9,8},{10,11... | collective-permute-start | bytes 2654216 | tf_op jit(solution)/shard_map/ppermute | solution.py:522
  100.1 8.7 %collective-permute-start.12 = (bf16[2,4,304,128]{3,2,1,0:T(8,128)(2,1)S(1)}, bf16[2,4,304,128]{3,2,1,0:T(8,128)(2,1)S(1)}, u32[]{:S(2)}, u32[]{:S(2)}) collective-permute-start(bf16[2,4,304,128]{3,2,1,0:T(8,128)(2,1)S(1)} %slice.84), channel_id=1, source_target_pairs={{0,128},{128,0},{256,384},{384,256},{1,129},{129,1},{257,385},{385... | collective-permute-start | bytes 1867784 | tf_op jit(solution)/shard_map/ppermute | solution.py:534
  109.0 6.2 %collective-permute-start.15 = (bf16[2,9,96,128]{3,2,1,0:T(8,128)(2,1)S(1)}, bf16[2,9,96,128]{3,2,1,0:T(8,128)(2,1)S(1)}, u32[]{:S(2)}, u32[]{:S(2)}) collective-permute-start(bf16[2,9,96,128]{3,2,1,0:T(8,128)(2,1)S(1)} %get-tuple-element.92), channel_id=1, source_target_pairs={{128,256},{256,128},{384,0},{0,384},{129,257},{257,129},{385,1},{1... | collective-permute-start | bytes 1327112 | tf_op jit(solution)/shard_map/ppermute | solution.py:538
  115.3 7.9 %collective-permute-done.12.received = bf16[2,4,304,128]{3,2,1,0:T(8,128)(2,1)S(1)} collective-permute-done((bf16[2,4,304,128]{3,2,1,0:T(8,128)(2,1)S(1)}, bf16[2,4,304,128]{3,2,1,0:T(8,128)(2,1)S(1)}, u32[]{:S(2)}, u32[]{:S(2)}) %collective-permute-start.12) | collective-permute-done | bytes 622624 | tf_op jit(solution)/shard_map/ppermute | solution.py:534
  123.3 6.2 %collective-permute-start.13 = (bf16[4,304,128]{2,1,0:T(8,128)(2,1)S(1)}, bf16[4,304,128]{2,1,0:T(8,128)(2,1)S(1)}, u32[]{:S(2)}, u32[]{:S(2)}) collective-permute-start(bf16[4,304,128]{2,1,0:T(8,128)(2,1)S(1)} %get-tuple-element.88), channel_id=1, source_target_pairs={{128,256},{256,128},{384,0},{0,384},{129,257},{257,129},{385,1},{1... | collective-permute-start | bytes 933896 | tf_op jit(solution)/shard_map/ppermute | solution.py:543
  132.2 4.5 %collective-permute-done.13.head_in = bf16[4,304,128]{2,1,0:T(8,128)(2,1)S(1)} collective-permute-done((bf16[4,304,128]{2,1,0:T(8,128)(2,1)S(1)}, bf16[4,304,128]{2,1,0:T(8,128)(2,1)S(1)}, u32[]{:S(2)}, u32[]{:S(2)}) %collective-permute-start.13) | collective-permute-done | bytes 311328 | tf_op jit(solution)/shard_map/ppermute | solution.py:543
  137.7 16.2 %all_to_all.10.parts = bf16[4,528,128]{2,1,0:T(8,128)(2,1)S(1)} all-to-all(bf16[4,528,128]{2,1,0:T(8,128)(2,1)S(1)} %shard_map.167), channel_id=1, replica_groups=mesh['y'=4,'zb'=2,'zq'=4,'zhi'=2,'x'=4,'core'=2] {'zq'}, dimensions={0} | all-to-all | bytes 1081344 | tf_op jit(solution)/shard_map/all_to_all | solution.py:402
  154.6 4.4 %collective-permute-start.17 = (bf16[416,128]{1,0:T(8,128)(2,1)S(1)}, bf16[416,128]{1,0:T(8,128)(2,1)S(1)}, u32[]{:S(2)}, u32[]{:S(2)}) collective-permute-start(bf16[416,128]{1,0:T(8,128)(2,1)S(1)} %get-tuple-element.95.sent), channel_id=1, source_target_pairs={{0,64},{64,0},{1,65},{65,1},{2,66},{66,2},{3,67},{67,3},{4,68},{68... | collective-permute-start | bytes 319496 | tf_op jit(solution)/shard_map/ppermute | solution.py:555
  159.0 7.3 %collective-permute-start.19 = (bf16[112,128]{1,0:T(8,128)(2,1)S(1)}, bf16[112,128]{1,0:T(8,128)(2,1)S(1)}, u32[]{:S(2)}, u32[]{:S(2)}) collective-permute-start(bf16[112,128]{1,0:T(8,128)(2,1)S(1)} %slice.71), channel_id=1, source_target_pairs={{0,72},{72,0},{8,64},{64,8},{1,73},{73,1},{9,65},{65,9},{2,74},{74... | collective-permute-start | bytes 86024 | tf_op jit(solution)/shard_map/ppermute | solution.py:557
  166.4 4.5 %collective-permute-start.18 = (bf16[112,128]{1,0:T(8,128)(2,1)S(1)}, bf16[112,128]{1,0:T(8,128)(2,1)S(1)}, u32[]{:S(2)}, u32[]{:S(2)}) collective-permute-start(bf16[112,128]{1,0:T(8,128)(2,1)S(1)} %get-tuple-element.96.mine), channel_id=1, source_target_pairs={{0,8},{8,0},{1,9},{9,1},{2,10},{10,2},{3,11},{11,3},{4,12},{12,4},... | collective-permute-start | bytes 86024 | tf_op jit(solution)/shard_map/ppermute | solution.py:556
  170.9 8.9 %collective-permute-done.18.one = bf16[112,128]{1,0:T(8,128)(2,1)S(1)} collective-permute-done((bf16[112,128]{1,0:T(8,128)(2,1)S(1)}, bf16[112,128]{1,0:T(8,128)(2,1)S(1)}, u32[]{:S(2)}, u32[]{:S(2)}) %collective-permute-start.18) | collective-permute-done | bytes 28704 | tf_op jit(solution)/shard_map/ppermute | solution.py:556
  180.5 3.5 %all-to-all-start.1 = ((bf16[4,304,128]{2,1,0:T(8,128)(2,1)}), bf16[4,304,128]{2,1,0:T(8,128)(2,1)S(1)}, u32[]{:S(2)}, u32[]{:S(2)}) async-start(bf16[4,304,128]{2,1,0:T(8,128)(2,1)} %get-tuple-element.97), calls=%async_computation.1 | async-start | bytes 622592 | tf_op jit(solution)/shard_map/all_to_all | solution.py:402
  186.8 5.8 %collective-permute-start.21 = (bf16[112,128]{1,0:T(8,128)(2,1)S(1)}, bf16[112,128]{1,0:T(8,128)(2,1)S(1)}, u32[]{:S(2)}, u32[]{:S(2)}) collective-permute-start(bf16[112,128]{1,0:T(8,128)(2,1)S(1)} %get-tuple-element.98.own), channel_id=1, source_target_pairs={{0,4},{2,6},{4,0},{6,2},{1,5},{3,7},{5,1},{7,3},{8,12},{10,14},{12... | collective-permute-start | bytes 86024 | tf_op jit(solution)/shard_map/ppermute | solution.py:567
  194.6 3.0 %collective-permute-done.22.three = bf16[112,128]{1,0:T(8,128)(2,1)S(1)} collective-permute-done((bf16[112,128]{1,0:T(8,128)(2,1)S(1)}, bf16[112,128]{1,0:T(8,128)(2,1)S(1)}, u32[]{:S(2)}, u32[]{:S(2)}) %collective-permute-start.22) | collective-permute-done | bytes 28704 | tf_op jit(solution)/shard_map/ppermute | solution.py:567
  199.6 4.6 %collective-permute-start.25 = (bf16[1216,128]{1,0:T(8,128)(2,1)S(1)}, bf16[1216,128]{1,0:T(8,128)(2,1)S(1)}, u32[]{:S(2)}, u32[]{:S(2)}) collective-permute-start(bf16[1216,128]{1,0:T(8,128)(2,1)S(1)} %bitcast.27), channel_id=1, source_target_pairs={{128,0},{256,128},{384,256},{0,384},{129,1},{257,129},{385,257},{1... | collective-permute-start | bytes 933896 | tf_op jit(solution)/shard_map/ppermute | solution.py:575
  204.1 6.9 %collective-permute-start.23 = (f32[112,128]{1,0:T(8,128)S(1)}, f32[112,128]{1,0:T(8,128)S(1)}, u32[]{:S(2)}, u32[]{:S(2)}) collective-permute-start(f32[112,128]{1,0:T(8,128)S(1)} %shard_map.170), channel_id=1, source_target_pairs={{0,1},{1,0},{2,3},{3,2},{4,5},{5,4},{6,7},{7,6},{8,9},{9,8},{10,11... | collective-permute-start | bytes 172040 | tf_op jit(solution)/shard_map/ppermute | solution.py:571
  213.1 4.6 %collective-permute-start.27 = (bf16[608,128]{1,0:T(8,128)(2,1)S(1)}, bf16[608,128]{1,0:T(8,128)(2,1)S(1)}, u32[]{:S(2)}, u32[]{:S(2)}) collective-permute-start(bf16[608,128]{1,0:T(8,128)(2,1)S(1)} %slice.86), channel_id=1, source_target_pairs={{128,0},{256,128},{384,256},{0,384},{129,1},{257,129},{385,257},{1... | collective-permute-start | bytes 466952 | tf_op jit(solution)/shard_map/ppermute | solution.py:577
  (101 shorter events, 49.6 us)
Async XLA Ops:
  2.5 8.6 %collective-permute-start = (bf16[128,768]{1,0:T(8,128)(2,1)}, bf16[128,768]{1,0:T(8,128)(2,1)S(1)}, u32[]{:S(2)}, u32[]{:S(2)}) collective-permute-start(bf16[128,768]{1,0:T(8,128)(2,1)} %get-tuple-element.107), channel_id=1, source_target_pairs={{0,16},{32,48},{64,80},{96,112},{128,144},{160,176},{192,208},{224... | collective-permute-start | bytes 589832 | tf_op jit(solution)/shard_map/ppermute | solution.py:398
  14.2 16.5 %collective-permute-start.3 = (bf16[528,256]{1,0:T(8,128)(2,1)S(1)}, bf16[528,256]{1,0:T(8,128)(2,1)S(1)}, u32[]{:S(2)}, u32[]{:S(2)}) collective-permute-start(bf16[528,256]{1,0:T(8,128)(2,1)S(1)} %get-tuple-element.58.refs_2_.refs_3_), channel_id=1, source_target_pairs={{16,32},{48,64},{80,96},{112,128},{144,160},{176,192},{208,224},{2... | collective-permute-start | bytes 811016 | tf_op jit(solution)/shard_map/ppermute | solution.py:398
  14.8 17.7 %collective-permute-start.7 = (bf16[528,256]{1,0:T(8,128)(2,1)S(1)}, bf16[528,256]{1,0:T(8,128)(2,1)S(1)}, u32[]{:S(2)}, u32[]{:S(2)}) collective-permute-start(bf16[528,256]{1,0:T(8,128)(2,1)S(1)} %get-tuple-element.59.refs_3_.refs_4_), channel_id=1, source_target_pairs={{0,16},{32,48},{64,80},{96,112},{128,144},{160,176},{192,208},{224... | collective-permute-start | bytes 811016 | tf_op jit(solution)/shard_map/ppermute | solution.py:398
  23.4 9.9 %collective-permute-start.2 = (bf16[528,256]{1,0:T(8,128)(2,1)S(1)}, bf16[528,256]{1,0:T(8,128)(2,1)S(1)}, u32[]{:S(2)}, u32[]{:S(2)}) collective-permute-start(bf16[528,256]{1,0:T(8,128)(2,1)S(1)} %get-tuple-element.57), channel_id=1, source_target_pairs={{160,96},{176,112},{288,224},{304,240},{416,352},{432,368},{64,128... | collective-permute-start | bytes 811016 | tf_op jit(solution)/shard_map/ppermute | solution.py:484
  30.6 7.2 %collective-permute-start.4 = (bf16[528,256]{1,0:T(8,128)(2,1)S(1)}, bf16[528,256]{1,0:T(8,128)(2,1)S(1)}, u32[]{:S(2)}, u32[]{:S(2)}) collective-permute-start(bf16[528,256]{1,0:T(8,128)(2,1)S(1)} %collective-permute-done.3.refs_5_), channel_id=1, source_target_pairs={{0,16},{32,48},{64,80},{96,112},{128,144},{160,176},{192,208},{224... | collective-permute-start | bytes 811016 | tf_op jit(solution)/shard_map/ppermute | solution.py:398
  33.3 46.6 %collective-permute-start.11 = (bf16[528,256]{1,0:T(8,128)(2,1)S(1)}, bf16[528,256]{1,0:T(8,128)(2,1)S(1)}, u32[]{:S(2)}, u32[]{:S(2)}) collective-permute-start(bf16[528,256]{1,0:T(8,128)(2,1)S(1)} %collective-permute-done.2), channel_id=1, source_target_pairs={{96,112},{224,240},{352,368},{480,496},{16,0},{144,128},{272,256},... | collective-permute-start | bytes 811016 | tf_op jit(solution)/shard_map/ppermute | solution.py:485
  37.8 39.6 %collective-permute-start.5 = (bf16[528,256]{1,0:T(8,128)(2,1)S(1)}, bf16[528,256]{1,0:T(8,128)(2,1)S(1)}, u32[]{:S(2)}, u32[]{:S(2)}) collective-permute-start(bf16[528,256]{1,0:T(8,128)(2,1)S(1)} %collective-permute-done.4.refs_6_), channel_id=1, source_target_pairs={{16,32},{48,64},{80,96},{144,160},{176,192},{208,224},{272,288},{3... | collective-permute-start | bytes 811016 | tf_op jit(solution)/shard_map/ppermute | solution.py:398
  38.5 38.3 %collective-permute-start.9 = (bf16[528,256]{1,0:T(8,128)(2,1)S(1)}, bf16[528,256]{1,0:T(8,128)(2,1)S(1)}, u32[]{:S(2)}, u32[]{:S(2)}) collective-permute-start(bf16[528,256]{1,0:T(8,128)(2,1)S(1)} %collective-permute-done.8.refs_5_), channel_id=1, source_target_pairs={{0,16},{32,48},{64,80},{96,112},{128,144},{160,176},{192,208},{224... | collective-permute-start | bytes 811016 | tf_op jit(solution)/shard_map/ppermute | solution.py:398
  77.5 7.2 %collective-permute-start.6 = (bf16[528,256]{1,0:T(8,128)(2,1)S(1)}, bf16[528,256]{1,0:T(8,128)(2,1)S(1)}, u32[]{:S(2)}, u32[]{:S(2)}) collective-permute-start(bf16[528,256]{1,0:T(8,128)(2,1)S(1)} %collective-permute-done.5), channel_id=1, source_target_pairs={{0,16},{32,48},{64,80},{96,112},{128,144},{160,176},{192,208},{224... | collective-permute-start | bytes 811016 | tf_op jit(solution)/shard_map/ppermute | solution.py:398
  90.5 18.3 %collective-permute-start.14 = (bf16[4,9,96,128]{3,2,1,0:T(8,128)(2,1)S(1)}, bf16[4,9,96,128]{3,2,1,0:T(8,128)(2,1)S(1)}, u32[]{:S(2)}, u32[]{:S(2)}) collective-permute-start(bf16[4,9,96,128]{3,2,1,0:T(8,128)(2,1)S(1)} %get-tuple-element.90), channel_id=1, source_target_pairs={{0,1},{1,0},{2,3},{3,2},{4,5},{5,4},{6,7},{7,6},{8,9},{9,8},{10,11... | collective-permute-start | bytes 2654216 | tf_op jit(solution)/shard_map/ppermute | solution.py:522
  100.1 23.1 %collective-permute-start.12 = (bf16[2,4,304,128]{3,2,1,0:T(8,128)(2,1)S(1)}, bf16[2,4,304,128]{3,2,1,0:T(8,128)(2,1)S(1)}, u32[]{:S(2)}, u32[]{:S(2)}) collective-permute-start(bf16[2,4,304,128]{3,2,1,0:T(8,128)(2,1)S(1)} %slice.84), channel_id=1, source_target_pairs={{0,128},{128,0},{256,384},{384,256},{1,129},{129,1},{257,385},{385... | collective-permute-start | bytes 1867784 | tf_op jit(solution)/shard_map/ppermute | solution.py:534
  109.0 20.6 %collective-permute-start.15 = (bf16[2,9,96,128]{3,2,1,0:T(8,128)(2,1)S(1)}, bf16[2,9,96,128]{3,2,1,0:T(8,128)(2,1)S(1)}, u32[]{:S(2)}, u32[]{:S(2)}) collective-permute-start(bf16[2,9,96,128]{3,2,1,0:T(8,128)(2,1)S(1)} %get-tuple-element.92), channel_id=1, source_target_pairs={{128,256},{256,128},{384,0},{0,384},{129,257},{257,129},{385,1},{1... | collective-permute-start | bytes 1327112 | tf_op jit(solution)/shard_map/ppermute | solution.py:538
  123.3 13.4 %collective-permute-start.13 = (bf16[4,304,128]{2,1,0:T(8,128)(2,1)S(1)}, bf16[4,304,128]{2,1,0:T(8,128)(2,1)S(1)}, u32[]{:S(2)}, u32[]{:S(2)}) collective-permute-start(bf16[4,304,128]{2,1,0:T(8,128)(2,1)S(1)} %get-tuple-element.88), channel_id=1, source_target_pairs={{128,256},{256,128},{384,0},{0,384},{129,257},{257,129},{385,1},{1... | collective-permute-start | bytes 933896 | tf_op jit(solution)/shard_map/ppermute | solution.py:543
  129.7 8.0 %collective-permute-start.16 = (bf16[9,96,128]{2,1,0:T(8,128)(2,1)S(1)}, bf16[9,96,128]{2,1,0:T(8,128)(2,1)S(1)}, u32[]{:S(2)}, u32[]{:S(2)}) collective-permute-start(bf16[9,96,128]{2,1,0:T(8,128)(2,1)S(1)} %get-tuple-element.94), channel_id=1, source_target_pairs={{0,128},{128,0},{256,384},{384,256},{1,129},{129,1},{257,385},{385... | collective-permute-start | bytes 663560 | tf_op jit(solution)/shard_map/ppermute | solution.py:544
  154.6 25.1 %collective-permute-start.17 = (bf16[416,128]{1,0:T(8,128)(2,1)S(1)}, bf16[416,128]{1,0:T(8,128)(2,1)S(1)}, u32[]{:S(2)}, u32[]{:S(2)}) collective-permute-start(bf16[416,128]{1,0:T(8,128)(2,1)S(1)} %get-tuple-element.95.sent), channel_id=1, source_target_pairs={{0,64},{64,0},{1,65},{65,1},{2,66},{66,2},{3,67},{67,3},{4,68},{68... | collective-permute-start | bytes 319496 | tf_op jit(solution)/shard_map/ppermute | solution.py:555
  159.0 11.8 %collective-permute-start.19 = (bf16[112,128]{1,0:T(8,128)(2,1)S(1)}, bf16[112,128]{1,0:T(8,128)(2,1)S(1)}, u32[]{:S(2)}, u32[]{:S(2)}) collective-permute-start(bf16[112,128]{1,0:T(8,128)(2,1)S(1)} %slice.71), channel_id=1, source_target_pairs={{0,72},{72,0},{8,64},{64,8},{1,73},{73,1},{9,65},{65,9},{2,74},{74... | collective-permute-start | bytes 86024 | tf_op jit(solution)/shard_map/ppermute | solution.py:557
  166.4 13.4 %collective-permute-start.18 = (bf16[112,128]{1,0:T(8,128)(2,1)S(1)}, bf16[112,128]{1,0:T(8,128)(2,1)S(1)}, u32[]{:S(2)}, u32[]{:S(2)}) collective-permute-start(bf16[112,128]{1,0:T(8,128)(2,1)S(1)} %get-tuple-element.96.mine), channel_id=1, source_target_pairs={{0,8},{8,0},{1,9},{9,1},{2,10},{10,2},{3,11},{11,3},{4,12},{12,4},... | collective-permute-start | bytes 86024 | tf_op jit(solution)/shard_map/ppermute | solution.py:556
  180.5 17.1 %all-to-all-start.1 = ((bf16[4,304,128]{2,1,0:T(8,128)(2,1)}), bf16[4,304,128]{2,1,0:T(8,128)(2,1)S(1)}, u32[]{:S(2)}, u32[]{:S(2)}) async-start(bf16[4,304,128]{2,1,0:T(8,128)(2,1)} %get-tuple-element.97), calls=%async_computation.1 | async-start | bytes 622592 | tf_op jit(solution)/shard_map/all_to_all | solution.py:402
  184.0 10.6 %collective-permute-start.20 = (bf16[112,128]{1,0:T(8,128)(2,1)S(1)}, bf16[112,128]{1,0:T(8,128)(2,1)S(1)}, u32[]{:S(2)}, u32[]{:S(2)}) collective-permute-start(bf16[112,128]{1,0:T(8,128)(2,1)S(1)} %get-tuple-element.98.own), channel_id=1, source_target_pairs={{0,2},{2,4},{4,6},{6,0},{1,3},{3,5},{5,7},{7,1},{8,10},{10,12},{12... | collective-permute-start | bytes 86024 | tf_op jit(solution)/shard_map/ppermute | solution.py:567
  186.8 7.8 %collective-permute-start.21 = (bf16[112,128]{1,0:T(8,128)(2,1)S(1)}, bf16[112,128]{1,0:T(8,128)(2,1)S(1)}, u32[]{:S(2)}, u32[]{:S(2)}) collective-permute-start(bf16[112,128]{1,0:T(8,128)(2,1)S(1)} %get-tuple-element.98.own), channel_id=1, source_target_pairs={{0,4},{2,6},{4,0},{6,2},{1,5},{3,7},{5,1},{7,3},{8,12},{10,14},{12... | collective-permute-start | bytes 86024 | tf_op jit(solution)/shard_map/ppermute | solution.py:567
  197.6 13.5 %collective-permute-start.24 = (bf16[1216,128]{1,0:T(8,128)(2,1)S(1)}, bf16[1216,128]{1,0:T(8,128)(2,1)S(1)}, u32[]{:S(2)}, u32[]{:S(2)}) collective-permute-start(bf16[1216,128]{1,0:T(8,128)(2,1)S(1)} %bitcast.26), channel_id=1, source_target_pairs={{0,128},{128,256},{256,384},{384,0},{1,129},{129,257},{257,385},{3... | collective-permute-start | bytes 933896 | tf_op jit(solution)/shard_map/ppermute | solution.py:574
  199.6 13.5 %collective-permute-start.25 = (bf16[1216,128]{1,0:T(8,128)(2,1)S(1)}, bf16[1216,128]{1,0:T(8,128)(2,1)S(1)}, u32[]{:S(2)}, u32[]{:S(2)}) collective-permute-start(bf16[1216,128]{1,0:T(8,128)(2,1)S(1)} %bitcast.27), channel_id=1, source_target_pairs={{128,0},{256,128},{384,256},{0,384},{129,1},{257,129},{385,257},{1... | collective-permute-start | bytes 933896 | tf_op jit(solution)/shard_map/ppermute | solution.py:575
  204.1 13.5 %collective-permute-start.23 = (f32[112,128]{1,0:T(8,128)S(1)}, f32[112,128]{1,0:T(8,128)S(1)}, u32[]{:S(2)}, u32[]{:S(2)}) collective-permute-start(f32[112,128]{1,0:T(8,128)S(1)} %shard_map.170), channel_id=1, source_target_pairs={{0,1},{1,0},{2,3},{3,2},{4,5},{5,4},{6,7},{7,6},{8,9},{9,8},{10,11... | collective-permute-start | bytes 172040 | tf_op jit(solution)/shard_map/ppermute | solution.py:571
  211.1 7.6 %collective-permute-start.26 = (bf16[608,128]{1,0:T(8,128)(2,1)S(1)}, bf16[608,128]{1,0:T(8,128)(2,1)S(1)}, u32[]{:S(2)}, u32[]{:S(2)}) collective-permute-start(bf16[608,128]{1,0:T(8,128)(2,1)S(1)} %slice.85), channel_id=1, source_target_pairs={{0,128},{128,256},{256,384},{384,0},{1,129},{129,257},{257,385},{3... | collective-permute-start | bytes 466952 | tf_op jit(solution)/shard_map/ppermute | solution.py:576
  (14 other events, 89.1 us)

commit v7 on v6

--- a/solution.py
+++ b/solution.py
@@ -97,9 +97,14 @@
     embed_out[...] = embed
     donor = dot(embed, donor_w[...]).astype(BF16)
     accept = dot(embed, accept_w[...]).astype(BF16)
-    even_feat[:rows, :] = jnp.where(is_odd, donor, accept)
-    odd_feat[:rows, :] = jnp.where(is_odd, accept, donor)
-    wide_feat[:rows, :] = jnp.where(odd[1] < 4, accept, donor)
+
+    def store(into, value):
+        into[:rows, :] = value
+
+    pl.when(odd[0] > 0)(lambda: (store(even_feat, donor), store(odd_feat, accept))[0])
+    pl.when(odd[0] <= 0)(lambda: (store(even_feat, accept), store(odd_feat, donor))[0])
+    pl.when(odd[1] < 4)(lambda: store(wide_feat, accept))
+    pl.when(odd[1] >= 4)(lambda: store(wide_feat, donor))
     even_feat[pl.ds(rows, SLOTS), :] = meta[...]
     odd_feat[pl.ds(rows, SLOTS), :] = meta[...]
     wide_feat[pl.ds(rows, SLOTS), :] = meta[...]
@@ -322,35 +327,38 @@
         both[zq, chunk_rows:, :] = jnp.concatenate(parts, axis=0).astype(BF16)
 
 
-def line_sum_kernel(place, parts, pick, send, mine):
+def line_sum_kernel(parts, heads, taps):
     total = parts[0].astype(F32)
     for zq in range(1, 4):
         total = total + parts[zq].astype(F32)
-    chunk_rows = CHUNK_ROWS + EXTRA_ROWS
-    send[:chunk_rows, :] = split_rows(total[:chunk_rows])
-    taps = total[chunk_rows:].astype(BF16)
+    chunk_rows = heads.shape[0]
+    heads[...] = split_rows(total[:chunk_rows])
+    taps[...] = total[chunk_rows:].astype(BF16)
+
+
+def far_sum_kernel(place, sent, received, own, one, two, three, pick, head, theirs, mine):
+    total = split_rows(sent[...].astype(F32) + received[...].astype(F32))
+    for zq in range(head.shape[0]):
+        head[zq] = total
+    even = own[...].astype(F32) + two[...].astype(F32)
+    total = (even + (one[...].astype(F32) + three[...].astype(F32))).astype(BF16)
     half = mine.shape[0]
     zb = place[2]
 
     def picked(which):
-        return dot(pick[pl.ds(pl.multiple_of(which * half, half), half), :], taps).astype(BF16)
-
-    send[chunk_rows:, :] = picked(1 - zb)
+        return dot(pick[pl.ds(pl.multiple_of(which * half, half), half), :], total).astype(BF16)
+
+    theirs[...] = picked(1 - zb)
     mine[...] = picked(zb)
 
 
-def far_sum_kernel(sent, received, mine, one, two, head, taps):
-    chunk_rows = head.shape[1]
-    total = split_rows(sent[:chunk_rows, :].astype(F32) + received[:chunk_rows, :].astype(F32))
-    for zq in range(head.shape[0]):
-        head[zq] = total
-    near = mine[...].astype(F32) + received[chunk_rows:, :].astype(F32)
-    taps[...] = (near + (one[...].astype(F32) + two[...].astype(F32))).astype(BF16)
-
-
-def line_total_kernel(own, one, two, three, total):
-    even = own[...].astype(F32) + two[...].astype(F32)
-    total[...] = even + (one[...].astype(F32) + three[...].astype(F32))
+def add_kernel(one, two, total):
+    total[...] = (one[...].astype(F32) + two[...].astype(F32)).astype(total.dtype)
+
+
+def order_kernel(place, own, other, both):
+    both[place[0]] = own[...]
+    both[1 - place[0]] = other[...]
 
 
 def finish_kernel(
@@ -415,7 +423,7 @@
     here = lax.axis_index(SEQ)
     line = here % 8
     odd = jnp.stack([here % 2, line]).astype(jnp.int32)
-    is_odd = odd[0] > 0
+    is_odd = here % 2 > 0
     start, end = tokens[:STEP], tokens[rows - STEP :]
     even_edge = swapped(jnp.where(is_odd, start, end), 0)
     odd_edge = swapped(jnp.where(is_odd, end, start), 1)
@@ -548,35 +556,34 @@
         heads_kept, heads_in, conv_kept, conv_in
     )
     parts = swap_parts(both, "zq")
-    sent, mine = call(
-        line_sum_kernel, [shape((chunk + 112, 128), BF16), shape((112, 128), BF16)],
-        [SM] + [VM] * 2, 8, quick,
-    )(place, parts, pick)
-    received = lax.ppermute(sent, "zb", [(0, 1), (1, 0)])
-    across = lax.ppermute(mine, "zhi", [(0, 1), (1, 0)])
-    corner = lax.ppermute(
-        sent[chunk:], ("zb", "zhi"), [(0, 3), (3, 0), (1, 2), (2, 1)]
-    )
-    head_parts, conv_sum = call(
-        far_sum_kernel, [shape((4, chunk, 128), BF16), shape((112, 128), BF16)], [VM] * 5, 8, quick
-    )(sent, received, mine, across, corner)
+    head_line, tap_line = call(
+        line_sum_kernel, [shape((chunk, 128), BF16), shape((224, 128), BF16)], [VM], 8, quick
+    )(parts)
+    received = lax.ppermute(head_line, "zb", [(0, 1), (1, 0)])
+    line = [lax.ppermute(tap_line, "x", [(i, (i + step) % 4) for i in range(4)]) for step in (1, 2, 3)]
+    half_taps = shape((112, 128), BF16)
+    head_parts, theirs, mine = call(
+        far_sum_kernel, [shape((4, chunk, 128), BF16), half_taps, half_taps], [SM] + [VM] * 7, 8, quick
+    )(place, head_line, received, tap_line, *line, pick)
+    other = lax.ppermute(theirs, "zb", [(0, 1), (1, 0)])
+    (conv_sum,) = call(add_kernel, [half_taps], [VM] * 2, 8, quick)(mine, other)
 
     head_rows = 4 * chunk
     head_sum = swap_parts(head_parts, "zq").reshape(head_rows, 128)
-    line = [
-        lax.ppermute(conv_sum, "x", [(i, (i + step) % 4) for i in range(4)]) for step in (1, 2, 3)
-    ]
-    (conv_sum,) = call(line_total_kernel, [shape((112, 128), F32)], [VM] * 4, 8, quick)(conv_sum, *line)
-    head_sum, conv_sum = lax.optimization_barrier((head_sum, conv_sum))
     other = lax.ppermute(conv_sum, "core", [(0, 1), (1, 0)])
+    (pieces,) = call(order_kernel, [shape((2, 112, 128), BF16)], [SM] + [VM] * 2, 8, quick)(
+        place, conv_sum, other
+    )
+    head_sum, pieces = lax.optimization_barrier((head_sum, pieces))
     around = [(i, (i + 1) % 4) for i in range(4)]
     back = [(j, i) for i, j in around]
     behind = lax.ppermute(head_sum, "y", around)
     ahead = lax.ppermute(head_sum, "y", back)
     low = lax.ppermute(behind[: head_rows // 2], "y", around)
     high = lax.ppermute(ahead[head_rows // 2 :], "y", back)
-    is_first = lax.axis_index("core") == 0
-    pieces = jnp.stack([jnp.where(is_first, conv_sum, other), jnp.where(is_first, other, conv_sum)])
+    other = lax.ppermute(pieces, "zhi", [(0, 1), (1, 0)])
+    other, _ = lax.optimization_barrier((other, low))
+    pieces = pieces.astype(F32) + other.astype(F32)
     pieces = pieces[:, : slabs * 12].reshape(2, tap_count, lanes, 12, 128)
     grad_conv = pieces.transpose(1, 0, 3, 2, 4).reshape(tap_count, 24, inner)
     head_weight = shape((channels, heads), BF16)

time: 225 us -> 229 us (1.018)
    ppermute x6, waiting for transfers between devices: 11.9 us -> 4.4 us  [the longest x1 3.14 us: on_device(): other = lax.ppermute(theirs, 'zb', [(0, 1), (1, 0)])]
    ppermute x1, waiting for transfers between devices: 0.01 us -> 5.19 us  [on_device(): behind = lax.ppermute(head_sum, 'y', around)]
    ppermute x6, starting transfers between devices: 26.8 us -> 31.2 us  [the longest x3 11.6 us: on_device(): lax.ppermute(tap_line, 'x', [(i, (i + step) % 4) for i in range(4)])]
    ppermute x1, starting transfers between devices: 6.24 us -> 3.76 us  [on_device(): heads_in = lax.ppermute(heads_send, 'y', second_pairs)]
    ppermute x1, starting transfers between devices: 6.24 us -> 3.76 us  [on_device(): other = lax.ppermute(conv_send, 'y', second_pairs)]
    ppermute x1, waiting for transfers between devices: 7.92 us -> 10.4 us  [on_device(): other = lax.ppermute(head_sum[2:], 'y', first_pairs)]
  transfers between devices with their start and end apart: 29 -> 29, of which waited for: 10 -> 11; matrix products, arithmetic and copies ran while one was open for 1% -> 1% of each run, Pallas kernels for 8% -> 8%
where the time goes in v7:
time: 229 us; the launch traced here: 225 us
  starting transfers between devices  132 us (58%)
  waiting for transfers between devices  39 us (17%)
  Pallas kernels  30.6 us (13%)
  blocking collectives  17.6 us (8%)
    ppermute x10, starting transfers between devices, swapped(): return lax.ppermute(block, SEQ, pairs + [(j, i) for i, j in pairs])  51.3 us
    all_to_all x1, blocking collectives, swap_parts(): return lax.all_to_all(parts, axis, 0, 0, tiled=True)  17.6 us
    ppermute x3, starting transfers between devices, on_device(): lax.ppermute(tap_line, 'x', [(i, (i + step) % 4) for i in range(4)])  11.6 us
    ppermute x10, waiting for transfers between devices, swapped(): return lax.ppermute(block, SEQ, pairs + [(j, i) for i, j in pairs])  11.5 us
    ppermute x1, waiting for transfers between devices, on_device(): other = lax.ppermute(head_sum[2:], 'y', first_pairs)  10.4 us
    ppermute x1, starting transfers between devices, on_device(): other = lax.ppermute(pieces, 'zhi', [(0, 1), (1, 0)])  9.94 us
    ppermute x1, starting transfers between devices, on_device(): other = lax.ppermute(head_sum[2:], 'y', first_pairs)  8.55 us
    pallas_call x4, Pallas kernels, on_device(): call(lambda *refs, distance=distance: pair_kernel(distance, *refs), acc_s...  8.33 us
  transfers between devices with their start and end apart: 29, of which 11 were waited for; matrix products, arithmetic and copies ran while one was open for 1% of the time, Pallas kernels for 8%

profile of v7, /device:TPU:1, one launch (start us, length us, event | category | flops | bytes accessed | tf_op | source)
XLA Modules:
  0.0 224.8 jit_solution(5435528575719914044)
XLA Ops:
  2.5 4.4 %collective-permute-start = (bf16[128,768]{1,0:T(8,128)(2,1)}, bf16[128,768]{1,0:T(8,128)(2,1)S(1)}, u32[]{:S(2)}, u32[]{:S(2)}) collective-permute-start(bf16[128,768]{1,0:T(8,128)(2,1)} %get-tuple-element.111), channel_id=1, source_target_pairs={{0,16},{32,48},{64,80},{96,112},{128,144},{160,176},{192,208},{224... | collective-permute-start | bytes 589832 | tf_op jit(solution)/shard_map/ppermute | solution.py:406
  14.9 8.5 %collective-permute-start.7 = (bf16[528,256]{1,0:T(8,128)(2,1)S(1)}, bf16[528,256]{1,0:T(8,128)(2,1)S(1)}, u32[]{:S(2)}, u32[]{:S(2)}) collective-permute-start(bf16[528,256]{1,0:T(8,128)(2,1)S(1)} %get-tuple-element.61.refs_3_.refs_4_), channel_id=1, source_target_pairs={{0,16},{32,48},{64,80},{96,112},{128,144},{160,176},{192,208},{224... | collective-permute-start | bytes 811016 | tf_op jit(solution)/shard_map/ppermute | solution.py:406
  24.2 3.9 %shard_map.161 = (bf16[256,768]{1,0:T(8,128)(2,1)S(1)}, f32[512,384]{1,0:T(8,128)S(1)}, bf16[768,768]{1,0:T(8,128)(2,1)S(1)}, bf16[384,512]{1,0:T(8,128)(2,1)S(1)}, bf16[768,512]{1,0:T(8,128)(2,1)S(1)}) custom-call(s32[2]{0:T(128)S(1)} %pad_add_fusion.1.odd, bf16[128,768]{1,0:T(8,128)(2,1)S(1)} %collective-permute-done.even_edge, ...), custom_call_target="tpu_custom_call" | custom-call | flops 6000000000 | bytes 1000000 | tf_op jit(solution)/shard_map/pallas_call | solution.py:474
  37.4 29.9 %collective-permute-start.9 = (bf16[528,256]{1,0:T(8,128)(2,1)S(1)}, bf16[528,256]{1,0:T(8,128)(2,1)S(1)}, u32[]{:S(2)}, u32[]{:S(2)}) collective-permute-start(bf16[528,256]{1,0:T(8,128)(2,1)S(1)} %collective-permute-done.8.refs_5_), channel_id=1, source_target_pairs={{0,16},{32,48},{64,80},{96,112},{128,144},{160,176},{192,208},{224... | collective-permute-start | bytes 811016 | tf_op jit(solution)/shard_map/ppermute | solution.py:406
  69.7 7.2 %collective-permute-done.9.refs_6_ = bf16[528,256]{1,0:T(8,128)(2,1)S(1)} collective-permute-done((bf16[528,256]{1,0:T(8,128)(2,1)S(1)}, bf16[528,256]{1,0:T(8,128)(2,1)S(1)}, u32[]{:S(2)}, u32[]{:S(2)}) %collective-permute-start.9) | collective-permute-done | bytes 270368 | tf_op jit(solution)/shard_map/ppermute | solution.py:406
  82.1 3.5 %collective-permute-done.6 = bf16[528,256]{1,0:T(8,128)(2,1)S(1)} collective-permute-done((bf16[528,256]{1,0:T(8,128)(2,1)S(1)}, bf16[528,256]{1,0:T(8,128)(2,1)S(1)}, u32[]{:S(2)}, u32[]{:S(2)}) %collective-permute-start.6) | collective-permute-done | bytes 270368 | tf_op jit(solution)/shard_map/ppermute | solution.py:406
  88.0 4.1 %shard_map.162 = (bf16[4,9,96,128]{3,2,1,0:T(8,128)(2,1)S(1)}, bf16[4,9,96,128]{3,2,1,0:T(8,128)(2,1)S(1)}, bf16[512,384]{1,0:T(8,128)(2,1)S(1)}, bf16[512,512]{1,0:T(8,128)(2,1)S(1)}) custom-call(s32[3]{0:T(128)S(1)} %pad_add_fusion.place, f32[512,256]{1,0:T(8,128)S(1)} %get-tuple-element.74.d_donor, f32[512,256]{1,0:T(8,128)S(1)} %get-tuple-element.75.d_accept, ...), custom_call_target="tpu_custom_call" | custom-call | flops 4000000000 | bytes 1000000 | tf_op jit(solution)/shard_map/pallas_call | solution.py:523
  92.1 5.9 %collective-permute-start.14 = (bf16[4,9,96,128]{3,2,1,0:T(8,128)(2,1)S(1)}, bf16[4,9,96,128]{3,2,1,0:T(8,128)(2,1)S(1)}, u32[]{:S(2)}, u32[]{:S(2)}) collective-permute-start(bf16[4,9,96,128]{3,2,1,0:T(8,128)(2,1)S(1)} %get-tuple-element.92), channel_id=1, source_target_pairs={{0,1},{1,0},{2,3},{3,2},{4,5},{5,4},{6,7},{7,6},{8,9},{9,8},{10,11... | collective-permute-start | bytes 2654216 | tf_op jit(solution)/shard_map/ppermute | solution.py:530
  100.7 8.5 %collective-permute-start.12 = (bf16[2,4,304,128]{3,2,1,0:T(8,128)(2,1)S(1)}, bf16[2,4,304,128]{3,2,1,0:T(8,128)(2,1)S(1)}, u32[]{:S(2)}, u32[]{:S(2)}) collective-permute-start(bf16[2,4,304,128]{3,2,1,0:T(8,128)(2,1)S(1)} %slice.80), channel_id=1, source_target_pairs={{0,128},{128,0},{256,384},{384,256},{1,129},{129,1},{257,385},{385... | collective-permute-start | bytes 1867784 | tf_op jit(solution)/shard_map/ppermute | solution.py:542
  109.5 3.8 %collective-permute-start.15 = (bf16[2,9,96,128]{3,2,1,0:T(8,128)(2,1)S(1)}, bf16[2,9,96,128]{3,2,1,0:T(8,128)(2,1)S(1)}, u32[]{:S(2)}, u32[]{:S(2)}) collective-permute-start(bf16[2,9,96,128]{3,2,1,0:T(8,128)(2,1)S(1)} %get-tuple-element.94), channel_id=1, source_target_pairs={{128,256},{256,128},{384,0},{0,384},{129,257},{257,129},{385,1},{1... | collective-permute-start | bytes 1327112 | tf_op jit(solution)/shard_map/ppermute | solution.py:546
  113.3 10.4 %collective-permute-done.12.received = bf16[2,4,304,128]{3,2,1,0:T(8,128)(2,1)S(1)} collective-permute-done((bf16[2,4,304,128]{3,2,1,0:T(8,128)(2,1)S(1)}, bf16[2,4,304,128]{3,2,1,0:T(8,128)(2,1)S(1)}, u32[]{:S(2)}, u32[]{:S(2)}) %collective-permute-start.12) | collective-permute-done | bytes 622624 | tf_op jit(solution)/shard_map/ppermute | solution.py:542
  123.8 3.8 %collective-permute-start.13 = (bf16[4,304,128]{2,1,0:T(8,128)(2,1)S(1)}, bf16[4,304,128]{2,1,0:T(8,128)(2,1)S(1)}, u32[]{:S(2)}, u32[]{:S(2)}) collective-permute-start(bf16[4,304,128]{2,1,0:T(8,128)(2,1)S(1)} %get-tuple-element.90), channel_id=1, source_target_pairs={{128,256},{256,128},{384,0},{0,384},{129,257},{257,129},{385,1},{1... | collective-permute-start | bytes 933896 | tf_op jit(solution)/shard_map/ppermute | solution.py:551
  130.2 5.0 %collective-permute-done.13.head_in = bf16[4,304,128]{2,1,0:T(8,128)(2,1)S(1)} collective-permute-done((bf16[4,304,128]{2,1,0:T(8,128)(2,1)S(1)}, bf16[4,304,128]{2,1,0:T(8,128)(2,1)S(1)}, u32[]{:S(2)}, u32[]{:S(2)}) %collective-permute-start.13) | collective-permute-done | bytes 311328 | tf_op jit(solution)/shard_map/ppermute | solution.py:551
  135.7 17.6 %all_to_all.10.parts = bf16[4,528,128]{2,1,0:T(8,128)(2,1)S(1)} all-to-all(bf16[4,528,128]{2,1,0:T(8,128)(2,1)S(1)} %shard_map.167), channel_id=1, replica_groups=mesh['y'=4,'zb'=2,'zq'=4,'zhi'=2,'x'=4,'core'=2] {'zq'}, dimensions={0} | all-to-all | bytes 1081344 | tf_op jit(solution)/shard_map/all_to_all | solution.py:410
  153.4 4.3 %collective-permute-start.17 = (bf16[304,128]{1,0:T(8,128)(2,1)S(1)}, bf16[304,128]{1,0:T(8,128)(2,1)S(1)}, u32[]{:S(2)}, u32[]{:S(2)}) collective-permute-start(bf16[304,128]{1,0:T(8,128)(2,1)S(1)} %get-tuple-element.97.sent), channel_id=1, source_target_pairs={{0,64},{64,0},{1,65},{65,1},{2,66},{66,2},{3,67},{67,3},{4,68},{68... | collective-permute-start | bytes 233480 | tf_op jit(solution)/shard_map/ppermute | solution.py:562
  160.9 4.4 %collective-permute-start.19 = (bf16[224,128]{1,0:T(8,128)(2,1)S(1)}, bf16[224,128]{1,0:T(8,128)(2,1)S(1)}, u32[]{:S(2)}, u32[]{:S(2)}) collective-permute-start(bf16[224,128]{1,0:T(8,128)(2,1)S(1)} %get-tuple-element.98.own), channel_id=1, source_target_pairs={{0,4},{2,6},{4,0},{6,2},{1,5},{3,7},{5,1},{7,3},{8,12},{10,14},{12... | collective-permute-start | bytes 172040 | tf_op jit(solution)/shard_map/ppermute | solution.py:563
  165.3 3.9 %collective-permute-start.20 = (bf16[224,128]{1,0:T(8,128)(2,1)S(1)}, bf16[224,128]{1,0:T(8,128)(2,1)S(1)}, u32[]{:S(2)}, u32[]{:S(2)}) collective-permute-start(bf16[224,128]{1,0:T(8,128)(2,1)S(1)} %get-tuple-element.98.own), channel_id=1, source_target_pairs={{0,6},{2,0},{4,2},{6,4},{1,7},{3,1},{5,3},{7,5},{8,14},{10,8},{12,... | collective-permute-start | bytes 172040 | tf_op jit(solution)/shard_map/ppermute | solution.py:563
  171.9 3.5 %all-to-all-start.1 = ((bf16[4,304,128]{2,1,0:T(8,128)(2,1)}), bf16[4,304,128]{2,1,0:T(8,128)(2,1)S(1)}, u32[]{:S(2)}, u32[]{:S(2)}) async-start(bf16[4,304,128]{2,1,0:T(8,128)(2,1)} %get-tuple-element.99), calls=%async_computation.1 | async-start | bytes 622592 | tf_op jit(solution)/shard_map/all_to_all | solution.py:410
  175.4 5.5 %collective-permute-start.21 = (bf16[112,128]{1,0:T(8,128)(2,1)S(1)}, bf16[112,128]{1,0:T(8,128)(2,1)S(1)}, u32[]{:S(2)}, u32[]{:S(2)}) collective-permute-start(bf16[112,128]{1,0:T(8,128)(2,1)S(1)} %get-tuple-element.101), channel_id=1, source_target_pairs={{0,64},{64,0},{1,65},{65,1},{2,66},{66,2},{3,67},{67,3},{4,68},{68... | collective-permute-start | bytes 86024 | tf_op jit(solution)/shard_map/ppermute | solution.py:568
  184.0 6.7 %collective-permute-start.22 = (bf16[112,128]{1,0:T(8,128)(2,1)S(1)}, bf16[112,128]{1,0:T(8,128)(2,1)S(1)}, u32[]{:S(2)}, u32[]{:S(2)}) collective-permute-start(bf16[112,128]{1,0:T(8,128)(2,1)S(1)} %shard_map.170.own), channel_id=1, source_target_pairs={{0,1},{1,0},{2,3},{3,2},{4,5},{5,4},{6,7},{7,6},{8,9},{9,8},{10,11... | collective-permute-start | bytes 86024 | tf_op jit(solution)/shard_map/ppermute | solution.py:573
  194.4 4.2 %collective-permute-start.26 = (bf16[1216,128]{1,0:T(8,128)(2,1)S(1)}, bf16[1216,128]{1,0:T(8,128)(2,1)S(1)}, u32[]{:S(2)}, u32[]{:S(2)}) collective-permute-start(bf16[1216,128]{1,0:T(8,128)(2,1)S(1)} %bitcast.23), channel_id=1, source_target_pairs={{128,0},{256,128},{384,256},{0,384},{129,1},{257,129},{385,257},{1... | collective-permute-start | bytes 933896 | tf_op jit(solution)/shard_map/ppermute | solution.py:581
  198.6 5.2 %collective-permute-done.24.behind = bf16[1216,128]{1,0:T(8,128)(2,1)S(1)} collective-permute-done((bf16[1216,128]{1,0:T(8,128)(2,1)S(1)}, bf16[1216,128]{1,0:T(8,128)(2,1)S(1)}, u32[]{:S(2)}, u32[]{:S(2)}) %collective-permute-start.24) | collective-permute-done | bytes 311328 | tf_op jit(solution)/shard_map/ppermute | solution.py:580
  205.7 9.9 %collective-permute-start.23 = (bf16[2,112,128]{2,1,0:T(8,128)(2,1)S(1)}, bf16[2,112,128]{2,1,0:T(8,128)(2,1)S(1)}, u32[]{:S(2)}, u32[]{:S(2)}) collective-permute-start(bf16[2,112,128]{2,1,0:T(8,128)(2,1)S(1)} %shard_map.171), channel_id=1, source_target_pairs={{0,8},{8,0},{1,9},{9,1},{2,10},{10,2},{3,11},{11,3},{4,12},{12,4},... | collective-permute-start | bytes 172040 | tf_op jit(solution)/shard_map/ppermute | solution.py:584
  215.7 4.6 %collective-permute-start.27 = (bf16[608,128]{1,0:T(8,128)(2,1)S(1)}, bf16[608,128]{1,0:T(8,128)(2,1)S(1)}, u32[]{:S(2)}, u32[]{:S(2)}) collective-permute-start(bf16[608,128]{1,0:T(8,128)(2,1)S(1)} %slice.84), channel_id=1, source_target_pairs={{128,0},{256,128},{384,256},{0,384},{129,1},{257,129},{385,257},{1... | collective-permute-start | bytes 466952 | tf_op jit(solution)/shard_map/ppermute | solution.py:583
  (100 shorter events, 54.2 us)
Async XLA Ops:
  2.5 8.6 %collective-permute-start = (bf16[128,768]{1,0:T(8,128)(2,1)}, bf16[128,768]{1,0:T(8,128)(2,1)S(1)}, u32[]{:S(2)}, u32[]{:S(2)}) collective-permute-start(bf16[128,768]{1,0:T(8,128)(2,1)} %get-tuple-element.111), channel_id=1, source_target_pairs={{0,16},{32,48},{64,80},{96,112},{128,144},{160,176},{192,208},{224... | collective-permute-start | bytes 589832 | tf_op jit(solution)/shard_map/ppermute | solution.py:406
  14.2 15.3 %collective-permute-start.3 = (bf16[528,256]{1,0:T(8,128)(2,1)S(1)}, bf16[528,256]{1,0:T(8,128)(2,1)S(1)}, u32[]{:S(2)}, u32[]{:S(2)}) collective-permute-start(bf16[528,256]{1,0:T(8,128)(2,1)S(1)} %get-tuple-element.60.refs_2_.refs_3_), channel_id=1, source_target_pairs={{16,32},{48,64},{80,96},{112,128},{144,160},{176,192},{208,224},{2... | collective-permute-start | bytes 811016 | tf_op jit(solution)/shard_map/ppermute | solution.py:406
  14.9 17.3 %collective-permute-start.7 = (bf16[528,256]{1,0:T(8,128)(2,1)S(1)}, bf16[528,256]{1,0:T(8,128)(2,1)S(1)}, u32[]{:S(2)}, u32[]{:S(2)}) collective-permute-start(bf16[528,256]{1,0:T(8,128)(2,1)S(1)} %get-tuple-element.61.refs_3_.refs_4_), channel_id=1, source_target_pairs={{0,16},{32,48},{64,80},{96,112},{128,144},{160,176},{192,208},{224... | collective-permute-start | bytes 811016 | tf_op jit(solution)/shard_map/ppermute | solution.py:406
  23.5 9.5 %collective-permute-start.2 = (bf16[528,256]{1,0:T(8,128)(2,1)S(1)}, bf16[528,256]{1,0:T(8,128)(2,1)S(1)}, u32[]{:S(2)}, u32[]{:S(2)}) collective-permute-start(bf16[528,256]{1,0:T(8,128)(2,1)S(1)} %get-tuple-element.59), channel_id=1, source_target_pairs={{160,96},{176,112},{288,224},{304,240},{416,352},{432,368},{64,128... | collective-permute-start | bytes 811016 | tf_op jit(solution)/shard_map/ppermute | solution.py:492
  29.5 7.2 %collective-permute-start.4 = (bf16[528,256]{1,0:T(8,128)(2,1)S(1)}, bf16[528,256]{1,0:T(8,128)(2,1)S(1)}, u32[]{:S(2)}, u32[]{:S(2)}) collective-permute-start(bf16[528,256]{1,0:T(8,128)(2,1)S(1)} %collective-permute-done.3.refs_5_), channel_id=1, source_target_pairs={{0,16},{32,48},{64,80},{96,112},{128,144},{160,176},{192,208},{224... | collective-permute-start | bytes 811016 | tf_op jit(solution)/shard_map/ppermute | solution.py:406
  33.0 47.0 %collective-permute-start.11 = (bf16[528,256]{1,0:T(8,128)(2,1)S(1)}, bf16[528,256]{1,0:T(8,128)(2,1)S(1)}, u32[]{:S(2)}, u32[]{:S(2)}) collective-permute-start(bf16[528,256]{1,0:T(8,128)(2,1)S(1)} %collective-permute-done.2), channel_id=1, source_target_pairs={{96,112},{224,240},{352,368},{480,496},{16,0},{144,128},{272,256},... | collective-permute-start | bytes 811016 | tf_op jit(solution)/shard_map/ppermute | solution.py:493
  36.7 40.8 %collective-permute-start.5 = (bf16[528,256]{1,0:T(8,128)(2,1)S(1)}, bf16[528,256]{1,0:T(8,128)(2,1)S(1)}, u32[]{:S(2)}, u32[]{:S(2)}) collective-permute-start(bf16[528,256]{1,0:T(8,128)(2,1)S(1)} %collective-permute-done.4.refs_6_), channel_id=1, source_target_pairs={{16,32},{48,64},{80,96},{144,160},{176,192},{208,224},{272,288},{3... | collective-permute-start | bytes 811016 | tf_op jit(solution)/shard_map/ppermute | solution.py:406
  37.4 39.5 %collective-permute-start.9 = (bf16[528,256]{1,0:T(8,128)(2,1)S(1)}, bf16[528,256]{1,0:T(8,128)(2,1)S(1)}, u32[]{:S(2)}, u32[]{:S(2)}) collective-permute-start(bf16[528,256]{1,0:T(8,128)(2,1)S(1)} %collective-permute-done.8.refs_5_), channel_id=1, source_target_pairs={{0,16},{32,48},{64,80},{96,112},{128,144},{160,176},{192,208},{224... | collective-permute-start | bytes 811016 | tf_op jit(solution)/shard_map/ppermute | solution.py:406
  77.6 8.0 %collective-permute-start.6 = (bf16[528,256]{1,0:T(8,128)(2,1)S(1)}, bf16[528,256]{1,0:T(8,128)(2,1)S(1)}, u32[]{:S(2)}, u32[]{:S(2)}) collective-permute-start(bf16[528,256]{1,0:T(8,128)(2,1)S(1)} %collective-permute-done.5), channel_id=1, source_target_pairs={{0,16},{32,48},{64,80},{96,112},{128,144},{160,176},{192,208},{224... | collective-permute-start | bytes 811016 | tf_op jit(solution)/shard_map/ppermute | solution.py:406
  92.1 17.2 %collective-permute-start.14 = (bf16[4,9,96,128]{3,2,1,0:T(8,128)(2,1)S(1)}, bf16[4,9,96,128]{3,2,1,0:T(8,128)(2,1)S(1)}, u32[]{:S(2)}, u32[]{:S(2)}) collective-permute-start(bf16[4,9,96,128]{3,2,1,0:T(8,128)(2,1)S(1)} %get-tuple-element.92), channel_id=1, source_target_pairs={{0,1},{1,0},{2,3},{3,2},{4,5},{5,4},{6,7},{7,6},{8,9},{9,8},{10,11... | collective-permute-start | bytes 2654216 | tf_op jit(solution)/shard_map/ppermute | solution.py:530
  100.7 22.9 %collective-permute-start.12 = (bf16[2,4,304,128]{3,2,1,0:T(8,128)(2,1)S(1)}, bf16[2,4,304,128]{3,2,1,0:T(8,128)(2,1)S(1)}, u32[]{:S(2)}, u32[]{:S(2)}) collective-permute-start(bf16[2,4,304,128]{3,2,1,0:T(8,128)(2,1)S(1)} %slice.80), channel_id=1, source_target_pairs={{0,128},{128,0},{256,384},{384,256},{1,129},{129,1},{257,385},{385... | collective-permute-start | bytes 1867784 | tf_op jit(solution)/shard_map/ppermute | solution.py:542
  109.5 18.1 %collective-permute-start.15 = (bf16[2,9,96,128]{3,2,1,0:T(8,128)(2,1)S(1)}, bf16[2,9,96,128]{3,2,1,0:T(8,128)(2,1)S(1)}, u32[]{:S(2)}, u32[]{:S(2)}) collective-permute-start(bf16[2,9,96,128]{3,2,1,0:T(8,128)(2,1)S(1)} %get-tuple-element.94), channel_id=1, source_target_pairs={{128,256},{256,128},{384,0},{0,384},{129,257},{257,129},{385,1},{1... | collective-permute-start | bytes 1327112 | tf_op jit(solution)/shard_map/ppermute | solution.py:546
  123.8 11.4 %collective-permute-start.13 = (bf16[4,304,128]{2,1,0:T(8,128)(2,1)S(1)}, bf16[4,304,128]{2,1,0:T(8,128)(2,1)S(1)}, u32[]{:S(2)}, u32[]{:S(2)}) collective-permute-start(bf16[4,304,128]{2,1,0:T(8,128)(2,1)S(1)} %get-tuple-element.90), channel_id=1, source_target_pairs={{128,256},{256,128},{384,0},{0,384},{129,257},{257,129},{385,1},{1... | collective-permute-start | bytes 933896 | tf_op jit(solution)/shard_map/ppermute | solution.py:551
  127.7 8.0 %collective-permute-start.16 = (bf16[9,96,128]{2,1,0:T(8,128)(2,1)S(1)}, bf16[9,96,128]{2,1,0:T(8,128)(2,1)S(1)}, u32[]{:S(2)}, u32[]{:S(2)}) collective-permute-start(bf16[9,96,128]{2,1,0:T(8,128)(2,1)S(1)} %get-tuple-element.96), channel_id=1, source_target_pairs={{0,128},{128,0},{256,384},{384,256},{1,129},{129,1},{257,385},{385... | collective-permute-start | bytes 663560 | tf_op jit(solution)/shard_map/ppermute | solution.py:552
  153.4 17.1 %collective-permute-start.17 = (bf16[304,128]{1,0:T(8,128)(2,1)S(1)}, bf16[304,128]{1,0:T(8,128)(2,1)S(1)}, u32[]{:S(2)}, u32[]{:S(2)}) collective-permute-start(bf16[304,128]{1,0:T(8,128)(2,1)S(1)} %get-tuple-element.97.sent), channel_id=1, source_target_pairs={{0,64},{64,0},{1,65},{65,1},{2,66},{66,2},{3,67},{67,3},{4,68},{68... | collective-permute-start | bytes 233480 | tf_op jit(solution)/shard_map/ppermute | solution.py:562
  157.7 11.6 %collective-permute-start.18 = (bf16[224,128]{1,0:T(8,128)(2,1)S(1)}, bf16[224,128]{1,0:T(8,128)(2,1)S(1)}, u32[]{:S(2)}, u32[]{:S(2)}) collective-permute-start(bf16[224,128]{1,0:T(8,128)(2,1)S(1)} %get-tuple-element.98.own), channel_id=1, source_target_pairs={{0,2},{2,4},{4,6},{6,0},{1,3},{3,5},{5,7},{7,1},{8,10},{10,12},{12... | collective-permute-start | bytes 172040 | tf_op jit(solution)/shard_map/ppermute | solution.py:563
  160.9 8.4 %collective-permute-start.19 = (bf16[224,128]{1,0:T(8,128)(2,1)S(1)}, bf16[224,128]{1,0:T(8,128)(2,1)S(1)}, u32[]{:S(2)}, u32[]{:S(2)}) collective-permute-start(bf16[224,128]{1,0:T(8,128)(2,1)S(1)} %get-tuple-element.98.own), channel_id=1, source_target_pairs={{0,4},{2,6},{4,0},{6,2},{1,5},{3,7},{5,1},{7,3},{8,12},{10,14},{12... | collective-permute-start | bytes 172040 | tf_op jit(solution)/shard_map/ppermute | solution.py:563
  171.9 20.2 %all-to-all-start.1 = ((bf16[4,304,128]{2,1,0:T(8,128)(2,1)}), bf16[4,304,128]{2,1,0:T(8,128)(2,1)S(1)}, u32[]{:S(2)}, u32[]{:S(2)}) async-start(bf16[4,304,128]{2,1,0:T(8,128)(2,1)} %get-tuple-element.99), calls=%async_computation.1 | async-start | bytes 622592 | tf_op jit(solution)/shard_map/all_to_all | solution.py:410
  175.4 8.6 %collective-permute-start.21 = (bf16[112,128]{1,0:T(8,128)(2,1)S(1)}, bf16[112,128]{1,0:T(8,128)(2,1)S(1)}, u32[]{:S(2)}, u32[]{:S(2)}) collective-permute-start(bf16[112,128]{1,0:T(8,128)(2,1)S(1)} %get-tuple-element.101), channel_id=1, source_target_pairs={{0,64},{64,0},{1,65},{65,1},{2,66},{66,2},{3,67},{67,3},{4,68},{68... | collective-permute-start | bytes 86024 | tf_op jit(solution)/shard_map/ppermute | solution.py:568
  184.0 7.5 %collective-permute-start.22 = (bf16[112,128]{1,0:T(8,128)(2,1)S(1)}, bf16[112,128]{1,0:T(8,128)(2,1)S(1)}, u32[]{:S(2)}, u32[]{:S(2)}) collective-permute-start(bf16[112,128]{1,0:T(8,128)(2,1)S(1)} %shard_map.170.own), channel_id=1, source_target_pairs={{0,1},{1,0},{2,3},{3,2},{4,5},{5,4},{6,7},{7,6},{8,9},{9,8},{10,11... | collective-permute-start | bytes 86024 | tf_op jit(solution)/shard_map/ppermute | solution.py:573
  192.1 11.7 %collective-permute-start.24 = (bf16[1216,128]{1,0:T(8,128)(2,1)S(1)}, bf16[1216,128]{1,0:T(8,128)(2,1)S(1)}, u32[]{:S(2)}, u32[]{:S(2)}) collective-permute-start(bf16[1216,128]{1,0:T(8,128)(2,1)S(1)} %bitcast.22), channel_id=1, source_target_pairs={{0,128},{128,256},{256,384},{384,0},{1,129},{129,257},{257,385},{3... | collective-permute-start | bytes 933896 | tf_op jit(solution)/shard_map/ppermute | solution.py:580
  194.4 21.3 %collective-permute-start.26 = (bf16[1216,128]{1,0:T(8,128)(2,1)S(1)}, bf16[1216,128]{1,0:T(8,128)(2,1)S(1)}, u32[]{:S(2)}, u32[]{:S(2)}) collective-permute-start(bf16[1216,128]{1,0:T(8,128)(2,1)S(1)} %bitcast.23), channel_id=1, source_target_pairs={{128,0},{256,128},{384,256},{0,384},{129,1},{257,129},{385,257},{1... | collective-permute-start | bytes 933896 | tf_op jit(solution)/shard_map/ppermute | solution.py:581
  203.8 16.5 %collective-permute-start.25 = (bf16[608,128]{1,0:T(8,128)(2,1)S(1)}, bf16[608,128]{1,0:T(8,128)(2,1)S(1)}, u32[]{:S(2)}, u32[]{:S(2)}) collective-permute-start(bf16[608,128]{1,0:T(8,128)(2,1)S(1)} %slice.81), channel_id=1, source_target_pairs={{0,128},{128,256},{256,384},{384,0},{1,129},{129,257},{257,385},{3... | collective-permute-start | bytes 466952 | tf_op jit(solution)/shard_map/ppermute | solution.py:582
  205.7 14.6 %collective-permute-start.23 = (bf16[2,112,128]{2,1,0:T(8,128)(2,1)S(1)}, bf16[2,112,128]{2,1,0:T(8,128)(2,1)S(1)}, u32[]{:S(2)}, u32[]{:S(2)}) collective-permute-start(bf16[2,112,128]{2,1,0:T(8,128)(2,1)S(1)} %shard_map.171), channel_id=1, source_target_pairs={{0,8},{8,0},{1,9},{9,1},{2,10},{10,2},{3,11},{11,3},{4,12},{12,4},... | collective-permute-start | bytes 172040 | tf_op jit(solution)/shard_map/ppermute | solution.py:584
  (14 other events, 106.9 us)

commit v8 on v6

--- a/solution.py
+++ b/solution.py
@@ -74,17 +74,21 @@
         factor[here, :] = (slope * unit).astype(BF16)
 
 
+def edge_kernel(edge, gain, hidden):
+    v = edge[...].astype(F32)
+    hidden[...] = gelu(v * rms(v) * gain[...]).astype(BF16)
+
+
 def forward_kernel(
-    odd, tok, mine, even_edge, odd_edge, gain, taps, point, donor_w, accept_w, meta,
-    hidden, conv_out, act_out, embed_out, even_feat, odd_feat, wide_feat,
+    odd, tok, mine, even_edge, odd_hidden, gain, taps, point, donor_w, accept_w, meta,
+    hidden, conv_out, act_out, embed_out, even_feat, odd_feat,
 ):
     rows = tok.shape[0]
     is_odd = odd[0] > 0
-    low = jnp.where(is_odd, even_edge[...], odd_edge[...])
-    high = jnp.where(is_odd, odd_edge[...], even_edge[...])
-    for edge, at in ((low, 0), (high, STEP + rows)):
-        v = edge.astype(F32)
-        hidden[pl.ds(at, STEP), :] = gelu(v * rms(v) * gain[...]).astype(BF16)
+    v = even_edge[...].astype(F32)
+    even_hidden = gelu(v * rms(v) * gain[...]).astype(BF16)
+    hidden[pl.ds(0, STEP), :] = jnp.where(is_odd, even_hidden, odd_hidden[...])
+    hidden[pl.ds(STEP + rows, STEP), :] = jnp.where(is_odd, odd_hidden[...], even_hidden)
     hidden[pl.ds(STEP, rows), :] = mine[...]
 
     conv = dot(hidden[:rows, :], taps[0])
@@ -99,10 +103,8 @@
     accept = dot(embed, accept_w[...]).astype(BF16)
     even_feat[:rows, :] = jnp.where(is_odd, donor, accept)
     odd_feat[:rows, :] = jnp.where(is_odd, accept, donor)
-    wide_feat[:rows, :] = jnp.where(odd[1] < 4, accept, donor)
     even_feat[pl.ds(rows, SLOTS), :] = meta[...]
     odd_feat[pl.ds(rows, SLOTS), :] = meta[...]
-    wide_feat[pl.ds(rows, SLOTS), :] = meta[...]
 
 
 def side_kernel(
@@ -322,30 +324,26 @@
         both[zq, chunk_rows:, :] = jnp.concatenate(parts, axis=0).astype(BF16)
 
 
-def line_sum_kernel(place, parts, pick, send, mine):
+def line_sum_kernel(parts, pick, heads, taps):
     total = parts[0].astype(F32)
     for zq in range(1, 4):
         total = total + parts[zq].astype(F32)
-    chunk_rows = CHUNK_ROWS + EXTRA_ROWS
-    send[:chunk_rows, :] = split_rows(total[:chunk_rows])
-    taps = total[chunk_rows:].astype(BF16)
-    half = mine.shape[0]
-    zb = place[2]
-
-    def picked(which):
-        return dot(pick[pl.ds(pl.multiple_of(which * half, half), half), :], taps).astype(BF16)
-
-    send[chunk_rows:, :] = picked(1 - zb)
-    mine[...] = picked(zb)
-
-
-def far_sum_kernel(sent, received, mine, one, two, head, taps):
-    chunk_rows = head.shape[1]
-    total = split_rows(sent[:chunk_rows, :].astype(F32) + received[:chunk_rows, :].astype(F32))
+    chunk_rows = heads.shape[0]
+    heads[...] = split_rows(total[:chunk_rows])
+    rest = total[chunk_rows:].astype(BF16)
+    half = taps.shape[1]
+    for zb in range(2):
+        picked = dot(pick[zb * half : (zb + 1) * half, :], rest).astype(BF16)
+        for zhi in range(2):
+            taps[zb * 2 + zhi] = picked
+
+
+def far_sum_kernel(sent, received, tap_parts, head, taps):
+    total = split_rows(sent[...].astype(F32) + received[...].astype(F32))
     for zq in range(head.shape[0]):
         head[zq] = total
-    near = mine[...].astype(F32) + received[chunk_rows:, :].astype(F32)
-    taps[...] = (near + (one[...].astype(F32) + two[...].astype(F32))).astype(BF16)
+    near = tap_parts[0].astype(F32) + tap_parts[1].astype(F32)
+    taps[...] = (near + (tap_parts[2].astype(F32) + tap_parts[3].astype(F32))).astype(BF16)
 
 
 def line_total_kernel(own, one, two, three, total):
@@ -413,9 +411,9 @@
     blocks = rows // PANEL
     shape = jax.ShapeDtypeStruct
     here = lax.axis_index(SEQ)
-    line = here % 8
-    odd = jnp.stack([here % 2, line]).astype(jnp.int32)
-    is_odd = odd[0] > 0
+    line = lax.axis_index(("zb", "zq"))
+    is_odd = (lax.axis_index("zq") & 1) > 0
+    odd = is_odd.astype(jnp.int32)[None]
     start, end = tokens[:STEP], tokens[rows - STEP :]
     even_edge = swapped(jnp.where(is_odd, start, end), 0)
     odd_edge = swapped(jnp.where(is_odd, end, start), 1)
@@ -439,8 +437,9 @@
     mine, factor = call(
         own_kernel, [shape((rows, channels), BF16)] * 2, [VM] * 2, 12, 2_000_000_000
     )(tokens, gain)
+    (odd_hidden,) = call(edge_kernel, [shape((STEP, channels), BF16)], [VM] * 2, 8, 2_000_000_000)(odd_edge, gain)
     feat = shape((rows + SLOTS, heads), BF16)
-    hidden, conv, act, embed, even_feat, odd_feat, wide_feat = call(
+    hidden, conv, act, embed, even_feat, odd_feat = call(
         forward_kernel,
         [
             shape((rows + 2 * STEP, channels), BF16),
@@ -449,20 +448,19 @@
             shape((rows, channels), BF16),
             feat,
             feat,
-            feat,
         ],
         [SM] + [VM] * 10,
         20,
         4_000_000_000,
     )(
-        odd, tokens, mine, even_edge, odd_edge, gain, dilated_tap_weight, point_weight,
+        odd, tokens, mine, even_edge, odd_hidden, gain, dilated_tap_weight, point_weight,
         donor_weight, acceptor_weight, meta_rows,
     )
 
     acc_shapes = [shape((rows, heads), F32), shape((rows, heads), F32), shape((PANEL, PANEL), F32)]
     acc = call(
         lambda *refs: pair_kernel(0, *refs), acc_shapes, [SM] * 2 + [VM] * 2, 12, 2_000_000_000
-    )(1 - odd[:1], meta, even_feat, odd_feat)
+    )(1 - odd, meta, even_feat, odd_feat)
     edge_factor, slope, hidden_t, act_t, embed_t = call(
         side_kernel,
         [
@@ -481,6 +479,7 @@
     wide_pairs = [(i + k, i - 4 + k) for i in starts if i > 0 for k in (2, 3)]
     wide_pairs += [(i + k, i + 4 + k) for i in starts if i + 8 < count for k in (4, 5)]
     relay_pairs = [(i + 6, i + 7) for i in starts] + [(i + 1, i) for i in starts]
+    wide_feat = jnp.where((line == 2) | (line == 5), even_feat, odd_feat)
     wide = lax.ppermute(wide_feat, SEQ, wide_pairs)
     relay = lax.ppermute(wide, SEQ, relay_pairs)
     at_end = (line == 0) | (line == 7)
@@ -497,14 +496,14 @@
         if distance == 4:
             short_use = jnp.where(near_end, wide, short_far)
             long_use = jnp.where(at_end, wide, long_far)
-        far_meta = jnp.where(odd[0] > 0, short_use[rows:, :8], long_use[rows:, :8]).astype(jnp.int32)
+        far_meta = jnp.where(is_odd, short_use[rows:, :8], long_use[rows:, :8]).astype(jnp.int32)
         acc = call(
             lambda *refs, distance=distance: pair_kernel(distance, *refs),
             acc_shapes,
             [SM] * 3 + [VM] * 7,
             12,
             2_500_000_000,
-        )(1 - odd[:1], meta, far_meta, even_feat, odd_feat, long_use, short_use, *acc)
+        )(1 - odd, meta, far_meta, even_feat, odd_feat, long_use, short_use, *acc)
 
     chunk = CHUNK_ROWS + EXTRA_ROWS
     lanes = inner // 128
@@ -548,18 +547,14 @@
         heads_kept, heads_in, conv_kept, conv_in
     )
     parts = swap_parts(both, "zq")
-    sent, mine = call(
-        line_sum_kernel, [shape((chunk + 112, 128), BF16), shape((112, 128), BF16)],
-        [SM] + [VM] * 2, 8, quick,
-    )(place, parts, pick)
-    received = lax.ppermute(sent, "zb", [(0, 1), (1, 0)])
-    across = lax.ppermute(mine, "zhi", [(0, 1), (1, 0)])
-    corner = lax.ppermute(
-        sent[chunk:], ("zb", "zhi"), [(0, 3), (3, 0), (1, 2), (2, 1)]
-    )
+    head_line, tap_line = call(
+        line_sum_kernel, [shape((chunk, 128), BF16), shape((4, 112, 128), BF16)], [VM] * 2, 8, quick
+    )(parts, pick)
+    received = lax.ppermute(head_line, "zb", [(0, 1), (1, 0)])
+    tap_parts = swap_parts(tap_line, ("zb", "zhi"))
     head_parts, conv_sum = call(
-        far_sum_kernel, [shape((4, chunk, 128), BF16), shape((112, 128), BF16)], [VM] * 5, 8, quick
-    )(sent, received, mine, across, corner)
+        far_sum_kernel, [shape((4, chunk, 128), BF16), shape((112, 128), BF16)], [VM] * 3, 8, quick
+    )(head_line, received, tap_parts)
 
     head_rows = 4 * chunk
     head_sum = swap_parts(head_parts, "zq").reshape(head_rows, 128)

time: 225 us -> 227 us (level)
  starting transfers between devices: 133 us -> 126 us
  waiting for transfers between devices: 37.7 us -> 41.5 us
  local copies, waits for them, and re-layouts: 1.19 us -> 4.73 us
    all_to_all x1 -> x2, starting transfers between devices: 3.45 us -> 13.4 us  [swap_parts(): return lax.all_to_all(parts, axis, 0, 0, tiled=True)]
    ppermute x3 -> x1, starting transfers between devices: 16.2 us -> 7.27 us  [on_device(): received = lax.ppermute(head_line, 'zb', [(0, 1), (1, 0)])]
    ppermute x1, starting transfers between devices: 8.68 us -> 2.7 us  [on_device(): other = lax.ppermute(head_sum[2:], 'y', first_pairs)]
    ppermute x10, waiting for transfers between devices: 11.3 us -> 15.8 us  [swapped(): return lax.ppermute(block, SEQ, pairs + [(j, i) for i, j in pairs])]
    unnamed x20 -> x28, local copies, waits for them, and re-layouts: 0.21 us -> 3.76 us
    ppermute x3 -> x1, waiting for transfers between devices: 8.89 us -> 11.3 us  [on_device(): received = lax.ppermute(head_line, 'zb', [(0, 1), (1, 0)])]
    ppermute x1, starting transfers between devices: 6.93 us -> 4.62 us  [on_device(): other = lax.ppermute(conv_sum, 'core', [(0, 1), (1, 0)])]
  transfers between devices with their start and end apart: 29 -> 28, of which waited for: 10 -> 9; matrix products, arithmetic and copies ran while one was open for 1% -> 1% of each run, Pallas kernels for 8% -> 8%
where the time goes in v8:
time: 227 us; the launch traced here: 224 us
  starting transfers between devices  126 us (56%)
  waiting for transfers between devices  41.5 us (18%)
  Pallas kernels  29.6 us (13%)
  blocking collectives  17.8 us (8%)
  local copies, waits for them, and re-layouts  4.73 us (2%)
    ppermute x10, starting transfers between devices, swapped(): return lax.ppermute(block, SEQ, pairs + [(j, i) for i, j in pairs])  48.2 us
    all_to_all x1, blocking collectives, swap_parts(): return lax.all_to_all(parts, axis, 0, 0, tiled=True)  17.8 us
    ppermute x10, waiting for transfers between devices, swapped(): return lax.ppermute(block, SEQ, pairs + [(j, i) for i, j in pairs])  15.8 us
    all_to_all x2, starting transfers between devices, swap_parts(): return lax.all_to_all(parts, axis, 0, 0, tiled=True)  13.4 us
    ppermute x3, starting transfers between devices, on_device(): lax.ppermute(conv_sum, 'x', [(i, (i + step) % 4) for i in range(4)])  11.6 us
    ppermute x1, waiting for transfers between devices, on_device(): received = lax.ppermute(head_line, 'zb', [(0, 1), (1, 0)])  11.3 us
    pallas_call x4, Pallas kernels, on_device(): call(lambda *refs, distance=distance: pair_kernel(distance, *refs), acc_s...  8.66 us
    ppermute x1, starting transfers between devices, on_device(): other = lax.ppermute(conv_send, 'y', second_pairs)  7.83 us
  transfers between devices with their start and end apart: 28, of which 9 were waited for; matrix products, arithmetic and copies ran while one was open for 1% of the time, Pallas kernels for 8%

profile of v8, /device:TPU:1, one launch (start us, length us, event | category | flops | bytes accessed | tf_op | source)
XLA Modules:
  0.0 223.8 jit_solution(17768110604192197910)
XLA Ops:
  3.1 7.2 %collective-permute-start = (bf16[128,768]{1,0:T(8,128)(2,1)S(1)}, bf16[128,768]{1,0:T(8,128)(2,1)S(1)}, u32[]{:S(2)}, u32[]{:S(2)}) collective-permute-start(bf16[128,768]{1,0:T(8,128)(2,1)S(1)} %get-tuple-element.105), channel_id=1, source_target_pairs={{0,16},{32,48},{64,80},{96,112},{128,144},{160,176},{192,208},{224... | collective-permute-start | bytes 589832 | tf_op jit(solution)/shard_map/ppermute | solution.py:396
  20.9 8.8 %collective-permute-start.7 = (bf16[528,256]{1,0:T(8,128)(2,1)S(1)}, bf16[528,256]{1,0:T(8,128)(2,1)S(1)}, u32[]{:S(2)}, u32[]{:S(2)}) collective-permute-start(bf16[528,256]{1,0:T(8,128)(2,1)S(1)} %get-tuple-element.57.refs_3_.refs_4_), channel_id=1, source_target_pairs={{0,16},{32,48},{64,80},{96,112},{128,144},{160,176},{192,208},{224... | collective-permute-start | bytes 811016 | tf_op jit(solution)/shard_map/ppermute | solution.py:396
  30.4 3.4 %shard_map.162 = (bf16[256,768]{1,0:T(8,128)(2,1)S(1)}, f32[512,384]{1,0:T(8,128)S(1)}, bf16[768,768]{1,0:T(8,128)(2,1)S(1)}, bf16[384,512]{1,0:T(8,128)(2,1)S(1)}, bf16[768,512]{1,0:T(8,128)(2,1)S(1)}) custom-call(s32[1]{0:T(128)} %bitcast.3.odd, bf16[128,768]{1,0:T(8,128)(2,1)S(1)} %collective-permute-done.even_edge, ...), custom_call_target="tpu_custom_call" | custom-call | flops 6000000000 | bytes 1000000 | tf_op jit(solution)/shard_map/pallas_call | solution.py:464
  42.3 9.1 %collective-permute-done.4.refs_6_ = bf16[528,256]{1,0:T(8,128)(2,1)S(1)} collective-permute-done((bf16[528,256]{1,0:T(8,128)(2,1)S(1)}, bf16[528,256]{1,0:T(8,128)(2,1)S(1)}, u32[]{:S(2)}, u32[]{:S(2)}) %collective-permute-start.4) | collective-permute-done | bytes 270368 | tf_op jit(solution)/shard_map/ppermute | solution.py:396
  52.1 21.8 %collective-permute-start.9 = (bf16[528,256]{1,0:T(8,128)(2,1)S(1)}, bf16[528,256]{1,0:T(8,128)(2,1)S(1)}, u32[]{:S(2)}, u32[]{:S(2)}) collective-permute-start(bf16[528,256]{1,0:T(8,128)(2,1)S(1)} %collective-permute-done.8.refs_5_), channel_id=1, source_target_pairs={{0,16},{32,48},{64,80},{96,112},{128,144},{160,176},{192,208},{224... | collective-permute-start | bytes 811016 | tf_op jit(solution)/shard_map/ppermute | solution.py:396
  76.0 4.0 %collective-permute-done.9.refs_6_ = bf16[528,256]{1,0:T(8,128)(2,1)S(1)} collective-permute-done((bf16[528,256]{1,0:T(8,128)(2,1)S(1)}, bf16[528,256]{1,0:T(8,128)(2,1)S(1)}, u32[]{:S(2)}, u32[]{:S(2)}) %collective-permute-start.9) | collective-permute-done | bytes 270368 | tf_op jit(solution)/shard_map/ppermute | solution.py:396
  80.6 4.6 %collective-permute-start.6 = (bf16[528,256]{1,0:T(8,128)(2,1)S(1)}, bf16[528,256]{1,0:T(8,128)(2,1)S(1)}, u32[]{:S(2)}, u32[]{:S(2)}) collective-permute-start(bf16[528,256]{1,0:T(8,128)(2,1)S(1)} %collective-permute-done.5), channel_id=1, source_target_pairs={{0,16},{32,48},{64,80},{96,112},{128,144},{160,176},{192,208},{224... | collective-permute-start | bytes 811016 | tf_op jit(solution)/shard_map/ppermute | solution.py:396
  92.1 4.1 %shard_map.163 = (bf16[4,9,96,128]{3,2,1,0:T(8,128)(2,1)S(1)}, bf16[4,9,96,128]{3,2,1,0:T(8,128)(2,1)S(1)}, bf16[512,384]{1,0:T(8,128)(2,1)S(1)}, bf16[512,512]{1,0:T(8,128)(2,1)S(1)}) custom-call(s32[3]{0:T(128)S(1)} %pad_add_fusion.place, f32[512,256]{1,0:T(8,128)S(1)} %get-tuple-element.70.d_donor, f32[512,256]{1,0:T(8,128)S(1)} %get-tuple-element.71.d_accept, ...), custom_call_target="tpu_custom_call" | custom-call | flops 4000000000 | bytes 1000000 | tf_op jit(solution)/shard_map/pallas_call | solution.py:514
  96.2 5.5 %collective-permute-start.14 = (bf16[4,9,96,128]{3,2,1,0:T(8,128)(2,1)S(1)}, bf16[4,9,96,128]{3,2,1,0:T(8,128)(2,1)S(1)}, u32[]{:S(2)}, u32[]{:S(2)}) collective-permute-start(bf16[4,9,96,128]{3,2,1,0:T(8,128)(2,1)S(1)} %get-tuple-element.88), channel_id=1, source_target_pairs={{0,1},{1,0},{2,3},{3,2},{4,5},{5,4},{6,7},{7,6},{8,9},{9,8},{10,11... | collective-permute-start | bytes 2654216 | tf_op jit(solution)/shard_map/ppermute | solution.py:521
  104.4 2.7 %collective-permute-start.12 = (bf16[2,4,304,128]{3,2,1,0:T(8,128)(2,1)S(1)}, bf16[2,4,304,128]{3,2,1,0:T(8,128)(2,1)S(1)}, u32[]{:S(2)}, u32[]{:S(2)}) collective-permute-start(bf16[2,4,304,128]{3,2,1,0:T(8,128)(2,1)S(1)} %slice.80), channel_id=1, source_target_pairs={{0,128},{128,0},{256,384},{384,256},{1,129},{129,1},{257,385},{385... | collective-permute-start | bytes 1867784 | tf_op jit(solution)/shard_map/ppermute | solution.py:533
  107.3 7.8 %collective-permute-start.15 = (bf16[2,9,96,128]{3,2,1,0:T(8,128)(2,1)S(1)}, bf16[2,9,96,128]{3,2,1,0:T(8,128)(2,1)S(1)}, u32[]{:S(2)}, u32[]{:S(2)}) collective-permute-start(bf16[2,9,96,128]{3,2,1,0:T(8,128)(2,1)S(1)} %get-tuple-element.90), channel_id=1, source_target_pairs={{128,256},{256,128},{384,0},{0,384},{129,257},{257,129},{385,1},{1... | collective-permute-start | bytes 1327112 | tf_op jit(solution)/shard_map/ppermute | solution.py:537
  115.1 6.8 %collective-permute-done.12.received = bf16[2,4,304,128]{3,2,1,0:T(8,128)(2,1)S(1)} collective-permute-done((bf16[2,4,304,128]{3,2,1,0:T(8,128)(2,1)S(1)}, bf16[2,4,304,128]{3,2,1,0:T(8,128)(2,1)S(1)}, u32[]{:S(2)}, u32[]{:S(2)}) %collective-permute-start.12) | collective-permute-done | bytes 622624 | tf_op jit(solution)/shard_map/ppermute | solution.py:533
  122.1 7.4 %collective-permute-start.13 = (bf16[4,304,128]{2,1,0:T(8,128)(2,1)S(1)}, bf16[4,304,128]{2,1,0:T(8,128)(2,1)S(1)}, u32[]{:S(2)}, u32[]{:S(2)}) collective-permute-start(bf16[4,304,128]{2,1,0:T(8,128)(2,1)S(1)} %get-tuple-element.86), channel_id=1, source_target_pairs={{128,256},{256,128},{384,0},{0,384},{129,257},{257,129},{385,1},{1... | collective-permute-start | bytes 933896 | tf_op jit(solution)/shard_map/ppermute | solution.py:542
  132.1 4.5 %collective-permute-done.13.head_in = bf16[4,304,128]{2,1,0:T(8,128)(2,1)S(1)} collective-permute-done((bf16[4,304,128]{2,1,0:T(8,128)(2,1)S(1)}, bf16[4,304,128]{2,1,0:T(8,128)(2,1)S(1)}, u32[]{:S(2)}, u32[]{:S(2)}) %collective-permute-start.13) | collective-permute-done | bytes 311328 | tf_op jit(solution)/shard_map/ppermute | solution.py:542
  137.6 17.8 %all_to_all.15.parts = bf16[4,528,128]{2,1,0:T(8,128)(2,1)S(1)} all-to-all(bf16[4,528,128]{2,1,0:T(8,128)(2,1)S(1)} %shard_map.168), channel_id=1, replica_groups=mesh['y'=4,'zb'=2,'zq'=4,'zhi'=2,'x'=4,'core'=2] {'zq'}, dimensions={0} | all-to-all | bytes 1081344 | tf_op jit(solution)/shard_map/all_to_all | solution.py:400
  156.3 9.9 %all-to-all-start.1 = ((bf16[4,112,128]{2,1,0:T(8,128)(2,1)}), bf16[4,112,128]{2,1,0:T(8,128)(2,1)S(1)}, u32[]{:S(2)}, u32[]{:S(2)}) async-start(bf16[4,112,128]{2,1,0:T(8,128)(2,1)} %get-tuple-element.94), calls=%async_computation.1 | async-start | bytes 229376 | tf_op jit(solution)/shard_map/all_to_all | solution.py:400
  166.2 7.3 %collective-permute-start.17 = (bf16[304,128]{1,0:T(8,128)(2,1)S(1)}, bf16[304,128]{1,0:T(8,128)(2,1)S(1)}, u32[]{:S(2)}, u32[]{:S(2)}) collective-permute-start(bf16[304,128]{1,0:T(8,128)(2,1)S(1)} %get-tuple-element.93.sent), channel_id=1, source_target_pairs={{0,64},{64,0},{1,65},{65,1},{2,66},{66,2},{3,67},{67,3},{4,68},{68... | collective-permute-start | bytes 233480 | tf_op jit(solution)/shard_map/ppermute | solution.py:553
  173.4 11.3 %collective-permute-done.17.received = bf16[304,128]{1,0:T(8,128)(2,1)S(1)} collective-permute-done((bf16[304,128]{1,0:T(8,128)(2,1)S(1)}, bf16[304,128]{1,0:T(8,128)(2,1)S(1)}, u32[]{:S(2)}, u32[]{:S(2)}) %collective-permute-start.17) | collective-permute-done | bytes 77856 | tf_op jit(solution)/shard_map/ppermute | solution.py:553
  185.5 3.5 %all-to-all-start.2 = ((bf16[4,304,128]{2,1,0:T(8,128)(2,1)}), bf16[4,304,128]{2,1,0:T(8,128)(2,1)S(1)}, u32[]{:S(2)}, u32[]{:S(2)}) async-start(bf16[4,304,128]{2,1,0:T(8,128)(2,1)} %get-tuple-element.95), calls=%async_computation.2 | async-start | bytes 622592 | tf_op jit(solution)/shard_map/all_to_all | solution.py:400
  190.9 5.7 %collective-permute-start.19 = (bf16[112,128]{1,0:T(8,128)(2,1)S(1)}, bf16[112,128]{1,0:T(8,128)(2,1)S(1)}, u32[]{:S(2)}, u32[]{:S(2)}) collective-permute-start(bf16[112,128]{1,0:T(8,128)(2,1)S(1)} %get-tuple-element.96.own), channel_id=1, source_target_pairs={{0,4},{2,6},{4,0},{6,2},{1,5},{3,7},{5,1},{7,3},{8,12},{10,14},{12... | collective-permute-start | bytes 86024 | tf_op jit(solution)/shard_map/ppermute | solution.py:562
  196.6 4.0 %collective-permute-start.20 = (bf16[112,128]{1,0:T(8,128)(2,1)S(1)}, bf16[112,128]{1,0:T(8,128)(2,1)S(1)}, u32[]{:S(2)}, u32[]{:S(2)}) collective-permute-start(bf16[112,128]{1,0:T(8,128)(2,1)S(1)} %get-tuple-element.96.own), channel_id=1, source_target_pairs={{0,6},{2,0},{4,2},{6,4},{1,7},{3,1},{5,3},{7,5},{8,14},{10,8},{12,... | collective-permute-start | bytes 86024 | tf_op jit(solution)/shard_map/ppermute | solution.py:562
  203.5 4.6 %collective-permute-start.23 = (bf16[1216,128]{1,0:T(8,128)(2,1)S(1)}, bf16[1216,128]{1,0:T(8,128)(2,1)S(1)}, u32[]{:S(2)}, u32[]{:S(2)}) collective-permute-start(bf16[1216,128]{1,0:T(8,128)(2,1)S(1)} %bitcast.26), channel_id=1, source_target_pairs={{128,0},{256,128},{384,256},{0,384},{129,1},{257,129},{385,257},{1... | collective-permute-start | bytes 933896 | tf_op jit(solution)/shard_map/ppermute | solution.py:570
  208.1 4.6 %collective-permute-start.21 = (f32[112,128]{1,0:T(8,128)S(1)}, f32[112,128]{1,0:T(8,128)S(1)}, u32[]{:S(2)}, u32[]{:S(2)}) collective-permute-start(f32[112,128]{1,0:T(8,128)S(1)} %shard_map.171), channel_id=1, source_target_pairs={{0,1},{1,0},{2,3},{3,2},{4,5},{5,4},{6,7},{7,6},{8,9},{9,8},{10,11... | collective-permute-start | bytes 172040 | tf_op jit(solution)/shard_map/ppermute | solution.py:566
  214.7 4.6 %collective-permute-start.25 = (bf16[608,128]{1,0:T(8,128)(2,1)S(1)}, bf16[608,128]{1,0:T(8,128)(2,1)S(1)}, u32[]{:S(2)}, u32[]{:S(2)}) collective-permute-start(bf16[608,128]{1,0:T(8,128)(2,1)S(1)} %slice.82), channel_id=1, source_target_pairs={{128,0},{256,128},{384,256},{0,384},{129,1},{257,129},{385,257},{1... | collective-permute-start | bytes 466952 | tf_op jit(solution)/shard_map/ppermute | solution.py:572
  (107 shorter events, 50.8 us)
Async XLA Ops:
  2.5 13.3 %collective-permute-start.1 = (bf16[128,768]{1,0:T(8,128)(2,1)}, bf16[128,768]{1,0:T(8,128)(2,1)S(1)}, u32[]{:S(2)}, u32[]{:S(2)}) collective-permute-start(bf16[128,768]{1,0:T(8,128)(2,1)} %get-tuple-element.104), channel_id=1, source_target_pairs={{16,32},{48,64},{80,96},{112,128},{144,160},{176,192},{208,224},{2... | collective-permute-start | bytes 589832 | tf_op jit(solution)/shard_map/ppermute | solution.py:396
  3.1 12.9 %collective-permute-start = (bf16[128,768]{1,0:T(8,128)(2,1)S(1)}, bf16[128,768]{1,0:T(8,128)(2,1)S(1)}, u32[]{:S(2)}, u32[]{:S(2)}) collective-permute-start(bf16[128,768]{1,0:T(8,128)(2,1)S(1)} %get-tuple-element.105), channel_id=1, source_target_pairs={{0,16},{32,48},{64,80},{96,112},{128,144},{160,176},{192,208},{224... | collective-permute-start | bytes 589832 | tf_op jit(solution)/shard_map/ppermute | solution.py:396
  20.2 15.1 %collective-permute-start.3 = (bf16[528,256]{1,0:T(8,128)(2,1)S(1)}, bf16[528,256]{1,0:T(8,128)(2,1)S(1)}, u32[]{:S(2)}, u32[]{:S(2)}) collective-permute-start(bf16[528,256]{1,0:T(8,128)(2,1)S(1)} %get-tuple-element.56.refs_2_.refs_3_), channel_id=1, source_target_pairs={{16,32},{48,64},{80,96},{112,128},{144,160},{176,192},{208,224},{2... | collective-permute-start | bytes 811016 | tf_op jit(solution)/shard_map/ppermute | solution.py:396
  20.9 16.7 %collective-permute-start.7 = (bf16[528,256]{1,0:T(8,128)(2,1)S(1)}, bf16[528,256]{1,0:T(8,128)(2,1)S(1)}, u32[]{:S(2)}, u32[]{:S(2)}) collective-permute-start(bf16[528,256]{1,0:T(8,128)(2,1)S(1)} %get-tuple-element.57.refs_3_.refs_4_), channel_id=1, source_target_pairs={{0,16},{32,48},{64,80},{96,112},{128,144},{160,176},{192,208},{224... | collective-permute-start | bytes 811016 | tf_op jit(solution)/shard_map/ppermute | solution.py:396
  29.7 8.6 %collective-permute-start.2 = (bf16[528,256]{1,0:T(8,128)(2,1)S(1)}, bf16[528,256]{1,0:T(8,128)(2,1)S(1)}, u32[]{:S(2)}, u32[]{:S(2)}) collective-permute-start(bf16[528,256]{1,0:T(8,128)(2,1)S(1)} %broadcast_select_fusion.2), channel_id=1, source_target_pairs={{160,96},{176,112},{288,224},{304,240},{416,352},{432,368},{64,128... | collective-permute-start | bytes 811016 | tf_op jit(solution)/shard_map/ppermute | solution.py:483
  35.3 16.2 %collective-permute-start.4 = (bf16[528,256]{1,0:T(8,128)(2,1)S(1)}, bf16[528,256]{1,0:T(8,128)(2,1)S(1)}, u32[]{:S(2)}, u32[]{:S(2)}) collective-permute-start(bf16[528,256]{1,0:T(8,128)(2,1)S(1)} %collective-permute-done.3.refs_5_), channel_id=1, source_target_pairs={{0,16},{32,48},{64,80},{96,112},{128,144},{160,176},{192,208},{224... | collective-permute-start | bytes 811016 | tf_op jit(solution)/shard_map/ppermute | solution.py:396
  37.6 14.5 %collective-permute-start.8 = (bf16[528,256]{1,0:T(8,128)(2,1)S(1)}, bf16[528,256]{1,0:T(8,128)(2,1)S(1)}, u32[]{:S(2)}, u32[]{:S(2)}) collective-permute-start(bf16[528,256]{1,0:T(8,128)(2,1)S(1)} %collective-permute-done.7.refs_6_), channel_id=1, source_target_pairs={{16,32},{48,64},{80,96},{112,128},{144,160},{176,192},{208,224},{2... | collective-permute-start | bytes 811016 | tf_op jit(solution)/shard_map/ppermute | solution.py:396
  38.3 46.9 %collective-permute-start.11 = (bf16[528,256]{1,0:T(8,128)(2,1)S(1)}, bf16[528,256]{1,0:T(8,128)(2,1)S(1)}, u32[]{:S(2)}, u32[]{:S(2)}) collective-permute-start(bf16[528,256]{1,0:T(8,128)(2,1)S(1)} %collective-permute-done.2), channel_id=1, source_target_pairs={{96,112},{224,240},{352,368},{480,496},{16,0},{144,128},{272,256},... | collective-permute-start | bytes 811016 | tf_op jit(solution)/shard_map/ppermute | solution.py:484
  51.4 29.2 %collective-permute-start.5 = (bf16[528,256]{1,0:T(8,128)(2,1)S(1)}, bf16[528,256]{1,0:T(8,128)(2,1)S(1)}, u32[]{:S(2)}, u32[]{:S(2)}) collective-permute-start(bf16[528,256]{1,0:T(8,128)(2,1)S(1)} %collective-permute-done.4.refs_6_), channel_id=1, source_target_pairs={{16,32},{48,64},{80,96},{144,160},{176,192},{208,224},{272,288},{3... | collective-permute-start | bytes 811016 | tf_op jit(solution)/shard_map/ppermute | solution.py:396
  52.1 27.8 %collective-permute-start.9 = (bf16[528,256]{1,0:T(8,128)(2,1)S(1)}, bf16[528,256]{1,0:T(8,128)(2,1)S(1)}, u32[]{:S(2)}, u32[]{:S(2)}) collective-permute-start(bf16[528,256]{1,0:T(8,128)(2,1)S(1)} %collective-permute-done.8.refs_5_), channel_id=1, source_target_pairs={{0,16},{32,48},{64,80},{96,112},{128,144},{160,176},{192,208},{224... | collective-permute-start | bytes 811016 | tf_op jit(solution)/shard_map/ppermute | solution.py:396
  80.6 9.7 %collective-permute-start.6 = (bf16[528,256]{1,0:T(8,128)(2,1)S(1)}, bf16[528,256]{1,0:T(8,128)(2,1)S(1)}, u32[]{:S(2)}, u32[]{:S(2)}) collective-permute-start(bf16[528,256]{1,0:T(8,128)(2,1)S(1)} %collective-permute-done.5), channel_id=1, source_target_pairs={{0,16},{32,48},{64,80},{96,112},{128,144},{160,176},{192,208},{224... | collective-permute-start | bytes 811016 | tf_op jit(solution)/shard_map/ppermute | solution.py:396
  96.2 10.9 %collective-permute-start.14 = (bf16[4,9,96,128]{3,2,1,0:T(8,128)(2,1)S(1)}, bf16[4,9,96,128]{3,2,1,0:T(8,128)(2,1)S(1)}, u32[]{:S(2)}, u32[]{:S(2)}) collective-permute-start(bf16[4,9,96,128]{3,2,1,0:T(8,128)(2,1)S(1)} %get-tuple-element.88), channel_id=1, source_target_pairs={{0,1},{1,0},{2,3},{3,2},{4,5},{5,4},{6,7},{7,6},{8,9},{9,8},{10,11... | collective-permute-start | bytes 2654216 | tf_op jit(solution)/shard_map/ppermute | solution.py:521
  104.4 17.5 %collective-permute-start.12 = (bf16[2,4,304,128]{3,2,1,0:T(8,128)(2,1)S(1)}, bf16[2,4,304,128]{3,2,1,0:T(8,128)(2,1)S(1)}, u32[]{:S(2)}, u32[]{:S(2)}) collective-permute-start(bf16[2,4,304,128]{3,2,1,0:T(8,128)(2,1)S(1)} %slice.80), channel_id=1, source_target_pairs={{0,128},{128,0},{256,384},{384,256},{1,129},{129,1},{257,385},{385... | collective-permute-start | bytes 1867784 | tf_op jit(solution)/shard_map/ppermute | solution.py:533
  107.3 22.1 %collective-permute-start.15 = (bf16[2,9,96,128]{3,2,1,0:T(8,128)(2,1)S(1)}, bf16[2,9,96,128]{3,2,1,0:T(8,128)(2,1)S(1)}, u32[]{:S(2)}, u32[]{:S(2)}) collective-permute-start(bf16[2,9,96,128]{3,2,1,0:T(8,128)(2,1)S(1)} %get-tuple-element.90), channel_id=1, source_target_pairs={{128,256},{256,128},{384,0},{0,384},{129,257},{257,129},{385,1},{1... | collective-permute-start | bytes 1327112 | tf_op jit(solution)/shard_map/ppermute | solution.py:537
  122.1 14.5 %collective-permute-start.13 = (bf16[4,304,128]{2,1,0:T(8,128)(2,1)S(1)}, bf16[4,304,128]{2,1,0:T(8,128)(2,1)S(1)}, u32[]{:S(2)}, u32[]{:S(2)}) collective-permute-start(bf16[4,304,128]{2,1,0:T(8,128)(2,1)S(1)} %get-tuple-element.86), channel_id=1, source_target_pairs={{128,256},{256,128},{384,0},{0,384},{129,257},{257,129},{385,1},{1... | collective-permute-start | bytes 933896 | tf_op jit(solution)/shard_map/ppermute | solution.py:542
  129.5 8.0 %collective-permute-start.16 = (bf16[9,96,128]{2,1,0:T(8,128)(2,1)S(1)}, bf16[9,96,128]{2,1,0:T(8,128)(2,1)S(1)}, u32[]{:S(2)}, u32[]{:S(2)}) collective-permute-start(bf16[9,96,128]{2,1,0:T(8,128)(2,1)S(1)} %get-tuple-element.92), channel_id=1, source_target_pairs={{0,128},{128,0},{256,384},{384,256},{1,129},{129,1},{257,385},{385... | collective-permute-start | bytes 663560 | tf_op jit(solution)/shard_map/ppermute | solution.py:543
  156.3 28.5 %all-to-all-start.1 = ((bf16[4,112,128]{2,1,0:T(8,128)(2,1)}), bf16[4,112,128]{2,1,0:T(8,128)(2,1)S(1)}, u32[]{:S(2)}, u32[]{:S(2)}) async-start(bf16[4,112,128]{2,1,0:T(8,128)(2,1)} %get-tuple-element.94), calls=%async_computation.1 | async-start | bytes 229376 | tf_op jit(solution)/shard_map/all_to_all | solution.py:400
  166.2 18.6 %collective-permute-start.17 = (bf16[304,128]{1,0:T(8,128)(2,1)S(1)}, bf16[304,128]{1,0:T(8,128)(2,1)S(1)}, u32[]{:S(2)}, u32[]{:S(2)}) collective-permute-start(bf16[304,128]{1,0:T(8,128)(2,1)S(1)} %get-tuple-element.93.sent), channel_id=1, source_target_pairs={{0,64},{64,0},{1,65},{65,1},{2,66},{66,2},{3,67},{67,3},{4,68},{68... | collective-permute-start | bytes 233480 | tf_op jit(solution)/shard_map/ppermute | solution.py:553
  185.5 16.1 %all-to-all-start.2 = ((bf16[4,304,128]{2,1,0:T(8,128)(2,1)}), bf16[4,304,128]{2,1,0:T(8,128)(2,1)S(1)}, u32[]{:S(2)}, u32[]{:S(2)}) async-start(bf16[4,304,128]{2,1,0:T(8,128)(2,1)} %get-tuple-element.95), calls=%async_computation.2 | async-start | bytes 622592 | tf_op jit(solution)/shard_map/all_to_all | solution.py:400
  188.9 11.6 %collective-permute-start.18 = (bf16[112,128]{1,0:T(8,128)(2,1)S(1)}, bf16[112,128]{1,0:T(8,128)(2,1)S(1)}, u32[]{:S(2)}, u32[]{:S(2)}) collective-permute-start(bf16[112,128]{1,0:T(8,128)(2,1)S(1)} %get-tuple-element.96.own), channel_id=1, source_target_pairs={{0,2},{2,4},{4,6},{6,0},{1,3},{3,5},{5,7},{7,1},{8,10},{10,12},{12... | collective-permute-start | bytes 86024 | tf_op jit(solution)/shard_map/ppermute | solution.py:562
  190.9 9.7 %collective-permute-start.19 = (bf16[112,128]{1,0:T(8,128)(2,1)S(1)}, bf16[112,128]{1,0:T(8,128)(2,1)S(1)}, u32[]{:S(2)}, u32[]{:S(2)}) collective-permute-start(bf16[112,128]{1,0:T(8,128)(2,1)S(1)} %get-tuple-element.96.own), channel_id=1, source_target_pairs={{0,4},{2,6},{4,0},{6,2},{1,5},{3,7},{5,1},{7,3},{8,12},{10,14},{12... | collective-permute-start | bytes 86024 | tf_op jit(solution)/shard_map/ppermute | solution.py:562
  201.6 11.1 %collective-permute-start.22 = (bf16[1216,128]{1,0:T(8,128)(2,1)S(1)}, bf16[1216,128]{1,0:T(8,128)(2,1)S(1)}, u32[]{:S(2)}, u32[]{:S(2)}) collective-permute-start(bf16[1216,128]{1,0:T(8,128)(2,1)S(1)} %bitcast.25), channel_id=1, source_target_pairs={{0,128},{128,256},{256,384},{384,0},{1,129},{129,257},{257,385},{3... | collective-permute-start | bytes 933896 | tf_op jit(solution)/shard_map/ppermute | solution.py:569
  203.5 11.2 %collective-permute-start.23 = (bf16[1216,128]{1,0:T(8,128)(2,1)S(1)}, bf16[1216,128]{1,0:T(8,128)(2,1)S(1)}, u32[]{:S(2)}, u32[]{:S(2)}) collective-permute-start(bf16[1216,128]{1,0:T(8,128)(2,1)S(1)} %bitcast.26), channel_id=1, source_target_pairs={{128,0},{256,128},{384,256},{0,384},{129,1},{257,129},{385,257},{1... | collective-permute-start | bytes 933896 | tf_op jit(solution)/shard_map/ppermute | solution.py:570
  208.1 11.2 %collective-permute-start.21 = (f32[112,128]{1,0:T(8,128)S(1)}, f32[112,128]{1,0:T(8,128)S(1)}, u32[]{:S(2)}, u32[]{:S(2)}) collective-permute-start(f32[112,128]{1,0:T(8,128)S(1)} %shard_map.171), channel_id=1, source_target_pairs={{0,1},{1,0},{2,3},{3,2},{4,5},{5,4},{6,7},{7,6},{8,9},{9,8},{10,11... | collective-permute-start | bytes 172040 | tf_op jit(solution)/shard_map/ppermute | solution.py:566
  (17 other events, 108.6 us)

commit v9 on v6

--- a/solution.py
+++ b/solution.py
@@ -74,17 +74,21 @@
         factor[here, :] = (slope * unit).astype(BF16)
 
 
+def edge_kernel(edge, gain, hidden):
+    v = edge[...].astype(F32)
+    hidden[...] = gelu(v * rms(v) * gain[...]).astype(BF16)
+
+
 def forward_kernel(
-    odd, tok, mine, even_edge, odd_edge, gain, taps, point, donor_w, accept_w, meta,
-    hidden, conv_out, act_out, embed_out, even_feat, odd_feat, wide_feat,
+    odd, tok, mine, even_edge, odd_hidden, gain, taps, point, donor_w, accept_w, meta,
+    hidden, conv_out, act_out, embed_out, even_feat, odd_feat,
 ):
     rows = tok.shape[0]
     is_odd = odd[0] > 0
-    low = jnp.where(is_odd, even_edge[...], odd_edge[...])
-    high = jnp.where(is_odd, odd_edge[...], even_edge[...])
-    for edge, at in ((low, 0), (high, STEP + rows)):
-        v = edge.astype(F32)
-        hidden[pl.ds(at, STEP), :] = gelu(v * rms(v) * gain[...]).astype(BF16)
+    v = even_edge[...].astype(F32)
+    even_hidden = gelu(v * rms(v) * gain[...]).astype(BF16)
+    hidden[pl.ds(0, STEP), :] = jnp.where(is_odd, even_hidden, odd_hidden[...])
+    hidden[pl.ds(STEP + rows, STEP), :] = jnp.where(is_odd, odd_hidden[...], even_hidden)
     hidden[pl.ds(STEP, rows), :] = mine[...]
 
     conv = dot(hidden[:rows, :], taps[0])
@@ -99,10 +103,8 @@
     accept = dot(embed, accept_w[...]).astype(BF16)
     even_feat[:rows, :] = jnp.where(is_odd, donor, accept)
     odd_feat[:rows, :] = jnp.where(is_odd, accept, donor)
-    wide_feat[:rows, :] = jnp.where(odd[1] < 4, accept, donor)
     even_feat[pl.ds(rows, SLOTS), :] = meta[...]
     odd_feat[pl.ds(rows, SLOTS), :] = meta[...]
-    wide_feat[pl.ds(rows, SLOTS), :] = meta[...]
 
 
 def side_kernel(
@@ -126,6 +128,10 @@
     embed_t[...] = dot_t(eye[...], embed[...]).astype(BF16)
     inner = act.shape[1]
     act_t[...] = dot_t(eye[:inner, :inner], act[...]).astype(BF16)
+
+
+def copy_kernel(source, target):
+    target[...] = source[...]
 
 
 def pair_kernel(distance, *refs):
@@ -413,9 +419,9 @@
     blocks = rows // PANEL
     shape = jax.ShapeDtypeStruct
     here = lax.axis_index(SEQ)
-    line = here % 8
-    odd = jnp.stack([here % 2, line]).astype(jnp.int32)
-    is_odd = odd[0] > 0
+    line = lax.axis_index(("zb", "zq"))
+    is_odd = (lax.axis_index("zq") & 1) > 0
+    odd = is_odd.astype(jnp.int32)[None]
     start, end = tokens[:STEP], tokens[rows - STEP :]
     even_edge = swapped(jnp.where(is_odd, start, end), 0)
     odd_edge = swapped(jnp.where(is_odd, end, start), 1)
@@ -439,8 +445,9 @@
     mine, factor = call(
         own_kernel, [shape((rows, channels), BF16)] * 2, [VM] * 2, 12, 2_000_000_000
     )(tokens, gain)
+    (odd_hidden,) = call(edge_kernel, [shape((STEP, channels), BF16)], [VM] * 2, 8, 2_000_000_000)(odd_edge, gain)
     feat = shape((rows + SLOTS, heads), BF16)
-    hidden, conv, act, embed, even_feat, odd_feat, wide_feat = call(
+    hidden, conv, act, embed, even_feat, odd_feat = call(
         forward_kernel,
         [
             shape((rows + 2 * STEP, channels), BF16),
@@ -449,20 +456,19 @@
             shape((rows, channels), BF16),
             feat,
             feat,
-            feat,
         ],
         [SM] + [VM] * 10,
         20,
         4_000_000_000,
     )(
-        odd, tokens, mine, even_edge, odd_edge, gain, dilated_tap_weight, point_weight,
+        odd, tokens, mine, even_edge, odd_hidden, gain, dilated_tap_weight, point_weight,
         donor_weight, acceptor_weight, meta_rows,
     )
 
     acc_shapes = [shape((rows, heads), F32), shape((rows, heads), F32), shape((PANEL, PANEL), F32)]
     acc = call(
         lambda *refs: pair_kernel(0, *refs), acc_shapes, [SM] * 2 + [VM] * 2, 12, 2_000_000_000
-    )(1 - odd[:1], meta, even_feat, odd_feat)
+    )(1 - odd, meta, even_feat, odd_feat)
     edge_factor, slope, hidden_t, act_t, embed_t = call(
         side_kernel,
         [
@@ -481,6 +487,7 @@
     wide_pairs = [(i + k, i - 4 + k) for i in starts if i > 0 for k in (2, 3)]
     wide_pairs += [(i + k, i + 4 + k) for i in starts if i + 8 < count for k in (4, 5)]
     relay_pairs = [(i + 6, i + 7) for i in starts] + [(i + 1, i) for i in starts]
+    wide_feat = jnp.where((line == 2) | (line == 5), even_feat, odd_feat)
     wide = lax.ppermute(wide_feat, SEQ, wide_pairs)
     relay = lax.ppermute(wide, SEQ, relay_pairs)
     at_end = (line == 0) | (line == 7)
@@ -489,6 +496,7 @@
     for distance in range(1, SPAN + 1):
         if distance == 1:
             short_far, long_far = swapped(odd_feat, 0), swapped(even_feat, 1)
+            (short_far,) = call(copy_kernel, [feat], [VM], 4, 2000000000)(short_far)
         else:
             short_far, long_far = swapped(long_far, 0), swapped(short_far, 1, distance <= 2)
         short_use, long_use = short_far, long_far
@@ -497,14 +505,14 @@
         if distance == 4:
             short_use = jnp.where(near_end, wide, short_far)
             long_use = jnp.where(at_end, wide, long_far)
-        far_meta = jnp.where(odd[0] > 0, short_use[rows:, :8], long_use[rows:, :8]).astype(jnp.int32)
+        far_meta = jnp.where(is_odd, short_use[rows:, :8], long_use[rows:, :8]).astype(jnp.int32)
         acc = call(
             lambda *refs, distance=distance: pair_kernel(distance, *refs),
             acc_shapes,
             [SM] * 3 + [VM] * 7,
             12,
             2_500_000_000,
-        )(1 - odd[:1], meta, far_meta, even_feat, odd_feat, long_use, short_use, *acc)
+        )(1 - odd, meta, far_meta, even_feat, odd_feat, long_use, short_use, *acc)
 
     chunk = CHUNK_ROWS + EXTRA_ROWS
     lanes = inner // 128

time: 225 us -> 229 us (1.018)
  starting transfers between devices: 133 us -> 125 us
  waiting for transfers between devices: 37.7 us -> 44.6 us
  local copies, waits for them, and re-layouts: 1.19 us -> 4.73 us
    ppermute x10, waiting for transfers between devices: 11.3 us -> 15.6 us  [swapped(): return lax.ppermute(block, SEQ, pairs + [(j, i) for i, j in pairs])]
    ppermute x1, starting transfers between devices: 6.83 us -> 2.64 us  [on_device(): received = lax.ppermute(send, 'core', [(0, 1), (1, 0)])]
    ppermute x1, starting transfers between devices: 8.68 us -> 4.91 us  [on_device(): other = lax.ppermute(head_sum[2:], 'y', first_pairs)]
    unnamed x20 -> x28, local copies, waits for them, and re-layouts: 0.21 us -> 3.76 us
    ppermute x1, waiting for transfers between devices: 7.92 us -> 10.8 us  [on_device(): other = lax.ppermute(head_sum[2:], 'y', first_pairs)]
    ppermute x1, starting transfers between devices: 6.24 us -> 3.32 us  [on_device(): other = lax.ppermute(conv_send, 'y', second_pairs)]
    ppermute x10, starting transfers between devices: 49.9 us -> 52.6 us  [swapped(): return lax.ppermute(block, SEQ, pairs + [(j, i) for i, j in pairs])]
    pallas_call x4, Pallas kernels: 7.31 us -> 9.69 us  [on_device(): call(lambda *refs, distance=distance: pair_kernel(distance, *refs), acc_s...]
  transfers between devices with their start and end apart: 29 -> 29, of which waited for: 10 -> 11; matrix products, arithmetic and copies ran while one was open for 1% -> 1% of each run, Pallas kernels for 8% -> 7%
where the time goes in v9:
time: 229 us; the launch traced here: 227 us
  starting transfers between devices  125 us (55%)
  waiting for transfers between devices  44.6 us (19%)
  Pallas kernels  30.6 us (13%)
  blocking collectives  18.3 us (8%)
  local copies, waits for them, and re-layouts  4.73 us (2%)
    ppermute x10, starting transfers between devices, swapped(): return lax.ppermute(block, SEQ, pairs + [(j, i) for i, j in pairs])  52.6 us
    all_to_all x1, blocking collectives, swap_parts(): return lax.all_to_all(parts, axis, 0, 0, tiled=True)  18.3 us
    ppermute x10, waiting for transfers between devices, swapped(): return lax.ppermute(block, SEQ, pairs + [(j, i) for i, j in pairs])  15.6 us
    ppermute x1, waiting for transfers between devices, on_device(): other = lax.ppermute(head_sum[2:], 'y', first_pairs)  10.8 us
    ppermute x3, starting transfers between devices, on_device(): lax.ppermute(conv_sum, 'x', [(i, (i + step) % 4) for i in range(4)])  10.5 us
    pallas_call x4, Pallas kernels, on_device(): call(lambda *refs, distance=distance: pair_kernel(distance, *refs), acc_s...  9.69 us
    ppermute x1, starting transfers between devices, on_device(): lax.ppermute(sent[chunk:], ('zb', 'zhi'), [(0, 3), (3, 0), (1, 2), (2, 1)])  9.43 us
    ppermute x1, waiting for transfers between devices, on_device(): across = lax.ppermute(mine, 'zhi', [(0, 1), (1, 0)])  8.21 us
  transfers between devices with their start and end apart: 29, of which 11 were waited for; matrix products, arithmetic and copies ran while one was open for 1% of the time, Pallas kernels for 7%

profile of v9, /device:TPU:1, one launch (start us, length us, event | category | flops | bytes accessed | tf_op | source)
XLA Modules:
  0.0 227.1 jit_solution(16687297978137712241)
XLA Ops:
  3.1 7.2 %collective-permute-start = (bf16[128,768]{1,0:T(8,128)(2,1)S(1)}, bf16[128,768]{1,0:T(8,128)(2,1)S(1)}, u32[]{:S(2)}, u32[]{:S(2)}) collective-permute-start(bf16[128,768]{1,0:T(8,128)(2,1)S(1)} %get-tuple-element.105), channel_id=1, source_target_pairs={{0,16},{32,48},{64,80},{96,112},{128,144},{160,176},{192,208},{224... | collective-permute-start | bytes 589832 | tf_op jit(solution)/shard_map/ppermute | solution.py:404
  22.8 3.4 %shard_map.163 = (bf16[256,768]{1,0:T(8,128)(2,1)S(1)}, f32[512,384]{1,0:T(8,128)S(1)}, bf16[768,768]{1,0:T(8,128)(2,1)S(1)}, bf16[384,512]{1,0:T(8,128)(2,1)S(1)}, bf16[768,512]{1,0:T(8,128)(2,1)S(1)}) custom-call(s32[1]{0:T(128)} %bitcast.3.odd, bf16[128,768]{1,0:T(8,128)(2,1)S(1)} %collective-permute-done.even_edge, ...), custom_call_target="tpu_custom_call" | custom-call | flops 6000000000 | bytes 1000000 | tf_op jit(solution)/shard_map/pallas_call | solution.py:472
  29.2 11.6 %collective-permute-start.4 = (bf16[528,256]{1,0:T(8,128)(2,1)S(1)}, bf16[528,256]{1,0:T(8,128)(2,1)S(1)}, u32[]{:S(2)}, u32[]{:S(2)}) collective-permute-start(bf16[528,256]{1,0:T(8,128)(2,1)S(1)} %collective-permute-done.3.refs_5_), channel_id=1, source_target_pairs={{0,16},{32,48},{64,80},{96,112},{128,144},{160,176},{192,208},{224... | collective-permute-start | bytes 811016 | tf_op jit(solution)/shard_map/ppermute | solution.py:404
  44.1 8.0 %collective-permute-done.4.refs_6_ = bf16[528,256]{1,0:T(8,128)(2,1)S(1)} collective-permute-done((bf16[528,256]{1,0:T(8,128)(2,1)S(1)}, bf16[528,256]{1,0:T(8,128)(2,1)S(1)}, u32[]{:S(2)}, u32[]{:S(2)}) %collective-permute-start.4) | collective-permute-done | bytes 270368 | tf_op jit(solution)/shard_map/ppermute | solution.py:404
  52.8 23.9 %collective-permute-start.9 = (bf16[528,256]{1,0:T(8,128)(2,1)S(1)}, bf16[528,256]{1,0:T(8,128)(2,1)S(1)}, u32[]{:S(2)}, u32[]{:S(2)}) collective-permute-start(bf16[528,256]{1,0:T(8,128)(2,1)S(1)} %collective-permute-done.8.refs_5_), channel_id=1, source_target_pairs={{0,16},{32,48},{64,80},{96,112},{128,144},{160,176},{192,208},{224... | collective-permute-start | bytes 811016 | tf_op jit(solution)/shard_map/ppermute | solution.py:404
  78.1 4.7 %collective-permute-done.9.refs_6_ = bf16[528,256]{1,0:T(8,128)(2,1)S(1)} collective-permute-done((bf16[528,256]{1,0:T(8,128)(2,1)S(1)}, bf16[528,256]{1,0:T(8,128)(2,1)S(1)}, u32[]{:S(2)}, u32[]{:S(2)}) %collective-permute-start.9) | collective-permute-done | bytes 270368 | tf_op jit(solution)/shard_map/ppermute | solution.py:404
  83.5 4.6 %collective-permute-start.6 = (bf16[528,256]{1,0:T(8,128)(2,1)S(1)}, bf16[528,256]{1,0:T(8,128)(2,1)S(1)}, u32[]{:S(2)}, u32[]{:S(2)}) collective-permute-start(bf16[528,256]{1,0:T(8,128)(2,1)S(1)} %collective-permute-done.5), channel_id=1, source_target_pairs={{0,16},{32,48},{64,80},{96,112},{128,144},{160,176},{192,208},{224... | collective-permute-start | bytes 811016 | tf_op jit(solution)/shard_map/ppermute | solution.py:404
  93.3 4.0 %shard_map.162 = (f32[512,256]{1,0:T(8,128)S(1)}, f32[512,256]{1,0:T(8,128)S(1)}, f32[128,128]{1,0:T(8,128)S(1)}) custom-call(s32[1]{0:T(128)S(6)} %sub.26.refs_0_, s32[16,8]{1,0:T(8,128)S(1)} %stack.37.refs_1_, s32[16,8]{1,0:T(8,128)S(1)} %fusion.11.refs_2_, bf16[528,256]{1,0:T(8,128)(2,1)S(1)} %get-tuple-element.56.refs_2_.refs_3_, ...), custom_call_target="tpu_custom_call" | custom-call | flops 2500000000 | bytes 1000000 | tf_op jit(solution)/shard_map/pallas_call | solution.py:509
  97.4 4.1 %shard_map.164 = (bf16[4,9,96,128]{3,2,1,0:T(8,128)(2,1)S(1)}, bf16[4,9,96,128]{3,2,1,0:T(8,128)(2,1)S(1)}, bf16[512,384]{1,0:T(8,128)(2,1)S(1)}, bf16[512,512]{1,0:T(8,128)(2,1)S(1)}) custom-call(s32[3]{0:T(128)S(1)} %pad_add_fusion.place, f32[512,256]{1,0:T(8,128)S(1)} %get-tuple-element.70.d_donor, f32[512,256]{1,0:T(8,128)S(1)} %get-tuple-element.71.d_accept, ...), custom_call_target="tpu_custom_call" | custom-call | flops 4000000000 | bytes 1000000 | tf_op jit(solution)/shard_map/pallas_call | solution.py:523
  106.9 4.9 %collective-permute-start.12 = (bf16[2,4,304,128]{3,2,1,0:T(8,128)(2,1)S(1)}, bf16[2,4,304,128]{3,2,1,0:T(8,128)(2,1)S(1)}, u32[]{:S(2)}, u32[]{:S(2)}) collective-permute-start(bf16[2,4,304,128]{3,2,1,0:T(8,128)(2,1)S(1)} %slice.84), channel_id=1, source_target_pairs={{0,128},{128,0},{256,384},{384,256},{1,129},{129,1},{257,385},{385... | collective-permute-start | bytes 1867784 | tf_op jit(solution)/shard_map/ppermute | solution.py:542
  112.0 3.3 %collective-permute-start.15 = (bf16[2,9,96,128]{3,2,1,0:T(8,128)(2,1)S(1)}, bf16[2,9,96,128]{3,2,1,0:T(8,128)(2,1)S(1)}, u32[]{:S(2)}, u32[]{:S(2)}) collective-permute-start(bf16[2,9,96,128]{3,2,1,0:T(8,128)(2,1)S(1)} %get-tuple-element.90), channel_id=1, source_target_pairs={{128,256},{256,128},{384,0},{0,384},{129,257},{257,129},{385,1},{1... | collective-permute-start | bytes 1327112 | tf_op jit(solution)/shard_map/ppermute | solution.py:546
  115.4 10.8 %collective-permute-done.12.received = bf16[2,4,304,128]{3,2,1,0:T(8,128)(2,1)S(1)} collective-permute-done((bf16[2,4,304,128]{3,2,1,0:T(8,128)(2,1)S(1)}, bf16[2,4,304,128]{3,2,1,0:T(8,128)(2,1)S(1)}, u32[]{:S(2)}, u32[]{:S(2)}) %collective-permute-start.12) | collective-permute-done | bytes 622624 | tf_op jit(solution)/shard_map/ppermute | solution.py:542
  126.4 4.2 %collective-permute-start.13 = (bf16[4,304,128]{2,1,0:T(8,128)(2,1)S(1)}, bf16[4,304,128]{2,1,0:T(8,128)(2,1)S(1)}, u32[]{:S(2)}, u32[]{:S(2)}) collective-permute-start(bf16[4,304,128]{2,1,0:T(8,128)(2,1)S(1)} %get-tuple-element.86), channel_id=1, source_target_pairs={{128,256},{256,128},{384,0},{0,384},{129,257},{257,129},{385,1},{1... | collective-permute-start | bytes 933896 | tf_op jit(solution)/shard_map/ppermute | solution.py:551
  132.6 5.2 %collective-permute-done.13.head_in = bf16[4,304,128]{2,1,0:T(8,128)(2,1)S(1)} collective-permute-done((bf16[4,304,128]{2,1,0:T(8,128)(2,1)S(1)}, bf16[4,304,128]{2,1,0:T(8,128)(2,1)S(1)}, u32[]{:S(2)}, u32[]{:S(2)}) %collective-permute-start.13) | collective-permute-done | bytes 311328 | tf_op jit(solution)/shard_map/ppermute | solution.py:551
  138.1 18.3 %all_to_all.10.parts = bf16[4,528,128]{2,1,0:T(8,128)(2,1)S(1)} all-to-all(bf16[4,528,128]{2,1,0:T(8,128)(2,1)S(1)} %shard_map.169), channel_id=1, replica_groups=mesh['y'=4,'zb'=2,'zq'=4,'zhi'=2,'x'=4,'core'=2] {'zq'}, dimensions={0} | all-to-all | bytes 1081344 | tf_op jit(solution)/shard_map/all_to_all | solution.py:408
  157.2 4.4 %collective-permute-start.17 = (bf16[416,128]{1,0:T(8,128)(2,1)S(1)}, bf16[416,128]{1,0:T(8,128)(2,1)S(1)}, u32[]{:S(2)}, u32[]{:S(2)}) collective-permute-start(bf16[416,128]{1,0:T(8,128)(2,1)S(1)} %get-tuple-element.93.sent), channel_id=1, source_target_pairs={{0,64},{64,0},{1,65},{65,1},{2,66},{66,2},{3,67},{67,3},{4,68},{68... | collective-permute-start | bytes 319496 | tf_op jit(solution)/shard_map/ppermute | solution.py:563
  161.5 9.4 %collective-permute-start.19 = (bf16[112,128]{1,0:T(8,128)(2,1)S(1)}, bf16[112,128]{1,0:T(8,128)(2,1)S(1)}, u32[]{:S(2)}, u32[]{:S(2)}) collective-permute-start(bf16[112,128]{1,0:T(8,128)(2,1)S(1)} %slice.71), channel_id=1, source_target_pairs={{0,72},{72,0},{8,64},{64,8},{1,73},{73,1},{9,65},{65,9},{2,74},{74... | collective-permute-start | bytes 86024 | tf_op jit(solution)/shard_map/ppermute | solution.py:565
  171.0 5.1 %collective-permute-start.18 = (bf16[112,128]{1,0:T(8,128)(2,1)S(1)}, bf16[112,128]{1,0:T(8,128)(2,1)S(1)}, u32[]{:S(2)}, u32[]{:S(2)}) collective-permute-start(bf16[112,128]{1,0:T(8,128)(2,1)S(1)} %get-tuple-element.94.mine), channel_id=1, source_target_pairs={{0,8},{8,0},{1,9},{9,1},{2,10},{10,2},{3,11},{11,3},{4,12},{12,4},... | collective-permute-start | bytes 86024 | tf_op jit(solution)/shard_map/ppermute | solution.py:564
  176.1 8.2 %collective-permute-done.18.one = bf16[112,128]{1,0:T(8,128)(2,1)S(1)} collective-permute-done((bf16[112,128]{1,0:T(8,128)(2,1)S(1)}, bf16[112,128]{1,0:T(8,128)(2,1)S(1)}, u32[]{:S(2)}, u32[]{:S(2)}) %collective-permute-start.18) | collective-permute-done | bytes 28704 | tf_op jit(solution)/shard_map/ppermute | solution.py:564
  185.1 3.5 %all-to-all-start.1 = ((bf16[4,304,128]{2,1,0:T(8,128)(2,1)}), bf16[4,304,128]{2,1,0:T(8,128)(2,1)S(1)}, u32[]{:S(2)}, u32[]{:S(2)}) async-start(bf16[4,304,128]{2,1,0:T(8,128)(2,1)} %get-tuple-element.95), calls=%async_computation.1 | async-start | bytes 622592 | tf_op jit(solution)/shard_map/all_to_all | solution.py:408
  191.6 5.5 %collective-permute-start.21 = (bf16[112,128]{1,0:T(8,128)(2,1)S(1)}, bf16[112,128]{1,0:T(8,128)(2,1)S(1)}, u32[]{:S(2)}, u32[]{:S(2)}) collective-permute-start(bf16[112,128]{1,0:T(8,128)(2,1)S(1)} %get-tuple-element.96.own), channel_id=1, source_target_pairs={{0,4},{2,6},{4,0},{6,2},{1,5},{3,7},{5,1},{7,3},{8,12},{10,14},{12... | collective-permute-start | bytes 86024 | tf_op jit(solution)/shard_map/ppermute | solution.py:575
  204.3 4.5 %collective-permute-start.25 = (bf16[1216,128]{1,0:T(8,128)(2,1)S(1)}, bf16[1216,128]{1,0:T(8,128)(2,1)S(1)}, u32[]{:S(2)}, u32[]{:S(2)}) collective-permute-start(bf16[1216,128]{1,0:T(8,128)(2,1)S(1)} %bitcast.26), channel_id=1, source_target_pairs={{128,0},{256,128},{384,256},{0,384},{129,1},{257,129},{385,257},{1... | collective-permute-start | bytes 933896 | tf_op jit(solution)/shard_map/ppermute | solution.py:583
  208.8 7.3 %collective-permute-start.23 = (f32[112,128]{1,0:T(8,128)S(1)}, f32[112,128]{1,0:T(8,128)S(1)}, u32[]{:S(2)}, u32[]{:S(2)}) collective-permute-start(f32[112,128]{1,0:T(8,128)S(1)} %shard_map.172), channel_id=1, source_target_pairs={{0,1},{1,0},{2,3},{3,2},{4,5},{5,4},{6,7},{7,6},{8,9},{9,8},{10,11... | collective-permute-start | bytes 172040 | tf_op jit(solution)/shard_map/ppermute | solution.py:579
  218.0 4.6 %collective-permute-start.27 = (bf16[608,128]{1,0:T(8,128)(2,1)S(1)}, bf16[608,128]{1,0:T(8,128)(2,1)S(1)}, u32[]{:S(2)}, u32[]{:S(2)}) collective-permute-start(bf16[608,128]{1,0:T(8,128)(2,1)S(1)} %slice.86), channel_id=1, source_target_pairs={{128,0},{256,128},{384,256},{0,384},{129,1},{257,129},{385,257},{1... | collective-permute-start | bytes 466952 | tf_op jit(solution)/shard_map/ppermute | solution.py:585
  (111 shorter events, 54.2 us)
Async XLA Ops:
  2.5 13.3 %collective-permute-start.1 = (bf16[128,768]{1,0:T(8,128)(2,1)}, bf16[128,768]{1,0:T(8,128)(2,1)S(1)}, u32[]{:S(2)}, u32[]{:S(2)}) collective-permute-start(bf16[128,768]{1,0:T(8,128)(2,1)} %get-tuple-element.104), channel_id=1, source_target_pairs={{16,32},{48,64},{80,96},{112,128},{144,160},{176,192},{208,224},{2... | collective-permute-start | bytes 589832 | tf_op jit(solution)/shard_map/ppermute | solution.py:404
  3.1 12.9 %collective-permute-start = (bf16[128,768]{1,0:T(8,128)(2,1)S(1)}, bf16[128,768]{1,0:T(8,128)(2,1)S(1)}, u32[]{:S(2)}, u32[]{:S(2)}) collective-permute-start(bf16[128,768]{1,0:T(8,128)(2,1)S(1)} %get-tuple-element.105), channel_id=1, source_target_pairs={{0,16},{32,48},{64,80},{96,112},{128,144},{160,176},{192,208},{224... | collective-permute-start | bytes 589832 | tf_op jit(solution)/shard_map/ppermute | solution.py:404
  20.2 8.3 %collective-permute-start.7 = (bf16[528,256]{1,0:T(8,128)(2,1)S(1)}, bf16[528,256]{1,0:T(8,128)(2,1)S(1)}, u32[]{:S(2)}, u32[]{:S(2)}) collective-permute-start(bf16[528,256]{1,0:T(8,128)(2,1)S(1)} %get-tuple-element.57.refs_3_.refs_4_), channel_id=1, source_target_pairs={{0,16},{32,48},{64,80},{96,112},{128,144},{160,176},{192,208},{224... | collective-permute-start | bytes 811016 | tf_op jit(solution)/shard_map/ppermute | solution.py:404
  27.7 13.2 %collective-permute-start.2 = (bf16[528,256]{1,0:T(8,128)(2,1)S(1)}, bf16[528,256]{1,0:T(8,128)(2,1)S(1)}, u32[]{:S(2)}, u32[]{:S(2)}) collective-permute-start(bf16[528,256]{1,0:T(8,128)(2,1)S(1)} %broadcast_select_fusion.2), channel_id=1, source_target_pairs={{160,96},{176,112},{288,224},{304,240},{416,352},{432,368},{64,128... | collective-permute-start | bytes 811016 | tf_op jit(solution)/shard_map/ppermute | solution.py:491
  28.5 24.3 %collective-permute-start.8 = (bf16[528,256]{1,0:T(8,128)(2,1)S(1)}, bf16[528,256]{1,0:T(8,128)(2,1)S(1)}, u32[]{:S(2)}, u32[]{:S(2)}) collective-permute-start(bf16[528,256]{1,0:T(8,128)(2,1)S(1)} %shard_map.157.refs_6_), channel_id=1, source_target_pairs={{16,32},{48,64},{80,96},{112,128},{144,160},{176,192},{208,224},{2... | collective-permute-start | bytes 811016 | tf_op jit(solution)/shard_map/ppermute | solution.py:404
  29.2 22.9 %collective-permute-start.4 = (bf16[528,256]{1,0:T(8,128)(2,1)S(1)}, bf16[528,256]{1,0:T(8,128)(2,1)S(1)}, u32[]{:S(2)}, u32[]{:S(2)}) collective-permute-start(bf16[528,256]{1,0:T(8,128)(2,1)S(1)} %collective-permute-done.3.refs_5_), channel_id=1, source_target_pairs={{0,16},{32,48},{64,80},{96,112},{128,144},{160,176},{192,208},{224... | collective-permute-start | bytes 811016 | tf_op jit(solution)/shard_map/ppermute | solution.py:404
  40.8 47.3 %collective-permute-start.11 = (bf16[528,256]{1,0:T(8,128)(2,1)S(1)}, bf16[528,256]{1,0:T(8,128)(2,1)S(1)}, u32[]{:S(2)}, u32[]{:S(2)}) collective-permute-start(bf16[528,256]{1,0:T(8,128)(2,1)S(1)} %collective-permute-done.2), channel_id=1, source_target_pairs={{96,112},{224,240},{352,368},{480,496},{16,0},{144,128},{272,256},... | collective-permute-start | bytes 811016 | tf_op jit(solution)/shard_map/ppermute | solution.py:492
  52.1 31.4 %collective-permute-start.5 = (bf16[528,256]{1,0:T(8,128)(2,1)S(1)}, bf16[528,256]{1,0:T(8,128)(2,1)S(1)}, u32[]{:S(2)}, u32[]{:S(2)}) collective-permute-start(bf16[528,256]{1,0:T(8,128)(2,1)S(1)} %collective-permute-done.4.refs_6_), channel_id=1, source_target_pairs={{16,32},{48,64},{80,96},{144,160},{176,192},{208,224},{272,288},{3... | collective-permute-start | bytes 811016 | tf_op jit(solution)/shard_map/ppermute | solution.py:404
  52.8 30.0 %collective-permute-start.9 = (bf16[528,256]{1,0:T(8,128)(2,1)S(1)}, bf16[528,256]{1,0:T(8,128)(2,1)S(1)}, u32[]{:S(2)}, u32[]{:S(2)}) collective-permute-start(bf16[528,256]{1,0:T(8,128)(2,1)S(1)} %collective-permute-done.8.refs_5_), channel_id=1, source_target_pairs={{0,16},{32,48},{64,80},{96,112},{128,144},{160,176},{192,208},{224... | collective-permute-start | bytes 811016 | tf_op jit(solution)/shard_map/ppermute | solution.py:404
  82.8 7.7 %collective-permute-start.10 = (bf16[528,256]{1,0:T(8,128)(2,1)S(1)}, bf16[528,256]{1,0:T(8,128)(2,1)S(1)}, u32[]{:S(2)}, u32[]{:S(2)}) collective-permute-start(bf16[528,256]{1,0:T(8,128)(2,1)S(1)} %collective-permute-done.9.refs_6_), channel_id=1, source_target_pairs={{16,32},{48,64},{80,96},{144,160},{176,192},{208,224},{272,288},{3... | collective-permute-start | bytes 811016 | tf_op jit(solution)/shard_map/ppermute | solution.py:404
  83.5 9.8 %collective-permute-start.6 = (bf16[528,256]{1,0:T(8,128)(2,1)S(1)}, bf16[528,256]{1,0:T(8,128)(2,1)S(1)}, u32[]{:S(2)}, u32[]{:S(2)}) collective-permute-start(bf16[528,256]{1,0:T(8,128)(2,1)S(1)} %collective-permute-done.5), channel_id=1, source_target_pairs={{0,16},{32,48},{64,80},{96,112},{128,144},{160,176},{192,208},{224... | collective-permute-start | bytes 811016 | tf_op jit(solution)/shard_map/ppermute | solution.py:404
  101.5 10.3 %collective-permute-start.14 = (bf16[4,9,96,128]{3,2,1,0:T(8,128)(2,1)S(1)}, bf16[4,9,96,128]{3,2,1,0:T(8,128)(2,1)S(1)}, u32[]{:S(2)}, u32[]{:S(2)}) collective-permute-start(bf16[4,9,96,128]{3,2,1,0:T(8,128)(2,1)S(1)} %get-tuple-element.88), channel_id=1, source_target_pairs={{0,1},{1,0},{2,3},{3,2},{4,5},{5,4},{6,7},{7,6},{8,9},{9,8},{10,11... | collective-permute-start | bytes 2654216 | tf_op jit(solution)/shard_map/ppermute | solution.py:530
  106.9 19.3 %collective-permute-start.12 = (bf16[2,4,304,128]{3,2,1,0:T(8,128)(2,1)S(1)}, bf16[2,4,304,128]{3,2,1,0:T(8,128)(2,1)S(1)}, u32[]{:S(2)}, u32[]{:S(2)}) collective-permute-start(bf16[2,4,304,128]{3,2,1,0:T(8,128)(2,1)S(1)} %slice.84), channel_id=1, source_target_pairs={{0,128},{128,0},{256,384},{384,256},{1,129},{129,1},{257,385},{385... | collective-permute-start | bytes 1867784 | tf_op jit(solution)/shard_map/ppermute | solution.py:542
  112.0 18.5 %collective-permute-start.15 = (bf16[2,9,96,128]{3,2,1,0:T(8,128)(2,1)S(1)}, bf16[2,9,96,128]{3,2,1,0:T(8,128)(2,1)S(1)}, u32[]{:S(2)}, u32[]{:S(2)}) collective-permute-start(bf16[2,9,96,128]{3,2,1,0:T(8,128)(2,1)S(1)} %get-tuple-element.90), channel_id=1, source_target_pairs={{128,256},{256,128},{384,0},{0,384},{129,257},{257,129},{385,1},{1... | collective-permute-start | bytes 1327112 | tf_op jit(solution)/shard_map/ppermute | solution.py:546
  126.4 11.4 %collective-permute-start.13 = (bf16[4,304,128]{2,1,0:T(8,128)(2,1)S(1)}, bf16[4,304,128]{2,1,0:T(8,128)(2,1)S(1)}, u32[]{:S(2)}, u32[]{:S(2)}) collective-permute-start(bf16[4,304,128]{2,1,0:T(8,128)(2,1)S(1)} %get-tuple-element.86), channel_id=1, source_target_pairs={{128,256},{256,128},{384,0},{0,384},{129,257},{257,129},{385,1},{1... | collective-permute-start | bytes 933896 | tf_op jit(solution)/shard_map/ppermute | solution.py:551
  157.2 27.2 %collective-permute-start.17 = (bf16[416,128]{1,0:T(8,128)(2,1)S(1)}, bf16[416,128]{1,0:T(8,128)(2,1)S(1)}, u32[]{:S(2)}, u32[]{:S(2)}) collective-permute-start(bf16[416,128]{1,0:T(8,128)(2,1)S(1)} %get-tuple-element.93.sent), channel_id=1, source_target_pairs={{0,64},{64,0},{1,65},{65,1},{2,66},{66,2},{3,67},{67,3},{4,68},{68... | collective-permute-start | bytes 319496 | tf_op jit(solution)/shard_map/ppermute | solution.py:563
  161.5 14.6 %collective-permute-start.19 = (bf16[112,128]{1,0:T(8,128)(2,1)S(1)}, bf16[112,128]{1,0:T(8,128)(2,1)S(1)}, u32[]{:S(2)}, u32[]{:S(2)}) collective-permute-start(bf16[112,128]{1,0:T(8,128)(2,1)S(1)} %slice.71), channel_id=1, source_target_pairs={{0,72},{72,0},{8,64},{64,8},{1,73},{73,1},{9,65},{65,9},{2,74},{74... | collective-permute-start | bytes 86024 | tf_op jit(solution)/shard_map/ppermute | solution.py:565
  171.0 13.4 %collective-permute-start.18 = (bf16[112,128]{1,0:T(8,128)(2,1)S(1)}, bf16[112,128]{1,0:T(8,128)(2,1)S(1)}, u32[]{:S(2)}, u32[]{:S(2)}) collective-permute-start(bf16[112,128]{1,0:T(8,128)(2,1)S(1)} %get-tuple-element.94.mine), channel_id=1, source_target_pairs={{0,8},{8,0},{1,9},{9,1},{2,10},{10,2},{3,11},{11,3},{4,12},{12,4},... | collective-permute-start | bytes 86024 | tf_op jit(solution)/shard_map/ppermute | solution.py:564
  185.1 17.2 %all-to-all-start.1 = ((bf16[4,304,128]{2,1,0:T(8,128)(2,1)}), bf16[4,304,128]{2,1,0:T(8,128)(2,1)S(1)}, u32[]{:S(2)}, u32[]{:S(2)}) async-start(bf16[4,304,128]{2,1,0:T(8,128)(2,1)} %get-tuple-element.95), calls=%async_computation.1 | async-start | bytes 622592 | tf_op jit(solution)/shard_map/all_to_all | solution.py:408
  188.6 10.5 %collective-permute-start.20 = (bf16[112,128]{1,0:T(8,128)(2,1)S(1)}, bf16[112,128]{1,0:T(8,128)(2,1)S(1)}, u32[]{:S(2)}, u32[]{:S(2)}) collective-permute-start(bf16[112,128]{1,0:T(8,128)(2,1)S(1)} %get-tuple-element.96.own), channel_id=1, source_target_pairs={{0,2},{2,4},{4,6},{6,0},{1,3},{3,5},{5,7},{7,1},{8,10},{10,12},{12... | collective-permute-start | bytes 86024 | tf_op jit(solution)/shard_map/ppermute | solution.py:575
  202.3 13.8 %collective-permute-start.24 = (bf16[1216,128]{1,0:T(8,128)(2,1)S(1)}, bf16[1216,128]{1,0:T(8,128)(2,1)S(1)}, u32[]{:S(2)}, u32[]{:S(2)}) collective-permute-start(bf16[1216,128]{1,0:T(8,128)(2,1)S(1)} %bitcast.25), channel_id=1, source_target_pairs={{0,128},{128,256},{256,384},{384,0},{1,129},{129,257},{257,385},{3... | collective-permute-start | bytes 933896 | tf_op jit(solution)/shard_map/ppermute | solution.py:582
  204.3 13.8 %collective-permute-start.25 = (bf16[1216,128]{1,0:T(8,128)(2,1)S(1)}, bf16[1216,128]{1,0:T(8,128)(2,1)S(1)}, u32[]{:S(2)}, u32[]{:S(2)}) collective-permute-start(bf16[1216,128]{1,0:T(8,128)(2,1)S(1)} %bitcast.26), channel_id=1, source_target_pairs={{128,0},{256,128},{384,256},{0,384},{129,1},{257,129},{385,257},{1... | collective-permute-start | bytes 933896 | tf_op jit(solution)/shard_map/ppermute | solution.py:583
  208.8 13.8 %collective-permute-start.23 = (f32[112,128]{1,0:T(8,128)S(1)}, f32[112,128]{1,0:T(8,128)S(1)}, u32[]{:S(2)}, u32[]{:S(2)}) collective-permute-start(f32[112,128]{1,0:T(8,128)S(1)} %shard_map.172), channel_id=1, source_target_pairs={{0,1},{1,0},{2,3},{3,2},{4,5},{5,4},{6,7},{7,6},{8,9},{9,8},{10,11... | collective-permute-start | bytes 172040 | tf_op jit(solution)/shard_map/ppermute | solution.py:579
  216.1 7.6 %collective-permute-start.26 = (bf16[608,128]{1,0:T(8,128)(2,1)S(1)}, bf16[608,128]{1,0:T(8,128)(2,1)S(1)}, u32[]{:S(2)}, u32[]{:S(2)}) collective-permute-start(bf16[608,128]{1,0:T(8,128)(2,1)S(1)} %slice.85), channel_id=1, source_target_pairs={{0,128},{128,256},{256,384},{384,0},{1,129},{129,257},{257,385},{3... | collective-permute-start | bytes 466952 | tf_op jit(solution)/shard_map/ppermute | solution.py:584
  (18 other events, 105.8 us)

commit v10 on v9

--- a/solution.py
+++ b/solution.py
@@ -489,17 +489,19 @@
     relay_pairs = [(i + 6, i + 7) for i in starts] + [(i + 1, i) for i in starts]
     wide_feat = jnp.where((line == 2) | (line == 5), even_feat, odd_feat)
     wide = lax.ppermute(wide_feat, SEQ, wide_pairs)
-    relay = lax.ppermute(wide, SEQ, relay_pairs)
     at_end = (line == 0) | (line == 7)
     near_end = (line == 1) | (line == 6)
     short_far, long_far = odd_feat, even_feat
     for distance in range(1, SPAN + 1):
         if distance == 1:
             short_far, long_far = swapped(odd_feat, 0), swapped(even_feat, 1)
-            (short_far,) = call(copy_kernel, [feat], [VM], 4, 2000000000)(short_far)
+            (short_far,) = call(copy_kernel, [feat], [VM], 4, 1000000)(short_far)
         else:
             short_far, long_far = swapped(long_far, 0), swapped(short_far, 1, distance <= 2)
         short_use, long_use = short_far, long_far
+        if distance == 2:
+            ready, _ = lax.optimization_barrier((wide, long_far))
+            relay = lax.ppermute(ready, SEQ, relay_pairs)
         if distance == 3:
             long_use = jnp.where(at_end, relay, long_far)
         if distance == 4:

time: 229 us -> 226 us (0.987)
  waiting for transfers between devices: 44.6 us -> 35.9 us
  starting transfers between devices: 125 us -> 131 us
    ppermute x10, waiting for transfers between devices: 15.6 us -> 8.95 us  [swapped(): return lax.ppermute(block, SEQ, pairs + [(j, i) for i, j in pairs])]
    ppermute x10, starting transfers between devices: 52.6 us -> 55.7 us  [swapped(): return lax.ppermute(block, SEQ, pairs + [(j, i) for i, j in pairs])]
  transfers between devices with their start and end apart: 29 -> 29, of which waited for: 11 -> 9; matrix products, arithmetic and copies ran while one was open for 1% -> 1% of each run, Pallas kernels for 7% -> 8%
where the time goes in v10:
time: 226 us; the launch traced here: 224 us
  starting transfers between devices  131 us (58%)
  waiting for transfers between devices  35.9 us (16%)
  Pallas kernels  31 us (14%)
  blocking collectives  16.7 us (7%)
  local copies, waits for them, and re-layouts  4.73 us (2%)
    ppermute x10, starting transfers between devices, swapped(): return lax.ppermute(block, SEQ, pairs + [(j, i) for i, j in pairs])  55.7 us
    all_to_all x1, blocking collectives, swap_parts(): return lax.all_to_all(parts, axis, 0, 0, tiled=True)  16.7 us
    ppermute x3, starting transfers between devices, on_device(): lax.ppermute(conv_sum, 'x', [(i, (i + step) % 4) for i in range(4)])  10.5 us
    ppermute x1, waiting for transfers between devices, on_device(): other = lax.ppermute(head_sum[2:], 'y', first_pairs)  9.82 us
    pallas_call x4, Pallas kernels, on_device(): call(lambda *refs, distance=distance: pair_kernel(distance, *refs), acc_s...  9.69 us
    ppermute x10, waiting for transfers between devices, swapped(): return lax.ppermute(block, SEQ, pairs + [(j, i) for i, j in pairs])  8.95 us
    ppermute x1, starting transfers between devices, on_device(): lax.ppermute(sent[chunk:], ('zb', 'zhi'), [(0, 3), (3, 0), (1, 2), (2, 1)])  7.48 us
    ppermute x1, starting transfers between devices, on_device(): other = lax.ppermute(conv_sum, 'core', [(0, 1), (1, 0)])  7.43 us
  transfers between devices with their start and end apart: 29, of which 9 were waited for; matrix products, arithmetic and copies ran while one was open for 1% of the time, Pallas kernels for 8%

profile of v10, /device:TPU:1, one launch (start us, length us, event | category | flops | bytes accessed | tf_op | source)
XLA Modules:
  0.0 223.6 jit_solution(5853055094367445024)
XLA Ops:
  3.1 7.2 %collective-permute-start = (bf16[128,768]{1,0:T(8,128)(2,1)S(1)}, bf16[128,768]{1,0:T(8,128)(2,1)S(1)}, u32[]{:S(2)}, u32[]{:S(2)}) collective-permute-start(bf16[128,768]{1,0:T(8,128)(2,1)S(1)} %get-tuple-element.107), channel_id=1, source_target_pairs={{0,16},{32,48},{64,80},{96,112},{128,144},{160,176},{192,208},{224... | collective-permute-start | bytes 589832 | tf_op jit(solution)/shard_map/ppermute | solution.py:404
  23.5 3.4 %shard_map.163 = (bf16[256,768]{1,0:T(8,128)(2,1)S(1)}, f32[512,384]{1,0:T(8,128)S(1)}, bf16[768,768]{1,0:T(8,128)(2,1)S(1)}, bf16[384,512]{1,0:T(8,128)(2,1)S(1)}, bf16[768,512]{1,0:T(8,128)(2,1)S(1)}) custom-call(s32[1]{0:T(128)} %bitcast.3.odd, bf16[128,768]{1,0:T(8,128)(2,1)S(1)} %collective-permute-done.even_edge, ...), custom_call_target="tpu_custom_call" | custom-call | flops 6000000000 | bytes 1000000 | tf_op jit(solution)/shard_map/pallas_call | solution.py:472
  29.5 10.5 %collective-permute-start.4 = (bf16[528,256]{1,0:T(8,128)(2,1)S(1)}, bf16[528,256]{1,0:T(8,128)(2,1)S(1)}, u32[]{:S(2)}, u32[]{:S(2)}) collective-permute-start(bf16[528,256]{1,0:T(8,128)(2,1)S(1)} %collective-permute-done.3.refs_5_), channel_id=1, source_target_pairs={{0,16},{32,48},{64,80},{96,112},{128,144},{160,176},{192,208},{224... | collective-permute-start | bytes 811016 | tf_op jit(solution)/shard_map/ppermute | solution.py:404
  44.0 26.9 %collective-permute-start.9 = (bf16[528,256]{1,0:T(8,128)(2,1)S(1)}, bf16[528,256]{1,0:T(8,128)(2,1)S(1)}, u32[]{:S(2)}, u32[]{:S(2)}) collective-permute-start(bf16[528,256]{1,0:T(8,128)(2,1)S(1)} %collective-permute-done.8.refs_5_), channel_id=1, source_target_pairs={{0,16},{32,48},{64,80},{96,112},{128,144},{160,176},{192,208},{224... | collective-permute-start | bytes 811016 | tf_op jit(solution)/shard_map/ppermute | solution.py:404
  74.0 5.2 %collective-permute-done.9.refs_6_ = bf16[528,256]{1,0:T(8,128)(2,1)S(1)} collective-permute-done((bf16[528,256]{1,0:T(8,128)(2,1)S(1)}, bf16[528,256]{1,0:T(8,128)(2,1)S(1)}, u32[]{:S(2)}, u32[]{:S(2)}) %collective-permute-start.9) | collective-permute-done | bytes 270368 | tf_op jit(solution)/shard_map/ppermute | solution.py:404
  79.9 5.8 %collective-permute-start.6 = (bf16[528,256]{1,0:T(8,128)(2,1)S(1)}, bf16[528,256]{1,0:T(8,128)(2,1)S(1)}, u32[]{:S(2)}, u32[]{:S(2)}) collective-permute-start(bf16[528,256]{1,0:T(8,128)(2,1)S(1)} %collective-permute-done.5), channel_id=1, source_target_pairs={{0,16},{32,48},{64,80},{96,112},{128,144},{160,176},{192,208},{224... | collective-permute-start | bytes 811016 | tf_op jit(solution)/shard_map/ppermute | solution.py:404
  87.4 3.7 %collective-permute-done.6 = bf16[528,256]{1,0:T(8,128)(2,1)S(1)} collective-permute-done((bf16[528,256]{1,0:T(8,128)(2,1)S(1)}, bf16[528,256]{1,0:T(8,128)(2,1)S(1)}, u32[]{:S(2)}, u32[]{:S(2)}) %collective-permute-start.6) | collective-permute-done | bytes 270368 | tf_op jit(solution)/shard_map/ppermute | solution.py:404
  94.2 4.1 %shard_map.164 = (bf16[4,9,96,128]{3,2,1,0:T(8,128)(2,1)S(1)}, bf16[4,9,96,128]{3,2,1,0:T(8,128)(2,1)S(1)}, bf16[512,384]{1,0:T(8,128)(2,1)S(1)}, bf16[512,512]{1,0:T(8,128)(2,1)S(1)}) custom-call(s32[3]{0:T(128)S(1)} %pad_add_fusion.place, f32[512,256]{1,0:T(8,128)S(1)} %get-tuple-element.72.d_donor, f32[512,256]{1,0:T(8,128)S(1)} %get-tuple-element.73.d_accept, ...), custom_call_target="tpu_custom_call" | custom-call | flops 4000000000 | bytes 1000000 | tf_op jit(solution)/shard_map/pallas_call | solution.py:525
  98.4 4.4 %collective-permute-start.14 = (bf16[4,9,96,128]{3,2,1,0:T(8,128)(2,1)S(1)}, bf16[4,9,96,128]{3,2,1,0:T(8,128)(2,1)S(1)}, u32[]{:S(2)}, u32[]{:S(2)}) collective-permute-start(bf16[4,9,96,128]{3,2,1,0:T(8,128)(2,1)S(1)} %get-tuple-element.90), channel_id=1, source_target_pairs={{0,1},{1,0},{2,3},{3,2},{4,5},{5,4},{6,7},{7,6},{8,9},{9,8},{10,11... | collective-permute-start | bytes 2654216 | tf_op jit(solution)/shard_map/ppermute | solution.py:532
  105.5 7.0 %collective-permute-start.12 = (bf16[2,4,304,128]{3,2,1,0:T(8,128)(2,1)S(1)}, bf16[2,4,304,128]{3,2,1,0:T(8,128)(2,1)S(1)}, u32[]{:S(2)}, u32[]{:S(2)}) collective-permute-start(bf16[2,4,304,128]{3,2,1,0:T(8,128)(2,1)S(1)} %slice.84), channel_id=1, source_target_pairs={{0,128},{128,0},{256,384},{384,256},{1,129},{129,1},{257,385},{385... | collective-permute-start | bytes 1867784 | tf_op jit(solution)/shard_map/ppermute | solution.py:544
  112.7 4.3 %collective-permute-start.15 = (bf16[2,9,96,128]{3,2,1,0:T(8,128)(2,1)S(1)}, bf16[2,9,96,128]{3,2,1,0:T(8,128)(2,1)S(1)}, u32[]{:S(2)}, u32[]{:S(2)}) collective-permute-start(bf16[2,9,96,128]{3,2,1,0:T(8,128)(2,1)S(1)} %get-tuple-element.92), channel_id=1, source_target_pairs={{128,256},{256,128},{384,0},{0,384},{129,257},{257,129},{385,1},{1... | collective-permute-start | bytes 1327112 | tf_op jit(solution)/shard_map/ppermute | solution.py:548
  117.1 9.8 %collective-permute-done.12.received = bf16[2,4,304,128]{3,2,1,0:T(8,128)(2,1)S(1)} collective-permute-done((bf16[2,4,304,128]{3,2,1,0:T(8,128)(2,1)S(1)}, bf16[2,4,304,128]{3,2,1,0:T(8,128)(2,1)S(1)}, u32[]{:S(2)}, u32[]{:S(2)}) %collective-permute-start.12) | collective-permute-done | bytes 622624 | tf_op jit(solution)/shard_map/ppermute | solution.py:544
  127.1 4.3 %collective-permute-start.13 = (bf16[4,304,128]{2,1,0:T(8,128)(2,1)S(1)}, bf16[4,304,128]{2,1,0:T(8,128)(2,1)S(1)}, u32[]{:S(2)}, u32[]{:S(2)}) collective-permute-start(bf16[4,304,128]{2,1,0:T(8,128)(2,1)S(1)} %get-tuple-element.88), channel_id=1, source_target_pairs={{128,256},{256,128},{384,0},{0,384},{129,257},{257,129},{385,1},{1... | collective-permute-start | bytes 933896 | tf_op jit(solution)/shard_map/ppermute | solution.py:553
  134.0 4.4 %collective-permute-done.13.head_in = bf16[4,304,128]{2,1,0:T(8,128)(2,1)S(1)} collective-permute-done((bf16[4,304,128]{2,1,0:T(8,128)(2,1)S(1)}, bf16[4,304,128]{2,1,0:T(8,128)(2,1)S(1)}, u32[]{:S(2)}, u32[]{:S(2)}) %collective-permute-start.13) | collective-permute-done | bytes 311328 | tf_op jit(solution)/shard_map/ppermute | solution.py:553
  139.6 16.7 %all_to_all.10.parts = bf16[4,528,128]{2,1,0:T(8,128)(2,1)S(1)} all-to-all(bf16[4,528,128]{2,1,0:T(8,128)(2,1)S(1)} %shard_map.169), channel_id=1, replica_groups=mesh['y'=4,'zb'=2,'zq'=4,'zhi'=2,'x'=4,'core'=2] {'zq'}, dimensions={0} | all-to-all | bytes 1081344 | tf_op jit(solution)/shard_map/all_to_all | solution.py:408
  159.7 7.5 %collective-permute-start.19 = (bf16[112,128]{1,0:T(8,128)(2,1)S(1)}, bf16[112,128]{1,0:T(8,128)(2,1)S(1)}, u32[]{:S(2)}, u32[]{:S(2)}) collective-permute-start(bf16[112,128]{1,0:T(8,128)(2,1)S(1)} %slice.71), channel_id=1, source_target_pairs={{0,72},{72,0},{8,64},{64,8},{1,73},{73,1},{9,65},{65,9},{2,74},{74... | collective-permute-start | bytes 86024 | tf_op jit(solution)/shard_map/ppermute | solution.py:567
  167.2 6.1 %collective-permute-start.18 = (bf16[112,128]{1,0:T(8,128)(2,1)S(1)}, bf16[112,128]{1,0:T(8,128)(2,1)S(1)}, u32[]{:S(2)}, u32[]{:S(2)}) collective-permute-start(bf16[112,128]{1,0:T(8,128)(2,1)S(1)} %get-tuple-element.96.mine), channel_id=1, source_target_pairs={{0,8},{8,0},{1,9},{9,1},{2,10},{10,2},{3,11},{11,3},{4,12},{12,4},... | collective-permute-start | bytes 86024 | tf_op jit(solution)/shard_map/ppermute | solution.py:566
  173.3 7.4 %collective-permute-done.18.one = bf16[112,128]{1,0:T(8,128)(2,1)S(1)} collective-permute-done((bf16[112,128]{1,0:T(8,128)(2,1)S(1)}, bf16[112,128]{1,0:T(8,128)(2,1)S(1)}, u32[]{:S(2)}, u32[]{:S(2)}) %collective-permute-start.18) | collective-permute-done | bytes 28704 | tf_op jit(solution)/shard_map/ppermute | solution.py:566
  181.4 3.5 %all-to-all-start.1 = ((bf16[4,304,128]{2,1,0:T(8,128)(2,1)}), bf16[4,304,128]{2,1,0:T(8,128)(2,1)S(1)}, u32[]{:S(2)}, u32[]{:S(2)}) async-start(bf16[4,304,128]{2,1,0:T(8,128)(2,1)} %get-tuple-element.97), calls=%async_computation.1 | async-start | bytes 622592 | tf_op jit(solution)/shard_map/all_to_all | solution.py:408
  184.9 4.0 %collective-permute-start.20 = (bf16[112,128]{1,0:T(8,128)(2,1)S(1)}, bf16[112,128]{1,0:T(8,128)(2,1)S(1)}, u32[]{:S(2)}, u32[]{:S(2)}) collective-permute-start(bf16[112,128]{1,0:T(8,128)(2,1)S(1)} %get-tuple-element.98.own), channel_id=1, source_target_pairs={{0,2},{2,4},{4,6},{6,0},{1,3},{3,5},{5,7},{7,1},{8,10},{10,12},{12... | collective-permute-start | bytes 86024 | tf_op jit(solution)/shard_map/ppermute | solution.py:577
  188.8 4.6 %collective-permute-start.21 = (bf16[112,128]{1,0:T(8,128)(2,1)S(1)}, bf16[112,128]{1,0:T(8,128)(2,1)S(1)}, u32[]{:S(2)}, u32[]{:S(2)}) collective-permute-start(bf16[112,128]{1,0:T(8,128)(2,1)S(1)} %get-tuple-element.98.own), channel_id=1, source_target_pairs={{0,4},{2,6},{4,0},{6,2},{1,5},{3,7},{5,1},{7,3},{8,12},{10,14},{12... | collective-permute-start | bytes 86024 | tf_op jit(solution)/shard_map/ppermute | solution.py:577
  200.4 4.6 %collective-permute-start.25 = (bf16[1216,128]{1,0:T(8,128)(2,1)S(1)}, bf16[1216,128]{1,0:T(8,128)(2,1)S(1)}, u32[]{:S(2)}, u32[]{:S(2)}) collective-permute-start(bf16[1216,128]{1,0:T(8,128)(2,1)S(1)} %bitcast.26), channel_id=1, source_target_pairs={{128,0},{256,128},{384,256},{0,384},{129,1},{257,129},{385,257},{1... | collective-permute-start | bytes 933896 | tf_op jit(solution)/shard_map/ppermute | solution.py:585
  205.0 7.4 %collective-permute-start.23 = (f32[112,128]{1,0:T(8,128)S(1)}, f32[112,128]{1,0:T(8,128)S(1)}, u32[]{:S(2)}, u32[]{:S(2)}) collective-permute-start(f32[112,128]{1,0:T(8,128)S(1)} %shard_map.172), channel_id=1, source_target_pairs={{0,1},{1,0},{2,3},{3,2},{4,5},{5,4},{6,7},{7,6},{8,9},{9,8},{10,11... | collective-permute-start | bytes 172040 | tf_op jit(solution)/shard_map/ppermute | solution.py:581
  214.4 4.6 %collective-permute-start.27 = (bf16[608,128]{1,0:T(8,128)(2,1)S(1)}, bf16[608,128]{1,0:T(8,128)(2,1)S(1)}, u32[]{:S(2)}, u32[]{:S(2)}) collective-permute-start(bf16[608,128]{1,0:T(8,128)(2,1)S(1)} %slice.86), channel_id=1, source_target_pairs={{128,0},{256,128},{384,256},{0,384},{129,1},{257,129},{385,257},{1... | collective-permute-start | bytes 466952 | tf_op jit(solution)/shard_map/ppermute | solution.py:587
  (111 shorter events, 54.0 us)
Async XLA Ops:
  2.5 13.3 %collective-permute-start.1 = (bf16[128,768]{1,0:T(8,128)(2,1)}, bf16[128,768]{1,0:T(8,128)(2,1)S(1)}, u32[]{:S(2)}, u32[]{:S(2)}) collective-permute-start(bf16[128,768]{1,0:T(8,128)(2,1)} %get-tuple-element.106), channel_id=1, source_target_pairs={{16,32},{48,64},{80,96},{112,128},{144,160},{176,192},{208,224},{2... | collective-permute-start | bytes 589832 | tf_op jit(solution)/shard_map/ppermute | solution.py:404
  3.1 12.9 %collective-permute-start = (bf16[128,768]{1,0:T(8,128)(2,1)S(1)}, bf16[128,768]{1,0:T(8,128)(2,1)S(1)}, u32[]{:S(2)}, u32[]{:S(2)}) collective-permute-start(bf16[128,768]{1,0:T(8,128)(2,1)S(1)} %get-tuple-element.107), channel_id=1, source_target_pairs={{0,16},{32,48},{64,80},{96,112},{128,144},{160,176},{192,208},{224... | collective-permute-start | bytes 589832 | tf_op jit(solution)/shard_map/ppermute | solution.py:404
  20.2 8.6 %collective-permute-start.7 = (bf16[528,256]{1,0:T(8,128)(2,1)S(1)}, bf16[528,256]{1,0:T(8,128)(2,1)S(1)}, u32[]{:S(2)}, u32[]{:S(2)}) collective-permute-start(bf16[528,256]{1,0:T(8,128)(2,1)S(1)} %get-tuple-element.58.refs_3_.refs_4_), channel_id=1, source_target_pairs={{0,16},{32,48},{64,80},{96,112},{128,144},{160,176},{192,208},{224... | collective-permute-start | bytes 811016 | tf_op jit(solution)/shard_map/ppermute | solution.py:404
  22.8 19.8 %collective-permute-start.2 = (bf16[528,256]{1,0:T(8,128)(2,1)S(1)}, bf16[528,256]{1,0:T(8,128)(2,1)S(1)}, u32[]{:S(2)}, u32[]{:S(2)}) collective-permute-start(bf16[528,256]{1,0:T(8,128)(2,1)S(1)} %broadcast_select_fusion.2), channel_id=1, source_target_pairs={{160,96},{176,112},{288,224},{304,240},{416,352},{432,368},{64,128... | collective-permute-start | bytes 811016 | tf_op jit(solution)/shard_map/ppermute | solution.py:491
  28.8 13.9 %collective-permute-start.8 = (bf16[528,256]{1,0:T(8,128)(2,1)S(1)}, bf16[528,256]{1,0:T(8,128)(2,1)S(1)}, u32[]{:S(2)}, u32[]{:S(2)}) collective-permute-start(bf16[528,256]{1,0:T(8,128)(2,1)S(1)} %shard_map.157.refs_6_), channel_id=1, source_target_pairs={{16,32},{48,64},{80,96},{112,128},{144,160},{176,192},{208,224},{2... | collective-permute-start | bytes 811016 | tf_op jit(solution)/shard_map/ppermute | solution.py:404
  29.5 41.4 %collective-permute-start.4 = (bf16[528,256]{1,0:T(8,128)(2,1)S(1)}, bf16[528,256]{1,0:T(8,128)(2,1)S(1)}, u32[]{:S(2)}, u32[]{:S(2)}) collective-permute-start(bf16[528,256]{1,0:T(8,128)(2,1)S(1)} %collective-permute-done.3.refs_5_), channel_id=1, source_target_pairs={{0,16},{32,48},{64,80},{96,112},{128,144},{160,176},{192,208},{224... | collective-permute-start | bytes 811016 | tf_op jit(solution)/shard_map/ppermute | solution.py:404
  42.7 43.0 %collective-permute-start.11 = (bf16[528,256]{1,0:T(8,128)(2,1)S(1)}, bf16[528,256]{1,0:T(8,128)(2,1)S(1)}, u32[]{:S(2)}, u32[]{:S(2)}) collective-permute-start(bf16[528,256]{1,0:T(8,128)(2,1)S(1)} %collective-permute-done.2), channel_id=1, source_target_pairs={{96,112},{224,240},{352,368},{480,496},{16,0},{144,128},{272,256},... | collective-permute-start | bytes 811016 | tf_op jit(solution)/shard_map/ppermute | solution.py:504
  44.0 35.2 %collective-permute-start.9 = (bf16[528,256]{1,0:T(8,128)(2,1)S(1)}, bf16[528,256]{1,0:T(8,128)(2,1)S(1)}, u32[]{:S(2)}, u32[]{:S(2)}) collective-permute-start(bf16[528,256]{1,0:T(8,128)(2,1)S(1)} %collective-permute-done.8.refs_5_), channel_id=1, source_target_pairs={{0,16},{32,48},{64,80},{96,112},{128,144},{160,176},{192,208},{224... | collective-permute-start | bytes 811016 | tf_op jit(solution)/shard_map/ppermute | solution.py:404
  70.9 8.9 %collective-permute-start.5 = (bf16[528,256]{1,0:T(8,128)(2,1)S(1)}, bf16[528,256]{1,0:T(8,128)(2,1)S(1)}, u32[]{:S(2)}, u32[]{:S(2)}) collective-permute-start(bf16[528,256]{1,0:T(8,128)(2,1)S(1)} %collective-permute-done.4.refs_6_), channel_id=1, source_target_pairs={{16,32},{48,64},{80,96},{144,160},{176,192},{208,224},{272,288},{3... | collective-permute-start | bytes 811016 | tf_op jit(solution)/shard_map/ppermute | solution.py:404
  79.2 8.2 %collective-permute-start.10 = (bf16[528,256]{1,0:T(8,128)(2,1)S(1)}, bf16[528,256]{1,0:T(8,128)(2,1)S(1)}, u32[]{:S(2)}, u32[]{:S(2)}) collective-permute-start(bf16[528,256]{1,0:T(8,128)(2,1)S(1)} %collective-permute-done.9.refs_6_), channel_id=1, source_target_pairs={{16,32},{48,64},{80,96},{144,160},{176,192},{208,224},{272,288},{3... | collective-permute-start | bytes 811016 | tf_op jit(solution)/shard_map/ppermute | solution.py:404
  79.9 11.3 %collective-permute-start.6 = (bf16[528,256]{1,0:T(8,128)(2,1)S(1)}, bf16[528,256]{1,0:T(8,128)(2,1)S(1)}, u32[]{:S(2)}, u32[]{:S(2)}) collective-permute-start(bf16[528,256]{1,0:T(8,128)(2,1)S(1)} %collective-permute-done.5), channel_id=1, source_target_pairs={{0,16},{32,48},{64,80},{96,112},{128,144},{160,176},{192,208},{224... | collective-permute-start | bytes 811016 | tf_op jit(solution)/shard_map/ppermute | solution.py:404
  98.4 14.2 %collective-permute-start.14 = (bf16[4,9,96,128]{3,2,1,0:T(8,128)(2,1)S(1)}, bf16[4,9,96,128]{3,2,1,0:T(8,128)(2,1)S(1)}, u32[]{:S(2)}, u32[]{:S(2)}) collective-permute-start(bf16[4,9,96,128]{3,2,1,0:T(8,128)(2,1)S(1)} %get-tuple-element.90), channel_id=1, source_target_pairs={{0,1},{1,0},{2,3},{3,2},{4,5},{5,4},{6,7},{7,6},{8,9},{9,8},{10,11... | collective-permute-start | bytes 2654216 | tf_op jit(solution)/shard_map/ppermute | solution.py:532
  105.5 21.4 %collective-permute-start.12 = (bf16[2,4,304,128]{3,2,1,0:T(8,128)(2,1)S(1)}, bf16[2,4,304,128]{3,2,1,0:T(8,128)(2,1)S(1)}, u32[]{:S(2)}, u32[]{:S(2)}) collective-permute-start(bf16[2,4,304,128]{3,2,1,0:T(8,128)(2,1)S(1)} %slice.84), channel_id=1, source_target_pairs={{0,128},{128,0},{256,384},{384,256},{1,129},{129,1},{257,385},{385... | collective-permute-start | bytes 1867784 | tf_op jit(solution)/shard_map/ppermute | solution.py:544
  112.7 18.7 %collective-permute-start.15 = (bf16[2,9,96,128]{3,2,1,0:T(8,128)(2,1)S(1)}, bf16[2,9,96,128]{3,2,1,0:T(8,128)(2,1)S(1)}, u32[]{:S(2)}, u32[]{:S(2)}) collective-permute-start(bf16[2,9,96,128]{3,2,1,0:T(8,128)(2,1)S(1)} %get-tuple-element.92), channel_id=1, source_target_pairs={{128,256},{256,128},{384,0},{0,384},{129,257},{257,129},{385,1},{1... | collective-permute-start | bytes 1327112 | tf_op jit(solution)/shard_map/ppermute | solution.py:548
  127.1 11.4 %collective-permute-start.13 = (bf16[4,304,128]{2,1,0:T(8,128)(2,1)S(1)}, bf16[4,304,128]{2,1,0:T(8,128)(2,1)S(1)}, u32[]{:S(2)}, u32[]{:S(2)}) collective-permute-start(bf16[4,304,128]{2,1,0:T(8,128)(2,1)S(1)} %get-tuple-element.88), channel_id=1, source_target_pairs={{128,256},{256,128},{384,0},{0,384},{129,257},{257,129},{385,1},{1... | collective-permute-start | bytes 933896 | tf_op jit(solution)/shard_map/ppermute | solution.py:553
  131.5 8.0 %collective-permute-start.16 = (bf16[9,96,128]{2,1,0:T(8,128)(2,1)S(1)}, bf16[9,96,128]{2,1,0:T(8,128)(2,1)S(1)}, u32[]{:S(2)}, u32[]{:S(2)}) collective-permute-start(bf16[9,96,128]{2,1,0:T(8,128)(2,1)S(1)} %get-tuple-element.94), channel_id=1, source_target_pairs={{0,128},{128,0},{256,384},{384,256},{1,129},{129,1},{257,385},{385... | collective-permute-start | bytes 663560 | tf_op jit(solution)/shard_map/ppermute | solution.py:554
  157.0 23.6 %collective-permute-start.17 = (bf16[416,128]{1,0:T(8,128)(2,1)S(1)}, bf16[416,128]{1,0:T(8,128)(2,1)S(1)}, u32[]{:S(2)}, u32[]{:S(2)}) collective-permute-start(bf16[416,128]{1,0:T(8,128)(2,1)S(1)} %get-tuple-element.95.sent), channel_id=1, source_target_pairs={{0,64},{64,0},{1,65},{65,1},{2,66},{66,2},{3,67},{67,3},{4,68},{68... | collective-permute-start | bytes 319496 | tf_op jit(solution)/shard_map/ppermute | solution.py:565
  159.7 13.6 %collective-permute-start.19 = (bf16[112,128]{1,0:T(8,128)(2,1)S(1)}, bf16[112,128]{1,0:T(8,128)(2,1)S(1)}, u32[]{:S(2)}, u32[]{:S(2)}) collective-permute-start(bf16[112,128]{1,0:T(8,128)(2,1)S(1)} %slice.71), channel_id=1, source_target_pairs={{0,72},{72,0},{8,64},{64,8},{1,73},{73,1},{9,65},{65,9},{2,74},{74... | collective-permute-start | bytes 86024 | tf_op jit(solution)/shard_map/ppermute | solution.py:567
  167.2 13.5 %collective-permute-start.18 = (bf16[112,128]{1,0:T(8,128)(2,1)S(1)}, bf16[112,128]{1,0:T(8,128)(2,1)S(1)}, u32[]{:S(2)}, u32[]{:S(2)}) collective-permute-start(bf16[112,128]{1,0:T(8,128)(2,1)S(1)} %get-tuple-element.96.mine), channel_id=1, source_target_pairs={{0,8},{8,0},{1,9},{9,1},{2,10},{10,2},{3,11},{11,3},{4,12},{12,4},... | collective-permute-start | bytes 86024 | tf_op jit(solution)/shard_map/ppermute | solution.py:566
  181.4 17.1 %all-to-all-start.1 = ((bf16[4,304,128]{2,1,0:T(8,128)(2,1)}), bf16[4,304,128]{2,1,0:T(8,128)(2,1)S(1)}, u32[]{:S(2)}, u32[]{:S(2)}) async-start(bf16[4,304,128]{2,1,0:T(8,128)(2,1)} %get-tuple-element.97), calls=%async_computation.1 | async-start | bytes 622592 | tf_op jit(solution)/shard_map/all_to_all | solution.py:408
  184.9 10.5 %collective-permute-start.20 = (bf16[112,128]{1,0:T(8,128)(2,1)S(1)}, bf16[112,128]{1,0:T(8,128)(2,1)S(1)}, u32[]{:S(2)}, u32[]{:S(2)}) collective-permute-start(bf16[112,128]{1,0:T(8,128)(2,1)S(1)} %get-tuple-element.98.own), channel_id=1, source_target_pairs={{0,2},{2,4},{4,6},{6,0},{1,3},{3,5},{5,7},{7,1},{8,10},{10,12},{12... | collective-permute-start | bytes 86024 | tf_op jit(solution)/shard_map/ppermute | solution.py:577
  198.5 14.0 %collective-permute-start.24 = (bf16[1216,128]{1,0:T(8,128)(2,1)S(1)}, bf16[1216,128]{1,0:T(8,128)(2,1)S(1)}, u32[]{:S(2)}, u32[]{:S(2)}) collective-permute-start(bf16[1216,128]{1,0:T(8,128)(2,1)S(1)} %bitcast.25), channel_id=1, source_target_pairs={{0,128},{128,256},{256,384},{384,0},{1,129},{129,257},{257,385},{3... | collective-permute-start | bytes 933896 | tf_op jit(solution)/shard_map/ppermute | solution.py:584
  200.4 14.0 %collective-permute-start.25 = (bf16[1216,128]{1,0:T(8,128)(2,1)S(1)}, bf16[1216,128]{1,0:T(8,128)(2,1)S(1)}, u32[]{:S(2)}, u32[]{:S(2)}) collective-permute-start(bf16[1216,128]{1,0:T(8,128)(2,1)S(1)} %bitcast.26), channel_id=1, source_target_pairs={{128,0},{256,128},{384,256},{0,384},{129,1},{257,129},{385,257},{1... | collective-permute-start | bytes 933896 | tf_op jit(solution)/shard_map/ppermute | solution.py:585
  205.0 14.0 %collective-permute-start.23 = (f32[112,128]{1,0:T(8,128)S(1)}, f32[112,128]{1,0:T(8,128)S(1)}, u32[]{:S(2)}, u32[]{:S(2)}) collective-permute-start(f32[112,128]{1,0:T(8,128)S(1)} %shard_map.172), channel_id=1, source_target_pairs={{0,1},{1,0},{2,3},{3,2},{4,5},{5,4},{6,7},{7,6},{8,9},{9,8},{10,11... | collective-permute-start | bytes 172040 | tf_op jit(solution)/shard_map/ppermute | solution.py:581
  (18 other events, 106.1 us)

commit v11 on v10

--- a/solution.py
+++ b/solution.py
@@ -486,9 +486,11 @@
     starts = range(0, count, 8)
     wide_pairs = [(i + k, i - 4 + k) for i in starts if i > 0 for k in (2, 3)]
     wide_pairs += [(i + k, i + 4 + k) for i in starts if i + 8 < count for k in (4, 5)]
-    relay_pairs = [(i + 6, i + 7) for i in starts] + [(i + 1, i) for i in starts]
+    wider_pairs = [(i + 2, i - 1) for i in starts if i > 0]
+    wider_pairs += [(i + 5, i + 8) for i in starts if i + 8 < count]
     wide_feat = jnp.where((line == 2) | (line == 5), even_feat, odd_feat)
     wide = lax.ppermute(wide_feat, SEQ, wide_pairs)
+    wider = lax.ppermute(wide_feat, SEQ, wider_pairs)
     at_end = (line == 0) | (line == 7)
     near_end = (line == 1) | (line == 6)
     short_far, long_far = odd_feat, even_feat
@@ -499,11 +501,8 @@
         else:
             short_far, long_far = swapped(long_far, 0), swapped(short_far, 1, distance <= 2)
         short_use, long_use = short_far, long_far
-        if distance == 2:
-            ready, _ = lax.optimization_barrier((wide, long_far))
-            relay = lax.ppermute(ready, SEQ, relay_pairs)
         if distance == 3:
-            long_use = jnp.where(at_end, relay, long_far)
+            long_use = jnp.where(at_end, wider, long_far)
         if distance == 4:
             short_use = jnp.where(near_end, wide, short_far)
             long_use = jnp.where(at_end, wide, long_far)

time: 226 us -> 234 us (1.035)
  waiting for transfers between devices: 35.9 us -> 51 us
  starting transfers between devices: 131 us -> 123 us
    ppermute x10, waiting for transfers between devices: 8.95 us -> 22.3 us  [swapped(): return lax.ppermute(block, SEQ, pairs + [(j, i) for i, j in pairs])]
    ppermute x10, starting transfers between devices: 55.7 us -> 52.3 us  [swapped(): return lax.ppermute(block, SEQ, pairs + [(j, i) for i, j in pairs])]
    ppermute x1, starting transfers between devices: 7.48 us -> 10.7 us  [on_device(): lax.ppermute(sent[chunk:], ('zb', 'zhi'), [(0, 3), (3, 0), (1, 2), (2, 1)])]
    ppermute x1, waiting for transfers between devices: 7.39 us -> 10.3 us  [on_device(): across = lax.ppermute(mine, 'zhi', [(0, 1), (1, 0)])]
    ppermute x1, starting transfers between devices: 6.08 us -> 3.18 us  [on_device(): across = lax.ppermute(mine, 'zhi', [(0, 1), (1, 0)])]
    ppermute x1, starting transfers between devices: 7.03 us -> 4.46 us  [on_device(): other = lax.ppermute(head_sum[2:], 'y', first_pairs)]
  transfers between devices with their start and end apart: 29 -> 29, of which waited for: 9 -> 9; matrix products, arithmetic and copies ran while one was open for 1% -> 1% of each run, Pallas kernels for 8% -> 7%
where the time goes in v11:
time: 234 us; the launch traced here: 231 us
  starting transfers between devices  123 us (53%)
  waiting for transfers between devices  51 us (22%)
  Pallas kernels  30.1 us (13%)
  blocking collectives  18.2 us (8%)
  local copies, waits for them, and re-layouts  4.73 us (2%)
    ppermute x10, starting transfers between devices, swapped(): return lax.ppermute(block, SEQ, pairs + [(j, i) for i, j in pairs])  52.3 us
    ppermute x10, waiting for transfers between devices, swapped(): return lax.ppermute(block, SEQ, pairs + [(j, i) for i, j in pairs])  22.3 us
    all_to_all x1, blocking collectives, swap_parts(): return lax.all_to_all(parts, axis, 0, 0, tiled=True)  18.2 us
    ppermute x1, waiting for transfers between devices, on_device(): other = lax.ppermute(head_sum[2:], 'y', first_pairs)  10.8 us
    ppermute x1, starting transfers between devices, on_device(): lax.ppermute(sent[chunk:], ('zb', 'zhi'), [(0, 3), (3, 0), (1, 2), (2, 1)])  10.7 us
    ppermute x1, waiting for transfers between devices, on_device(): across = lax.ppermute(mine, 'zhi', [(0, 1), (1, 0)])  10.3 us
    ppermute x3, starting transfers between devices, on_device(): lax.ppermute(conv_sum, 'x', [(i, (i + step) % 4) for i in range(4)])  9.83 us
    pallas_call x4, Pallas kernels, on_device(): call(lambda *refs, distance=distance: pair_kernel(distance, *refs), acc_s...  8.33 us
  transfers between devices with their start and end apart: 29, of which 9 were waited for; matrix products, arithmetic and copies ran while one was open for 1% of the time, Pallas kernels for 7%

profile of v11, /device:TPU:1, one launch (start us, length us, event | category | flops | bytes accessed | tf_op | source)
XLA Modules:
  0.0 231.3 jit_solution(4458234875528193570)
XLA Ops:
  3.1 7.2 %collective-permute-start = (bf16[128,768]{1,0:T(8,128)(2,1)S(1)}, bf16[128,768]{1,0:T(8,128)(2,1)S(1)}, u32[]{:S(2)}, u32[]{:S(2)}) collective-permute-start(bf16[128,768]{1,0:T(8,128)(2,1)S(1)} %get-tuple-element.105), channel_id=1, source_target_pairs={{0,16},{32,48},{64,80},{96,112},{128,144},{160,176},{192,208},{224... | collective-permute-start | bytes 589832 | tf_op jit(solution)/shard_map/ppermute | solution.py:404
  24.2 3.4 %shard_map.163 = (bf16[256,768]{1,0:T(8,128)(2,1)S(1)}, f32[512,384]{1,0:T(8,128)S(1)}, bf16[768,768]{1,0:T(8,128)(2,1)S(1)}, bf16[384,512]{1,0:T(8,128)(2,1)S(1)}, bf16[768,512]{1,0:T(8,128)(2,1)S(1)}) custom-call(s32[1]{0:T(128)} %bitcast.3.odd, bf16[128,768]{1,0:T(8,128)(2,1)S(1)} %collective-permute-done.even_edge, ...), custom_call_target="tpu_custom_call" | custom-call | flops 6000000000 | bytes 1000000 | tf_op jit(solution)/shard_map/pallas_call | solution.py:472
  30.6 9.2 %collective-permute-start.4 = (bf16[528,256]{1,0:T(8,128)(2,1)S(1)}, bf16[528,256]{1,0:T(8,128)(2,1)S(1)}, u32[]{:S(2)}, u32[]{:S(2)}) collective-permute-start(bf16[528,256]{1,0:T(8,128)(2,1)S(1)} %collective-permute-done.3.refs_5_), channel_id=1, source_target_pairs={{0,16},{32,48},{64,80},{96,112},{128,144},{160,176},{192,208},{224... | collective-permute-start | bytes 811016 | tf_op jit(solution)/shard_map/ppermute | solution.py:404
  41.5 14.5 %collective-permute-done.4.refs_6_ = bf16[528,256]{1,0:T(8,128)(2,1)S(1)} collective-permute-done((bf16[528,256]{1,0:T(8,128)(2,1)S(1)}, bf16[528,256]{1,0:T(8,128)(2,1)S(1)}, u32[]{:S(2)}, u32[]{:S(2)}) %collective-permute-start.4) | collective-permute-done | bytes 270368 | tf_op jit(solution)/shard_map/ppermute | solution.py:404
  56.7 25.9 %collective-permute-start.9 = (bf16[528,256]{1,0:T(8,128)(2,1)S(1)}, bf16[528,256]{1,0:T(8,128)(2,1)S(1)}, u32[]{:S(2)}, u32[]{:S(2)}) collective-permute-start(bf16[528,256]{1,0:T(8,128)(2,1)S(1)} %collective-permute-done.8.refs_5_), channel_id=1, source_target_pairs={{0,16},{32,48},{64,80},{96,112},{128,144},{160,176},{192,208},{224... | collective-permute-start | bytes 811016 | tf_op jit(solution)/shard_map/ppermute | solution.py:404
  84.2 4.4 %collective-permute-done.9.refs_6_ = bf16[528,256]{1,0:T(8,128)(2,1)S(1)} collective-permute-done((bf16[528,256]{1,0:T(8,128)(2,1)S(1)}, bf16[528,256]{1,0:T(8,128)(2,1)S(1)}, u32[]{:S(2)}, u32[]{:S(2)}) %collective-permute-start.9) | collective-permute-done | bytes 270368 | tf_op jit(solution)/shard_map/ppermute | solution.py:404
  89.3 4.6 %collective-permute-start.6 = (bf16[528,256]{1,0:T(8,128)(2,1)S(1)}, bf16[528,256]{1,0:T(8,128)(2,1)S(1)}, u32[]{:S(2)}, u32[]{:S(2)}) collective-permute-start(bf16[528,256]{1,0:T(8,128)(2,1)S(1)} %collective-permute-done.5), channel_id=1, source_target_pairs={{0,16},{32,48},{64,80},{96,112},{128,144},{160,176},{192,208},{224... | collective-permute-start | bytes 811016 | tf_op jit(solution)/shard_map/ppermute | solution.py:404
  95.7 3.4 %collective-permute-done.6 = bf16[528,256]{1,0:T(8,128)(2,1)S(1)} collective-permute-done((bf16[528,256]{1,0:T(8,128)(2,1)S(1)}, bf16[528,256]{1,0:T(8,128)(2,1)S(1)}, u32[]{:S(2)}, u32[]{:S(2)}) %collective-permute-start.6) | collective-permute-done | bytes 270368 | tf_op jit(solution)/shard_map/ppermute | solution.py:404
  99.2 3.4 %shard_map.162 = (f32[512,256]{1,0:T(8,128)S(1)}, f32[512,256]{1,0:T(8,128)S(1)}, f32[128,128]{1,0:T(8,128)S(1)}) custom-call(s32[1]{0:T(128)S(6)} %sub.26.refs_0_, s32[16,8]{1,0:T(8,128)S(1)} %stack.37.refs_1_, s32[16,8]{1,0:T(8,128)S(1)} %fusion.11.refs_2_, bf16[528,256]{1,0:T(8,128)(2,1)S(1)} %get-tuple-element.56.refs_2_.refs_3_, ...), custom_call_target="tpu_custom_call" | custom-call | flops 2500000000 | bytes 1000000 | tf_op jit(solution)/shard_map/pallas_call | solution.py:510
  102.6 4.1 %shard_map.164 = (bf16[4,9,96,128]{3,2,1,0:T(8,128)(2,1)S(1)}, bf16[4,9,96,128]{3,2,1,0:T(8,128)(2,1)S(1)}, bf16[512,384]{1,0:T(8,128)(2,1)S(1)}, bf16[512,512]{1,0:T(8,128)(2,1)S(1)}) custom-call(s32[3]{0:T(128)S(1)} %pad_add_fusion.place, f32[512,256]{1,0:T(8,128)S(1)} %get-tuple-element.70.d_donor, f32[512,256]{1,0:T(8,128)S(1)} %get-tuple-element.71.d_accept, ...), custom_call_target="tpu_custom_call" | custom-call | flops 4000000000 | bytes 1000000 | tf_op jit(solution)/shard_map/pallas_call | solution.py:524
  112.8 4.5 %collective-permute-start.12 = (bf16[2,4,304,128]{3,2,1,0:T(8,128)(2,1)S(1)}, bf16[2,4,304,128]{3,2,1,0:T(8,128)(2,1)S(1)}, u32[]{:S(2)}, u32[]{:S(2)}) collective-permute-start(bf16[2,4,304,128]{3,2,1,0:T(8,128)(2,1)S(1)} %slice.84), channel_id=1, source_target_pairs={{0,128},{128,0},{256,384},{384,256},{1,129},{129,1},{257,385},{385... | collective-permute-start | bytes 1867784 | tf_op jit(solution)/shard_map/ppermute | solution.py:543
  117.5 3.4 %collective-permute-start.15 = (bf16[2,9,96,128]{3,2,1,0:T(8,128)(2,1)S(1)}, bf16[2,9,96,128]{3,2,1,0:T(8,128)(2,1)S(1)}, u32[]{:S(2)}, u32[]{:S(2)}) collective-permute-start(bf16[2,9,96,128]{3,2,1,0:T(8,128)(2,1)S(1)} %get-tuple-element.90), channel_id=1, source_target_pairs={{128,256},{256,128},{384,0},{0,384},{129,257},{257,129},{385,1},{1... | collective-permute-start | bytes 1327112 | tf_op jit(solution)/shard_map/ppermute | solution.py:547
  120.9 10.8 %collective-permute-done.12.received = bf16[2,4,304,128]{3,2,1,0:T(8,128)(2,1)S(1)} collective-permute-done((bf16[2,4,304,128]{3,2,1,0:T(8,128)(2,1)S(1)}, bf16[2,4,304,128]{3,2,1,0:T(8,128)(2,1)S(1)}, u32[]{:S(2)}, u32[]{:S(2)}) %collective-permute-start.12) | collective-permute-done | bytes 622624 | tf_op jit(solution)/shard_map/ppermute | solution.py:543
  137.8 5.4 %collective-permute-done.13.head_in = bf16[4,304,128]{2,1,0:T(8,128)(2,1)S(1)} collective-permute-done((bf16[4,304,128]{2,1,0:T(8,128)(2,1)S(1)}, bf16[4,304,128]{2,1,0:T(8,128)(2,1)S(1)}, u32[]{:S(2)}, u32[]{:S(2)}) %collective-permute-start.13) | collective-permute-done | bytes 311328 | tf_op jit(solution)/shard_map/ppermute | solution.py:552
  143.3 18.2 %all_to_all.10.parts = bf16[4,528,128]{2,1,0:T(8,128)(2,1)S(1)} all-to-all(bf16[4,528,128]{2,1,0:T(8,128)(2,1)S(1)} %shard_map.169), channel_id=1, replica_groups=mesh['y'=4,'zb'=2,'zq'=4,'zhi'=2,'x'=4,'core'=2] {'zq'}, dimensions={0} | all-to-all | bytes 1081344 | tf_op jit(solution)/shard_map/all_to_all | solution.py:408
  162.3 4.1 %collective-permute-start.17 = (bf16[416,128]{1,0:T(8,128)(2,1)S(1)}, bf16[416,128]{1,0:T(8,128)(2,1)S(1)}, u32[]{:S(2)}, u32[]{:S(2)}) collective-permute-start(bf16[416,128]{1,0:T(8,128)(2,1)S(1)} %get-tuple-element.93.sent), channel_id=1, source_target_pairs={{0,64},{64,0},{1,65},{65,1},{2,66},{66,2},{3,67},{67,3},{4,68},{68... | collective-permute-start | bytes 319496 | tf_op jit(solution)/shard_map/ppermute | solution.py:564
  166.4 10.7 %collective-permute-start.19 = (bf16[112,128]{1,0:T(8,128)(2,1)S(1)}, bf16[112,128]{1,0:T(8,128)(2,1)S(1)}, u32[]{:S(2)}, u32[]{:S(2)}) collective-permute-start(bf16[112,128]{1,0:T(8,128)(2,1)S(1)} %slice.71), channel_id=1, source_target_pairs={{0,72},{72,0},{8,64},{64,8},{1,73},{73,1},{9,65},{65,9},{2,74},{74... | collective-permute-start | bytes 86024 | tf_op jit(solution)/shard_map/ppermute | solution.py:566
  180.4 10.3 %collective-permute-done.18.one = bf16[112,128]{1,0:T(8,128)(2,1)S(1)} collective-permute-done((bf16[112,128]{1,0:T(8,128)(2,1)S(1)}, bf16[112,128]{1,0:T(8,128)(2,1)S(1)}, u32[]{:S(2)}, u32[]{:S(2)}) %collective-permute-start.18) | collective-permute-done | bytes 28704 | tf_op jit(solution)/shard_map/ppermute | solution.py:565
  191.5 3.5 %all-to-all-start.1 = ((bf16[4,304,128]{2,1,0:T(8,128)(2,1)}), bf16[4,304,128]{2,1,0:T(8,128)(2,1)S(1)}, u32[]{:S(2)}, u32[]{:S(2)}) async-start(bf16[4,304,128]{2,1,0:T(8,128)(2,1)} %get-tuple-element.95), calls=%async_computation.1 | async-start | bytes 622592 | tf_op jit(solution)/shard_map/all_to_all | solution.py:408
  196.9 3.9 %collective-permute-start.21 = (bf16[112,128]{1,0:T(8,128)(2,1)S(1)}, bf16[112,128]{1,0:T(8,128)(2,1)S(1)}, u32[]{:S(2)}, u32[]{:S(2)}) collective-permute-start(bf16[112,128]{1,0:T(8,128)(2,1)S(1)} %get-tuple-element.96.own), channel_id=1, source_target_pairs={{0,4},{2,6},{4,0},{6,2},{1,5},{3,7},{5,1},{7,3},{8,12},{10,14},{12... | collective-permute-start | bytes 86024 | tf_op jit(solution)/shard_map/ppermute | solution.py:576
  200.8 4.0 %collective-permute-start.22 = (bf16[112,128]{1,0:T(8,128)(2,1)S(1)}, bf16[112,128]{1,0:T(8,128)(2,1)S(1)}, u32[]{:S(2)}, u32[]{:S(2)}) collective-permute-start(bf16[112,128]{1,0:T(8,128)(2,1)S(1)} %get-tuple-element.96.own), channel_id=1, source_target_pairs={{0,6},{2,0},{4,2},{6,4},{1,7},{3,1},{5,3},{7,5},{8,14},{10,8},{12,... | collective-permute-start | bytes 86024 | tf_op jit(solution)/shard_map/ppermute | solution.py:576
  208.8 3.4 %collective-permute-start.25 = (bf16[1216,128]{1,0:T(8,128)(2,1)S(1)}, bf16[1216,128]{1,0:T(8,128)(2,1)S(1)}, u32[]{:S(2)}, u32[]{:S(2)}) collective-permute-start(bf16[1216,128]{1,0:T(8,128)(2,1)S(1)} %bitcast.26), channel_id=1, source_target_pairs={{128,0},{256,128},{384,256},{0,384},{129,1},{257,129},{385,257},{1... | collective-permute-start | bytes 933896 | tf_op jit(solution)/shard_map/ppermute | solution.py:584
  212.3 7.9 %collective-permute-start.23 = (f32[112,128]{1,0:T(8,128)S(1)}, f32[112,128]{1,0:T(8,128)S(1)}, u32[]{:S(2)}, u32[]{:S(2)}) collective-permute-start(f32[112,128]{1,0:T(8,128)S(1)} %shard_map.172), channel_id=1, source_target_pairs={{0,1},{1,0},{2,3},{3,2},{4,5},{5,4},{6,7},{7,6},{8,9},{9,8},{10,11... | collective-permute-start | bytes 172040 | tf_op jit(solution)/shard_map/ppermute | solution.py:580
  222.2 4.6 %collective-permute-start.27 = (bf16[608,128]{1,0:T(8,128)(2,1)S(1)}, bf16[608,128]{1,0:T(8,128)(2,1)S(1)}, u32[]{:S(2)}, u32[]{:S(2)}) collective-permute-start(bf16[608,128]{1,0:T(8,128)(2,1)S(1)} %slice.86), channel_id=1, source_target_pairs={{128,0},{256,128},{384,256},{0,384},{129,1},{257,129},{385,257},{1... | collective-permute-start | bytes 466952 | tf_op jit(solution)/shard_map/ppermute | solution.py:586
  (111 shorter events, 54.4 us)
Async XLA Ops:
  2.5 13.3 %collective-permute-start.1 = (bf16[128,768]{1,0:T(8,128)(2,1)}, bf16[128,768]{1,0:T(8,128)(2,1)S(1)}, u32[]{:S(2)}, u32[]{:S(2)}) collective-permute-start(bf16[128,768]{1,0:T(8,128)(2,1)} %get-tuple-element.104), channel_id=1, source_target_pairs={{16,32},{48,64},{80,96},{112,128},{144,160},{176,192},{208,224},{2... | collective-permute-start | bytes 589832 | tf_op jit(solution)/shard_map/ppermute | solution.py:404
  3.1 12.9 %collective-permute-start = (bf16[128,768]{1,0:T(8,128)(2,1)S(1)}, bf16[128,768]{1,0:T(8,128)(2,1)S(1)}, u32[]{:S(2)}, u32[]{:S(2)}) collective-permute-start(bf16[128,768]{1,0:T(8,128)(2,1)S(1)} %get-tuple-element.105), channel_id=1, source_target_pairs={{0,16},{32,48},{64,80},{96,112},{128,144},{160,176},{192,208},{224... | collective-permute-start | bytes 589832 | tf_op jit(solution)/shard_map/ppermute | solution.py:404
  20.2 9.7 %collective-permute-start.7 = (bf16[528,256]{1,0:T(8,128)(2,1)S(1)}, bf16[528,256]{1,0:T(8,128)(2,1)S(1)}, u32[]{:S(2)}, u32[]{:S(2)}) collective-permute-start(bf16[528,256]{1,0:T(8,128)(2,1)S(1)} %get-tuple-element.57.refs_3_.refs_4_), channel_id=1, source_target_pairs={{0,16},{32,48},{64,80},{96,112},{128,144},{160,176},{192,208},{224... | collective-permute-start | bytes 811016 | tf_op jit(solution)/shard_map/ppermute | solution.py:404
  22.1 8.5 %collective-permute-start.3 = (bf16[528,256]{1,0:T(8,128)(2,1)S(1)}, bf16[528,256]{1,0:T(8,128)(2,1)S(1)}, u32[]{:S(2)}, u32[]{:S(2)}) collective-permute-start(bf16[528,256]{1,0:T(8,128)(2,1)S(1)} %get-tuple-element.56.refs_2_.refs_3_), channel_id=1, source_target_pairs={{16,32},{48,64},{80,96},{112,128},{144,160},{176,192},{208,224},{2... | collective-permute-start | bytes 811016 | tf_op jit(solution)/shard_map/ppermute | solution.py:404
  22.8 71.1 %collective-permute-start.11 = (bf16[528,256]{1,0:T(8,128)(2,1)S(1)}, bf16[528,256]{1,0:T(8,128)(2,1)S(1)}, u32[]{:S(2)}, u32[]{:S(2)}) collective-permute-start(bf16[528,256]{1,0:T(8,128)(2,1)S(1)} %broadcast_select_fusion.2), channel_id=1, source_target_pairs={{160,112},{288,240},{416,368},{80,128},{208,256},{336,384},{161,11... | collective-permute-start | bytes 811016 | tf_op jit(solution)/shard_map/ppermute | solution.py:493
  23.5 72.2 %collective-permute-start.2 = (bf16[528,256]{1,0:T(8,128)(2,1)S(1)}, bf16[528,256]{1,0:T(8,128)(2,1)S(1)}, u32[]{:S(2)}, u32[]{:S(2)}) collective-permute-start(bf16[528,256]{1,0:T(8,128)(2,1)S(1)} %broadcast_select_fusion.2), channel_id=1, source_target_pairs={{160,96},{176,112},{288,224},{304,240},{416,352},{432,368},{64,128... | collective-permute-start | bytes 811016 | tf_op jit(solution)/shard_map/ppermute | solution.py:492
  29.9 26.8 %collective-permute-start.8 = (bf16[528,256]{1,0:T(8,128)(2,1)S(1)}, bf16[528,256]{1,0:T(8,128)(2,1)S(1)}, u32[]{:S(2)}, u32[]{:S(2)}) collective-permute-start(bf16[528,256]{1,0:T(8,128)(2,1)S(1)} %shard_map.157.refs_6_), channel_id=1, source_target_pairs={{16,32},{48,64},{80,96},{112,128},{144,160},{176,192},{208,224},{2... | collective-permute-start | bytes 811016 | tf_op jit(solution)/shard_map/ppermute | solution.py:404
  30.6 25.4 %collective-permute-start.4 = (bf16[528,256]{1,0:T(8,128)(2,1)S(1)}, bf16[528,256]{1,0:T(8,128)(2,1)S(1)}, u32[]{:S(2)}, u32[]{:S(2)}) collective-permute-start(bf16[528,256]{1,0:T(8,128)(2,1)S(1)} %collective-permute-done.3.refs_5_), channel_id=1, source_target_pairs={{0,16},{32,48},{64,80},{96,112},{128,144},{160,176},{192,208},{224... | collective-permute-start | bytes 811016 | tf_op jit(solution)/shard_map/ppermute | solution.py:404
  56.0 33.4 %collective-permute-start.5 = (bf16[528,256]{1,0:T(8,128)(2,1)S(1)}, bf16[528,256]{1,0:T(8,128)(2,1)S(1)}, u32[]{:S(2)}, u32[]{:S(2)}) collective-permute-start(bf16[528,256]{1,0:T(8,128)(2,1)S(1)} %collective-permute-done.4.refs_6_), channel_id=1, source_target_pairs={{16,32},{48,64},{80,96},{144,160},{176,192},{208,224},{272,288},{3... | collective-permute-start | bytes 811016 | tf_op jit(solution)/shard_map/ppermute | solution.py:404
  56.7 32.0 %collective-permute-start.9 = (bf16[528,256]{1,0:T(8,128)(2,1)S(1)}, bf16[528,256]{1,0:T(8,128)(2,1)S(1)}, u32[]{:S(2)}, u32[]{:S(2)}) collective-permute-start(bf16[528,256]{1,0:T(8,128)(2,1)S(1)} %collective-permute-done.8.refs_5_), channel_id=1, source_target_pairs={{0,16},{32,48},{64,80},{96,112},{128,144},{160,176},{192,208},{224... | collective-permute-start | bytes 811016 | tf_op jit(solution)/shard_map/ppermute | solution.py:404
  89.3 9.8 %collective-permute-start.6 = (bf16[528,256]{1,0:T(8,128)(2,1)S(1)}, bf16[528,256]{1,0:T(8,128)(2,1)S(1)}, u32[]{:S(2)}, u32[]{:S(2)}) collective-permute-start(bf16[528,256]{1,0:T(8,128)(2,1)S(1)} %collective-permute-done.5), channel_id=1, source_target_pairs={{0,16},{32,48},{64,80},{96,112},{128,144},{160,176},{192,208},{224... | collective-permute-start | bytes 811016 | tf_op jit(solution)/shard_map/ppermute | solution.py:404
  106.7 10.5 %collective-permute-start.14 = (bf16[4,9,96,128]{3,2,1,0:T(8,128)(2,1)S(1)}, bf16[4,9,96,128]{3,2,1,0:T(8,128)(2,1)S(1)}, u32[]{:S(2)}, u32[]{:S(2)}) collective-permute-start(bf16[4,9,96,128]{3,2,1,0:T(8,128)(2,1)S(1)} %get-tuple-element.88), channel_id=1, source_target_pairs={{0,1},{1,0},{2,3},{3,2},{4,5},{5,4},{6,7},{7,6},{8,9},{9,8},{10,11... | collective-permute-start | bytes 2654216 | tf_op jit(solution)/shard_map/ppermute | solution.py:531
  112.8 18.9 %collective-permute-start.12 = (bf16[2,4,304,128]{3,2,1,0:T(8,128)(2,1)S(1)}, bf16[2,4,304,128]{3,2,1,0:T(8,128)(2,1)S(1)}, u32[]{:S(2)}, u32[]{:S(2)}) collective-permute-start(bf16[2,4,304,128]{3,2,1,0:T(8,128)(2,1)S(1)} %slice.84), channel_id=1, source_target_pairs={{0,128},{128,0},{256,384},{384,256},{1,129},{129,1},{257,385},{385... | collective-permute-start | bytes 1867784 | tf_op jit(solution)/shard_map/ppermute | solution.py:543
  117.5 17.6 %collective-permute-start.15 = (bf16[2,9,96,128]{3,2,1,0:T(8,128)(2,1)S(1)}, bf16[2,9,96,128]{3,2,1,0:T(8,128)(2,1)S(1)}, u32[]{:S(2)}, u32[]{:S(2)}) collective-permute-start(bf16[2,9,96,128]{3,2,1,0:T(8,128)(2,1)S(1)} %get-tuple-element.90), channel_id=1, source_target_pairs={{128,256},{256,128},{384,0},{0,384},{129,257},{257,129},{385,1},{1... | collective-permute-start | bytes 1327112 | tf_op jit(solution)/shard_map/ppermute | solution.py:547
  131.8 11.4 %collective-permute-start.13 = (bf16[4,304,128]{2,1,0:T(8,128)(2,1)S(1)}, bf16[4,304,128]{2,1,0:T(8,128)(2,1)S(1)}, u32[]{:S(2)}, u32[]{:S(2)}) collective-permute-start(bf16[4,304,128]{2,1,0:T(8,128)(2,1)S(1)} %get-tuple-element.86), channel_id=1, source_target_pairs={{128,256},{256,128},{384,0},{0,384},{129,257},{257,129},{385,1},{1... | collective-permute-start | bytes 933896 | tf_op jit(solution)/shard_map/ppermute | solution.py:552
  135.1 8.1 %collective-permute-start.16 = (bf16[9,96,128]{2,1,0:T(8,128)(2,1)S(1)}, bf16[9,96,128]{2,1,0:T(8,128)(2,1)S(1)}, u32[]{:S(2)}, u32[]{:S(2)}) collective-permute-start(bf16[9,96,128]{2,1,0:T(8,128)(2,1)S(1)} %get-tuple-element.92), channel_id=1, source_target_pairs={{0,128},{128,0},{256,384},{384,256},{1,129},{129,1},{257,385},{385... | collective-permute-start | bytes 663560 | tf_op jit(solution)/shard_map/ppermute | solution.py:553
  162.3 28.4 %collective-permute-start.17 = (bf16[416,128]{1,0:T(8,128)(2,1)S(1)}, bf16[416,128]{1,0:T(8,128)(2,1)S(1)}, u32[]{:S(2)}, u32[]{:S(2)}) collective-permute-start(bf16[416,128]{1,0:T(8,128)(2,1)S(1)} %get-tuple-element.93.sent), channel_id=1, source_target_pairs={{0,64},{64,0},{1,65},{65,1},{2,66},{66,2},{3,67},{67,3},{4,68},{68... | collective-permute-start | bytes 319496 | tf_op jit(solution)/shard_map/ppermute | solution.py:564
  166.4 13.9 %collective-permute-start.19 = (bf16[112,128]{1,0:T(8,128)(2,1)S(1)}, bf16[112,128]{1,0:T(8,128)(2,1)S(1)}, u32[]{:S(2)}, u32[]{:S(2)}) collective-permute-start(bf16[112,128]{1,0:T(8,128)(2,1)S(1)} %slice.71), channel_id=1, source_target_pairs={{0,72},{72,0},{8,64},{64,8},{1,73},{73,1},{9,65},{65,9},{2,74},{74... | collective-permute-start | bytes 86024 | tf_op jit(solution)/shard_map/ppermute | solution.py:566
  177.2 13.5 %collective-permute-start.18 = (bf16[112,128]{1,0:T(8,128)(2,1)S(1)}, bf16[112,128]{1,0:T(8,128)(2,1)S(1)}, u32[]{:S(2)}, u32[]{:S(2)}) collective-permute-start(bf16[112,128]{1,0:T(8,128)(2,1)S(1)} %get-tuple-element.94.mine), channel_id=1, source_target_pairs={{0,8},{8,0},{1,9},{9,1},{2,10},{10,2},{3,11},{11,3},{4,12},{12,4},... | collective-permute-start | bytes 86024 | tf_op jit(solution)/shard_map/ppermute | solution.py:565
  191.5 14.3 %all-to-all-start.1 = ((bf16[4,304,128]{2,1,0:T(8,128)(2,1)}), bf16[4,304,128]{2,1,0:T(8,128)(2,1)S(1)}, u32[]{:S(2)}, u32[]{:S(2)}) async-start(bf16[4,304,128]{2,1,0:T(8,128)(2,1)} %get-tuple-element.95), calls=%async_computation.1 | async-start | bytes 622592 | tf_op jit(solution)/shard_map/all_to_all | solution.py:408
  194.9 9.9 %collective-permute-start.20 = (bf16[112,128]{1,0:T(8,128)(2,1)S(1)}, bf16[112,128]{1,0:T(8,128)(2,1)S(1)}, u32[]{:S(2)}, u32[]{:S(2)}) collective-permute-start(bf16[112,128]{1,0:T(8,128)(2,1)S(1)} %get-tuple-element.96.own), channel_id=1, source_target_pairs={{0,2},{2,4},{4,6},{6,0},{1,3},{3,5},{5,7},{7,1},{8,10},{10,12},{12... | collective-permute-start | bytes 86024 | tf_op jit(solution)/shard_map/ppermute | solution.py:576
  205.8 14.4 %collective-permute-start.24 = (bf16[1216,128]{1,0:T(8,128)(2,1)S(1)}, bf16[1216,128]{1,0:T(8,128)(2,1)S(1)}, u32[]{:S(2)}, u32[]{:S(2)}) collective-permute-start(bf16[1216,128]{1,0:T(8,128)(2,1)S(1)} %bitcast.25), channel_id=1, source_target_pairs={{0,128},{128,256},{256,384},{384,0},{1,129},{129,257},{257,385},{3... | collective-permute-start | bytes 933896 | tf_op jit(solution)/shard_map/ppermute | solution.py:583
  208.8 13.3 %collective-permute-start.25 = (bf16[1216,128]{1,0:T(8,128)(2,1)S(1)}, bf16[1216,128]{1,0:T(8,128)(2,1)S(1)}, u32[]{:S(2)}, u32[]{:S(2)}) collective-permute-start(bf16[1216,128]{1,0:T(8,128)(2,1)S(1)} %bitcast.26), channel_id=1, source_target_pairs={{128,0},{256,128},{384,256},{0,384},{129,1},{257,129},{385,257},{1... | collective-permute-start | bytes 933896 | tf_op jit(solution)/shard_map/ppermute | solution.py:584
  212.3 14.5 %collective-permute-start.23 = (f32[112,128]{1,0:T(8,128)S(1)}, f32[112,128]{1,0:T(8,128)S(1)}, u32[]{:S(2)}, u32[]{:S(2)}) collective-permute-start(f32[112,128]{1,0:T(8,128)S(1)} %shard_map.172), channel_id=1, source_target_pairs={{0,1},{1,0},{2,3},{3,2},{4,5},{5,4},{6,7},{7,6},{8,9},{9,8},{10,11... | collective-permute-start | bytes 172040 | tf_op jit(solution)/shard_map/ppermute | solution.py:580
  (18 other events, 108.2 us)

commit v12 on v9

--- a/solution.py
+++ b/solution.py
@@ -128,10 +128,6 @@
     embed_t[...] = dot_t(eye[...], embed[...]).astype(BF16)
     inner = act.shape[1]
     act_t[...] = dot_t(eye[:inner, :inner], act[...]).astype(BF16)
-
-
-def copy_kernel(source, target):
-    target[...] = source[...]
 
 
 def pair_kernel(distance, *refs):
@@ -496,7 +492,6 @@
     for distance in range(1, SPAN + 1):
         if distance == 1:
             short_far, long_far = swapped(odd_feat, 0), swapped(even_feat, 1)
-            (short_far,) = call(copy_kernel, [feat], [VM], 4, 2000000000)(short_far)
         else:
             short_far, long_far = swapped(long_far, 0), swapped(short_far, 1, distance <= 2)
         short_use, long_use = short_far, long_far

time: 229 us -> 227 us (level)
  starting transfers between devices: 125 us -> 129 us
  waiting for transfers between devices: 44.6 us -> 41.2 us
    ppermute x10, starting transfers between devices: 52.6 us -> 46.1 us  [swapped(): return lax.ppermute(block, SEQ, pairs + [(j, i) for i, j in pairs])]
    ppermute x1, waiting for transfers between devices: 10.8 us -> 5.15 us  [on_device(): other = lax.ppermute(head_sum[2:], 'y', first_pairs)]
    ppermute x1, starting transfers between devices: 3.32 us -> 9.01 us  [on_device(): other = lax.ppermute(conv_send, 'y', second_pairs)]
    ppermute x1, starting transfers between devices: 4.18 us -> 9.01 us  [on_device(): heads_in = lax.ppermute(heads_send, 'y', second_pairs)]
    ppermute x10, waiting for transfers between devices: 15.6 us -> 18.5 us  [swapped(): return lax.ppermute(block, SEQ, pairs + [(j, i) for i, j in pairs])]
  transfers between devices with their start and end apart: 29 -> 29, of which waited for: 11 -> 10; matrix products, arithmetic and copies ran while one was open for 1% -> 1% of each run, Pallas kernels for 7% -> 7%
where the time goes in v12:
time: 227 us; the launch traced here: 225 us
  starting transfers between devices  129 us (57%)
  waiting for transfers between devices  41.2 us (18%)
  Pallas kernels  29.7 us (13%)
  blocking collectives  16.2 us (7%)
  local copies, waits for them, and re-layouts  4.73 us (2%)
    ppermute x10, starting transfers between devices, swapped(): return lax.ppermute(block, SEQ, pairs + [(j, i) for i, j in pairs])  46.1 us
    ppermute x10, waiting for transfers between devices, swapped(): return lax.ppermute(block, SEQ, pairs + [(j, i) for i, j in pairs])  18.5 us
    all_to_all x1, blocking collectives, swap_parts(): return lax.all_to_all(parts, axis, 0, 0, tiled=True)  16.2 us
    ppermute x3, starting transfers between devices, on_device(): lax.ppermute(conv_sum, 'x', [(i, (i + step) % 4) for i in range(4)])  10.9 us
    ppermute x1, starting transfers between devices, on_device(): heads_in = lax.ppermute(heads_send, 'y', second_pairs)  9.01 us
    ppermute x1, starting transfers between devices, on_device(): other = lax.ppermute(conv_send, 'y', second_pairs)  9.01 us
    pallas_call x4, Pallas kernels, on_device(): call(lambda *refs, distance=distance: pair_kernel(distance, *refs), acc_s...  7.99 us
    ppermute x1, waiting for transfers between devices, on_device(): across = lax.ppermute(mine, 'zhi', [(0, 1), (1, 0)])  7.78 us
  transfers between devices with their start and end apart: 29, of which 10 were waited for; matrix products, arithmetic and copies ran while one was open for 1% of the time, Pallas kernels for 7%

profile of v12, /device:TPU:1, one launch (start us, length us, event | category | flops | bytes accessed | tf_op | source)
XLA Modules:
  0.0 224.7 jit_solution(11852749556778344119)
XLA Ops:
  3.1 7.2 %collective-permute-start = (bf16[128,768]{1,0:T(8,128)(2,1)S(1)}, bf16[128,768]{1,0:T(8,128)(2,1)S(1)}, u32[]{:S(2)}, u32[]{:S(2)}) collective-permute-start(bf16[128,768]{1,0:T(8,128)(2,1)S(1)} %get-tuple-element.105), channel_id=1, source_target_pairs={{0,16},{32,48},{64,80},{96,112},{128,144},{160,176},{192,208},{224... | collective-permute-start | bytes 589832 | tf_op jit(solution)/shard_map/ppermute | solution.py:400
  20.9 8.8 %collective-permute-start.7 = (bf16[528,256]{1,0:T(8,128)(2,1)S(1)}, bf16[528,256]{1,0:T(8,128)(2,1)S(1)}, u32[]{:S(2)}, u32[]{:S(2)}) collective-permute-start(bf16[528,256]{1,0:T(8,128)(2,1)S(1)} %get-tuple-element.57.refs_3_.refs_4_), channel_id=1, source_target_pairs={{0,16},{32,48},{64,80},{96,112},{128,144},{160,176},{192,208},{224... | collective-permute-start | bytes 811016 | tf_op jit(solution)/shard_map/ppermute | solution.py:400
  41.7 11.4 %collective-permute-done.4.refs_6_ = bf16[528,256]{1,0:T(8,128)(2,1)S(1)} collective-permute-done((bf16[528,256]{1,0:T(8,128)(2,1)S(1)}, bf16[528,256]{1,0:T(8,128)(2,1)S(1)}, u32[]{:S(2)}, u32[]{:S(2)}) %collective-permute-start.4) | collective-permute-done | bytes 270368 | tf_op jit(solution)/shard_map/ppermute | solution.py:400
  53.8 20.2 %collective-permute-start.9 = (bf16[528,256]{1,0:T(8,128)(2,1)S(1)}, bf16[528,256]{1,0:T(8,128)(2,1)S(1)}, u32[]{:S(2)}, u32[]{:S(2)}) collective-permute-start(bf16[528,256]{1,0:T(8,128)(2,1)S(1)} %collective-permute-done.8.refs_5_), channel_id=1, source_target_pairs={{0,16},{32,48},{64,80},{96,112},{128,144},{160,176},{192,208},{224... | collective-permute-start | bytes 811016 | tf_op jit(solution)/shard_map/ppermute | solution.py:400
  76.0 4.0 %collective-permute-done.9.refs_6_ = bf16[528,256]{1,0:T(8,128)(2,1)S(1)} collective-permute-done((bf16[528,256]{1,0:T(8,128)(2,1)S(1)}, bf16[528,256]{1,0:T(8,128)(2,1)S(1)}, u32[]{:S(2)}, u32[]{:S(2)}) %collective-permute-start.9) | collective-permute-done | bytes 270368 | tf_op jit(solution)/shard_map/ppermute | solution.py:400
  80.7 4.6 %collective-permute-start.6 = (bf16[528,256]{1,0:T(8,128)(2,1)S(1)}, bf16[528,256]{1,0:T(8,128)(2,1)S(1)}, u32[]{:S(2)}, u32[]{:S(2)}) collective-permute-start(bf16[528,256]{1,0:T(8,128)(2,1)S(1)} %collective-permute-done.5), channel_id=1, source_target_pairs={{0,16},{32,48},{64,80},{96,112},{128,144},{160,176},{192,208},{224... | collective-permute-start | bytes 811016 | tf_op jit(solution)/shard_map/ppermute | solution.py:400
  92.9 4.1 %shard_map.163 = (bf16[4,9,96,128]{3,2,1,0:T(8,128)(2,1)S(1)}, bf16[4,9,96,128]{3,2,1,0:T(8,128)(2,1)S(1)}, bf16[512,384]{1,0:T(8,128)(2,1)S(1)}, bf16[512,512]{1,0:T(8,128)(2,1)S(1)}) custom-call(s32[3]{0:T(128)S(1)} %pad_add_fusion.place, f32[512,256]{1,0:T(8,128)S(1)} %get-tuple-element.70.d_donor, f32[512,256]{1,0:T(8,128)S(1)} %get-tuple-element.71.d_accept, ...), custom_call_target="tpu_custom_call" | custom-call | flops 4000000000 | bytes 1000000 | tf_op jit(solution)/shard_map/pallas_call | solution.py:518
  97.0 3.7 %collective-permute-start.14 = (bf16[4,9,96,128]{3,2,1,0:T(8,128)(2,1)S(1)}, bf16[4,9,96,128]{3,2,1,0:T(8,128)(2,1)S(1)}, u32[]{:S(2)}, u32[]{:S(2)}) collective-permute-start(bf16[4,9,96,128]{3,2,1,0:T(8,128)(2,1)S(1)} %get-tuple-element.88), channel_id=1, source_target_pairs={{0,1},{1,0},{2,3},{3,2},{4,5},{5,4},{6,7},{7,6},{8,9},{9,8},{10,11... | collective-permute-start | bytes 2654216 | tf_op jit(solution)/shard_map/ppermute | solution.py:525
  103.4 4.0 %collective-permute-start.12 = (bf16[2,4,304,128]{3,2,1,0:T(8,128)(2,1)S(1)}, bf16[2,4,304,128]{3,2,1,0:T(8,128)(2,1)S(1)}, u32[]{:S(2)}, u32[]{:S(2)}) collective-permute-start(bf16[2,4,304,128]{3,2,1,0:T(8,128)(2,1)S(1)} %slice.84), channel_id=1, source_target_pairs={{0,128},{128,0},{256,384},{384,256},{1,129},{129,1},{257,385},{385... | collective-permute-start | bytes 1867784 | tf_op jit(solution)/shard_map/ppermute | solution.py:537
  107.7 9.0 %collective-permute-start.15 = (bf16[2,9,96,128]{3,2,1,0:T(8,128)(2,1)S(1)}, bf16[2,9,96,128]{3,2,1,0:T(8,128)(2,1)S(1)}, u32[]{:S(2)}, u32[]{:S(2)}) collective-permute-start(bf16[2,9,96,128]{3,2,1,0:T(8,128)(2,1)S(1)} %get-tuple-element.90), channel_id=1, source_target_pairs={{128,256},{256,128},{384,0},{0,384},{129,257},{257,129},{385,1},{1... | collective-permute-start | bytes 1327112 | tf_op jit(solution)/shard_map/ppermute | solution.py:541
  116.7 5.1 %collective-permute-done.12.received = bf16[2,4,304,128]{3,2,1,0:T(8,128)(2,1)S(1)} collective-permute-done((bf16[2,4,304,128]{3,2,1,0:T(8,128)(2,1)S(1)}, bf16[2,4,304,128]{3,2,1,0:T(8,128)(2,1)S(1)}, u32[]{:S(2)}, u32[]{:S(2)}) %collective-permute-start.12) | collective-permute-done | bytes 622624 | tf_op jit(solution)/shard_map/ppermute | solution.py:537
  122.0 9.0 %collective-permute-start.13 = (bf16[4,304,128]{2,1,0:T(8,128)(2,1)S(1)}, bf16[4,304,128]{2,1,0:T(8,128)(2,1)S(1)}, u32[]{:S(2)}, u32[]{:S(2)}) collective-permute-start(bf16[4,304,128]{2,1,0:T(8,128)(2,1)S(1)} %get-tuple-element.86), channel_id=1, source_target_pairs={{128,256},{256,128},{384,0},{0,384},{129,257},{257,129},{385,1},{1... | collective-permute-start | bytes 933896 | tf_op jit(solution)/shard_map/ppermute | solution.py:546
  133.6 4.5 %collective-permute-done.13.head_in = bf16[4,304,128]{2,1,0:T(8,128)(2,1)S(1)} collective-permute-done((bf16[4,304,128]{2,1,0:T(8,128)(2,1)S(1)}, bf16[4,304,128]{2,1,0:T(8,128)(2,1)S(1)}, u32[]{:S(2)}, u32[]{:S(2)}) %collective-permute-start.13) | collective-permute-done | bytes 311328 | tf_op jit(solution)/shard_map/ppermute | solution.py:546
  139.1 16.2 %all_to_all.10.parts = bf16[4,528,128]{2,1,0:T(8,128)(2,1)S(1)} all-to-all(bf16[4,528,128]{2,1,0:T(8,128)(2,1)S(1)} %shard_map.168), channel_id=1, replica_groups=mesh['y'=4,'zb'=2,'zq'=4,'zhi'=2,'x'=4,'core'=2] {'zq'}, dimensions={0} | all-to-all | bytes 1081344 | tf_op jit(solution)/shard_map/all_to_all | solution.py:404
  156.1 4.2 %collective-permute-start.17 = (bf16[416,128]{1,0:T(8,128)(2,1)S(1)}, bf16[416,128]{1,0:T(8,128)(2,1)S(1)}, u32[]{:S(2)}, u32[]{:S(2)}) collective-permute-start(bf16[416,128]{1,0:T(8,128)(2,1)S(1)} %get-tuple-element.93.sent), channel_id=1, source_target_pairs={{0,64},{64,0},{1,65},{65,1},{2,66},{66,2},{3,67},{67,3},{4,68},{68... | collective-permute-start | bytes 319496 | tf_op jit(solution)/shard_map/ppermute | solution.py:558
  160.3 7.6 %collective-permute-start.19 = (bf16[112,128]{1,0:T(8,128)(2,1)S(1)}, bf16[112,128]{1,0:T(8,128)(2,1)S(1)}, u32[]{:S(2)}, u32[]{:S(2)}) collective-permute-start(bf16[112,128]{1,0:T(8,128)(2,1)S(1)} %slice.71), channel_id=1, source_target_pairs={{0,72},{72,0},{8,64},{64,8},{1,73},{73,1},{9,65},{65,9},{2,74},{74... | collective-permute-start | bytes 86024 | tf_op jit(solution)/shard_map/ppermute | solution.py:560
  167.9 5.6 %collective-permute-start.18 = (bf16[112,128]{1,0:T(8,128)(2,1)S(1)}, bf16[112,128]{1,0:T(8,128)(2,1)S(1)}, u32[]{:S(2)}, u32[]{:S(2)}) collective-permute-start(bf16[112,128]{1,0:T(8,128)(2,1)S(1)} %get-tuple-element.94.mine), channel_id=1, source_target_pairs={{0,8},{8,0},{1,9},{9,1},{2,10},{10,2},{3,11},{11,3},{4,12},{12,4},... | collective-permute-start | bytes 86024 | tf_op jit(solution)/shard_map/ppermute | solution.py:559
  173.6 7.8 %collective-permute-done.18.one = bf16[112,128]{1,0:T(8,128)(2,1)S(1)} collective-permute-done((bf16[112,128]{1,0:T(8,128)(2,1)S(1)}, bf16[112,128]{1,0:T(8,128)(2,1)S(1)}, u32[]{:S(2)}, u32[]{:S(2)}) %collective-permute-start.18) | collective-permute-done | bytes 28704 | tf_op jit(solution)/shard_map/ppermute | solution.py:559
  182.1 3.5 %all-to-all-start.1 = ((bf16[4,304,128]{2,1,0:T(8,128)(2,1)}), bf16[4,304,128]{2,1,0:T(8,128)(2,1)S(1)}, u32[]{:S(2)}, u32[]{:S(2)}) async-start(bf16[4,304,128]{2,1,0:T(8,128)(2,1)} %get-tuple-element.95), calls=%async_computation.1 | async-start | bytes 622592 | tf_op jit(solution)/shard_map/all_to_all | solution.py:404
  185.6 3.7 %collective-permute-start.20 = (bf16[112,128]{1,0:T(8,128)(2,1)S(1)}, bf16[112,128]{1,0:T(8,128)(2,1)S(1)}, u32[]{:S(2)}, u32[]{:S(2)}) collective-permute-start(bf16[112,128]{1,0:T(8,128)(2,1)S(1)} %get-tuple-element.96.own), channel_id=1, source_target_pairs={{0,2},{2,4},{4,6},{6,0},{1,3},{3,5},{5,7},{7,1},{8,10},{10,12},{12... | collective-permute-start | bytes 86024 | tf_op jit(solution)/shard_map/ppermute | solution.py:570
  189.3 5.2 %collective-permute-start.21 = (bf16[112,128]{1,0:T(8,128)(2,1)S(1)}, bf16[112,128]{1,0:T(8,128)(2,1)S(1)}, u32[]{:S(2)}, u32[]{:S(2)}) collective-permute-start(bf16[112,128]{1,0:T(8,128)(2,1)S(1)} %get-tuple-element.96.own), channel_id=1, source_target_pairs={{0,4},{2,6},{4,0},{6,2},{1,5},{3,7},{5,1},{7,3},{8,12},{10,14},{12... | collective-permute-start | bytes 86024 | tf_op jit(solution)/shard_map/ppermute | solution.py:570
  201.5 4.6 %collective-permute-start.25 = (bf16[1216,128]{1,0:T(8,128)(2,1)S(1)}, bf16[1216,128]{1,0:T(8,128)(2,1)S(1)}, u32[]{:S(2)}, u32[]{:S(2)}) collective-permute-start(bf16[1216,128]{1,0:T(8,128)(2,1)S(1)} %bitcast.26), channel_id=1, source_target_pairs={{128,0},{256,128},{384,256},{0,384},{129,1},{257,129},{385,257},{1... | collective-permute-start | bytes 933896 | tf_op jit(solution)/shard_map/ppermute | solution.py:578
  206.1 7.4 %collective-permute-start.23 = (f32[112,128]{1,0:T(8,128)S(1)}, f32[112,128]{1,0:T(8,128)S(1)}, u32[]{:S(2)}, u32[]{:S(2)}) collective-permute-start(f32[112,128]{1,0:T(8,128)S(1)} %shard_map.171), channel_id=1, source_target_pairs={{0,1},{1,0},{2,3},{3,2},{4,5},{5,4},{6,7},{7,6},{8,9},{9,8},{10,11... | collective-permute-start | bytes 172040 | tf_op jit(solution)/shard_map/ppermute | solution.py:574
  215.6 4.6 %collective-permute-start.27 = (bf16[608,128]{1,0:T(8,128)(2,1)S(1)}, bf16[608,128]{1,0:T(8,128)(2,1)S(1)}, u32[]{:S(2)}, u32[]{:S(2)}) collective-permute-start(bf16[608,128]{1,0:T(8,128)(2,1)S(1)} %slice.86), channel_id=1, source_target_pairs={{128,0},{256,128},{384,256},{0,384},{129,1},{257,129},{385,257},{1... | collective-permute-start | bytes 466952 | tf_op jit(solution)/shard_map/ppermute | solution.py:580
  (110 shorter events, 56.4 us)
Async XLA Ops:
  2.5 13.3 %collective-permute-start.1 = (bf16[128,768]{1,0:T(8,128)(2,1)}, bf16[128,768]{1,0:T(8,128)(2,1)S(1)}, u32[]{:S(2)}, u32[]{:S(2)}) collective-permute-start(bf16[128,768]{1,0:T(8,128)(2,1)} %get-tuple-element.104), channel_id=1, source_target_pairs={{16,32},{48,64},{80,96},{112,128},{144,160},{176,192},{208,224},{2... | collective-permute-start | bytes 589832 | tf_op jit(solution)/shard_map/ppermute | solution.py:400
  3.1 12.9 %collective-permute-start = (bf16[128,768]{1,0:T(8,128)(2,1)S(1)}, bf16[128,768]{1,0:T(8,128)(2,1)S(1)}, u32[]{:S(2)}, u32[]{:S(2)}) collective-permute-start(bf16[128,768]{1,0:T(8,128)(2,1)S(1)} %get-tuple-element.105), channel_id=1, source_target_pairs={{0,16},{32,48},{64,80},{96,112},{128,144},{160,176},{192,208},{224... | collective-permute-start | bytes 589832 | tf_op jit(solution)/shard_map/ppermute | solution.py:400
  20.2 15.9 %collective-permute-start.3 = (bf16[528,256]{1,0:T(8,128)(2,1)S(1)}, bf16[528,256]{1,0:T(8,128)(2,1)S(1)}, u32[]{:S(2)}, u32[]{:S(2)}) collective-permute-start(bf16[528,256]{1,0:T(8,128)(2,1)S(1)} %get-tuple-element.56.refs_2_.refs_3_), channel_id=1, source_target_pairs={{16,32},{48,64},{80,96},{112,128},{144,160},{176,192},{208,224},{2... | collective-permute-start | bytes 811016 | tf_op jit(solution)/shard_map/ppermute | solution.py:400
  20.9 17.1 %collective-permute-start.7 = (bf16[528,256]{1,0:T(8,128)(2,1)S(1)}, bf16[528,256]{1,0:T(8,128)(2,1)S(1)}, u32[]{:S(2)}, u32[]{:S(2)}) collective-permute-start(bf16[528,256]{1,0:T(8,128)(2,1)S(1)} %get-tuple-element.57.refs_3_.refs_4_), channel_id=1, source_target_pairs={{0,16},{32,48},{64,80},{96,112},{128,144},{160,176},{192,208},{224... | collective-permute-start | bytes 811016 | tf_op jit(solution)/shard_map/ppermute | solution.py:400
  29.7 9.0 %collective-permute-start.2 = (bf16[528,256]{1,0:T(8,128)(2,1)S(1)}, bf16[528,256]{1,0:T(8,128)(2,1)S(1)}, u32[]{:S(2)}, u32[]{:S(2)}) collective-permute-start(bf16[528,256]{1,0:T(8,128)(2,1)S(1)} %broadcast_select_fusion.2), channel_id=1, source_target_pairs={{160,96},{176,112},{288,224},{304,240},{416,352},{432,368},{64,128... | collective-permute-start | bytes 811016 | tf_op jit(solution)/shard_map/ppermute | solution.py:487
  36.1 17.0 %collective-permute-start.4 = (bf16[528,256]{1,0:T(8,128)(2,1)S(1)}, bf16[528,256]{1,0:T(8,128)(2,1)S(1)}, u32[]{:S(2)}, u32[]{:S(2)}) collective-permute-start(bf16[528,256]{1,0:T(8,128)(2,1)S(1)} %collective-permute-done.3.refs_5_), channel_id=1, source_target_pairs={{0,16},{32,48},{64,80},{96,112},{128,144},{160,176},{192,208},{224... | collective-permute-start | bytes 811016 | tf_op jit(solution)/shard_map/ppermute | solution.py:400
  38.0 15.7 %collective-permute-start.8 = (bf16[528,256]{1,0:T(8,128)(2,1)S(1)}, bf16[528,256]{1,0:T(8,128)(2,1)S(1)}, u32[]{:S(2)}, u32[]{:S(2)}) collective-permute-start(bf16[528,256]{1,0:T(8,128)(2,1)S(1)} %collective-permute-done.7.refs_6_), channel_id=1, source_target_pairs={{16,32},{48,64},{80,96},{112,128},{144,160},{176,192},{208,224},{2... | collective-permute-start | bytes 811016 | tf_op jit(solution)/shard_map/ppermute | solution.py:400
  38.7 46.6 %collective-permute-start.11 = (bf16[528,256]{1,0:T(8,128)(2,1)S(1)}, bf16[528,256]{1,0:T(8,128)(2,1)S(1)}, u32[]{:S(2)}, u32[]{:S(2)}) collective-permute-start(bf16[528,256]{1,0:T(8,128)(2,1)S(1)} %collective-permute-done.2), channel_id=1, source_target_pairs={{96,112},{224,240},{352,368},{480,496},{16,0},{144,128},{272,256},... | collective-permute-start | bytes 811016 | tf_op jit(solution)/shard_map/ppermute | solution.py:488
  53.1 27.6 %collective-permute-start.5 = (bf16[528,256]{1,0:T(8,128)(2,1)S(1)}, bf16[528,256]{1,0:T(8,128)(2,1)S(1)}, u32[]{:S(2)}, u32[]{:S(2)}) collective-permute-start(bf16[528,256]{1,0:T(8,128)(2,1)S(1)} %collective-permute-done.4.refs_6_), channel_id=1, source_target_pairs={{16,32},{48,64},{80,96},{144,160},{176,192},{208,224},{272,288},{3... | collective-permute-start | bytes 811016 | tf_op jit(solution)/shard_map/ppermute | solution.py:400
  53.8 26.3 %collective-permute-start.9 = (bf16[528,256]{1,0:T(8,128)(2,1)S(1)}, bf16[528,256]{1,0:T(8,128)(2,1)S(1)}, u32[]{:S(2)}, u32[]{:S(2)}) collective-permute-start(bf16[528,256]{1,0:T(8,128)(2,1)S(1)} %collective-permute-done.8.refs_5_), channel_id=1, source_target_pairs={{0,16},{32,48},{64,80},{96,112},{128,144},{160,176},{192,208},{224... | collective-permute-start | bytes 811016 | tf_op jit(solution)/shard_map/ppermute | solution.py:400
  80.7 9.7 %collective-permute-start.6 = (bf16[528,256]{1,0:T(8,128)(2,1)S(1)}, bf16[528,256]{1,0:T(8,128)(2,1)S(1)}, u32[]{:S(2)}, u32[]{:S(2)}) collective-permute-start(bf16[528,256]{1,0:T(8,128)(2,1)S(1)} %collective-permute-done.5), channel_id=1, source_target_pairs={{0,16},{32,48},{64,80},{96,112},{128,144},{160,176},{192,208},{224... | collective-permute-start | bytes 811016 | tf_op jit(solution)/shard_map/ppermute | solution.py:400
  97.0 10.4 %collective-permute-start.14 = (bf16[4,9,96,128]{3,2,1,0:T(8,128)(2,1)S(1)}, bf16[4,9,96,128]{3,2,1,0:T(8,128)(2,1)S(1)}, u32[]{:S(2)}, u32[]{:S(2)}) collective-permute-start(bf16[4,9,96,128]{3,2,1,0:T(8,128)(2,1)S(1)} %get-tuple-element.88), channel_id=1, source_target_pairs={{0,1},{1,0},{2,3},{3,2},{4,5},{5,4},{6,7},{7,6},{8,9},{9,8},{10,11... | collective-permute-start | bytes 2654216 | tf_op jit(solution)/shard_map/ppermute | solution.py:525
  103.4 18.4 %collective-permute-start.12 = (bf16[2,4,304,128]{3,2,1,0:T(8,128)(2,1)S(1)}, bf16[2,4,304,128]{3,2,1,0:T(8,128)(2,1)S(1)}, u32[]{:S(2)}, u32[]{:S(2)}) collective-permute-start(bf16[2,4,304,128]{3,2,1,0:T(8,128)(2,1)S(1)} %slice.84), channel_id=1, source_target_pairs={{0,128},{128,0},{256,384},{384,256},{1,129},{129,1},{257,385},{385... | collective-permute-start | bytes 1867784 | tf_op jit(solution)/shard_map/ppermute | solution.py:537
  107.7 23.3 %collective-permute-start.15 = (bf16[2,9,96,128]{3,2,1,0:T(8,128)(2,1)S(1)}, bf16[2,9,96,128]{3,2,1,0:T(8,128)(2,1)S(1)}, u32[]{:S(2)}, u32[]{:S(2)}) collective-permute-start(bf16[2,9,96,128]{3,2,1,0:T(8,128)(2,1)S(1)} %get-tuple-element.90), channel_id=1, source_target_pairs={{128,256},{256,128},{384,0},{0,384},{129,257},{257,129},{385,1},{1... | collective-permute-start | bytes 1327112 | tf_op jit(solution)/shard_map/ppermute | solution.py:541
  122.0 16.2 %collective-permute-start.13 = (bf16[4,304,128]{2,1,0:T(8,128)(2,1)S(1)}, bf16[4,304,128]{2,1,0:T(8,128)(2,1)S(1)}, u32[]{:S(2)}, u32[]{:S(2)}) collective-permute-start(bf16[4,304,128]{2,1,0:T(8,128)(2,1)S(1)} %get-tuple-element.86), channel_id=1, source_target_pairs={{128,256},{256,128},{384,0},{0,384},{129,257},{257,129},{385,1},{1... | collective-permute-start | bytes 933896 | tf_op jit(solution)/shard_map/ppermute | solution.py:546
  131.1 8.0 %collective-permute-start.16 = (bf16[9,96,128]{2,1,0:T(8,128)(2,1)S(1)}, bf16[9,96,128]{2,1,0:T(8,128)(2,1)S(1)}, u32[]{:S(2)}, u32[]{:S(2)}) collective-permute-start(bf16[9,96,128]{2,1,0:T(8,128)(2,1)S(1)} %get-tuple-element.92), channel_id=1, source_target_pairs={{0,128},{128,0},{256,384},{384,256},{1,129},{129,1},{257,385},{385... | collective-permute-start | bytes 663560 | tf_op jit(solution)/shard_map/ppermute | solution.py:547
  156.1 25.3 %collective-permute-start.17 = (bf16[416,128]{1,0:T(8,128)(2,1)S(1)}, bf16[416,128]{1,0:T(8,128)(2,1)S(1)}, u32[]{:S(2)}, u32[]{:S(2)}) collective-permute-start(bf16[416,128]{1,0:T(8,128)(2,1)S(1)} %get-tuple-element.93.sent), channel_id=1, source_target_pairs={{0,64},{64,0},{1,65},{65,1},{2,66},{66,2},{3,67},{67,3},{4,68},{68... | collective-permute-start | bytes 319496 | tf_op jit(solution)/shard_map/ppermute | solution.py:558
  160.3 13.3 %collective-permute-start.19 = (bf16[112,128]{1,0:T(8,128)(2,1)S(1)}, bf16[112,128]{1,0:T(8,128)(2,1)S(1)}, u32[]{:S(2)}, u32[]{:S(2)}) collective-permute-start(bf16[112,128]{1,0:T(8,128)(2,1)S(1)} %slice.71), channel_id=1, source_target_pairs={{0,72},{72,0},{8,64},{64,8},{1,73},{73,1},{9,65},{65,9},{2,74},{74... | collective-permute-start | bytes 86024 | tf_op jit(solution)/shard_map/ppermute | solution.py:560
  167.9 13.4 %collective-permute-start.18 = (bf16[112,128]{1,0:T(8,128)(2,1)S(1)}, bf16[112,128]{1,0:T(8,128)(2,1)S(1)}, u32[]{:S(2)}, u32[]{:S(2)}) collective-permute-start(bf16[112,128]{1,0:T(8,128)(2,1)S(1)} %get-tuple-element.94.mine), channel_id=1, source_target_pairs={{0,8},{8,0},{1,9},{9,1},{2,10},{10,2},{3,11},{11,3},{4,12},{12,4},... | collective-permute-start | bytes 86024 | tf_op jit(solution)/shard_map/ppermute | solution.py:559
  182.1 17.5 %all-to-all-start.1 = ((bf16[4,304,128]{2,1,0:T(8,128)(2,1)}), bf16[4,304,128]{2,1,0:T(8,128)(2,1)S(1)}, u32[]{:S(2)}, u32[]{:S(2)}) async-start(bf16[4,304,128]{2,1,0:T(8,128)(2,1)} %get-tuple-element.95), calls=%async_computation.1 | async-start | bytes 622592 | tf_op jit(solution)/shard_map/all_to_all | solution.py:404
  185.6 10.9 %collective-permute-start.20 = (bf16[112,128]{1,0:T(8,128)(2,1)S(1)}, bf16[112,128]{1,0:T(8,128)(2,1)S(1)}, u32[]{:S(2)}, u32[]{:S(2)}) collective-permute-start(bf16[112,128]{1,0:T(8,128)(2,1)S(1)} %get-tuple-element.96.own), channel_id=1, source_target_pairs={{0,2},{2,4},{4,6},{6,0},{1,3},{3,5},{5,7},{7,1},{8,10},{10,12},{12... | collective-permute-start | bytes 86024 | tf_op jit(solution)/shard_map/ppermute | solution.py:570
  199.6 13.9 %collective-permute-start.24 = (bf16[1216,128]{1,0:T(8,128)(2,1)S(1)}, bf16[1216,128]{1,0:T(8,128)(2,1)S(1)}, u32[]{:S(2)}, u32[]{:S(2)}) collective-permute-start(bf16[1216,128]{1,0:T(8,128)(2,1)S(1)} %bitcast.25), channel_id=1, source_target_pairs={{0,128},{128,256},{256,384},{384,0},{1,129},{129,257},{257,385},{3... | collective-permute-start | bytes 933896 | tf_op jit(solution)/shard_map/ppermute | solution.py:577
  201.5 14.0 %collective-permute-start.25 = (bf16[1216,128]{1,0:T(8,128)(2,1)S(1)}, bf16[1216,128]{1,0:T(8,128)(2,1)S(1)}, u32[]{:S(2)}, u32[]{:S(2)}) collective-permute-start(bf16[1216,128]{1,0:T(8,128)(2,1)S(1)} %bitcast.26), channel_id=1, source_target_pairs={{128,0},{256,128},{384,256},{0,384},{129,1},{257,129},{385,257},{1... | collective-permute-start | bytes 933896 | tf_op jit(solution)/shard_map/ppermute | solution.py:578
  206.1 14.0 %collective-permute-start.23 = (f32[112,128]{1,0:T(8,128)S(1)}, f32[112,128]{1,0:T(8,128)S(1)}, u32[]{:S(2)}, u32[]{:S(2)}) collective-permute-start(f32[112,128]{1,0:T(8,128)S(1)} %shard_map.171), channel_id=1, source_target_pairs={{0,1},{1,0},{2,3},{3,2},{4,5},{5,4},{6,7},{7,6},{8,9},{9,8},{10,11... | collective-permute-start | bytes 172040 | tf_op jit(solution)/shard_map/ppermute | solution.py:574
  (18 other events, 112.4 us)

commit v13 on v6

--- a/solution.py
+++ b/solution.py
@@ -348,9 +348,8 @@
     taps[...] = (near + (one[...].astype(F32) + two[...].astype(F32))).astype(BF16)
 
 
-def line_total_kernel(own, one, two, three, total):
-    even = own[...].astype(F32) + two[...].astype(F32)
-    total[...] = even + (one[...].astype(F32) + three[...].astype(F32))
+def add_kernel(one, two, total):
+    total[...] = (one[...].astype(F32) + two[...].astype(F32)).astype(total.dtype)
 
 
 def finish_kernel(
@@ -563,10 +562,10 @@
 
     head_rows = 4 * chunk
     head_sum = swap_parts(head_parts, "zq").reshape(head_rows, 128)
-    line = [
-        lax.ppermute(conv_sum, "x", [(i, (i + step) % 4) for i in range(4)]) for step in (1, 2, 3)
-    ]
-    (conv_sum,) = call(line_total_kernel, [shape((112, 128), F32)], [VM] * 4, 8, quick)(conv_sum, *line)
+    other = lax.ppermute(conv_sum, "x", first_pairs)
+    (conv_sum,) = call(add_kernel, [shape((112, 128), BF16)], [VM] * 2, 8, quick)(conv_sum, other)
+    other = lax.ppermute(conv_sum, "x", second_pairs)
+    (conv_sum,) = call(add_kernel, [shape((112, 128), F32)], [VM] * 2, 8, quick)(conv_sum, other)
     head_sum, conv_sum = lax.optimization_barrier((head_sum, conv_sum))
     other = lax.ppermute(conv_sum, "core", [(0, 1), (1, 0)])
     around = [(i, (i + 1) % 4) for i in range(4)]

time: 225 us -> 223 us (level)
  starting transfers between devices: 133 us -> 128 us
    ppermute x3 -> x2, starting transfers between devices: 10.6 us -> 7.13 us  [the longest x1 3.82 us: on_device(): other = lax.ppermute(conv_sum, 'x', second_pairs)]
    pallas_call x4, Pallas kernels: 7.31 us -> 9.69 us  [on_device(): call(lambda *refs, distance=distance: pair_kernel(distance, *refs), acc_s...]
    ppermute x1, starting transfers between devices: 6.83 us -> 4.57 us  [on_device(): received = lax.ppermute(send, 'core', [(0, 1), (1, 0)])]
  transfers between devices with their start and end apart: 29 -> 28, of which waited for: 10 -> 11; matrix products, arithmetic and copies ran while one was open for 1% -> 1% of each run, Pallas kernels for 8% -> 8%
where the time goes in v13:
time: 223 us; the launch traced here: 221 us
  starting transfers between devices  128 us (57%)
  waiting for transfers between devices  39.8 us (18%)
  Pallas kernels  32.2 us (14%)
  blocking collectives  16.4 us (7%)
  other arithmetic  2.23 us (1%)
    ppermute x10, starting transfers between devices, swapped(): return lax.ppermute(block, SEQ, pairs + [(j, i) for i, j in pairs])  50.2 us
    all_to_all x1, blocking collectives, swap_parts(): return lax.all_to_all(parts, axis, 0, 0, tiled=True)  16.4 us
    ppermute x10, waiting for transfers between devices, swapped(): return lax.ppermute(block, SEQ, pairs + [(j, i) for i, j in pairs])  10.7 us
    ppermute x1, waiting for transfers between devices, on_device(): across = lax.ppermute(mine, 'zhi', [(0, 1), (1, 0)])  10.3 us
    pallas_call x4, Pallas kernels, on_device(): call(lambda *refs, distance=distance: pair_kernel(distance, *refs), acc_s...  9.69 us
    ppermute x1, starting transfers between devices, on_device(): other = lax.ppermute(head_sum[2:], 'y', first_pairs)  9.51 us
    ppermute x1, waiting for transfers between devices, on_device(): other = lax.ppermute(head_sum[2:], 'y', first_pairs)  8.89 us
    ppermute x1, starting transfers between devices, on_device(): other = lax.ppermute(conv_sum, 'core', [(0, 1), (1, 0)])  8.38 us
  transfers between devices with their start and end apart: 28, of which 11 were waited for; matrix products, arithmetic and copies ran while one was open for 1% of the time, Pallas kernels for 8%

profile of v13, /device:TPU:1, one launch (start us, length us, event | category | flops | bytes accessed | tf_op | source)
XLA Modules:
  0.0 221.4 jit_solution(16072874324069805516)
XLA Ops:
  2.5 4.4 %collective-permute-start = (bf16[128,768]{1,0:T(8,128)(2,1)}, bf16[128,768]{1,0:T(8,128)(2,1)S(1)}, u32[]{:S(2)}, u32[]{:S(2)}) collective-permute-start(bf16[128,768]{1,0:T(8,128)(2,1)} %get-tuple-element.107), channel_id=1, source_target_pairs={{0,16},{32,48},{64,80},{96,112},{128,144},{160,176},{192,208},{224... | collective-permute-start | bytes 589832 | tf_op jit(solution)/shard_map/ppermute | solution.py:397
  14.8 8.5 %collective-permute-start.7 = (bf16[528,256]{1,0:T(8,128)(2,1)S(1)}, bf16[528,256]{1,0:T(8,128)(2,1)S(1)}, u32[]{:S(2)}, u32[]{:S(2)}) collective-permute-start(bf16[528,256]{1,0:T(8,128)(2,1)S(1)} %get-tuple-element.59.refs_3_.refs_4_), channel_id=1, source_target_pairs={{0,16},{32,48},{64,80},{96,112},{128,144},{160,176},{192,208},{224... | collective-permute-start | bytes 811016 | tf_op jit(solution)/shard_map/ppermute | solution.py:397
  24.1 3.9 %shard_map.161 = (bf16[256,768]{1,0:T(8,128)(2,1)S(1)}, f32[512,384]{1,0:T(8,128)S(1)}, bf16[768,768]{1,0:T(8,128)(2,1)S(1)}, bf16[384,512]{1,0:T(8,128)(2,1)S(1)}, bf16[768,512]{1,0:T(8,128)(2,1)S(1)}) custom-call(s32[2]{0:T(128)S(1)} %pad_add_fusion.1.odd, bf16[128,768]{1,0:T(8,128)(2,1)S(1)} %collective-permute-done.even_edge, ...), custom_call_target="tpu_custom_call" | custom-call | flops 6000000000 | bytes 1000000 | tf_op jit(solution)/shard_map/pallas_call | solution.py:465
  38.1 29.7 %collective-permute-start.9 = (bf16[528,256]{1,0:T(8,128)(2,1)S(1)}, bf16[528,256]{1,0:T(8,128)(2,1)S(1)}, u32[]{:S(2)}, u32[]{:S(2)}) collective-permute-start(bf16[528,256]{1,0:T(8,128)(2,1)S(1)} %collective-permute-done.8.refs_5_), channel_id=1, source_target_pairs={{0,16},{32,48},{64,80},{96,112},{128,144},{160,176},{192,208},{224... | collective-permute-start | bytes 811016 | tf_op jit(solution)/shard_map/ppermute | solution.py:397
  67.8 3.0 %shard_map.158 = (f32[512,256]{1,0:T(8,128)S(1)}, f32[512,256]{1,0:T(8,128)S(1)}, f32[128,128]{1,0:T(8,128)S(1)}) custom-call(s32[1]{0:T(128)S(6)} %sub.26.refs_0_, s32[16,8]{1,0:T(8,128)S(1)} %stack.47.refs_1_, s32[16,8]{1,0:T(8,128)S(1)} %fusion.9.refs_2_, bf16[528,256]{1,0:T(8,128)(2,1)S(1)} %get-tuple-element.58.refs_2_.refs_3_, ...), custom_call_target="tpu_custom_call" | custom-call | flops 2500000000 | bytes 1000000 | tf_op jit(solution)/shard_map/pallas_call | solution.py:500
  70.8 5.9 %collective-permute-done.9.refs_6_ = bf16[528,256]{1,0:T(8,128)(2,1)S(1)} collective-permute-done((bf16[528,256]{1,0:T(8,128)(2,1)S(1)}, bf16[528,256]{1,0:T(8,128)(2,1)S(1)}, u32[]{:S(2)}, u32[]{:S(2)}) %collective-permute-start.9) | collective-permute-done | bytes 270368 | tf_op jit(solution)/shard_map/ppermute | solution.py:397
  88.2 4.1 %shard_map.162 = (bf16[4,9,96,128]{3,2,1,0:T(8,128)(2,1)S(1)}, bf16[4,9,96,128]{3,2,1,0:T(8,128)(2,1)S(1)}, bf16[512,384]{1,0:T(8,128)(2,1)S(1)}, bf16[512,512]{1,0:T(8,128)(2,1)S(1)}) custom-call(s32[3]{0:T(128)S(1)} %pad_add_fusion.place, f32[512,256]{1,0:T(8,128)S(1)} %get-tuple-element.72.d_donor, f32[512,256]{1,0:T(8,128)S(1)} %get-tuple-element.73.d_accept, ...), custom_call_target="tpu_custom_call" | custom-call | flops 4000000000 | bytes 1000000 | tf_op jit(solution)/shard_map/pallas_call | solution.py:514
  92.3 4.6 %collective-permute-start.14 = (bf16[4,9,96,128]{3,2,1,0:T(8,128)(2,1)S(1)}, bf16[4,9,96,128]{3,2,1,0:T(8,128)(2,1)S(1)}, u32[]{:S(2)}, u32[]{:S(2)}) collective-permute-start(bf16[4,9,96,128]{3,2,1,0:T(8,128)(2,1)S(1)} %get-tuple-element.90), channel_id=1, source_target_pairs={{0,1},{1,0},{2,3},{3,2},{4,5},{5,4},{6,7},{7,6},{8,9},{9,8},{10,11... | collective-permute-start | bytes 2654216 | tf_op jit(solution)/shard_map/ppermute | solution.py:521
  99.6 9.5 %collective-permute-start.12 = (bf16[2,4,304,128]{3,2,1,0:T(8,128)(2,1)S(1)}, bf16[2,4,304,128]{3,2,1,0:T(8,128)(2,1)S(1)}, u32[]{:S(2)}, u32[]{:S(2)}) collective-permute-start(bf16[2,4,304,128]{3,2,1,0:T(8,128)(2,1)S(1)} %slice.84), channel_id=1, source_target_pairs={{0,128},{128,0},{256,384},{384,256},{1,129},{129,1},{257,385},{385... | collective-permute-start | bytes 1867784 | tf_op jit(solution)/shard_map/ppermute | solution.py:533
  109.4 5.3 %collective-permute-start.15 = (bf16[2,9,96,128]{3,2,1,0:T(8,128)(2,1)S(1)}, bf16[2,9,96,128]{3,2,1,0:T(8,128)(2,1)S(1)}, u32[]{:S(2)}, u32[]{:S(2)}) collective-permute-start(bf16[2,9,96,128]{3,2,1,0:T(8,128)(2,1)S(1)} %get-tuple-element.92), channel_id=1, source_target_pairs={{128,256},{256,128},{384,0},{0,384},{129,257},{257,129},{385,1},{1... | collective-permute-start | bytes 1327112 | tf_op jit(solution)/shard_map/ppermute | solution.py:537
  114.6 8.9 %collective-permute-done.12.received = bf16[2,4,304,128]{3,2,1,0:T(8,128)(2,1)S(1)} collective-permute-done((bf16[2,4,304,128]{3,2,1,0:T(8,128)(2,1)S(1)}, bf16[2,4,304,128]{3,2,1,0:T(8,128)(2,1)S(1)}, u32[]{:S(2)}, u32[]{:S(2)}) %collective-permute-start.12) | collective-permute-done | bytes 622624 | tf_op jit(solution)/shard_map/ppermute | solution.py:533
  123.7 5.3 %collective-permute-start.13 = (bf16[4,304,128]{2,1,0:T(8,128)(2,1)S(1)}, bf16[4,304,128]{2,1,0:T(8,128)(2,1)S(1)}, u32[]{:S(2)}, u32[]{:S(2)}) collective-permute-start(bf16[4,304,128]{2,1,0:T(8,128)(2,1)S(1)} %get-tuple-element.88), channel_id=1, source_target_pairs={{128,256},{256,128},{384,0},{0,384},{129,257},{257,129},{385,1},{1... | collective-permute-start | bytes 933896 | tf_op jit(solution)/shard_map/ppermute | solution.py:542
  131.6 4.5 %collective-permute-done.13.head_in = bf16[4,304,128]{2,1,0:T(8,128)(2,1)S(1)} collective-permute-done((bf16[4,304,128]{2,1,0:T(8,128)(2,1)S(1)}, bf16[4,304,128]{2,1,0:T(8,128)(2,1)S(1)}, u32[]{:S(2)}, u32[]{:S(2)}) %collective-permute-start.13) | collective-permute-done | bytes 311328 | tf_op jit(solution)/shard_map/ppermute | solution.py:542
  137.1 16.4 %all_to_all.10.parts = bf16[4,528,128]{2,1,0:T(8,128)(2,1)S(1)} all-to-all(bf16[4,528,128]{2,1,0:T(8,128)(2,1)S(1)} %shard_map.167), channel_id=1, replica_groups=mesh['y'=4,'zb'=2,'zq'=4,'zhi'=2,'x'=4,'core'=2] {'zq'}, dimensions={0} | all-to-all | bytes 1081344 | tf_op jit(solution)/shard_map/all_to_all | solution.py:401
  154.2 5.0 %collective-permute-start.17 = (bf16[416,128]{1,0:T(8,128)(2,1)S(1)}, bf16[416,128]{1,0:T(8,128)(2,1)S(1)}, u32[]{:S(2)}, u32[]{:S(2)}) collective-permute-start(bf16[416,128]{1,0:T(8,128)(2,1)S(1)} %get-tuple-element.95.sent), channel_id=1, source_target_pairs={{0,64},{64,0},{1,65},{65,1},{2,66},{66,2},{3,67},{67,3},{4,68},{68... | collective-permute-start | bytes 319496 | tf_op jit(solution)/shard_map/ppermute | solution.py:554
  159.3 8.0 %collective-permute-start.19 = (bf16[112,128]{1,0:T(8,128)(2,1)S(1)}, bf16[112,128]{1,0:T(8,128)(2,1)S(1)}, u32[]{:S(2)}, u32[]{:S(2)}) collective-permute-start(bf16[112,128]{1,0:T(8,128)(2,1)S(1)} %slice.71), channel_id=1, source_target_pairs={{0,72},{72,0},{8,64},{64,8},{1,73},{73,1},{9,65},{65,9},{2,74},{74... | collective-permute-start | bytes 86024 | tf_op jit(solution)/shard_map/ppermute | solution.py:556
  167.3 3.2 %collective-permute-start.18 = (bf16[112,128]{1,0:T(8,128)(2,1)S(1)}, bf16[112,128]{1,0:T(8,128)(2,1)S(1)}, u32[]{:S(2)}, u32[]{:S(2)}) collective-permute-start(bf16[112,128]{1,0:T(8,128)(2,1)S(1)} %get-tuple-element.96.mine), channel_id=1, source_target_pairs={{0,8},{8,0},{1,9},{9,1},{2,10},{10,2},{3,11},{11,3},{4,12},{12,4},... | collective-permute-start | bytes 86024 | tf_op jit(solution)/shard_map/ppermute | solution.py:555
  170.5 10.3 %collective-permute-done.18.one = bf16[112,128]{1,0:T(8,128)(2,1)S(1)} collective-permute-done((bf16[112,128]{1,0:T(8,128)(2,1)S(1)}, bf16[112,128]{1,0:T(8,128)(2,1)S(1)}, u32[]{:S(2)}, u32[]{:S(2)}) %collective-permute-start.18) | collective-permute-done | bytes 28704 | tf_op jit(solution)/shard_map/ppermute | solution.py:555
  181.5 3.5 %all-to-all-start.1 = ((bf16[4,304,128]{2,1,0:T(8,128)(2,1)}), bf16[4,304,128]{2,1,0:T(8,128)(2,1)S(1)}, u32[]{:S(2)}, u32[]{:S(2)}) async-start(bf16[4,304,128]{2,1,0:T(8,128)(2,1)} %get-tuple-element.97), calls=%async_computation.1 | async-start | bytes 622592 | tf_op jit(solution)/shard_map/all_to_all | solution.py:401
  184.9 3.3 %collective-permute-start.20 = (bf16[112,128]{1,0:T(8,128)(2,1)S(1)}, bf16[112,128]{1,0:T(8,128)(2,1)S(1)}, u32[]{:S(2)}, u32[]{:S(2)}) collective-permute-start(bf16[112,128]{1,0:T(8,128)(2,1)S(1)} %get-tuple-element.98.one), channel_id=1, source_target_pairs={{0,2},{2,0},{4,6},{6,4},{1,3},{3,1},{5,7},{7,5},{8,10},{10,8},{12,... | collective-permute-start | bytes 86024 | tf_op jit(solution)/shard_map/ppermute | solution.py:565
  189.6 3.8 %collective-permute-start.21 = (bf16[112,128]{1,0:T(8,128)(2,1)S(1)}, bf16[112,128]{1,0:T(8,128)(2,1)S(1)}, u32[]{:S(2)}, u32[]{:S(2)}) collective-permute-start(bf16[112,128]{1,0:T(8,128)(2,1)S(1)} %shard_map.170.one), channel_id=1, source_target_pairs={{2,4},{4,2},{6,0},{0,6},{3,5},{5,3},{7,1},{1,7},{10,12},{12,10},{1... | collective-permute-start | bytes 86024 | tf_op jit(solution)/shard_map/ppermute | solution.py:567
  197.8 4.1 %collective-permute-start.24 = (bf16[1216,128]{1,0:T(8,128)(2,1)S(1)}, bf16[1216,128]{1,0:T(8,128)(2,1)S(1)}, u32[]{:S(2)}, u32[]{:S(2)}) collective-permute-start(bf16[1216,128]{1,0:T(8,128)(2,1)S(1)} %bitcast.27), channel_id=1, source_target_pairs={{128,0},{256,128},{384,256},{0,384},{129,1},{257,129},{385,257},{1... | collective-permute-start | bytes 933896 | tf_op jit(solution)/shard_map/ppermute | solution.py:574
  201.9 8.4 %collective-permute-start.22 = (f32[112,128]{1,0:T(8,128)S(1)}, f32[112,128]{1,0:T(8,128)S(1)}, u32[]{:S(2)}, u32[]{:S(2)}) collective-permute-start(f32[112,128]{1,0:T(8,128)S(1)} %shard_map.171), channel_id=1, source_target_pairs={{0,1},{1,0},{2,3},{3,2},{4,5},{5,4},{6,7},{7,6},{8,9},{9,8},{10,11... | collective-permute-start | bytes 172040 | tf_op jit(solution)/shard_map/ppermute | solution.py:570
  212.3 4.6 %collective-permute-start.26 = (bf16[608,128]{1,0:T(8,128)(2,1)S(1)}, bf16[608,128]{1,0:T(8,128)(2,1)S(1)}, u32[]{:S(2)}, u32[]{:S(2)}) collective-permute-start(bf16[608,128]{1,0:T(8,128)(2,1)S(1)} %slice.86), channel_id=1, source_target_pairs={{128,0},{256,128},{384,256},{0,384},{129,1},{257,129},{385,257},{1... | collective-permute-start | bytes 466952 | tf_op jit(solution)/shard_map/ppermute | solution.py:576
  (100 shorter events, 51.3 us)
Async XLA Ops:
  2.5 8.6 %collective-permute-start = (bf16[128,768]{1,0:T(8,128)(2,1)}, bf16[128,768]{1,0:T(8,128)(2,1)S(1)}, u32[]{:S(2)}, u32[]{:S(2)}) collective-permute-start(bf16[128,768]{1,0:T(8,128)(2,1)} %get-tuple-element.107), channel_id=1, source_target_pairs={{0,16},{32,48},{64,80},{96,112},{128,144},{160,176},{192,208},{224... | collective-permute-start | bytes 589832 | tf_op jit(solution)/shard_map/ppermute | solution.py:397
  14.2 16.1 %collective-permute-start.3 = (bf16[528,256]{1,0:T(8,128)(2,1)S(1)}, bf16[528,256]{1,0:T(8,128)(2,1)S(1)}, u32[]{:S(2)}, u32[]{:S(2)}) collective-permute-start(bf16[528,256]{1,0:T(8,128)(2,1)S(1)} %get-tuple-element.58.refs_2_.refs_3_), channel_id=1, source_target_pairs={{16,32},{48,64},{80,96},{112,128},{144,160},{176,192},{208,224},{2... | collective-permute-start | bytes 811016 | tf_op jit(solution)/shard_map/ppermute | solution.py:397
  14.8 17.3 %collective-permute-start.7 = (bf16[528,256]{1,0:T(8,128)(2,1)S(1)}, bf16[528,256]{1,0:T(8,128)(2,1)S(1)}, u32[]{:S(2)}, u32[]{:S(2)}) collective-permute-start(bf16[528,256]{1,0:T(8,128)(2,1)S(1)} %get-tuple-element.59.refs_3_.refs_4_), channel_id=1, source_target_pairs={{0,16},{32,48},{64,80},{96,112},{128,144},{160,176},{192,208},{224... | collective-permute-start | bytes 811016 | tf_op jit(solution)/shard_map/ppermute | solution.py:397
  23.4 9.5 %collective-permute-start.2 = (bf16[528,256]{1,0:T(8,128)(2,1)S(1)}, bf16[528,256]{1,0:T(8,128)(2,1)S(1)}, u32[]{:S(2)}, u32[]{:S(2)}) collective-permute-start(bf16[528,256]{1,0:T(8,128)(2,1)S(1)} %get-tuple-element.57), channel_id=1, source_target_pairs={{160,96},{176,112},{288,224},{304,240},{416,352},{432,368},{64,128... | collective-permute-start | bytes 811016 | tf_op jit(solution)/shard_map/ppermute | solution.py:483
  30.2 7.2 %collective-permute-start.4 = (bf16[528,256]{1,0:T(8,128)(2,1)S(1)}, bf16[528,256]{1,0:T(8,128)(2,1)S(1)}, u32[]{:S(2)}, u32[]{:S(2)}) collective-permute-start(bf16[528,256]{1,0:T(8,128)(2,1)S(1)} %collective-permute-done.3.refs_5_), channel_id=1, source_target_pairs={{0,16},{32,48},{64,80},{96,112},{128,144},{160,176},{192,208},{224... | collective-permute-start | bytes 811016 | tf_op jit(solution)/shard_map/ppermute | solution.py:397
  32.2 5.9 %collective-permute-start.8 = (bf16[528,256]{1,0:T(8,128)(2,1)S(1)}, bf16[528,256]{1,0:T(8,128)(2,1)S(1)}, u32[]{:S(2)}, u32[]{:S(2)}) collective-permute-start(bf16[528,256]{1,0:T(8,128)(2,1)S(1)} %collective-permute-done.7.refs_6_), channel_id=1, source_target_pairs={{16,32},{48,64},{80,96},{112,128},{144,160},{176,192},{208,224},{2... | collective-permute-start | bytes 811016 | tf_op jit(solution)/shard_map/ppermute | solution.py:397
  32.9 47.0 %collective-permute-start.11 = (bf16[528,256]{1,0:T(8,128)(2,1)S(1)}, bf16[528,256]{1,0:T(8,128)(2,1)S(1)}, u32[]{:S(2)}, u32[]{:S(2)}) collective-permute-start(bf16[528,256]{1,0:T(8,128)(2,1)S(1)} %collective-permute-done.2), channel_id=1, source_target_pairs={{96,112},{224,240},{352,368},{480,496},{16,0},{144,128},{272,256},... | collective-permute-start | bytes 811016 | tf_op jit(solution)/shard_map/ppermute | solution.py:484
  37.4 40.0 %collective-permute-start.5 = (bf16[528,256]{1,0:T(8,128)(2,1)S(1)}, bf16[528,256]{1,0:T(8,128)(2,1)S(1)}, u32[]{:S(2)}, u32[]{:S(2)}) collective-permute-start(bf16[528,256]{1,0:T(8,128)(2,1)S(1)} %collective-permute-done.4.refs_6_), channel_id=1, source_target_pairs={{16,32},{48,64},{80,96},{144,160},{176,192},{208,224},{272,288},{3... | collective-permute-start | bytes 811016 | tf_op jit(solution)/shard_map/ppermute | solution.py:397
  38.1 38.7 %collective-permute-start.9 = (bf16[528,256]{1,0:T(8,128)(2,1)S(1)}, bf16[528,256]{1,0:T(8,128)(2,1)S(1)}, u32[]{:S(2)}, u32[]{:S(2)}) collective-permute-start(bf16[528,256]{1,0:T(8,128)(2,1)S(1)} %collective-permute-done.8.refs_5_), channel_id=1, source_target_pairs={{0,16},{32,48},{64,80},{96,112},{128,144},{160,176},{192,208},{224... | collective-permute-start | bytes 811016 | tf_op jit(solution)/shard_map/ppermute | solution.py:397
  77.5 8.0 %collective-permute-start.6 = (bf16[528,256]{1,0:T(8,128)(2,1)S(1)}, bf16[528,256]{1,0:T(8,128)(2,1)S(1)}, u32[]{:S(2)}, u32[]{:S(2)}) collective-permute-start(bf16[528,256]{1,0:T(8,128)(2,1)S(1)} %collective-permute-done.5), channel_id=1, source_target_pairs={{0,16},{32,48},{64,80},{96,112},{128,144},{160,176},{192,208},{224... | collective-permute-start | bytes 811016 | tf_op jit(solution)/shard_map/ppermute | solution.py:397
  92.3 16.8 %collective-permute-start.14 = (bf16[4,9,96,128]{3,2,1,0:T(8,128)(2,1)S(1)}, bf16[4,9,96,128]{3,2,1,0:T(8,128)(2,1)S(1)}, u32[]{:S(2)}, u32[]{:S(2)}) collective-permute-start(bf16[4,9,96,128]{3,2,1,0:T(8,128)(2,1)S(1)} %get-tuple-element.90), channel_id=1, source_target_pairs={{0,1},{1,0},{2,3},{3,2},{4,5},{5,4},{6,7},{7,6},{8,9},{9,8},{10,11... | collective-permute-start | bytes 2654216 | tf_op jit(solution)/shard_map/ppermute | solution.py:521
  99.6 23.9 %collective-permute-start.12 = (bf16[2,4,304,128]{3,2,1,0:T(8,128)(2,1)S(1)}, bf16[2,4,304,128]{3,2,1,0:T(8,128)(2,1)S(1)}, u32[]{:S(2)}, u32[]{:S(2)}) collective-permute-start(bf16[2,4,304,128]{3,2,1,0:T(8,128)(2,1)S(1)} %slice.84), channel_id=1, source_target_pairs={{0,128},{128,0},{256,384},{384,256},{1,129},{129,1},{257,385},{385... | collective-permute-start | bytes 1867784 | tf_op jit(solution)/shard_map/ppermute | solution.py:533
  109.4 19.6 %collective-permute-start.15 = (bf16[2,9,96,128]{3,2,1,0:T(8,128)(2,1)S(1)}, bf16[2,9,96,128]{3,2,1,0:T(8,128)(2,1)S(1)}, u32[]{:S(2)}, u32[]{:S(2)}) collective-permute-start(bf16[2,9,96,128]{3,2,1,0:T(8,128)(2,1)S(1)} %get-tuple-element.92), channel_id=1, source_target_pairs={{128,256},{256,128},{384,0},{0,384},{129,257},{257,129},{385,1},{1... | collective-permute-start | bytes 1327112 | tf_op jit(solution)/shard_map/ppermute | solution.py:537
  123.7 12.4 %collective-permute-start.13 = (bf16[4,304,128]{2,1,0:T(8,128)(2,1)S(1)}, bf16[4,304,128]{2,1,0:T(8,128)(2,1)S(1)}, u32[]{:S(2)}, u32[]{:S(2)}) collective-permute-start(bf16[4,304,128]{2,1,0:T(8,128)(2,1)S(1)} %get-tuple-element.88), channel_id=1, source_target_pairs={{128,256},{256,128},{384,0},{0,384},{129,257},{257,129},{385,1},{1... | collective-permute-start | bytes 933896 | tf_op jit(solution)/shard_map/ppermute | solution.py:542
  129.0 8.0 %collective-permute-start.16 = (bf16[9,96,128]{2,1,0:T(8,128)(2,1)S(1)}, bf16[9,96,128]{2,1,0:T(8,128)(2,1)S(1)}, u32[]{:S(2)}, u32[]{:S(2)}) collective-permute-start(bf16[9,96,128]{2,1,0:T(8,128)(2,1)S(1)} %get-tuple-element.94), channel_id=1, source_target_pairs={{0,128},{128,0},{256,384},{384,256},{1,129},{129,1},{257,385},{385... | collective-permute-start | bytes 663560 | tf_op jit(solution)/shard_map/ppermute | solution.py:543
  154.2 26.5 %collective-permute-start.17 = (bf16[416,128]{1,0:T(8,128)(2,1)S(1)}, bf16[416,128]{1,0:T(8,128)(2,1)S(1)}, u32[]{:S(2)}, u32[]{:S(2)}) collective-permute-start(bf16[416,128]{1,0:T(8,128)(2,1)S(1)} %get-tuple-element.95.sent), channel_id=1, source_target_pairs={{0,64},{64,0},{1,65},{65,1},{2,66},{66,2},{3,67},{67,3},{4,68},{68... | collective-permute-start | bytes 319496 | tf_op jit(solution)/shard_map/ppermute | solution.py:554
  159.3 11.2 %collective-permute-start.19 = (bf16[112,128]{1,0:T(8,128)(2,1)S(1)}, bf16[112,128]{1,0:T(8,128)(2,1)S(1)}, u32[]{:S(2)}, u32[]{:S(2)}) collective-permute-start(bf16[112,128]{1,0:T(8,128)(2,1)S(1)} %slice.71), channel_id=1, source_target_pairs={{0,72},{72,0},{8,64},{64,8},{1,73},{73,1},{9,65},{65,9},{2,74},{74... | collective-permute-start | bytes 86024 | tf_op jit(solution)/shard_map/ppermute | solution.py:556
  167.3 13.4 %collective-permute-start.18 = (bf16[112,128]{1,0:T(8,128)(2,1)S(1)}, bf16[112,128]{1,0:T(8,128)(2,1)S(1)}, u32[]{:S(2)}, u32[]{:S(2)}) collective-permute-start(bf16[112,128]{1,0:T(8,128)(2,1)S(1)} %get-tuple-element.96.mine), channel_id=1, source_target_pairs={{0,8},{8,0},{1,9},{9,1},{2,10},{10,2},{3,11},{11,3},{4,12},{12,4},... | collective-permute-start | bytes 86024 | tf_op jit(solution)/shard_map/ppermute | solution.py:555
  181.5 13.9 %all-to-all-start.1 = ((bf16[4,304,128]{2,1,0:T(8,128)(2,1)}), bf16[4,304,128]{2,1,0:T(8,128)(2,1)S(1)}, u32[]{:S(2)}, u32[]{:S(2)}) async-start(bf16[4,304,128]{2,1,0:T(8,128)(2,1)} %get-tuple-element.97), calls=%async_computation.1 | async-start | bytes 622592 | tf_op jit(solution)/shard_map/all_to_all | solution.py:401
  195.4 14.9 %collective-permute-start.23 = (bf16[1216,128]{1,0:T(8,128)(2,1)S(1)}, bf16[1216,128]{1,0:T(8,128)(2,1)S(1)}, u32[]{:S(2)}, u32[]{:S(2)}) collective-permute-start(bf16[1216,128]{1,0:T(8,128)(2,1)S(1)} %bitcast.26), channel_id=1, source_target_pairs={{0,128},{128,256},{256,384},{384,0},{1,129},{129,257},{257,385},{3... | collective-permute-start | bytes 933896 | tf_op jit(solution)/shard_map/ppermute | solution.py:573
  197.8 14.4 %collective-permute-start.24 = (bf16[1216,128]{1,0:T(8,128)(2,1)S(1)}, bf16[1216,128]{1,0:T(8,128)(2,1)S(1)}, u32[]{:S(2)}, u32[]{:S(2)}) collective-permute-start(bf16[1216,128]{1,0:T(8,128)(2,1)S(1)} %bitcast.27), channel_id=1, source_target_pairs={{128,0},{256,128},{384,256},{0,384},{129,1},{257,129},{385,257},{1... | collective-permute-start | bytes 933896 | tf_op jit(solution)/shard_map/ppermute | solution.py:574
  201.9 15.0 %collective-permute-start.22 = (f32[112,128]{1,0:T(8,128)S(1)}, f32[112,128]{1,0:T(8,128)S(1)}, u32[]{:S(2)}, u32[]{:S(2)}) collective-permute-start(f32[112,128]{1,0:T(8,128)S(1)} %shard_map.171), channel_id=1, source_target_pairs={{0,1},{1,0},{2,3},{3,2},{4,5},{5,4},{6,7},{7,6},{8,9},{9,8},{10,11... | collective-permute-start | bytes 172040 | tf_op jit(solution)/shard_map/ppermute | solution.py:570
  210.3 7.6 %collective-permute-start.25 = (bf16[608,128]{1,0:T(8,128)(2,1)S(1)}, bf16[608,128]{1,0:T(8,128)(2,1)S(1)}, u32[]{:S(2)}, u32[]{:S(2)}) collective-permute-start(bf16[608,128]{1,0:T(8,128)(2,1)S(1)} %slice.85), channel_id=1, source_target_pairs={{0,128},{128,256},{256,384},{384,0},{1,129},{129,257},{257,385},{3... | collective-permute-start | bytes 466952 | tf_op jit(solution)/shard_map/ppermute | solution.py:575
  212.3 6.7 %collective-permute-start.26 = (bf16[608,128]{1,0:T(8,128)(2,1)S(1)}, bf16[608,128]{1,0:T(8,128)(2,1)S(1)}, u32[]{:S(2)}, u32[]{:S(2)}) collective-permute-start(bf16[608,128]{1,0:T(8,128)(2,1)S(1)} %slice.86), channel_id=1, source_target_pairs={{128,0},{256,128},{384,256},{0,384},{129,1},{257,129},{385,257},{1... | collective-permute-start | bytes 466952 | tf_op jit(solution)/shard_map/ppermute | solution.py:576
  (13 other events, 82.4 us)

commit v14 on v12

--- a/solution.py
+++ b/solution.py
@@ -350,9 +350,8 @@
     taps[...] = (near + (one[...].astype(F32) + two[...].astype(F32))).astype(BF16)
 
 
-def line_total_kernel(own, one, two, three, total):
-    even = own[...].astype(F32) + two[...].astype(F32)
-    total[...] = even + (one[...].astype(F32) + three[...].astype(F32))
+def add_kernel(one, two, total):
+    total[...] = (one[...].astype(F32) + two[...].astype(F32)).astype(total.dtype)
 
 
 def finish_kernel(
@@ -566,10 +565,10 @@
 
     head_rows = 4 * chunk
     head_sum = swap_parts(head_parts, "zq").reshape(head_rows, 128)
-    line = [
-        lax.ppermute(conv_sum, "x", [(i, (i + step) % 4) for i in range(4)]) for step in (1, 2, 3)
-    ]
-    (conv_sum,) = call(line_total_kernel, [shape((112, 128), F32)], [VM] * 4, 8, quick)(conv_sum, *line)
+    other = lax.ppermute(conv_sum, "x", first_pairs)
+    (conv_sum,) = call(add_kernel, [shape((112, 128), BF16)], [VM] * 2, 8, quick)(conv_sum, other)
+    other = lax.ppermute(conv_sum, "x", second_pairs)
+    (conv_sum,) = call(add_kernel, [shape((112, 128), F32)], [VM] * 2, 8, quick)(conv_sum, other)
     head_sum, conv_sum = lax.optimization_barrier((head_sum, conv_sum))
     other = lax.ppermute(conv_sum, "core", [(0, 1), (1, 0)])
     around = [(i, (i + 1) % 4) for i in range(4)]

time: 227 us -> 226 us (level)
  starting transfers between devices: 129 us -> 123 us
  waiting for transfers between devices: 41.2 us -> 44.3 us
    ppermute x3 -> x2, starting transfers between devices: 10.9 us -> 6.92 us  [the longest x1 4.91 us: on_device(): other = lax.ppermute(conv_sum, 'x', second_pairs)]
    ppermute x10, starting transfers between devices: 46.1 us -> 49.9 us  [swapped(): return lax.ppermute(block, SEQ, pairs + [(j, i) for i, j in pairs])]
    ppermute x10, waiting for transfers between devices: 18.5 us -> 15.7 us  [swapped(): return lax.ppermute(block, SEQ, pairs + [(j, i) for i, j in pairs])]
    ppermute x1, waiting for transfers between devices: 5.15 us -> 7.89 us  [on_device(): other = lax.ppermute(head_sum[2:], 'y', first_pairs)]
    ppermute x1, starting transfers between devices: 9.01 us -> 6.27 us  [on_device(): heads_in = lax.ppermute(heads_send, 'y', second_pairs)]
    ppermute x1, waiting for transfers between devices: 7.78 us -> 10.2 us  [on_device(): across = lax.ppermute(mine, 'zhi', [(0, 1), (1, 0)])]
  transfers between devices with their start and end apart: 29 -> 28, of which waited for: 10 -> 11; matrix products, arithmetic and copies ran while one was open for 1% -> 1% of each run, Pallas kernels for 7% -> 7%
where the time goes in v14:
time: 226 us; the launch traced here: 224 us
  starting transfers between devices  123 us (54%)
  waiting for transfers between devices  44.3 us (20%)
  Pallas kernels  29.1 us (13%)
  blocking collectives  18.3 us (8%)
  local copies, waits for them, and re-layouts  4.71 us (2%)
    ppermute x10, starting transfers between devices, swapped(): return lax.ppermute(block, SEQ, pairs + [(j, i) for i, j in pairs])  49.9 us
    all_to_all x1, blocking collectives, swap_parts(): return lax.all_to_all(parts, axis, 0, 0, tiled=True)  18.3 us
    ppermute x10, waiting for transfers between devices, swapped(): return lax.ppermute(block, SEQ, pairs + [(j, i) for i, j in pairs])  15.7 us
    ppermute x1, waiting for transfers between devices, on_device(): across = lax.ppermute(mine, 'zhi', [(0, 1), (1, 0)])  10.2 us
    pallas_call x4, Pallas kernels, on_device(): call(lambda *refs, distance=distance: pair_kernel(distance, *refs), acc_s...  8.66 us
    ppermute x1, starting transfers between devices, on_device(): other = lax.ppermute(conv_sum, 'core', [(0, 1), (1, 0)])  8 us
    ppermute x1, starting transfers between devices, on_device(): lax.ppermute(sent[chunk:], ('zb', 'zhi'), [(0, 3), (3, 0), (1, 2), (2, 1)])  7.95 us
    ppermute x1, waiting for transfers between devices, on_device(): other = lax.ppermute(head_sum[2:], 'y', first_pairs)  7.89 us
  transfers between devices with their start and end apart: 28, of which 11 were waited for; matrix products, arithmetic and copies ran while one was open for 1% of the time, Pallas kernels for 7%

profile of v14, /device:TPU:1, one launch (start us, length us, event | category | flops | bytes accessed | tf_op | source)
XLA Modules:
  0.0 224.1 jit_solution(10240258919190614127)
XLA Ops:
  3.1 7.2 %collective-permute-start = (bf16[128,768]{1,0:T(8,128)(2,1)S(1)}, bf16[128,768]{1,0:T(8,128)(2,1)S(1)}, u32[]{:S(2)}, u32[]{:S(2)}) collective-permute-start(bf16[128,768]{1,0:T(8,128)(2,1)S(1)} %get-tuple-element.105), channel_id=1, source_target_pairs={{0,16},{32,48},{64,80},{96,112},{128,144},{160,176},{192,208},{224... | collective-permute-start | bytes 589832 | tf_op jit(solution)/shard_map/ppermute | solution.py:399
  20.8 8.8 %collective-permute-start.7 = (bf16[528,256]{1,0:T(8,128)(2,1)S(1)}, bf16[528,256]{1,0:T(8,128)(2,1)S(1)}, u32[]{:S(2)}, u32[]{:S(2)}) collective-permute-start(bf16[528,256]{1,0:T(8,128)(2,1)S(1)} %get-tuple-element.57.refs_3_.refs_4_), channel_id=1, source_target_pairs={{0,16},{32,48},{64,80},{96,112},{128,144},{160,176},{192,208},{224... | collective-permute-start | bytes 811016 | tf_op jit(solution)/shard_map/ppermute | solution.py:399
  30.4 3.4 %shard_map.162 = (bf16[256,768]{1,0:T(8,128)(2,1)S(1)}, f32[512,384]{1,0:T(8,128)S(1)}, bf16[768,768]{1,0:T(8,128)(2,1)S(1)}, bf16[384,512]{1,0:T(8,128)(2,1)S(1)}, bf16[768,512]{1,0:T(8,128)(2,1)S(1)}) custom-call(s32[1]{0:T(128)} %bitcast.3.odd, bf16[128,768]{1,0:T(8,128)(2,1)S(1)} %collective-permute-done.even_edge, ...), custom_call_target="tpu_custom_call" | custom-call | flops 6000000000 | bytes 1000000 | tf_op jit(solution)/shard_map/pallas_call | solution.py:467
  41.6 8.7 %collective-permute-done.4.refs_6_ = bf16[528,256]{1,0:T(8,128)(2,1)S(1)} collective-permute-done((bf16[528,256]{1,0:T(8,128)(2,1)S(1)}, bf16[528,256]{1,0:T(8,128)(2,1)S(1)}, u32[]{:S(2)}, u32[]{:S(2)}) %collective-permute-start.4) | collective-permute-done | bytes 270368 | tf_op jit(solution)/shard_map/ppermute | solution.py:399
  51.0 23.1 %collective-permute-start.9 = (bf16[528,256]{1,0:T(8,128)(2,1)S(1)}, bf16[528,256]{1,0:T(8,128)(2,1)S(1)}, u32[]{:S(2)}, u32[]{:S(2)}) collective-permute-start(bf16[528,256]{1,0:T(8,128)(2,1)S(1)} %collective-permute-done.8.refs_5_), channel_id=1, source_target_pairs={{0,16},{32,48},{64,80},{96,112},{128,144},{160,176},{192,208},{224... | collective-permute-start | bytes 811016 | tf_op jit(solution)/shard_map/ppermute | solution.py:399
  76.8 3.5 %collective-permute-done.9.refs_6_ = bf16[528,256]{1,0:T(8,128)(2,1)S(1)} collective-permute-done((bf16[528,256]{1,0:T(8,128)(2,1)S(1)}, bf16[528,256]{1,0:T(8,128)(2,1)S(1)}, u32[]{:S(2)}, u32[]{:S(2)}) %collective-permute-start.9) | collective-permute-done | bytes 270368 | tf_op jit(solution)/shard_map/ppermute | solution.py:399
  80.9 4.6 %collective-permute-start.6 = (bf16[528,256]{1,0:T(8,128)(2,1)S(1)}, bf16[528,256]{1,0:T(8,128)(2,1)S(1)}, u32[]{:S(2)}, u32[]{:S(2)}) collective-permute-start(bf16[528,256]{1,0:T(8,128)(2,1)S(1)} %collective-permute-done.5), channel_id=1, source_target_pairs={{0,16},{32,48},{64,80},{96,112},{128,144},{160,176},{192,208},{224... | collective-permute-start | bytes 811016 | tf_op jit(solution)/shard_map/ppermute | solution.py:399
  87.3 3.5 %collective-permute-done.6 = bf16[528,256]{1,0:T(8,128)(2,1)S(1)} collective-permute-done((bf16[528,256]{1,0:T(8,128)(2,1)S(1)}, bf16[528,256]{1,0:T(8,128)(2,1)S(1)}, u32[]{:S(2)}, u32[]{:S(2)}) %collective-permute-start.6) | collective-permute-done | bytes 270368 | tf_op jit(solution)/shard_map/ppermute | solution.py:399
  93.2 4.1 %shard_map.163 = (bf16[4,9,96,128]{3,2,1,0:T(8,128)(2,1)S(1)}, bf16[4,9,96,128]{3,2,1,0:T(8,128)(2,1)S(1)}, bf16[512,384]{1,0:T(8,128)(2,1)S(1)}, bf16[512,512]{1,0:T(8,128)(2,1)S(1)}) custom-call(s32[3]{0:T(128)S(1)} %pad_add_fusion.place, f32[512,256]{1,0:T(8,128)S(1)} %get-tuple-element.70.d_donor, f32[512,256]{1,0:T(8,128)S(1)} %get-tuple-element.71.d_accept, ...), custom_call_target="tpu_custom_call" | custom-call | flops 4000000000 | bytes 1000000 | tf_op jit(solution)/shard_map/pallas_call | solution.py:517
  97.4 4.6 %collective-permute-start.14 = (bf16[4,9,96,128]{3,2,1,0:T(8,128)(2,1)S(1)}, bf16[4,9,96,128]{3,2,1,0:T(8,128)(2,1)S(1)}, u32[]{:S(2)}, u32[]{:S(2)}) collective-permute-start(bf16[4,9,96,128]{3,2,1,0:T(8,128)(2,1)S(1)} %get-tuple-element.88), channel_id=1, source_target_pairs={{0,1},{1,0},{2,3},{3,2},{4,5},{5,4},{6,7},{7,6},{8,9},{9,8},{10,11... | collective-permute-start | bytes 2654216 | tf_op jit(solution)/shard_map/ppermute | solution.py:524
  107.6 6.8 %collective-permute-start.15 = (bf16[2,9,96,128]{3,2,1,0:T(8,128)(2,1)S(1)}, bf16[2,9,96,128]{3,2,1,0:T(8,128)(2,1)S(1)}, u32[]{:S(2)}, u32[]{:S(2)}) collective-permute-start(bf16[2,9,96,128]{3,2,1,0:T(8,128)(2,1)S(1)} %get-tuple-element.90), channel_id=1, source_target_pairs={{128,256},{256,128},{384,0},{0,384},{129,257},{257,129},{385,1},{1... | collective-permute-start | bytes 1327112 | tf_op jit(solution)/shard_map/ppermute | solution.py:540
  114.4 7.9 %collective-permute-done.12.received = bf16[2,4,304,128]{3,2,1,0:T(8,128)(2,1)S(1)} collective-permute-done((bf16[2,4,304,128]{3,2,1,0:T(8,128)(2,1)S(1)}, bf16[2,4,304,128]{3,2,1,0:T(8,128)(2,1)S(1)}, u32[]{:S(2)}, u32[]{:S(2)}) %collective-permute-start.12) | collective-permute-done | bytes 622624 | tf_op jit(solution)/shard_map/ppermute | solution.py:536
  122.4 6.3 %collective-permute-start.13 = (bf16[4,304,128]{2,1,0:T(8,128)(2,1)S(1)}, bf16[4,304,128]{2,1,0:T(8,128)(2,1)S(1)}, u32[]{:S(2)}, u32[]{:S(2)}) collective-permute-start(bf16[4,304,128]{2,1,0:T(8,128)(2,1)S(1)} %get-tuple-element.86), channel_id=1, source_target_pairs={{128,256},{256,128},{384,0},{0,384},{129,257},{257,129},{385,1},{1... | collective-permute-start | bytes 933896 | tf_op jit(solution)/shard_map/ppermute | solution.py:545
  131.3 4.5 %collective-permute-done.13.head_in = bf16[4,304,128]{2,1,0:T(8,128)(2,1)S(1)} collective-permute-done((bf16[4,304,128]{2,1,0:T(8,128)(2,1)S(1)}, bf16[4,304,128]{2,1,0:T(8,128)(2,1)S(1)}, u32[]{:S(2)}, u32[]{:S(2)}) %collective-permute-start.13) | collective-permute-done | bytes 311328 | tf_op jit(solution)/shard_map/ppermute | solution.py:545
  136.8 18.3 %all_to_all.10.parts = bf16[4,528,128]{2,1,0:T(8,128)(2,1)S(1)} all-to-all(bf16[4,528,128]{2,1,0:T(8,128)(2,1)S(1)} %shard_map.168), channel_id=1, replica_groups=mesh['y'=4,'zb'=2,'zq'=4,'zhi'=2,'x'=4,'core'=2] {'zq'}, dimensions={0} | all-to-all | bytes 1081344 | tf_op jit(solution)/shard_map/all_to_all | solution.py:403
  155.9 5.8 %collective-permute-start.17 = (bf16[416,128]{1,0:T(8,128)(2,1)S(1)}, bf16[416,128]{1,0:T(8,128)(2,1)S(1)}, u32[]{:S(2)}, u32[]{:S(2)}) collective-permute-start(bf16[416,128]{1,0:T(8,128)(2,1)S(1)} %get-tuple-element.93.sent), channel_id=1, source_target_pairs={{0,64},{64,0},{1,65},{65,1},{2,66},{66,2},{3,67},{67,3},{4,68},{68... | collective-permute-start | bytes 319496 | tf_op jit(solution)/shard_map/ppermute | solution.py:557
  161.8 8.0 %collective-permute-start.19 = (bf16[112,128]{1,0:T(8,128)(2,1)S(1)}, bf16[112,128]{1,0:T(8,128)(2,1)S(1)}, u32[]{:S(2)}, u32[]{:S(2)}) collective-permute-start(bf16[112,128]{1,0:T(8,128)(2,1)S(1)} %slice.71), channel_id=1, source_target_pairs={{0,72},{72,0},{8,64},{64,8},{1,73},{73,1},{9,65},{65,9},{2,74},{74... | collective-permute-start | bytes 86024 | tf_op jit(solution)/shard_map/ppermute | solution.py:559
  169.7 3.5 %collective-permute-start.18 = (bf16[112,128]{1,0:T(8,128)(2,1)S(1)}, bf16[112,128]{1,0:T(8,128)(2,1)S(1)}, u32[]{:S(2)}, u32[]{:S(2)}) collective-permute-start(bf16[112,128]{1,0:T(8,128)(2,1)S(1)} %get-tuple-element.94.mine), channel_id=1, source_target_pairs={{0,8},{8,0},{1,9},{9,1},{2,10},{10,2},{3,11},{11,3},{4,12},{12,4},... | collective-permute-start | bytes 86024 | tf_op jit(solution)/shard_map/ppermute | solution.py:558
  173.2 10.2 %collective-permute-done.18.one = bf16[112,128]{1,0:T(8,128)(2,1)S(1)} collective-permute-done((bf16[112,128]{1,0:T(8,128)(2,1)S(1)}, bf16[112,128]{1,0:T(8,128)(2,1)S(1)}, u32[]{:S(2)}, u32[]{:S(2)}) %collective-permute-start.18) | collective-permute-done | bytes 28704 | tf_op jit(solution)/shard_map/ppermute | solution.py:558
  184.2 3.5 %all-to-all-start.1 = ((bf16[4,304,128]{2,1,0:T(8,128)(2,1)}), bf16[4,304,128]{2,1,0:T(8,128)(2,1)S(1)}, u32[]{:S(2)}, u32[]{:S(2)}) async-start(bf16[4,304,128]{2,1,0:T(8,128)(2,1)} %get-tuple-element.95), calls=%async_computation.1 | async-start | bytes 622592 | tf_op jit(solution)/shard_map/all_to_all | solution.py:403
  192.3 4.9 %collective-permute-start.21 = (bf16[112,128]{1,0:T(8,128)(2,1)S(1)}, bf16[112,128]{1,0:T(8,128)(2,1)S(1)}, u32[]{:S(2)}, u32[]{:S(2)}) collective-permute-start(bf16[112,128]{1,0:T(8,128)(2,1)S(1)} %shard_map.171.one), channel_id=1, source_target_pairs={{2,4},{4,2},{6,0},{0,6},{3,5},{5,3},{7,1},{1,7},{10,12},{12,10},{1... | collective-permute-start | bytes 86024 | tf_op jit(solution)/shard_map/ppermute | solution.py:570
  200.4 4.6 %collective-permute-start.24 = (bf16[1216,128]{1,0:T(8,128)(2,1)S(1)}, bf16[1216,128]{1,0:T(8,128)(2,1)S(1)}, u32[]{:S(2)}, u32[]{:S(2)}) collective-permute-start(bf16[1216,128]{1,0:T(8,128)(2,1)S(1)} %bitcast.26), channel_id=1, source_target_pairs={{128,0},{256,128},{384,256},{0,384},{129,1},{257,129},{385,257},{1... | collective-permute-start | bytes 933896 | tf_op jit(solution)/shard_map/ppermute | solution.py:577
  205.0 8.0 %collective-permute-start.22 = (f32[112,128]{1,0:T(8,128)S(1)}, f32[112,128]{1,0:T(8,128)S(1)}, u32[]{:S(2)}, u32[]{:S(2)}) collective-permute-start(f32[112,128]{1,0:T(8,128)S(1)} %shard_map.172), channel_id=1, source_target_pairs={{0,1},{1,0},{2,3},{3,2},{4,5},{5,4},{6,7},{7,6},{8,9},{9,8},{10,11... | collective-permute-start | bytes 172040 | tf_op jit(solution)/shard_map/ppermute | solution.py:573
  215.0 4.6 %collective-permute-start.26 = (bf16[608,128]{1,0:T(8,128)(2,1)S(1)}, bf16[608,128]{1,0:T(8,128)(2,1)S(1)}, u32[]{:S(2)}, u32[]{:S(2)}) collective-permute-start(bf16[608,128]{1,0:T(8,128)(2,1)S(1)} %slice.86), channel_id=1, source_target_pairs={{128,0},{256,128},{384,256},{0,384},{129,1},{257,129},{385,257},{1... | collective-permute-start | bytes 466952 | tf_op jit(solution)/shard_map/ppermute | solution.py:579
  (109 shorter events, 53.7 us)
Async XLA Ops:
  2.5 13.2 %collective-permute-start.1 = (bf16[128,768]{1,0:T(8,128)(2,1)}, bf16[128,768]{1,0:T(8,128)(2,1)S(1)}, u32[]{:S(2)}, u32[]{:S(2)}) collective-permute-start(bf16[128,768]{1,0:T(8,128)(2,1)} %get-tuple-element.104), channel_id=1, source_target_pairs={{16,32},{48,64},{80,96},{112,128},{144,160},{176,192},{208,224},{2... | collective-permute-start | bytes 589832 | tf_op jit(solution)/shard_map/ppermute | solution.py:399
  3.1 12.8 %collective-permute-start = (bf16[128,768]{1,0:T(8,128)(2,1)S(1)}, bf16[128,768]{1,0:T(8,128)(2,1)S(1)}, u32[]{:S(2)}, u32[]{:S(2)}) collective-permute-start(bf16[128,768]{1,0:T(8,128)(2,1)S(1)} %get-tuple-element.105), channel_id=1, source_target_pairs={{0,16},{32,48},{64,80},{96,112},{128,144},{160,176},{192,208},{224... | collective-permute-start | bytes 589832 | tf_op jit(solution)/shard_map/ppermute | solution.py:399
  20.2 14.7 %collective-permute-start.3 = (bf16[528,256]{1,0:T(8,128)(2,1)S(1)}, bf16[528,256]{1,0:T(8,128)(2,1)S(1)}, u32[]{:S(2)}, u32[]{:S(2)}) collective-permute-start(bf16[528,256]{1,0:T(8,128)(2,1)S(1)} %get-tuple-element.56.refs_2_.refs_3_), channel_id=1, source_target_pairs={{16,32},{48,64},{80,96},{112,128},{144,160},{176,192},{208,224},{2... | collective-permute-start | bytes 811016 | tf_op jit(solution)/shard_map/ppermute | solution.py:399
  20.8 16.8 %collective-permute-start.7 = (bf16[528,256]{1,0:T(8,128)(2,1)S(1)}, bf16[528,256]{1,0:T(8,128)(2,1)S(1)}, u32[]{:S(2)}, u32[]{:S(2)}) collective-permute-start(bf16[528,256]{1,0:T(8,128)(2,1)S(1)} %get-tuple-element.57.refs_3_.refs_4_), channel_id=1, source_target_pairs={{0,16},{32,48},{64,80},{96,112},{128,144},{160,176},{192,208},{224... | collective-permute-start | bytes 811016 | tf_op jit(solution)/shard_map/ppermute | solution.py:399
  29.7 8.6 %collective-permute-start.2 = (bf16[528,256]{1,0:T(8,128)(2,1)S(1)}, bf16[528,256]{1,0:T(8,128)(2,1)S(1)}, u32[]{:S(2)}, u32[]{:S(2)}) collective-permute-start(bf16[528,256]{1,0:T(8,128)(2,1)S(1)} %broadcast_select_fusion.2), channel_id=1, source_target_pairs={{160,96},{176,112},{288,224},{304,240},{416,352},{432,368},{64,128... | collective-permute-start | bytes 811016 | tf_op jit(solution)/shard_map/ppermute | solution.py:486
  34.8 15.5 %collective-permute-start.4 = (bf16[528,256]{1,0:T(8,128)(2,1)S(1)}, bf16[528,256]{1,0:T(8,128)(2,1)S(1)}, u32[]{:S(2)}, u32[]{:S(2)}) collective-permute-start(bf16[528,256]{1,0:T(8,128)(2,1)S(1)} %collective-permute-done.3.refs_5_), channel_id=1, source_target_pairs={{0,16},{32,48},{64,80},{96,112},{128,144},{160,176},{192,208},{224... | collective-permute-start | bytes 811016 | tf_op jit(solution)/shard_map/ppermute | solution.py:399
  37.6 13.4 %collective-permute-start.8 = (bf16[528,256]{1,0:T(8,128)(2,1)S(1)}, bf16[528,256]{1,0:T(8,128)(2,1)S(1)}, u32[]{:S(2)}, u32[]{:S(2)}) collective-permute-start(bf16[528,256]{1,0:T(8,128)(2,1)S(1)} %collective-permute-done.7.refs_6_), channel_id=1, source_target_pairs={{16,32},{48,64},{80,96},{112,128},{144,160},{176,192},{208,224},{2... | collective-permute-start | bytes 811016 | tf_op jit(solution)/shard_map/ppermute | solution.py:399
  38.3 47.2 %collective-permute-start.11 = (bf16[528,256]{1,0:T(8,128)(2,1)S(1)}, bf16[528,256]{1,0:T(8,128)(2,1)S(1)}, u32[]{:S(2)}, u32[]{:S(2)}) collective-permute-start(bf16[528,256]{1,0:T(8,128)(2,1)S(1)} %collective-permute-done.2), channel_id=1, source_target_pairs={{96,112},{224,240},{352,368},{480,496},{16,0},{144,128},{272,256},... | collective-permute-start | bytes 811016 | tf_op jit(solution)/shard_map/ppermute | solution.py:487
  50.3 30.6 %collective-permute-start.5 = (bf16[528,256]{1,0:T(8,128)(2,1)S(1)}, bf16[528,256]{1,0:T(8,128)(2,1)S(1)}, u32[]{:S(2)}, u32[]{:S(2)}) collective-permute-start(bf16[528,256]{1,0:T(8,128)(2,1)S(1)} %collective-permute-done.4.refs_6_), channel_id=1, source_target_pairs={{16,32},{48,64},{80,96},{144,160},{176,192},{208,224},{272,288},{3... | collective-permute-start | bytes 811016 | tf_op jit(solution)/shard_map/ppermute | solution.py:399
  51.0 29.3 %collective-permute-start.9 = (bf16[528,256]{1,0:T(8,128)(2,1)S(1)}, bf16[528,256]{1,0:T(8,128)(2,1)S(1)}, u32[]{:S(2)}, u32[]{:S(2)}) collective-permute-start(bf16[528,256]{1,0:T(8,128)(2,1)S(1)} %collective-permute-done.8.refs_5_), channel_id=1, source_target_pairs={{0,16},{32,48},{64,80},{96,112},{128,144},{160,176},{192,208},{224... | collective-permute-start | bytes 811016 | tf_op jit(solution)/shard_map/ppermute | solution.py:399
  80.9 9.8 %collective-permute-start.6 = (bf16[528,256]{1,0:T(8,128)(2,1)S(1)}, bf16[528,256]{1,0:T(8,128)(2,1)S(1)}, u32[]{:S(2)}, u32[]{:S(2)}) collective-permute-start(bf16[528,256]{1,0:T(8,128)(2,1)S(1)} %collective-permute-done.5), channel_id=1, source_target_pairs={{0,16},{32,48},{64,80},{96,112},{128,144},{160,176},{192,208},{224... | collective-permute-start | bytes 811016 | tf_op jit(solution)/shard_map/ppermute | solution.py:399
  97.4 10.0 %collective-permute-start.14 = (bf16[4,9,96,128]{3,2,1,0:T(8,128)(2,1)S(1)}, bf16[4,9,96,128]{3,2,1,0:T(8,128)(2,1)S(1)}, u32[]{:S(2)}, u32[]{:S(2)}) collective-permute-start(bf16[4,9,96,128]{3,2,1,0:T(8,128)(2,1)S(1)} %get-tuple-element.88), channel_id=1, source_target_pairs={{0,1},{1,0},{2,3},{3,2},{4,5},{5,4},{6,7},{7,6},{8,9},{9,8},{10,11... | collective-permute-start | bytes 2654216 | tf_op jit(solution)/shard_map/ppermute | solution.py:524
  104.7 17.5 %collective-permute-start.12 = (bf16[2,4,304,128]{3,2,1,0:T(8,128)(2,1)S(1)}, bf16[2,4,304,128]{3,2,1,0:T(8,128)(2,1)S(1)}, u32[]{:S(2)}, u32[]{:S(2)}) collective-permute-start(bf16[2,4,304,128]{3,2,1,0:T(8,128)(2,1)S(1)} %slice.84), channel_id=1, source_target_pairs={{0,128},{128,0},{256,384},{384,256},{1,129},{129,1},{257,385},{385... | collective-permute-start | bytes 1867784 | tf_op jit(solution)/shard_map/ppermute | solution.py:536
  107.6 21.1 %collective-permute-start.15 = (bf16[2,9,96,128]{3,2,1,0:T(8,128)(2,1)S(1)}, bf16[2,9,96,128]{3,2,1,0:T(8,128)(2,1)S(1)}, u32[]{:S(2)}, u32[]{:S(2)}) collective-permute-start(bf16[2,9,96,128]{3,2,1,0:T(8,128)(2,1)S(1)} %get-tuple-element.90), channel_id=1, source_target_pairs={{128,256},{256,128},{384,0},{0,384},{129,257},{257,129},{385,1},{1... | collective-permute-start | bytes 1327112 | tf_op jit(solution)/shard_map/ppermute | solution.py:540
  122.4 13.4 %collective-permute-start.13 = (bf16[4,304,128]{2,1,0:T(8,128)(2,1)S(1)}, bf16[4,304,128]{2,1,0:T(8,128)(2,1)S(1)}, u32[]{:S(2)}, u32[]{:S(2)}) collective-permute-start(bf16[4,304,128]{2,1,0:T(8,128)(2,1)S(1)} %get-tuple-element.86), channel_id=1, source_target_pairs={{128,256},{256,128},{384,0},{0,384},{129,257},{257,129},{385,1},{1... | collective-permute-start | bytes 933896 | tf_op jit(solution)/shard_map/ppermute | solution.py:545
  128.8 8.0 %collective-permute-start.16 = (bf16[9,96,128]{2,1,0:T(8,128)(2,1)S(1)}, bf16[9,96,128]{2,1,0:T(8,128)(2,1)S(1)}, u32[]{:S(2)}, u32[]{:S(2)}) collective-permute-start(bf16[9,96,128]{2,1,0:T(8,128)(2,1)S(1)} %get-tuple-element.92), channel_id=1, source_target_pairs={{0,128},{128,0},{256,384},{384,256},{1,129},{129,1},{257,385},{385... | collective-permute-start | bytes 663560 | tf_op jit(solution)/shard_map/ppermute | solution.py:546
  155.9 27.5 %collective-permute-start.17 = (bf16[416,128]{1,0:T(8,128)(2,1)S(1)}, bf16[416,128]{1,0:T(8,128)(2,1)S(1)}, u32[]{:S(2)}, u32[]{:S(2)}) collective-permute-start(bf16[416,128]{1,0:T(8,128)(2,1)S(1)} %get-tuple-element.93.sent), channel_id=1, source_target_pairs={{0,64},{64,0},{1,65},{65,1},{2,66},{66,2},{3,67},{67,3},{4,68},{68... | collective-permute-start | bytes 319496 | tf_op jit(solution)/shard_map/ppermute | solution.py:557
  161.8 11.5 %collective-permute-start.19 = (bf16[112,128]{1,0:T(8,128)(2,1)S(1)}, bf16[112,128]{1,0:T(8,128)(2,1)S(1)}, u32[]{:S(2)}, u32[]{:S(2)}) collective-permute-start(bf16[112,128]{1,0:T(8,128)(2,1)S(1)} %slice.71), channel_id=1, source_target_pairs={{0,72},{72,0},{8,64},{64,8},{1,73},{73,1},{9,65},{65,9},{2,74},{74... | collective-permute-start | bytes 86024 | tf_op jit(solution)/shard_map/ppermute | solution.py:559
  169.7 13.7 %collective-permute-start.18 = (bf16[112,128]{1,0:T(8,128)(2,1)S(1)}, bf16[112,128]{1,0:T(8,128)(2,1)S(1)}, u32[]{:S(2)}, u32[]{:S(2)}) collective-permute-start(bf16[112,128]{1,0:T(8,128)(2,1)S(1)} %get-tuple-element.94.mine), channel_id=1, source_target_pairs={{0,8},{8,0},{1,9},{9,1},{2,10},{10,2},{3,11},{11,3},{4,12},{12,4},... | collective-permute-start | bytes 86024 | tf_op jit(solution)/shard_map/ppermute | solution.py:558
  184.2 14.3 %all-to-all-start.1 = ((bf16[4,304,128]{2,1,0:T(8,128)(2,1)}), bf16[4,304,128]{2,1,0:T(8,128)(2,1)S(1)}, u32[]{:S(2)}, u32[]{:S(2)}) async-start(bf16[4,304,128]{2,1,0:T(8,128)(2,1)} %get-tuple-element.95), calls=%async_computation.1 | async-start | bytes 622592 | tf_op jit(solution)/shard_map/all_to_all | solution.py:403
  198.4 14.5 %collective-permute-start.23 = (bf16[1216,128]{1,0:T(8,128)(2,1)S(1)}, bf16[1216,128]{1,0:T(8,128)(2,1)S(1)}, u32[]{:S(2)}, u32[]{:S(2)}) collective-permute-start(bf16[1216,128]{1,0:T(8,128)(2,1)S(1)} %bitcast.25), channel_id=1, source_target_pairs={{0,128},{128,256},{256,384},{384,0},{1,129},{129,257},{257,385},{3... | collective-permute-start | bytes 933896 | tf_op jit(solution)/shard_map/ppermute | solution.py:576
  200.4 14.6 %collective-permute-start.24 = (bf16[1216,128]{1,0:T(8,128)(2,1)S(1)}, bf16[1216,128]{1,0:T(8,128)(2,1)S(1)}, u32[]{:S(2)}, u32[]{:S(2)}) collective-permute-start(bf16[1216,128]{1,0:T(8,128)(2,1)S(1)} %bitcast.26), channel_id=1, source_target_pairs={{128,0},{256,128},{384,256},{0,384},{129,1},{257,129},{385,257},{1... | collective-permute-start | bytes 933896 | tf_op jit(solution)/shard_map/ppermute | solution.py:577
  205.0 14.6 %collective-permute-start.22 = (f32[112,128]{1,0:T(8,128)S(1)}, f32[112,128]{1,0:T(8,128)S(1)}, u32[]{:S(2)}, u32[]{:S(2)}) collective-permute-start(f32[112,128]{1,0:T(8,128)S(1)} %shard_map.172), channel_id=1, source_target_pairs={{0,1},{1,0},{2,3},{3,2},{4,5},{5,4},{6,7},{7,6},{8,9},{9,8},{10,11... | collective-permute-start | bytes 172040 | tf_op jit(solution)/shard_map/ppermute | solution.py:573
  213.0 7.6 %collective-permute-start.25 = (bf16[608,128]{1,0:T(8,128)(2,1)S(1)}, bf16[608,128]{1,0:T(8,128)(2,1)S(1)}, u32[]{:S(2)}, u32[]{:S(2)}) collective-permute-start(bf16[608,128]{1,0:T(8,128)(2,1)S(1)} %slice.85), channel_id=1, source_target_pairs={{0,128},{128,256},{256,384},{384,0},{1,129},{129,257},{257,385},{3... | collective-permute-start | bytes 466952 | tf_op jit(solution)/shard_map/ppermute | solution.py:578
  (17 other events, 106.0 us)
